TPU v7x, 32 devices: a whole 2x2x4 slice. The times are simulated.
32 devices in a mesh: ctx: 16 (over z, y, core), fsdp: 2 (over x).
Axes of the slice: x: 2, y: 2, z: 4, core: 2. Of those that a mesh axis runs over, the one named last changes fastest.
Arguments:
- tokens: bfloat16 [2048, 4096], P('ctx', 'fsdp'), may hold values from -130 to 130, as said below
- w_query: bfloat16 [4096, 4096], P('ctx', 'fsdp'), may hold values from -0.09375 to 0.09375
- key_matrix: bfloat16 [4096, 1024], P('ctx', 'fsdp'), may hold values from -0.09375 to 0.09375
- value_matrix: bfloat16 [4096, 1024], P('ctx', 'fsdp'), may hold values from -0.09375 to 0.09375
- w_out: bfloat16 [4096, 4096], P('fsdp', 'ctx'), may hold values from -0.75 to 0.75
Outputs:
- mixed: bfloat16 [2048, 4096], P('ctx', 'fsdp')
Inputs may be any that keep to these rules, and one draw needn't show every extreme that they name: `tokens`: no structure of the entries is promised.
All inputs are finite; a program needn't handle non-finite values.
Results may differ from a plain program's by a relative error of at most 0.014.
The roundings to bfloat16 on the way count: a program that leaves them out, or rounds other values in their place, can miss the bound.
Values may be sent and summed in bfloat16 or wider, within the bound.
No kernel may reach another device: no remote copies, remote signals or barrier semaphores. Data moves between devices by JAX's collectives and lax.ppermute only.
A program may use at most 128 MiB of HBM per device.

v0:
```python
import math

import jax
import jax.numpy as jnp
from jax import lax
from jax.sharding import PartitionSpec as P

HEAD_SIZE = 128


def rotate_heads(values, positions):
    tok_count = values.shape[0]
    head_count = values.shape[1] // HEAD_SIZE
    half_dim = HEAD_SIZE // 2
    inverse_freq = jnp.power(
        jnp.float32(500000.0), -jnp.arange(half_dim, dtype=jnp.float32) * 2.0 / HEAD_SIZE
    )
    angles = positions.astype(jnp.float32)[:, None] * inverse_freq[None, :]
    cosine = jnp.cos(angles)[:, None, :]
    sine_table = jnp.sin(angles)[:, None, :]
    shaped = values.reshape(tok_count, head_count, HEAD_SIZE)
    first_half = shaped[:, :, :half_dim]
    second = shaped[:, :, half_dim:]
    turned = jnp.concatenate(
        [first_half * cosine - second * sine_table, second * cosine + first_half * sine_table],
        axis=2,
    )
    return turned.reshape(tok_count, head_count * HEAD_SIZE).astype(jnp.bfloat16)


def body(tokens, w_query, key_matrix, value_matrix, w_out):
    features = lax.all_gather(tokens, "fsdp", axis=1, tiled=True)
    tok_count = features.shape[0]
    positions = lax.axis_index("ctx") * tok_count + jnp.arange(tok_count, dtype=jnp.int32)

    def add_rows(weight_piece):
        return jnp.dot(features, weight_piece, preferred_element_type=jnp.float32)

    query_sum = add_rows(lax.all_gather(w_query, "ctx", axis=0, tiled=True))
    key_sum = add_rows(lax.all_gather(key_matrix, "ctx", axis=0, tiled=True))
    value_sum = add_rows(lax.all_gather(value_matrix, "ctx", axis=0, tiled=True))
    queries = rotate_heads(query_sum, positions)
    projected_keys = rotate_heads(key_sum, positions)
    projected_values = value_sum.astype(jnp.bfloat16)
    kv_heads = projected_keys.shape[1] // HEAD_SIZE
    queries_per_group = queries.shape[1] // projected_keys.shape[1]
    stacked = (
        queries.reshape(tok_count, kv_heads, queries_per_group, HEAD_SIZE)
        .transpose(1, 2, 0, 3)
        .reshape(kv_heads, queries_per_group * tok_count, HEAD_SIZE)
    )
    query_pos = jnp.tile(positions, queries_per_group)
    score_scale = 1.0 / math.sqrt(HEAD_SIZE)

    def update(attn_state, key_block, value_block, key_start):
        row_max, row_total, accum = attn_state
        block_rows = key_block.shape[0]
        key_heads = key_block.reshape(block_rows, kv_heads, HEAD_SIZE)
        value_heads = value_block.reshape(block_rows, kv_heads, HEAD_SIZE)
        scores = (
            jnp.einsum("gqd,kgd->gqk", stacked, key_heads, preferred_element_type=jnp.float32)
            * score_scale
        )
        key_pos = key_start + jnp.arange(block_rows, dtype=jnp.int32)
        allowed = (key_pos[None, :] <= query_pos[:, None])[None]
        masked = jnp.where(allowed, scores, jnp.float32(-1e30))
        new_max = jnp.maximum(row_max, jnp.max(masked, axis=2))
        exp_weights = jnp.where(allowed, jnp.exp(masked - new_max[:, :, None]), jnp.float32(0.0))
        factor = jnp.exp(row_max - new_max)
        row_total = row_total * factor + jnp.sum(exp_weights, axis=2)
        accum = accum * factor[:, :, None] + jnp.einsum(
            "gqk,kgd->gqd",
            exp_weights.astype(jnp.bfloat16),
            value_heads,
            preferred_element_type=jnp.float32,
        )
        return (new_max, row_total, accum)

    query_rows = queries_per_group * tok_count
    initial = (
        jnp.full((kv_heads, query_rows), -1e30, jnp.float32),
        jnp.zeros((kv_heads, query_rows), jnp.float32),
        jnp.zeros((kv_heads, query_rows, HEAD_SIZE), jnp.float32),
    )
    key_piece = lax.all_gather(projected_keys, "ctx", axis=0, tiled=True)
    value_piece = lax.all_gather(projected_values, "ctx", axis=0, tiled=True)
    block_rows = min(tok_count, key_piece.shape[0])
    block_count = key_piece.shape[0] // block_rows

    def advance(block_index, carried):
        key_start = block_index * block_rows
        key_block = lax.dynamic_slice_in_dim(key_piece, block_index * block_rows, block_rows, 0)
        value_block = lax.dynamic_slice_in_dim(value_piece, block_index * block_rows, block_rows, 0)
        return update(carried, key_block, value_block, key_start)

    row_max, row_total, accum = lax.fori_loop(0, block_count, advance, initial)
    normed = accum / row_total[:, :, None]
    attn_out = (
        normed.reshape(kv_heads, queries_per_group, tok_count, HEAD_SIZE)
        .transpose(2, 0, 1, 3)
        .reshape(tok_count, kv_heads * queries_per_group * HEAD_SIZE)
        .astype(jnp.bfloat16)
    )
    partial_out = jnp.dot(
        attn_out,
        lax.all_gather(w_out, "ctx", axis=1, tiled=True),
        preferred_element_type=jnp.float32,
    )
    return lax.psum_scatter(
        partial_out.astype(jnp.bfloat16), "fsdp", scatter_dimension=1, tiled=True
    )


def solution(mesh):
    in_specs = (
        P("ctx", "fsdp"),
        P("ctx", "fsdp"),
        P("ctx", "fsdp"),
        P("ctx", "fsdp"),
        P("fsdp", "ctx"),
    )
    out_specs = P("ctx", "fsdp")
    return jax.shard_map(body, mesh=mesh, in_specs=in_specs, out_specs=out_specs, check_vma=False)
```

profile of v0, /device:TPU:0, one launch (start us, length us, event | category | flops | bytes accessed | tf_op | source)
XLA Modules:
  0.0 514.8 jit_solution(2823537085960351632)
XLA Ops:
  6.5 0.7 all-gather.8.cloned.1.call-update
  9.7 23.2 %all-gather.8.cloned.1.call-done = bf16[128,4096]{1,0:T(8,128)(2,1)} async-done(((bf16[128,2048]{1,0:T(8,128)(2,1)}), bf16[128,4096]{1,0:T(8,128)(2,1)}) %all-gather.8.cloned.1.call-update) | async-done | bytes 1048592 | tf_op jit(solution)/shard_map/all_gather | solution.py:32
  32.9 52.8 %all-gather.10.cloned.1.call-done = bf16[4096,512]{1,0:T(8,128)(2,1)} async-done(((bf16[256,512]{1,0:T(8,128)(2,1)}), bf16[4096,512]{1,0:T(8,128)(2,1)}) %all-gather.10.cloned.1.call-update) | async-done | bytes 4194320 | tf_op jit(solution)/shard_map/all_gather | solution.py:40
  85.7 3.2 fusion.14
  89.5 0.8 copy.17
  90.4 46.6 %all-gather.16.cloned.1.call-done = bf16[4096,512]{1,0:T(8,128)(2,1)} async-done(((bf16[256,512]{1,0:T(8,128)(2,1)}), bf16[4096,512]{1,0:T(8,128)(2,1)}) %all-gather.16.cloned.1.call-update) | async-done | bytes 4194320 | tf_op jit(solution)/shard_map/all_gather | solution.py:41
  137.0 3.6 convolution_convert_fusion.1
  140.6 0.7 all-gather.20.cloned.1.call-update
  141.4 123.0 %all-gather.14.cloned.1.call-done = bf16[4096,2048]{1,0:T(8,128)(2,1)} async-done(((bf16[256,2048]{1,0:T(8,128)(2,1)}), bf16[4096,2048]{1,0:T(8,128)(2,1)}) %all-gather.14.cloned.1.call-update) | async-done | bytes 16777232 | tf_op jit(solution)/shard_map/all_gather | solution.py:39
  264.4 8.1 %convolution_bitcast_fusion = f32[16,8,16,128]{3,1,2,0:T(8,128)S(1)} fusion(bf16[128,4096]{1,0:T(8,128)(2,1)S(1)} %copy-done, bf16[4096,2048]{1,0:T(8,128)(2,1)} %all-gather.14.cloned.1.call-done), kind=kOutput, calls=%fused_computation.23 | convolution fusion | flops 2147483648 | bytes 18874368 | tf_op jit(solution)/shard_map/dot_general | solution.py:37
  273.7 32.1 %all-gather.12.cloned.1.call-done = bf16[2048,512]{0,1:T(8,128)(2,1)} async-done(((bf16[128,512]{0,1:T(8,128)(2,1)}), bf16[2048,512]{0,1:T(8,128)(2,1)}) %all-gather.12.cloned.1.call-update) | async-done | bytes 2097168 | tf_op jit(solution)/shard_map/all_gather | solution.py:85
  305.8 42.4 %all-gather.18.cloned.1.call-done = bf16[2048,512]{1,0:T(8,128)(2,1)} async-done(((bf16[128,512]{1,0:T(8,128)(2,1)}), bf16[2048,512]{1,0:T(8,128)(2,1)}) %all-gather.18.cloned.1.call-update) | async-done | bytes 2097168 | tf_op jit(solution)/shard_map/all_gather | solution.py:86
  348.2 56.6 %while.18 = (s32[]{:T(128)}, f32[4,512]{1,0:T(4,128)S(1)}, f32[4,512]{1,0:T(4,128)S(1)}, f32[4,512,128]{2,1,0:T(8,128)S(1)}, bf16[2048,512]{0,1:T(8,128)(2,1)}, ...) while((s32[]{:T(128)}, f32[4,512]{1,0:T(4,128)S(1)}, ...), condition=%wide.region_3.4_spmd.clone, body=%wide.region_0.3_spmd.clone.sunk | while | flops 137439360 | bytes 7214779 | solution.py:96
  348.2 0.9 constant_dynamic-slice_fusion.4
  349.9 0.9 constant_dynamic-slice_fusion.5
  350.9 0.7 convolution_add_fusion.2
  351.7 0.9 constant_dynamic-slice_fusion.4
  353.4 0.9 constant_dynamic-slice_fusion.5
  354.5 0.7 convolution_add_fusion.2
  355.2 0.9 constant_dynamic-slice_fusion.4
  357.0 0.9 constant_dynamic-slice_fusion.5
  358.0 0.7 convolution_add_fusion.2
  358.8 0.9 constant_dynamic-slice_fusion.4
  360.5 0.9 constant_dynamic-slice_fusion.5
  361.6 0.7 convolution_add_fusion.2
  362.3 0.9 constant_dynamic-slice_fusion.4
  364.1 0.9 constant_dynamic-slice_fusion.5
  365.1 0.7 convolution_add_fusion.2
  365.9 0.9 constant_dynamic-slice_fusion.4
  367.6 0.9 constant_dynamic-slice_fusion.5
  368.6 0.7 convolution_add_fusion.2
  369.4 0.9 constant_dynamic-slice_fusion.4
  371.1 0.9 constant_dynamic-slice_fusion.5
  372.2 0.7 convolution_add_fusion.2
  372.9 0.9 constant_dynamic-slice_fusion.4
  374.6 0.9 constant_dynamic-slice_fusion.5
  375.7 0.7 convolution_add_fusion.2
  376.5 0.9 constant_dynamic-slice_fusion.4
  378.2 0.9 constant_dynamic-slice_fusion.5
  379.2 0.7 convolution_add_fusion.2
  380.0 0.9 constant_dynamic-slice_fusion.4
  381.7 0.9 constant_dynamic-slice_fusion.5
  382.8 0.7 convolution_add_fusion.2
  383.5 0.9 constant_dynamic-slice_fusion.4
  385.2 0.9 constant_dynamic-slice_fusion.5
  386.3 0.7 convolution_add_fusion.2
  387.0 0.9 constant_dynamic-slice_fusion.4
  388.8 0.9 constant_dynamic-slice_fusion.5
  389.8 0.7 convolution_add_fusion.2
  390.6 0.9 constant_dynamic-slice_fusion.4
  392.3 0.9 constant_dynamic-slice_fusion.5
  393.3 0.7 convolution_add_fusion.2
  394.1 0.9 constant_dynamic-slice_fusion.4
  395.8 0.9 constant_dynamic-slice_fusion.5
  396.9 0.7 convolution_add_fusion.2
  397.6 0.9 constant_dynamic-slice_fusion.4
  399.3 0.9 constant_dynamic-slice_fusion.5
  400.4 0.7 convolution_add_fusion.2
  401.2 1.0 constant_dynamic-slice_fusion.4
  402.9 0.9 constant_dynamic-slice_fusion.5
  404.0 0.7 convolution_add_fusion.2
  405.4 75.0 %all-gather.20.cloned.1.call-done = bf16[2048,4096]{1,0:T(8,128)(2,1)} async-done(((bf16[2048,256]{1,0:T(8,128)(2,1)}), bf16[2048,4096]{1,0:T(8,128)(2,1)}) %all-gather.20.cloned.1.call-update) | async-done | bytes 16777232 | tf_op jit(solution)/shard_map/all_gather | solution.py:106
  480.4 9.1 %convolution_convert_fusion = bf16[128,4096]{1,0:T(8,128)(2,1)} fusion(bf16[128,2048]{0,1:T(8,128)(2,1)S(1)} %bitcast.47, bf16[2048,4096]{1,0:T(8,128)(2,1)} %all-gather.20.cloned.1.call-done), kind=kOutput, calls=%fused_computation.22 | convolution fusion | flops 2148007936 | bytes 18350080 | tf_op jit(solution)/shard_map/dot_general | solution.py:104
  489.6 18.4 %reduce-scatter.2.cloned.1.call-done = bf16[128,2048]{1,0:T(8,128)(2,1)} async-done(((bf16[128,4096]{1,0:T(8,128)(2,1)}), bf16[128,2048]{1,0:T(8,128)(2,1)}) %reduce-scatter.2.cloned.1.call-update) | async-done | bytes 524304 | tf_op jit(solution)/shard_map/reduce_scatter | solution.py:109
  (176 shorter events, 18.8 us)
Async XLA Ops:
  6.5 26.4 %all-gather.8.cloned.1.call-start = ((), (), s32[]{:S(2)}) async-start(), calls=%async_computation.1 | async-start | bytes 1572864 | tf_op jit(solution)/shard_map/all_gather | solution.py:32
  7.3 78.4 %all-gather.10.cloned.1.call-start = ((), (), s32[]{:S(2)}) async-start(), calls=%async_computation.2 | async-start | bytes 4456448 | tf_op jit(solution)/shard_map/all_gather | solution.py:40
  8.0 128.9 %all-gather.16.cloned.1.call-start = ((), (), s32[]{:S(2)}) async-start(), calls=%async_computation.5 | async-start | bytes 4456448 | tf_op jit(solution)/shard_map/all_gather | solution.py:41
  8.7 255.6 %all-gather.14.cloned.1.call-start = ((), (), s32[]{:S(2)}) async-start(), calls=%async_computation.4 | async-start | bytes 17825792 | tf_op jit(solution)/shard_map/all_gather | solution.py:39
  9.3 296.5 %all-gather.12.cloned.1.call-start = ((), (), s32[]{:S(2)}) async-start(), calls=%async_computation.3 | async-start | bytes 2228224 | tf_op jit(solution)/shard_map/all_gather | solution.py:85
  32.9 104.0 %copy-start = (bf16[128,4096]{1,0:T(8,128)(2,1)S(1)}, bf16[128,4096]{1,0:T(8,128)(2,1)}, u32[]{:S(2)}) copy-start(bf16[128,4096]{1,0:T(8,128)(2,1)} %all-gather.8.cloned.1.call-done) | copy-start | bytes 3145732
  90.3 257.8 %all-gather.18.cloned.1.call-start = ((), (), s32[]{:S(2)}) async-start(), calls=%async_computation.6 | async-start | bytes 2228224 | tf_op jit(solution)/shard_map/all_gather | solution.py:86
  140.5 339.9 %all-gather.20.cloned.1.call-start = ((), (), s32[]{:S(2)}) async-start(), calls=%async_computation.7 | async-start | bytes 17825792 | tf_op jit(solution)/shard_map/all_gather | solution.py:106
  141.3 366.7 %reduce-scatter.2.cloned.1.call-start = ((), (), s32[]{:S(2)}) async-start(), calls=%async_computation.8 | async-start | bytes 1572864 | tf_op jit(solution)/shard_map/reduce_scatter | solution.py:109
Sparse Core Ops, SparseCore 0:
  8.9 23.9 all-gather.7
  35.1 50.5 all-gather.9
  87.9 49.0 all-gather.15
  139.0 125.3 all-gather.13
  266.4 39.3 all-gather.11
  307.8 40.3 all-gather.17
  350.3 130.0 all-gather.19
  489.7 18.2 reduce-scatter.1
where the time goes:
time: 516 us; the launch traced here: 515 us
  waiting for transfers between devices  417 us (81%)
  matrix products  41.9 us (8%)
  local copies, waits for them, and re-layouts  33 us (6%)
  between operations  13.6 us (3%)
  other arithmetic  7.6 us (1%)
    all_gather x1, waiting for transfers between devices, body(): query_sum = add_rows(lax.all_gather(w_query, 'ctx', axis=0, tiled=True))  123 us
    all_gather x1, waiting for transfers between devices, body(): lax.all_gather(w_out, 'ctx', axis=1, tiled=True)  75 us
    all_gather x1, waiting for transfers between devices, body(): key_sum = add_rows(lax.all_gather(key_matrix, 'ctx', axis=0, tiled=True))  52.8 us
    all_gather x1, waiting for transfers between devices, body(): lax.all_gather(value_matrix, 'ctx', axis=0, tiled=True)  46.6 us
    all_gather x1, waiting for transfers between devices, body(): value_piece = lax.all_gather(projected_values, 'ctx', axis=0, tiled=True)  42.4 us
    all_gather x1, waiting for transfers between devices, body(): key_piece = lax.all_gather(projected_keys, 'ctx', axis=0, tiled=True)  32.1 us
    all_gather x1, waiting for transfers between devices, body(): features = lax.all_gather(tokens, 'fsdp', axis=1, tiled=True)  23.2 us
    reduce_scatter x1, waiting for transfers between devices, body(): lax.psum_scatter(partial_out.astype(jnp.bfloat16), 'fsdp', scatter_dimens...  18.4 us
  transfers between devices with their start and end apart: 8, of which 8 were waited for; matrix products, arithmetic and copies ran while one was open for 14% of the time, Pallas kernels for 0%

commit v1 on v0

--- a/solution.py
+++ b/solution.py
@@ -1,23 +1,33 @@
+import functools
 import math
 
 import jax
 import jax.numpy as jnp
 from jax import lax
+from jax.experimental import pallas as pl
+from jax.experimental.pallas import tpu as pltpu
 from jax.sharding import PartitionSpec as P
 
 HEAD_SIZE = 128
+AXES = ("ctx", "fsdp")
+VMEM_LIMIT = 48 * 1024 * 1024
+
+
+def rotary_tables(positions):
+    half_dim = HEAD_SIZE // 2
+    inverse_freq = jnp.power(
+        jnp.float32(500000.0), -jnp.arange(half_dim, dtype=jnp.float32) * 2.0 / HEAD_SIZE
+    )
+    angles = positions.astype(jnp.float32)[:, None] * inverse_freq[None, :]
+    return jnp.cos(angles), jnp.sin(angles)
 
 
 def rotate_heads(values, positions):
     tok_count = values.shape[0]
     head_count = values.shape[1] // HEAD_SIZE
     half_dim = HEAD_SIZE // 2
-    inverse_freq = jnp.power(
-        jnp.float32(500000.0), -jnp.arange(half_dim, dtype=jnp.float32) * 2.0 / HEAD_SIZE
-    )
-    angles = positions.astype(jnp.float32)[:, None] * inverse_freq[None, :]
-    cosine = jnp.cos(angles)[:, None, :]
-    sine_table = jnp.sin(angles)[:, None, :]
+    cosine, sine_table = rotary_tables(positions)
+    cosine, sine_table = cosine[:, None, :], sine_table[:, None, :]
     shaped = values.reshape(tok_count, head_count, HEAD_SIZE)
     first_half = shaped[:, :, :half_dim]
     second = shaped[:, :, half_dim:]
@@ -28,7 +38,7 @@
     return turned.reshape(tok_count, head_count * HEAD_SIZE).astype(jnp.bfloat16)
 
 
-def body(tokens, w_query, key_matrix, value_matrix, w_out):
+def gathered_body(tokens, w_query, key_matrix, value_matrix, w_out):
     features = lax.all_gather(tokens, "fsdp", axis=1, tiled=True)
     tok_count = features.shape[0]
     positions = lax.axis_index("ctx") * tok_count + jnp.arange(tok_count, dtype=jnp.int32)
@@ -111,6 +121,344 @@
     )
 
 
+def moves(target):
+    pairs = []
+    for i in range(32):
+        z, y, c, x = i // 8, i // 4 % 2, i // 2 % 2, i % 2
+        tz, ty, tc, tx = target(z, y, c, x)
+        pairs.append((i, tz * 8 + ty * 4 + tc * 2 + tx))
+    return pairs
+
+
+def move(array, target):
+    return lax.ppermute(array, AXES, moves(target))
+
+
+def across_z(array, m):
+    return move(array, lambda z, y, c, x: (z ^ m, y, c, x))
+
+
+def across_y(array):
+    return move(array, lambda z, y, c, x: (z, 1 - y, c, x))
+
+
+def across_core(array):
+    return move(array, lambda z, y, c, x: (z, y, 1 - c, x))
+
+
+def across_x(array):
+    return move(array, lambda z, y, c, x: (z, y, c, 1 - x))
+
+
+def any_specs(count):
+    return [pl.BlockSpec(memory_space=pl.ANY)] * count
+
+
+def smem_spec():
+    return pl.BlockSpec(memory_space=pltpu.SMEM)
+
+
+def vmem_spec():
+    return pl.BlockSpec(memory_space=pltpu.VMEM)
+
+
+def load_projection(place, token_refs, weight_refs, tok, wgt, sems):
+    ctx, x = place[0], place[1]
+    rows, half = token_refs[0].shape
+    copies = []
+    for m in range(4):
+        for rx in range(2):
+            into = tok.at[pl.ds(m * rows, rows), pl.ds(pl.multiple_of((x ^ rx) * half, half), half)]
+            copies.append((token_refs[m * 2 + rx], into))
+    for r, ref in enumerate(weight_refs):
+        for m in range(4):
+            block = ctx ^ (4 * m + r)
+            depth = ref.shape[1]
+            copies.append((ref.at[m], wgt.at[pl.ds(pl.multiple_of(block * depth, depth), depth)]))
+    handles = [pltpu.make_async_copy(s, d, sems.at[i]) for i, (s, d) in enumerate(copies)]
+    for handle in handles:
+        handle.start()
+    for handle in handles:
+        handle.wait()
+
+
+def rotated(values, cosine, sine):
+    turned = jnp.concatenate([values[:, HEAD_SIZE // 2 :], values[:, : HEAD_SIZE // 2]], axis=1)
+    return values * cosine + turned * sine
+
+
+def kv_kernel(place, *refs):
+    token_refs, weight_refs = refs[:8], refs[8:12]
+    cosine, sine, out, tok, wgt, sems = refs[12:]
+    load_projection(place, token_refs, weight_refs, tok, wgt, sems)
+    rows = tok.shape[0] // 4
+    values = jnp.dot(tok[...], wgt[...], preferred_element_type=jnp.float32)
+    keys = rotated(values[:, :HEAD_SIZE], cosine[...], sine[...]).astype(jnp.bfloat16)
+    vals = values[:, HEAD_SIZE:].astype(jnp.bfloat16)
+    for m in range(4):
+        out[m, :, :HEAD_SIZE] = keys[m * rows : (m + 1) * rows]
+        out[m, :, HEAD_SIZE:] = vals[m * rows : (m + 1) * rows]
+
+
+def query_kernel(place, *refs):
+    token_refs, weight_refs = refs[:8], refs[8:12]
+    cosine, sine, out, tok, wgt, sems = refs[12:]
+    load_projection(place, token_refs, weight_refs, tok, wgt, sems)
+    rows = tok.shape[0] // 4
+    heads = wgt.shape[1] // HEAD_SIZE
+    for pair in range(heads // 2):
+        values = jnp.dot(
+            tok[...],
+            wgt[:, pair * 2 * HEAD_SIZE : (pair + 1) * 2 * HEAD_SIZE],
+            preferred_element_type=jnp.float32,
+        )
+        for k in range(2):
+            one = rotated(values[:, k * HEAD_SIZE : (k + 1) * HEAD_SIZE], cosine[...], sine[...])
+            one = one.astype(jnp.bfloat16)
+            head = pair * 2 + k
+            for m in range(4):
+                out[m, head * rows : (head + 1) * rows, :] = one[m * rows : (m + 1) * rows]
+
+
+def project(kernel, out_shape, place, tokens, weights, cosine, sine):
+    rows, half = tokens[0].shape
+    _, depth, width = weights[0].shape
+    flops = 2 * 4 * rows * 16 * depth * width
+    return pl.pallas_call(
+        kernel,
+        out_shape=jax.ShapeDtypeStruct(out_shape, jnp.bfloat16),
+        in_specs=[smem_spec()] + any_specs(12) + [vmem_spec()] * 2,
+        out_specs=vmem_spec(),
+        scratch_shapes=[
+            pltpu.VMEM((4 * rows, 2 * half), jnp.bfloat16),
+            pltpu.VMEM((16 * depth, width), jnp.bfloat16),
+            pltpu.SemaphoreType.DMA((24,)),
+        ],
+        compiler_params=pltpu.CompilerParams(vmem_limit_bytes=VMEM_LIMIT),
+        cost_estimate=pl.CostEstimate(flops=flops, bytes_accessed=8 << 20, transcendentals=0),
+    )(place, *tokens, *weights, cosine, sine)
+
+
+def attend_kernel(place, queries, kv0, kv1, kv2, kv3, mine, other, store, sems):
+    ctx, x = place[0], place[1]
+    rows = kv0.shape[1]
+    handles = []
+    for r, ref in enumerate((kv0, kv1, kv2, kv3)):
+        for m in range(4):
+            block = ctx ^ (4 * m + r)
+            into = store.at[pl.ds(pl.multiple_of(block * rows, rows), rows)]
+            handles.append(pltpu.make_async_copy(ref.at[m], into, sems.at[4 * r + m]))
+    for handle in handles:
+        handle.start()
+    for handle in handles:
+        handle.wait()
+    z, e = ctx // 4, ctx % 4
+    scale = 1.0 / math.sqrt(HEAD_SIZE)
+    span = 4 * rows
+    heads = queries.shape[1] // rows
+    group = 2
+    for block in range(4):
+        count = (block + 1) * span
+        slot = z ^ block
+        keys, values = store[:count, :HEAD_SIZE], store[:count, HEAD_SIZE:]
+        row = lax.broadcasted_iota(jnp.int32, (group * rows, span), 0) % rows + e * rows
+        column = lax.broadcasted_iota(jnp.int32, (group * rows, span), 1)
+        allowed = column <= row
+        for first in range(0, heads, group):
+            query = queries[slot, pl.ds(first * rows, group * rows), :]
+            scores = lax.dot_general(
+                query, keys, (((1,), (1,)), ((), ())), preferred_element_type=jnp.float32
+            ) * jnp.float32(scale)
+            last = jnp.where(allowed, scores[:, count - span :], jnp.float32(-1e30))
+            scores = jnp.concatenate([scores[:, : count - span], last], axis=1) if block else last
+            top = jnp.max(scores, axis=1, keepdims=True)
+            weights = jnp.exp(scores - top)
+            total = jnp.sum(weights, axis=1, keepdims=True)
+            summed = jnp.dot(
+                weights.astype(jnp.bfloat16), values, preferred_element_type=jnp.float32
+            )
+            normed = (summed / total).astype(jnp.bfloat16)
+            for k in range(group):
+                head = first + k
+                piece = normed[k * rows : (k + 1) * rows]
+
+                @pl.when(x == block // 2)
+                def _():
+                    mine[block % 2, :, head * HEAD_SIZE : (head + 1) * HEAD_SIZE] = piece
+
+                @pl.when(x != block // 2)
+                def _():
+                    other[block % 2, :, head * HEAD_SIZE : (head + 1) * HEAD_SIZE] = piece
+
+
+def attend(place, queries, kv):
+    _, stacked, _ = queries.shape
+    rows = kv[0].shape[1]
+    heads = stacked // rows
+    shape = jax.ShapeDtypeStruct((2, rows, heads * HEAD_SIZE), jnp.bfloat16)
+    work = 4 * stacked * 16 * rows * HEAD_SIZE
+    return pl.pallas_call(
+        attend_kernel,
+        out_shape=(shape, shape),
+        in_specs=[smem_spec(), vmem_spec()] + any_specs(4),
+        out_specs=(vmem_spec(), vmem_spec()),
+        scratch_shapes=[
+            pltpu.VMEM((16 * rows, 2 * HEAD_SIZE), jnp.bfloat16),
+            pltpu.SemaphoreType.DMA((16,)),
+        ],
+        compiler_params=pltpu.CompilerParams(vmem_limit_bytes=VMEM_LIMIT),
+        cost_estimate=pl.CostEstimate(
+            flops=4 * work, bytes_accessed=4 << 20, transcendentals=4 * stacked * 16 * rows
+        ),
+    )(place, queries, *kv)
+
+
+def output_kernel(place, *refs):
+    attn_refs, weight_refs = refs[:8], refs[8:16]
+    out0, out1, attn, wgt, sems = refs[16:]
+    ctx, x = place[0], place[1]
+    z, y, c = ctx // 4, ctx // 2 % 2, ctx % 2
+    _, rows, width = attn_refs[0].shape
+    depth, cols = weight_refs[0].shape
+    handles = []
+    for rx in range(2):
+        for m in range(4):
+            at = (x ^ rx) * depth + (z ^ m) * width
+            into = attn.at[:, :, pl.ds(pl.multiple_of(at, width), width)]
+            n = rx * 4 + m
+            handles.append(pltpu.make_async_copy(attn_refs[n], into, sems.at[n]))
+    for n in range(8):
+        ry, rx, rc = n // 4, n // 2 % 2, n % 2
+        at = ((y ^ ry) * 2 + (c ^ rc)) * cols
+        into = wgt.at[
+            pl.ds(pl.multiple_of((x ^ rx) * depth, depth), depth),
+            pl.ds(pl.multiple_of(at, cols), cols),
+        ]
+        handles.append(pltpu.make_async_copy(weight_refs[n], into, sems.at[8 + n]))
+    for handle in handles:
+        handle.start()
+    for handle in handles:
+        handle.wait()
+    low = z % 2
+    for part in range(4):
+        at = slice(part * cols, (part + 1) * cols)
+        terms = []
+        for f in range(2):
+            term = jnp.dot(
+                attn[:, :, f * depth : (f + 1) * depth].reshape(2 * rows, depth),
+                wgt[f * depth : (f + 1) * depth, at],
+                preferred_element_type=jnp.float32,
+            )
+            terms.append(term.astype(jnp.bfloat16).astype(jnp.float32))
+        mixed = (terms[0] + terms[1]).astype(jnp.bfloat16)
+        first, second = mixed[:rows], mixed[rows:]
+
+        @pl.when(low == 0)
+        def _():
+            out0[:, at] = first
+            out1[:, at] = second
+
+        @pl.when(low == 1)
+        def _():
+            out0[:, at] = second
+            out1[:, at] = first
+
+
+def project_out(place, attn, weights):
+    _, rows, width = attn[0].shape
+    depth, cols = weights[0].shape
+    shape = jax.ShapeDtypeStruct((rows, 4 * cols), jnp.bfloat16)
+    return pl.pallas_call(
+        output_kernel,
+        out_shape=(shape, shape),
+        in_specs=[smem_spec()] + any_specs(16),
+        out_specs=(vmem_spec(), vmem_spec()),
+        scratch_shapes=[
+            pltpu.VMEM((2, rows, 2 * depth), jnp.bfloat16),
+            pltpu.VMEM((2 * depth, 4 * cols), jnp.bfloat16),
+            pltpu.SemaphoreType.DMA((16,)),
+        ],
+        compiler_params=pltpu.CompilerParams(vmem_limit_bytes=VMEM_LIMIT),
+        cost_estimate=pl.CostEstimate(
+            flops=2 * 2 * rows * 2 * depth * 4 * cols, bytes_accessed=12 << 20, transcendentals=0
+        ),
+    )(place, *attn, *weights)
+
+
+def spread_weights(weight, z):
+    width = weight.shape[1] // 4
+
+    def piece(m):
+        return lax.dynamic_slice_in_dim(weight, (z ^ m) * width, width, 1)
+
+    own = jnp.stack([piece(0)] + [across_z(piece(m), m) for m in (1, 2, 3)])
+    over_y = across_y(own)
+    return [own, across_core(own), over_y, across_core(over_y)]
+
+
+def split_body(tokens, w_query, key_matrix, value_matrix, w_out):
+    ctx, x = lax.axis_index("ctx"), lax.axis_index("fsdp")
+    place = jnp.stack([ctx, x]).astype(jnp.int32)
+    z = ctx // 4
+    rows = tokens.shape[0]
+
+    head_major = jnp.concatenate(
+        [
+            key_matrix.reshape(-1, 4, HEAD_SIZE),
+            value_matrix.reshape(-1, 4, HEAD_SIZE),
+        ],
+        axis=2,
+    ).reshape(key_matrix.shape[0], -1)
+    kv_weights = spread_weights(head_major, z)
+    over_z = [tokens] + [across_z(tokens, m) for m in (1, 2, 3)]
+    token_pieces = []
+    for piece in over_z:
+        token_pieces += [piece, across_x(piece)]
+
+    slot = jnp.arange(4, dtype=jnp.int32)[:, None]
+    positions = (ctx ^ (4 * slot)) * rows + jnp.arange(rows, dtype=jnp.int32)[None, :]
+    cosine, sine = rotary_tables(positions.reshape(-1))
+    cosine = jnp.concatenate([cosine, cosine], axis=1)
+    sine = jnp.concatenate([-sine, sine], axis=1)
+
+    own_kv = project(
+        kv_kernel, (4, rows, 2 * HEAD_SIZE), place, token_pieces, kv_weights, cosine, sine
+    )
+    y_kv = across_y(own_kv)
+    kv = [own_kv, across_core(own_kv), y_kv, across_core(y_kv)]
+
+    query_weights = spread_weights(w_query, z)
+    group = w_query.shape[1] // 4
+    queries = project(
+        query_kernel,
+        (4, group // HEAD_SIZE * rows, HEAD_SIZE),
+        place,
+        token_pieces,
+        query_weights,
+        cosine,
+        sine,
+    )
+    mine, other = attend(place, queries, kv)
+    from_x = across_x(other)
+    attn = [mine] + [across_z(mine, m) for m in (1, 2, 3)]
+    attn += [from_x] + [across_z(from_x, m) for m in (1, 2, 3)]
+
+    y_out = across_y(w_out)
+    out_weights = []
+    for piece in (w_out, across_x(w_out), y_out, across_x(y_out)):
+        out_weights += [piece, across_core(piece)]
+    first, second = project_out(place, attn, out_weights)
+
+    def home(m):
+        return lambda z, y, c, x: (2 * x + (z % 2 ^ m), y, c, z // 2)
+
+    first, second = move(first, home(0)), move(second, home(1))
+    odd = z % 2 == 1
+    return jnp.concatenate(
+        [jnp.where(odd, second, first), jnp.where(odd, first, second)], axis=1
+    )
+
+
 def solution(mesh):
     in_specs = (
         P("ctx", "fsdp"),
@@ -120,4 +468,6 @@
         P("fsdp", "ctx"),
     )
     out_specs = P("ctx", "fsdp")
+    split = mesh.shape["ctx"] == 16 and mesh.shape["fsdp"] == 2
+    body = split_body if split else gathered_body
     return jax.shard_map(body, mesh=mesh, in_specs=in_specs, out_specs=out_specs, check_vma=False)

time: 516 us -> 263 us (0.51)
  the two profiles are of different devices: /device:TPU:0 before, /device:TPU:2 now
where the time goes in v1:
time: 263 us
  waiting for transfers between devices  165 us (63%)
  starting transfers between devices  56.3 us (21%)
  Pallas kernels  26.8 us (10%)
  local copies, waits for them, and re-layouts  10.5 us (4%)
  other arithmetic  3.67 us (1%)
    ppermute x38, waiting for transfers between devices, move(): return lax.ppermute(array, AXES, moves(target))  165 us
    ppermute x38, starting transfers between devices, move(): return lax.ppermute(array, AXES, moves(target))  56.3 us
    pallas_call x2, Pallas kernels, project(): pl.pallas_call(kernel, out_shape=jax.ShapeDtypeStruct(out_shape, jnp.bflo...  10.9 us
    unnamed x35, local copies, waits for them, and re-layouts  9.23 us
    pallas_call x1, Pallas kernels, attend(): pl.pallas_call(attend_kernel, out_shape=(shape, shape), in_specs=[smem_sp...  9.05 us
    pallas_call x1, Pallas kernels, project_out(): pl.pallas_call(output_kernel, out_shape=(shape, shape), in_specs=[smem_sp...  6.93 us
  transfers between devices with their start and end apart: 38, of which 16 were waited for; matrix products, arithmetic and copies ran while one was open for 1% of the time, Pallas kernels for 8%

profile of v1, /device:TPU:2, one launch (start us, length us, event | category | flops | bytes accessed | tf_op | source)
XLA Modules:
  0.0 263.0 jit_solution(4497547870908796402)
XLA Ops:
  0.0 1.1 reshape.39
  1.1 0.3 pad_maximum_fusion.1
  1.7 3.7 %collective-permute-start.15 = (bf16[256,256]{1,0:T(8,128)(2,1)S(1)}, bf16[256,256]{1,0:T(8,128)(2,1)S(1)}, u32[]{:S(2)}, u32[]{:S(2)}) collective-permute-start(bf16[256,256]{1,0:T(8,128)(2,1)S(1)} %get-tuple-element.20), channel_id=1, source_target_pairs={{0,24},{1,25},{2,26},{3,27},{4,28},{5,29},{6,30},{7,31},{8,16},{9,... | collective-permute-start | bytes 393224 | tf_op jit(solution)/shard_map/ppermute | solution.py:134
  5.3 1.0 collective-permute-start.5
  6.5 2.9 %collective-permute-start.9 = (bf16[256,512]{1,0:T(8,128)(2,1)S(1)}, bf16[256,512]{1,0:T(8,128)(2,1)S(1)}, u32[]{:S(2)}, u32[]{:S(2)}) collective-permute-start(bf16[256,512]{1,0:T(8,128)(2,1)S(1)} %get-tuple-element.15), channel_id=1, source_target_pairs={{0,24},{1,25},{2,26},{3,27},{4,28},{5,29},{6,30},{7,31},{8,16},{9,... | collective-permute-start | bytes 786440 | tf_op jit(solution)/shard_map/ppermute | solution.py:134
  9.4 0.5 collective-permute-start.14
  9.9 13.6 %collective-permute-start.13 = (bf16[256,256]{1,0:T(8,128)(2,1)S(1)}, bf16[256,256]{1,0:T(8,128)(2,1)S(1)}, u32[]{:S(2)}, u32[]{:S(2)}) collective-permute-start(bf16[256,256]{1,0:T(8,128)(2,1)S(1)} %get-tuple-element.22), channel_id=1, source_target_pairs={{0,8},{1,9},{2,10},{3,11},{4,12},{5,13},{6,14},{7,15},{8,0},{9,1},... | collective-permute-start | bytes 393224 | tf_op jit(solution)/shard_map/ppermute | solution.py:134
  23.5 26.6 %collective-permute-done.14 = bf16[256,256]{1,0:T(8,128)(2,1)S(1)} collective-permute-done((bf16[256,256]{1,0:T(8,128)(2,1)S(1)}, bf16[256,256]{1,0:T(8,128)(2,1)S(1)}, u32[]{:S(2)}, u32[]{:S(2)}) %collective-permute-start.14) | collective-permute-done | bytes 131104 | tf_op jit(solution)/shard_map/ppermute | solution.py:134
  50.1 2.9 %collective-permute-start.3 = (bf16[128,2048]{1,0:T(8,128)(2,1)S(1)}, bf16[128,2048]{1,0:T(8,128)(2,1)S(1)}, u32[]{:S(2)}, u32[]{:S(2)}) collective-permute-start(bf16[128,2048]{1,0:T(8,128)(2,1)S(1)} %copy-done), channel_id=1, source_target_pairs={{0,16},{1,17},{2,18},{3,19},{4,20},{5,21},{6,22},{7,23},{8,24},{9,... | collective-permute-start | bytes 1572872 | tf_op jit(solution)/shard_map/ppermute | solution.py:134
  53.0 0.2 collective-permute-start.1
  53.2 0.5 collective-permute-start
  53.8 21.1 %collective-permute-done.8 = bf16[256,512]{1,0:T(8,128)(2,1)S(1)} collective-permute-done((bf16[256,512]{1,0:T(8,128)(2,1)S(1)}, bf16[256,512]{1,0:T(8,128)(2,1)S(1)}, u32[]{:S(2)}, u32[]{:S(2)}) %collective-permute-start.8) | collective-permute-done | bytes 262176 | tf_op jit(solution)/shard_map/ppermute | solution.py:134
  75.0 1.5 collective-permute-start.17
  76.5 9.6 %collective-permute-done.3.refs_4_ = bf16[128,2048]{1,0:T(8,128)(2,1)S(1)} collective-permute-done((bf16[128,2048]{1,0:T(8,128)(2,1)S(1)}, bf16[128,2048]{1,0:T(8,128)(2,1)S(1)}, u32[]{:S(2)}, u32[]{:S(2)}) %collective-permute-start.3) | collective-permute-done | bytes 524320 | tf_op jit(solution)/shard_map/ppermute | solution.py:134
  86.1 0.5 collective-permute-start.6
  86.6 1.5 collective-permute-start.4
  88.1 1.5 collective-permute-start.32
  89.7 1.1 pad_maximum_fusion.refs_8_
  90.8 0.5 collective-permute-start.11
  91.3 0.9 copy-done.9
  92.1 0.5 collective-permute-start.2
  92.7 8.2 %collective-permute-done.6.refs_7_ = bf16[128,2048]{1,0:T(8,128)(2,1)S(1)} collective-permute-done((bf16[128,2048]{1,0:T(8,128)(2,1)S(1)}, bf16[128,2048]{1,0:T(8,128)(2,1)S(1)}, u32[]{:S(2)}, u32[]{:S(2)}) %collective-permute-start.6) | collective-permute-done | bytes 524320 | tf_op jit(solution)/shard_map/ppermute | solution.py:134
  100.9 0.5 collective-permute-start.30
  101.4 10.7 %collective-permute-done.4.refs_5_ = bf16[128,2048]{1,0:T(8,128)(2,1)S(1)} collective-permute-done((bf16[128,2048]{1,0:T(8,128)(2,1)S(1)}, bf16[128,2048]{1,0:T(8,128)(2,1)S(1)}, u32[]{:S(2)}, u32[]{:S(2)}) %collective-permute-start.4) | collective-permute-done | bytes 524320 | tf_op jit(solution)/shard_map/ppermute | solution.py:134
  112.1 0.8 copy-done.3
  113.0 10.4 %collective-permute-done.2.refs_3_ = bf16[128,2048]{1,0:T(8,128)(2,1)S(1)} collective-permute-done((bf16[128,2048]{1,0:T(8,128)(2,1)S(1)}, bf16[128,2048]{1,0:T(8,128)(2,1)S(1)}, u32[]{:S(2)}, u32[]{:S(2)}) %collective-permute-start.2) | collective-permute-done | bytes 524320 | tf_op jit(solution)/shard_map/ppermute | solution.py:134
  123.4 0.8 copy-done.5
  124.2 1.0 fusion
  125.2 0.6 collective-permute-start.34
  125.8 0.2 pad_maximum_fusion.4
  126.0 9.5 %collective-permute-done.11.refs_10_ = bf16[4,256,512]{2,1,0:T(8,128)(2,1)} collective-permute-done((bf16[4,256,512]{2,1,0:T(8,128)(2,1)}, bf16[4,256,512]{2,1,0:T(8,128)(2,1)}, u32[]{:S(2)}, u32[]{:S(2)}) %collective-permute-start.11) | collective-permute-done | bytes 1048608 | tf_op jit(solution)/shard_map/ppermute | solution.py:134
  135.5 1.0 copy-done.2
  136.6 1.0 copy-done.4
  137.6 1.0 copy-done.6
  138.7 1.0 copy-done.8
  139.7 1.0 copy-done.10
  140.7 5.2 %shard_map.56.kv0 = bf16[4,128,256]{2,1,0:T(8,128)(2,1)S(1)} custom-call(s32[2]{0:T(128)S(1)} %pad_add_fusion.place, bf16[128,2048]{1,0:T(8,128)(2,1)S(1)} %copy-done, bf16[128,2048]{1,0:T(8,128)(2,1)S(1)} %collective-permute-done.refs_1_, bf16[128,2048]{1,0:T(8,128)(2,1)S(1)} %collective-permute-done.1.refs_2_, bf16[128,2048]{1,0:T(8,128)(2,1)S(1)} %copy-done.6, ...), custom_call_target="tpu_custom_call" | custom-call | flops 1073741824 | bytes 8388608 | tf_op jit(solution)/shard_map/pallas_call | solution.py:227
  145.9 1.6 collective-permute-start.20
  147.5 0.2 collective-permute-start.19
  147.7 0.3 collective-permute-start.29
  148.0 6.7 %collective-permute-done.20.kv2 = bf16[4,128,256]{2,1,0:T(8,128)(2,1)S(1)} collective-permute-done((bf16[4,128,256]{2,1,0:T(8,128)(2,1)S(1)}, bf16[4,128,256]{2,1,0:T(8,128)(2,1)S(1)}, u32[]{:S(2)}, u32[]{:S(2)}) %collective-permute-start.20) | collective-permute-done | bytes 262176 | tf_op jit(solution)/shard_map/ppermute | solution.py:134
  154.7 0.5 collective-permute-start.33
  155.2 12.3 %collective-permute-done.34.refs_14_ = bf16[2048,256]{1,0:T(8,128)(2,1)} collective-permute-done((bf16[2048,256]{1,0:T(8,128)(2,1)}, bf16[2048,256]{1,0:T(8,128)(2,1)}, u32[]{:S(2)}, u32[]{:S(2)}) %collective-permute-start.34) | collective-permute-done | bytes 1048608 | tf_op jit(solution)/shard_map/ppermute | solution.py:134
  167.5 0.5 collective-permute-start.21
  168.0 0.5 copy-done.11
  168.5 5.7 %shard_map.55.queries = bf16[4,512,128]{2,1,0:T(8,128)(2,1)S(1)} custom-call(s32[2]{0:T(128)S(1)} %pad_add_fusion.place, bf16[128,2048]{1,0:T(8,128)(2,1)S(1)} %copy-done, bf16[128,2048]{1,0:T(8,128)(2,1)S(1)} %collective-permute-done.refs_1_, bf16[128,2048]{1,0:T(8,128)(2,1)S(1)} %collective-permute-done.1.refs_2_, bf16[128,2048]{1,0:T(8,128)(2,1)S(1)} %copy-done.6, ...), custom_call_target="tpu_custom_call" | custom-call | flops 2147483648 | bytes 8388608 | tf_op jit(solution)/shard_map/pallas_call | solution.py:227
  174.2 9.0 %shard_map.57 = (bf16[2,128,512]{2,1,0:T(8,128)(2,1)S(1)}, bf16[2,128,512]{2,1,0:T(8,128)(2,1)S(1)}) custom-call(s32[2]{0:T(128)S(1)} %pad_add_fusion.place, bf16[4,512,128]{2,1,0:T(8,128)(2,1)S(1)} %shard_map.55.queries, bf16[4,128,256]{2,1,0:T(8,128)(2,1)S(1)} %shard_map.56.kv0, bf16[4,128,256]{2,1,0:T(8,128)(2,1)S(1)} %collective-permute-done.19.kv1, ...), custom_call_target="tpu_custom_call" | custom-call | flops 2147483648 | bytes 4194304 | tf_op jit(solution)/shard_map/pallas_call | solution.py:300
  183.2 0.6 collective-permute-start.25
  183.8 1.5 collective-permute-start.24
  185.4 2.8 %collective-permute-start.22 = (bf16[2,128,512]{2,1,0:T(8,128)(2,1)S(1)}, bf16[2,128,512]{2,1,0:T(8,128)(2,1)S(1)}, u32[]{:S(2)}, u32[]{:S(2)}) collective-permute-start(bf16[2,128,512]{2,1,0:T(8,128)(2,1)S(1)} %get-tuple-element.9.refs_0_), channel_id=1, source_target_pairs={{0,8},{1,9},{2,10},{3,11},{4,12},{5,13},{6,14},{7,15},{8,0},{9,1},... | collective-permute-start | bytes 786440 | tf_op jit(solution)/shard_map/ppermute | solution.py:134
  188.2 3.8 %collective-permute-done.25.refs_4_ = bf16[2,128,512]{2,1,0:T(8,128)(2,1)S(1)} collective-permute-done((bf16[2,128,512]{2,1,0:T(8,128)(2,1)S(1)}, bf16[2,128,512]{2,1,0:T(8,128)(2,1)S(1)}, u32[]{:S(2)}, u32[]{:S(2)}) %collective-permute-start.25) | collective-permute-done | bytes 262176 | tf_op jit(solution)/shard_map/ppermute | solution.py:134
  192.0 1.5 collective-permute-start.28
  193.6 1.3 collective-permute-done.24.refs_3_
  194.9 8.8 %collective-permute-start.27 = (bf16[2,128,512]{2,1,0:T(8,128)(2,1)S(1)}, bf16[2,128,512]{2,1,0:T(8,128)(2,1)S(1)}, u32[]{:S(2)}, u32[]{:S(2)}) collective-permute-start(bf16[2,128,512]{2,1,0:T(8,128)(2,1)S(1)} %collective-permute-done.25.refs_4_), channel_id=1, source_target_pairs={{0,16},{1,17},{2,18},{3,19},{4,20},{5,21},{6,22},{7,23},{8,24},{9,... | collective-permute-start | bytes 786440 | tf_op jit(solution)/shard_map/ppermute | solution.py:134
  203.8 15.5 %collective-permute-done.23.refs_2_ = bf16[2,128,512]{2,1,0:T(8,128)(2,1)S(1)} collective-permute-done((bf16[2,128,512]{2,1,0:T(8,128)(2,1)S(1)}, bf16[2,128,512]{2,1,0:T(8,128)(2,1)S(1)}, u32[]{:S(2)}, u32[]{:S(2)}) %collective-permute-start.23) | collective-permute-done | bytes 262176 | tf_op jit(solution)/shard_map/ppermute | solution.py:134
  219.2 10.6 %collective-permute-done.27.refs_6_ = bf16[2,128,512]{2,1,0:T(8,128)(2,1)S(1)} collective-permute-done((bf16[2,128,512]{2,1,0:T(8,128)(2,1)S(1)}, bf16[2,128,512]{2,1,0:T(8,128)(2,1)S(1)}, u32[]{:S(2)}, u32[]{:S(2)}) %collective-permute-start.27) | collective-permute-done | bytes 262176 | tf_op jit(solution)/shard_map/ppermute | solution.py:134
  229.9 1.9 collective-permute-done.26.refs_5_
  231.8 1.0 copy-done.15
  232.7 6.9 %shard_map.58 = (bf16[128,1024]{1,0:T(8,128)(2,1)S(1)}, bf16[128,1024]{1,0:T(8,128)(2,1)S(1)}) custom-call(s32[2]{0:T(128)S(1)} %pad_add_fusion.place, bf16[2,128,512]{2,1,0:T(8,128)(2,1)S(1)} %get-tuple-element.9.refs_0_, bf16[2,128,512]{2,1,0:T(8,128)(2,1)S(1)} %collective-permute-done.22.refs_1_, ...), custom_call_target="tpu_custom_call" | custom-call | flops 2147483648 | bytes 12582912 | tf_op jit(solution)/shard_map/pallas_call | solution.py:371
  239.7 3.3 %collective-permute-start.36 = (bf16[128,1024]{1,0:T(8,128)(2,1)S(1)}, bf16[128,1024]{1,0:T(8,128)(2,1)S(1)}, u32[]{:S(2)}, u32[]{:S(2)}) collective-permute-start(bf16[128,1024]{1,0:T(8,128)(2,1)S(1)} %get-tuple-element.11), channel_id=1, source_target_pairs={{0,8},{1,24},{2,10},{3,26},{4,12},{5,28},{6,14},{7,30},{8,0},{9,16... | collective-permute-start | bytes 786440 | tf_op jit(solution)/shard_map/ppermute | solution.py:134
  243.0 1.9 collective-permute-start.37
  245.0 6.2 %collective-permute-done.36 = bf16[128,1024]{1,0:T(8,128)(2,1)S(1)} collective-permute-done((bf16[128,1024]{1,0:T(8,128)(2,1)S(1)}, bf16[128,1024]{1,0:T(8,128)(2,1)S(1)}, u32[]{:S(2)}, u32[]{:S(2)}) %collective-permute-start.36) | collective-permute-done | bytes 262176 | tf_op jit(solution)/shard_map/ppermute | solution.py:134
  251.1 11.0 %collective-permute-done.37 = bf16[128,1024]{1,0:T(8,128)(2,1)S(1)} collective-permute-done((bf16[128,1024]{1,0:T(8,128)(2,1)S(1)}, bf16[128,1024]{1,0:T(8,128)(2,1)S(1)}, u32[]{:S(2)}, u32[]{:S(2)}) %collective-permute-start.37) | collective-permute-done | bytes 262176 | tf_op jit(solution)/shard_map/ppermute | solution.py:134
  262.2 0.8 pad_maximum_fusion.3
  (66 shorter events, 0.8 us)
Async XLA Ops:
  0.0 1.1 copy-start.16
  1.4 4.9 %copy-start.12 = (bf16[256,2048]{1,0:T(8,128)(2,1)S(1)}, bf16[256,2048]{1,0:T(8,128)(2,1)}, u32[]{:S(2)}) copy-start(bf16[256,2048]{1,0:T(8,128)(2,1)} %param.6) | copy-start | bytes 3145732
  1.6 3.8 %copy-start = (bf16[128,2048]{1,0:T(8,128)(2,1)S(1)}, bf16[128,2048]{1,0:T(8,128)(2,1)}, u32[]{:S(2)}) copy-start(bf16[128,2048]{1,0:T(8,128)(2,1)} %refs_0_.3) | copy-start | bytes 1572868
  1.7 8.3 %collective-permute-start.15 = (bf16[256,256]{1,0:T(8,128)(2,1)S(1)}, bf16[256,256]{1,0:T(8,128)(2,1)S(1)}, u32[]{:S(2)}, u32[]{:S(2)}) collective-permute-start(bf16[256,256]{1,0:T(8,128)(2,1)S(1)} %get-tuple-element.20), channel_id=1, source_target_pairs={{0,24},{1,25},{2,26},{3,27},{4,28},{5,29},{6,30},{7,31},{8,16},{9,... | collective-permute-start | bytes 393224 | tf_op jit(solution)/shard_map/ppermute | solution.py:134
  5.3 71.2 %collective-permute-start.5 = (bf16[128,2048]{1,0:T(8,128)(2,1)S(1)}, bf16[128,2048]{1,0:T(8,128)(2,1)S(1)}, u32[]{:S(2)}, u32[]{:S(2)}) collective-permute-start(bf16[128,2048]{1,0:T(8,128)(2,1)S(1)} %copy-done), channel_id=1, source_target_pairs={{0,24},{1,25},{2,26},{3,27},{4,28},{5,29},{6,30},{7,31},{8,16},{9,... | collective-permute-start | bytes 1572872 | tf_op jit(solution)/shard_map/ppermute | solution.py:134
  6.4 46.6 %collective-permute-start.7 = (bf16[256,512]{1,0:T(8,128)(2,1)S(1)}, bf16[256,512]{1,0:T(8,128)(2,1)S(1)}, u32[]{:S(2)}, u32[]{:S(2)}) collective-permute-start(bf16[256,512]{1,0:T(8,128)(2,1)S(1)} %get-tuple-element.14), channel_id=1, source_target_pairs={{0,8},{1,9},{2,10},{3,11},{4,12},{5,13},{6,14},{7,15},{8,0},{9,1},... | collective-permute-start | bytes 786440 | tf_op jit(solution)/shard_map/ppermute | solution.py:134
  6.5 46.8 %collective-permute-start.9 = (bf16[256,512]{1,0:T(8,128)(2,1)S(1)}, bf16[256,512]{1,0:T(8,128)(2,1)S(1)}, u32[]{:S(2)}, u32[]{:S(2)}) collective-permute-start(bf16[256,512]{1,0:T(8,128)(2,1)S(1)} %get-tuple-element.15), channel_id=1, source_target_pairs={{0,24},{1,25},{2,26},{3,27},{4,28},{5,29},{6,30},{7,31},{8,16},{9,... | collective-permute-start | bytes 786440 | tf_op jit(solution)/shard_map/ppermute | solution.py:134
  9.4 40.7 %collective-permute-start.14 = (bf16[256,256]{1,0:T(8,128)(2,1)S(1)}, bf16[256,256]{1,0:T(8,128)(2,1)S(1)}, u32[]{:S(2)}, u32[]{:S(2)}) collective-permute-start(bf16[256,256]{1,0:T(8,128)(2,1)S(1)} %get-tuple-element.21), channel_id=1, source_target_pairs={{0,16},{1,17},{2,18},{3,19},{4,20},{5,21},{6,22},{7,23},{8,24},{9,... | collective-permute-start | bytes 393224 | tf_op jit(solution)/shard_map/ppermute | solution.py:134
  9.9 40.2 %collective-permute-start.13 = (bf16[256,256]{1,0:T(8,128)(2,1)S(1)}, bf16[256,256]{1,0:T(8,128)(2,1)S(1)}, u32[]{:S(2)}, u32[]{:S(2)}) collective-permute-start(bf16[256,256]{1,0:T(8,128)(2,1)S(1)} %get-tuple-element.22), channel_id=1, source_target_pairs={{0,8},{1,9},{2,10},{3,11},{4,12},{5,13},{6,14},{7,15},{8,0},{9,1},... | collective-permute-start | bytes 393224 | tf_op jit(solution)/shard_map/ppermute | solution.py:134
  50.1 24.9 %collective-permute-start.8 = (bf16[256,512]{1,0:T(8,128)(2,1)S(1)}, bf16[256,512]{1,0:T(8,128)(2,1)S(1)}, u32[]{:S(2)}, u32[]{:S(2)}) collective-permute-start(bf16[256,512]{1,0:T(8,128)(2,1)S(1)} %get-tuple-element.16), channel_id=1, source_target_pairs={{0,16},{1,17},{2,18},{3,19},{4,20},{5,21},{6,22},{7,23},{8,24},{9,... | collective-permute-start | bytes 786440 | tf_op jit(solution)/shard_map/ppermute | solution.py:134
  50.1 36.0 %collective-permute-start.3 = (bf16[128,2048]{1,0:T(8,128)(2,1)S(1)}, bf16[128,2048]{1,0:T(8,128)(2,1)S(1)}, u32[]{:S(2)}, u32[]{:S(2)}) collective-permute-start(bf16[128,2048]{1,0:T(8,128)(2,1)S(1)} %copy-done), channel_id=1, source_target_pairs={{0,16},{1,17},{2,18},{3,19},{4,20},{5,21},{6,22},{7,23},{8,24},{9,... | collective-permute-start | bytes 1572872 | tf_op jit(solution)/shard_map/ppermute | solution.py:134
  53.0 33.6 %collective-permute-start.1 = (bf16[128,2048]{1,0:T(8,128)(2,1)S(1)}, bf16[128,2048]{1,0:T(8,128)(2,1)S(1)}, u32[]{:S(2)}, u32[]{:S(2)}) collective-permute-start(bf16[128,2048]{1,0:T(8,128)(2,1)S(1)} %copy-done), channel_id=1, source_target_pairs={{0,8},{1,9},{2,10},{3,11},{4,12},{5,13},{6,14},{7,15},{8,0},{9,1},... | collective-permute-start | bytes 1572872 | tf_op jit(solution)/shard_map/ppermute | solution.py:134
  53.2 34.9 %collective-permute-start = (bf16[128,2048]{1,0:T(8,128)(2,1)S(1)}, bf16[128,2048]{1,0:T(8,128)(2,1)S(1)}, u32[]{:S(2)}, u32[]{:S(2)}) collective-permute-start(bf16[128,2048]{1,0:T(8,128)(2,1)S(1)} %copy-done), channel_id=1, source_target_pairs={{0,1},{1,0},{2,3},{3,2},{4,5},{5,4},{6,7},{7,6},{8,9},{9,8},{10,11... | collective-permute-start | bytes 1572872 | tf_op jit(solution)/shard_map/ppermute | solution.py:134
  53.8 36.9 %copy-start.7 = (bf16[4,256,256]{2,1,0:T(8,128)(2,1)}, bf16[4,256,256]{2,1,0:T(8,128)(2,1)S(1)}, u32[]{:S(2)}) copy-start(bf16[4,256,256]{2,1,0:T(8,128)(2,1)S(1)} %pad_maximum_fusion.2.refs_8_) | copy-start | bytes 1572868
  75.0 15.8 %collective-permute-start.17 = (bf16[4,256,256]{2,1,0:T(8,128)(2,1)S(1)}, bf16[4,256,256]{2,1,0:T(8,128)(2,1)}, u32[]{:S(2)}, u32[]{:S(2)}) collective-permute-start(bf16[4,256,256]{2,1,0:T(8,128)(2,1)S(1)} %pad_maximum_fusion.2.refs_8_), channel_id=1, source_target_pairs={{0,4},{1,5},{2,6},{3,7},{4,0},{5,1},{6,2},{7,3},{8,12},{9,13},{10,... | collective-permute-start | bytes 1572872 | tf_op jit(solution)/shard_map/ppermute | solution.py:134
  76.5 14.8 %collective-permute-start.16 = (bf16[4,256,256]{2,1,0:T(8,128)(2,1)S(1)}, bf16[4,256,256]{2,1,0:T(8,128)(2,1)S(1)}, u32[]{:S(2)}, u32[]{:S(2)}) collective-permute-start(bf16[4,256,256]{2,1,0:T(8,128)(2,1)S(1)} %pad_maximum_fusion.2.refs_8_), channel_id=1, source_target_pairs={{0,2},{1,3},{2,0},{3,1},{4,6},{5,7},{6,4},{7,5},{8,10},{9,11},{10,... | collective-permute-start | bytes 1572872 | tf_op jit(solution)/shard_map/ppermute | solution.py:134
  86.1 14.8 %collective-permute-start.6 = (bf16[128,2048]{1,0:T(8,128)(2,1)S(1)}, bf16[128,2048]{1,0:T(8,128)(2,1)S(1)}, u32[]{:S(2)}, u32[]{:S(2)}) collective-permute-start(bf16[128,2048]{1,0:T(8,128)(2,1)S(1)} %collective-permute-done.5.refs_6_), channel_id=1, source_target_pairs={{0,1},{1,0},{2,3},{3,2},{4,5},{5,4},{6,7},{7,6},{8,9},{9,8},{10,11... | collective-permute-start | bytes 1572872 | tf_op jit(solution)/shard_map/ppermute | solution.py:134
  86.6 25.5 %collective-permute-start.4 = (bf16[128,2048]{1,0:T(8,128)(2,1)S(1)}, bf16[128,2048]{1,0:T(8,128)(2,1)S(1)}, u32[]{:S(2)}, u32[]{:S(2)}) collective-permute-start(bf16[128,2048]{1,0:T(8,128)(2,1)S(1)} %collective-permute-done.3.refs_4_), channel_id=1, source_target_pairs={{0,1},{1,0},{2,3},{3,2},{4,5},{5,4},{6,7},{7,6},{8,9},{9,8},{10,11... | collective-permute-start | bytes 1572872 | tf_op jit(solution)/shard_map/ppermute | solution.py:134
  88.1 37.0 %collective-permute-start.32 = (bf16[2048,256]{1,0:T(8,128)(2,1)}, bf16[2048,256]{1,0:T(8,128)(2,1)}, u32[]{:S(2)}, u32[]{:S(2)}) collective-permute-start(bf16[2048,256]{1,0:T(8,128)(2,1)} %refs_8_.1), channel_id=1, source_target_pairs={{0,4},{1,5},{2,6},{3,7},{4,0},{5,1},{6,2},{7,3},{8,12},{9,13},{10,... | collective-permute-start | bytes 3145736 | tf_op jit(solution)/shard_map/ppermute | solution.py:134
  90.8 44.7 %collective-permute-start.11 = (bf16[4,256,512]{2,1,0:T(8,128)(2,1)}, bf16[4,256,512]{2,1,0:T(8,128)(2,1)}, u32[]{:S(2)}, u32[]{:S(2)}) collective-permute-start(bf16[4,256,512]{2,1,0:T(8,128)(2,1)} %pad_maximum_fusion.refs_8_), channel_id=1, source_target_pairs={{0,4},{1,5},{2,6},{3,7},{4,0},{5,1},{6,2},{7,3},{8,12},{9,13},{10,... | collective-permute-start | bytes 3145736 | tf_op jit(solution)/shard_map/ppermute | solution.py:134
  91.3 0.9 copy-start.9
  92.1 31.2 %collective-permute-start.2 = (bf16[128,2048]{1,0:T(8,128)(2,1)S(1)}, bf16[128,2048]{1,0:T(8,128)(2,1)S(1)}, u32[]{:S(2)}, u32[]{:S(2)}) collective-permute-start(bf16[128,2048]{1,0:T(8,128)(2,1)S(1)} %collective-permute-done.1.refs_2_), channel_id=1, source_target_pairs={{0,1},{1,0},{2,3},{3,2},{4,5},{5,4},{6,7},{7,6},{8,9},{9,8},{10,11... | collective-permute-start | bytes 1572872 | tf_op jit(solution)/shard_map/ppermute | solution.py:134
  100.9 24.9 %copy-start.1 = (bf16[128,2048]{1,0:T(8,128)(2,1)}, bf16[128,2048]{1,0:T(8,128)(2,1)S(1)}, u32[]{:S(2)}) copy-start(bf16[128,2048]{1,0:T(8,128)(2,1)S(1)} %collective-permute-done.6.refs_7_) | copy-start | bytes 1572868
  100.9 46.6 %collective-permute-start.30 = (bf16[2048,256]{1,0:T(8,128)(2,1)}, bf16[2048,256]{1,0:T(8,128)(2,1)}, u32[]{:S(2)}, u32[]{:S(2)}) collective-permute-start(bf16[2048,256]{1,0:T(8,128)(2,1)} %refs_8_.1), channel_id=1, source_target_pairs={{0,1},{1,0},{2,3},{3,2},{4,5},{5,4},{6,7},{7,6},{8,9},{9,8},{10,11... | collective-permute-start | bytes 3145736 | tf_op jit(solution)/shard_map/ppermute | solution.py:134
  112.1 0.8 copy-start.3
  112.9 34.8 %collective-permute-start.10 = (bf16[4,256,512]{2,1,0:T(8,128)(2,1)}, bf16[4,256,512]{2,1,0:T(8,128)(2,1)}, u32[]{:S(2)}, u32[]{:S(2)}) collective-permute-start(bf16[4,256,512]{2,1,0:T(8,128)(2,1)} %pad_maximum_fusion.refs_8_), channel_id=1, source_target_pairs={{0,2},{1,3},{2,0},{3,1},{4,6},{5,7},{6,4},{7,5},{8,10},{9,11},{10,... | collective-permute-start | bytes 3145736 | tf_op jit(solution)/shard_map/ppermute | solution.py:134
  123.4 0.8 copy-start.5
  124.2 11.4 %collective-permute-start.18 = (bf16[4,256,256]{2,1,0:T(8,128)(2,1)}, bf16[4,256,256]{2,1,0:T(8,128)(2,1)}, u32[]{:S(2)}, u32[]{:S(2)}) collective-permute-start(bf16[4,256,256]{2,1,0:T(8,128)(2,1)} %collective-permute-done.17.refs_10_), channel_id=1, source_target_pairs={{0,2},{1,3},{2,0},{3,1},{4,6},{5,7},{6,4},{7,5},{8,10},{9,11},{10,... | collective-permute-start | bytes 1572872 | tf_op jit(solution)/shard_map/ppermute | solution.py:134
  125.2 42.3 %collective-permute-start.34 = (bf16[2048,256]{1,0:T(8,128)(2,1)}, bf16[2048,256]{1,0:T(8,128)(2,1)}, u32[]{:S(2)}, u32[]{:S(2)}) collective-permute-start(bf16[2048,256]{1,0:T(8,128)(2,1)} %collective-permute-done.32.refs_12_), channel_id=1, source_target_pairs={{0,1},{1,0},{2,3},{3,2},{4,5},{5,4},{6,7},{7,6},{8,9},{9,8},{10,11... | collective-permute-start | bytes 3145736 | tf_op jit(solution)/shard_map/ppermute | solution.py:134
  135.4 32.0 %collective-permute-start.12 = (bf16[4,256,512]{2,1,0:T(8,128)(2,1)}, bf16[4,256,512]{2,1,0:T(8,128)(2,1)S(1)}, u32[]{:S(2)}, u32[]{:S(2)}) collective-permute-start(bf16[4,256,512]{2,1,0:T(8,128)(2,1)} %collective-permute-done.11.refs_10_), channel_id=1, source_target_pairs={{0,2},{1,3},{2,0},{3,1},{4,6},{5,7},{6,4},{7,5},{8,10},{9,11},{10,... | collective-permute-start | bytes 3145736 | tf_op jit(solution)/shard_map/ppermute | solution.py:134
  135.5 1.0 copy-start.2
  136.6 1.0 copy-start.4
  137.6 1.0 copy-start.6
  138.7 1.0 copy-start.8
  139.7 1.0 copy-start.10
  145.9 8.8 %collective-permute-start.20 = (bf16[4,128,256]{2,1,0:T(8,128)(2,1)S(1)}, bf16[4,128,256]{2,1,0:T(8,128)(2,1)S(1)}, u32[]{:S(2)}, u32[]{:S(2)}) collective-permute-start(bf16[4,128,256]{2,1,0:T(8,128)(2,1)S(1)} %shard_map.56.kv0), channel_id=1, source_target_pairs={{0,4},{1,5},{2,6},{3,7},{4,0},{5,1},{6,2},{7,3},{8,12},{9,13},{10,... | collective-permute-start | bytes 786440 | tf_op jit(solution)/shard_map/ppermute | solution.py:134
  147.5 7.2 %collective-permute-start.19 = (bf16[4,128,256]{2,1,0:T(8,128)(2,1)S(1)}, bf16[4,128,256]{2,1,0:T(8,128)(2,1)S(1)}, u32[]{:S(2)}, u32[]{:S(2)}) collective-permute-start(bf16[4,128,256]{2,1,0:T(8,128)(2,1)S(1)} %shard_map.56.kv0), channel_id=1, source_target_pairs={{0,2},{1,3},{2,0},{3,1},{4,6},{5,7},{6,4},{7,5},{8,10},{9,11},{10,... | collective-permute-start | bytes 786440 | tf_op jit(solution)/shard_map/ppermute | solution.py:134
  147.7 36.1 %collective-permute-start.29 = (bf16[2048,256]{1,0:T(8,128)(2,1)}, bf16[2048,256]{1,0:T(8,128)(2,1)S(1)}, u32[]{:S(2)}, u32[]{:S(2)}) collective-permute-start(bf16[2048,256]{1,0:T(8,128)(2,1)} %refs_8_.1), channel_id=1, source_target_pairs={{0,2},{1,3},{2,0},{3,1},{4,6},{5,7},{6,4},{7,5},{8,10},{9,11},{10,... | collective-permute-start | bytes 3145736 | tf_op jit(solution)/shard_map/ppermute | solution.py:134
  154.7 30.7 %collective-permute-start.31 = (bf16[2048,256]{1,0:T(8,128)(2,1)}, bf16[2048,256]{1,0:T(8,128)(2,1)S(1)}, u32[]{:S(2)}, u32[]{:S(2)}) collective-permute-start(bf16[2048,256]{1,0:T(8,128)(2,1)} %collective-permute-done.30.refs_10_), channel_id=1, source_target_pairs={{0,2},{1,3},{2,0},{3,1},{4,6},{5,7},{6,4},{7,5},{8,10},{9,11},{10,... | collective-permute-start | bytes 3145736 | tf_op jit(solution)/shard_map/ppermute | solution.py:134
  154.7 30.7 %collective-permute-start.33 = (bf16[2048,256]{1,0:T(8,128)(2,1)}, bf16[2048,256]{1,0:T(8,128)(2,1)S(1)}, u32[]{:S(2)}, u32[]{:S(2)}) collective-permute-start(bf16[2048,256]{1,0:T(8,128)(2,1)} %collective-permute-done.32.refs_12_), channel_id=1, source_target_pairs={{0,2},{1,3},{2,0},{3,1},{4,6},{5,7},{6,4},{7,5},{8,10},{9,11},{10,... | collective-permute-start | bytes 3145736 | tf_op jit(solution)/shard_map/ppermute | solution.py:134
  167.5 64.3 %collective-permute-start.35 = (bf16[2048,256]{1,0:T(8,128)(2,1)}, bf16[2048,256]{1,0:T(8,128)(2,1)S(1)}, u32[]{:S(2)}, u32[]{:S(2)}) collective-permute-start(bf16[2048,256]{1,0:T(8,128)(2,1)} %collective-permute-done.34.refs_14_), channel_id=1, source_target_pairs={{0,2},{1,3},{2,0},{3,1},{4,6},{5,7},{6,4},{7,5},{8,10},{9,11},{10,... | collective-permute-start | bytes 3145736 | tf_op jit(solution)/shard_map/ppermute | solution.py:134
  167.5 1.0 copy-start.11
  167.5 6.7 %collective-permute-start.21 = (bf16[4,128,256]{2,1,0:T(8,128)(2,1)S(1)}, bf16[4,128,256]{2,1,0:T(8,128)(2,1)S(1)}, u32[]{:S(2)}, u32[]{:S(2)}) collective-permute-start(bf16[4,128,256]{2,1,0:T(8,128)(2,1)S(1)} %collective-permute-done.20.kv2), channel_id=1, source_target_pairs={{0,2},{1,3},{2,0},{3,1},{4,6},{5,7},{6,4},{7,5},{8,10},{9,11},{10,... | collective-permute-start | bytes 786440 | tf_op jit(solution)/shard_map/ppermute | solution.py:134
  183.2 8.8 %collective-permute-start.25 = (bf16[2,128,512]{2,1,0:T(8,128)(2,1)S(1)}, bf16[2,128,512]{2,1,0:T(8,128)(2,1)S(1)}, u32[]{:S(2)}, u32[]{:S(2)}) collective-permute-start(bf16[2,128,512]{2,1,0:T(8,128)(2,1)S(1)} %get-tuple-element.10), channel_id=1, source_target_pairs={{0,1},{1,0},{2,3},{3,2},{4,5},{5,4},{6,7},{7,6},{8,9},{9,8},{10,11... | collective-permute-start | bytes 786440 | tf_op jit(solution)/shard_map/ppermute | solution.py:134
  183.8 11.1 %collective-permute-start.24 = (bf16[2,128,512]{2,1,0:T(8,128)(2,1)S(1)}, bf16[2,128,512]{2,1,0:T(8,128)(2,1)S(1)}, u32[]{:S(2)}, u32[]{:S(2)}) collective-permute-start(bf16[2,128,512]{2,1,0:T(8,128)(2,1)S(1)} %get-tuple-element.9.refs_0_), channel_id=1, source_target_pairs={{0,24},{1,25},{2,26},{3,27},{4,28},{5,29},{6,30},{7,31},{8,16},{9,... | collective-permute-start | bytes 786440 | tf_op jit(solution)/shard_map/ppermute | solution.py:134
  185.4 46.4 %copy-start.13 = (bf16[2048,256]{1,0:T(8,128)(2,1)}, bf16[2048,256]{1,0:T(8,128)(2,1)S(1)}, u32[]{:S(2)}) copy-start(bf16[2048,256]{1,0:T(8,128)(2,1)S(1)} %collective-permute-done.31.refs_11_) | copy-start | bytes 3145732
  185.4 33.8 %collective-permute-start.23 = (bf16[2,128,512]{2,1,0:T(8,128)(2,1)S(1)}, bf16[2,128,512]{2,1,0:T(8,128)(2,1)S(1)}, u32[]{:S(2)}, u32[]{:S(2)}) collective-permute-start(bf16[2,128,512]{2,1,0:T(8,128)(2,1)S(1)} %get-tuple-element.9.refs_0_), channel_id=1, source_target_pairs={{0,16},{1,17},{2,18},{3,19},{4,20},{5,21},{6,22},{7,23},{8,24},{9,... | collective-permute-start | bytes 786440 | tf_op jit(solution)/shard_map/ppermute | solution.py:134
  185.4 46.4 %copy-start.14 = (bf16[2048,256]{1,0:T(8,128)(2,1)}, bf16[2048,256]{1,0:T(8,128)(2,1)S(1)}, u32[]{:S(2)}) copy-start(bf16[2048,256]{1,0:T(8,128)(2,1)S(1)} %collective-permute-done.33.refs_13_) | copy-start | bytes 3145732
  185.4 33.8 %collective-permute-start.22 = (bf16[2,128,512]{2,1,0:T(8,128)(2,1)S(1)}, bf16[2,128,512]{2,1,0:T(8,128)(2,1)S(1)}, u32[]{:S(2)}, u32[]{:S(2)}) collective-permute-start(bf16[2,128,512]{2,1,0:T(8,128)(2,1)S(1)} %get-tuple-element.9.refs_0_), channel_id=1, source_target_pairs={{0,8},{1,9},{2,10},{3,11},{4,12},{5,13},{6,14},{7,15},{8,0},{9,1},... | collective-permute-start | bytes 786440 | tf_op jit(solution)/shard_map/ppermute | solution.py:134
  192.0 27.2 %collective-permute-start.28 = (bf16[2,128,512]{2,1,0:T(8,128)(2,1)S(1)}, bf16[2,128,512]{2,1,0:T(8,128)(2,1)S(1)}, u32[]{:S(2)}, u32[]{:S(2)}) collective-permute-start(bf16[2,128,512]{2,1,0:T(8,128)(2,1)S(1)} %collective-permute-done.25.refs_4_), channel_id=1, source_target_pairs={{0,24},{1,25},{2,26},{3,27},{4,28},{5,29},{6,30},{7,31},{8,16},{9,... | collective-permute-start | bytes 786440 | tf_op jit(solution)/shard_map/ppermute | solution.py:134
  194.9 34.9 %collective-permute-start.27 = (bf16[2,128,512]{2,1,0:T(8,128)(2,1)S(1)}, bf16[2,128,512]{2,1,0:T(8,128)(2,1)S(1)}, u32[]{:S(2)}, u32[]{:S(2)}) collective-permute-start(bf16[2,128,512]{2,1,0:T(8,128)(2,1)S(1)} %collective-permute-done.25.refs_4_), channel_id=1, source_target_pairs={{0,16},{1,17},{2,18},{3,19},{4,20},{5,21},{6,22},{7,23},{8,24},{9,... | collective-permute-start | bytes 786440 | tf_op jit(solution)/shard_map/ppermute | solution.py:134
  219.2 12.5 %collective-permute-start.26 = (bf16[2,128,512]{2,1,0:T(8,128)(2,1)S(1)}, bf16[2,128,512]{2,1,0:T(8,128)(2,1)S(1)}, u32[]{:S(2)}, u32[]{:S(2)}) collective-permute-start(bf16[2,128,512]{2,1,0:T(8,128)(2,1)S(1)} %collective-permute-done.25.refs_4_), channel_id=1, source_target_pairs={{0,8},{1,9},{2,10},{3,11},{4,12},{5,13},{6,14},{7,15},{8,0},{9,1},... | collective-permute-start | bytes 786440 | tf_op jit(solution)/shard_map/ppermute | solution.py:134
  231.7 1.0 copy-start.15
  239.7 11.5 %collective-permute-start.36 = (bf16[128,1024]{1,0:T(8,128)(2,1)S(1)}, bf16[128,1024]{1,0:T(8,128)(2,1)S(1)}, u32[]{:S(2)}, u32[]{:S(2)}) collective-permute-start(bf16[128,1024]{1,0:T(8,128)(2,1)S(1)} %get-tuple-element.11), channel_id=1, source_target_pairs={{0,8},{1,24},{2,10},{3,26},{4,12},{5,28},{6,14},{7,30},{8,0},{9,16... | collective-permute-start | bytes 786440 | tf_op jit(solution)/shard_map/ppermute | solution.py:134
  243.0 19.1 %collective-permute-start.37 = (bf16[128,1024]{1,0:T(8,128)(2,1)S(1)}, bf16[128,1024]{1,0:T(8,128)(2,1)S(1)}, u32[]{:S(2)}, u32[]{:S(2)}) collective-permute-start(bf16[128,1024]{1,0:T(8,128)(2,1)S(1)} %get-tuple-element.12), channel_id=1, source_target_pairs={{0,0},{1,16},{2,2},{3,18},{4,4},{5,20},{6,6},{7,22},{8,8},{9,24},{... | collective-permute-start | bytes 786440 | tf_op jit(solution)/shard_map/ppermute | solution.py:134

commit v2 on v1

--- a/solution.py
+++ b/solution.py
@@ -10,7 +10,7 @@
 
 HEAD_SIZE = 128
 AXES = ("ctx", "fsdp")
-VMEM_LIMIT = 48 * 1024 * 1024
+VMEM_LIMIT = 18 * 1024 * 1024
 
 
 def rotary_tables(positions):
@@ -162,19 +162,20 @@
     return pl.BlockSpec(memory_space=pltpu.VMEM)
 
 
-def load_projection(place, token_refs, weight_refs, tok, wgt, sems):
+def load_projection(place, token_refs, weight_refs, plan, first_column, tok, wgt, sems):
     ctx, x = place[0], place[1]
     rows, half = token_refs[0].shape
+    depth, width = wgt.shape[0] // 16, wgt.shape[1]
     copies = []
     for m in range(4):
         for rx in range(2):
             into = tok.at[pl.ds(m * rows, rows), pl.ds(pl.multiple_of((x ^ rx) * half, half), half)]
             copies.append((token_refs[m * 2 + rx], into))
-    for r, ref in enumerate(weight_refs):
-        for m in range(4):
-            block = ctx ^ (4 * m + r)
-            depth = ref.shape[1]
-            copies.append((ref.at[m], wgt.at[pl.ds(pl.multiple_of(block * depth, depth), depth)]))
+    for ref, blocks in zip(weight_refs, plan, strict=True):
+        at = first_column if ref.shape[-1] > width else 0
+        for k, relative in enumerate(blocks):
+            into = wgt.at[pl.ds(pl.multiple_of((ctx ^ relative) * depth, depth), depth)]
+            copies.append((ref.at[k, :, pl.ds(at, width)], into))
     handles = [pltpu.make_async_copy(s, d, sems.at[i]) for i, (s, d) in enumerate(copies)]
     for handle in handles:
         handle.start()
@@ -187,10 +188,10 @@
     return values * cosine + turned * sine
 
 
-def kv_kernel(place, *refs):
-    token_refs, weight_refs = refs[:8], refs[8:12]
-    cosine, sine, out, tok, wgt, sems = refs[12:]
-    load_projection(place, token_refs, weight_refs, tok, wgt, sems)
+def kv_kernel(plan, place, *refs):
+    token_refs, weight_refs = refs[:8], refs[8:-6]
+    cosine, sine, out, tok, wgt, sems = refs[-6:]
+    load_projection(place, token_refs, weight_refs, plan, 0, tok, wgt, sems)
     rows = tok.shape[0] // 4
     values = jnp.dot(tok[...], wgt[...], preferred_element_type=jnp.float32)
     keys = rotated(values[:, :HEAD_SIZE], cosine[...], sine[...]).astype(jnp.bfloat16)
@@ -200,10 +201,10 @@
         out[m, :, HEAD_SIZE:] = vals[m * rows : (m + 1) * rows]
 
 
-def query_kernel(place, *refs):
-    token_refs, weight_refs = refs[:8], refs[8:12]
-    cosine, sine, out, tok, wgt, sems = refs[12:]
-    load_projection(place, token_refs, weight_refs, tok, wgt, sems)
+def query_kernel(plan, place, *refs):
+    token_refs, weight_refs = refs[:8], refs[8:-6]
+    cosine, sine, out, tok, wgt, sems = refs[-6:]
+    load_projection(place, token_refs, weight_refs, plan, 2 * HEAD_SIZE, tok, wgt, sems)
     rows = tok.shape[0] // 4
     heads = wgt.shape[1] // HEAD_SIZE
     for pair in range(heads // 2):
@@ -220,14 +221,14 @@
                 out[m, head * rows : (head + 1) * rows, :] = one[m * rows : (m + 1) * rows]
 
 
-def project(kernel, out_shape, place, tokens, weights, cosine, sine):
+def project(kernel, out_shape, place, tokens, weights, plan, width, cosine, sine):
     rows, half = tokens[0].shape
-    _, depth, width = weights[0].shape
-    flops = 2 * 4 * rows * 16 * depth * width
+    depth = weights[0].shape[1]
+    flops = 16 * 4 * rows * 16 * depth * HEAD_SIZE * 4
     return pl.pallas_call(
-        kernel,
+        functools.partial(kernel, plan),
         out_shape=jax.ShapeDtypeStruct(out_shape, jnp.bfloat16),
-        in_specs=[smem_spec()] + any_specs(12) + [vmem_spec()] * 2,
+        in_specs=[smem_spec()] + any_specs(8 + len(weights)) + [vmem_spec()] * 2,
         out_specs=vmem_spec(),
         scratch_shapes=[
             pltpu.VMEM((4 * rows, 2 * half), jnp.bfloat16),
@@ -308,7 +309,7 @@
         ],
         compiler_params=pltpu.CompilerParams(vmem_limit_bytes=VMEM_LIMIT),
         cost_estimate=pl.CostEstimate(
-            flops=4 * work, bytes_accessed=4 << 20, transcendentals=4 * stacked * 16 * rows
+            flops=20 * work, bytes_accessed=4 << 20, transcendentals=4 * stacked * 16 * rows
         ),
     )(place, queries, *kv)
 
@@ -385,15 +386,8 @@
     )(place, *attn, *weights)
 
 
-def spread_weights(weight, z):
-    width = weight.shape[1] // 4
-
-    def piece(m):
-        return lax.dynamic_slice_in_dim(weight, (z ^ m) * width, width, 1)
-
-    own = jnp.stack([piece(0)] + [across_z(piece(m), m) for m in (1, 2, 3)])
-    over_y = across_y(own)
-    return [own, across_core(own), over_y, across_core(over_y)]
+def after(array, *earlier):
+    return lax.optimization_barrier((array,) + earlier)[0]
 
 
 def split_body(tokens, w_query, key_matrix, value_matrix, w_out):
@@ -401,19 +395,51 @@
     place = jnp.stack([ctx, x]).astype(jnp.int32)
     z = ctx // 4
     rows = tokens.shape[0]
-
-    head_major = jnp.concatenate(
-        [
-            key_matrix.reshape(-1, 4, HEAD_SIZE),
-            value_matrix.reshape(-1, 4, HEAD_SIZE),
-        ],
-        axis=2,
-    ).reshape(key_matrix.shape[0], -1)
-    kv_weights = spread_weights(head_major, z)
-    over_z = [tokens] + [across_z(tokens, m) for m in (1, 2, 3)]
-    token_pieces = []
-    for piece in over_z:
-        token_pieces += [piece, across_x(piece)]
+    group = w_query.shape[1] // 4
+
+    def columns(weight, head, width):
+        return lax.dynamic_slice_in_dim(weight, head * width, width, 1)
+
+    def pair(head):
+        parts = [columns(w, head, HEAD_SIZE) for w in (key_matrix, value_matrix)]
+        return jnp.concatenate(parts, axis=1)
+
+    wide = 2 * HEAD_SIZE
+
+    tok1 = across_z(tokens, 1)
+    tok2 = across_z(tokens, 2)
+    other0 = across_x(tokens)
+    x_out = across_x(w_out)
+    own = jnp.concatenate([pair(z), columns(w_query, z, group)], axis=1)
+    own_y = across_y(own)
+    y_out = across_y(after(w_out, own_y))
+    far_half = [columns(w, 1 - z // 2, wide) for w in (key_matrix, value_matrix)]
+    far = across_z(after(jnp.concatenate(far_half, axis=1), tok1, other0, own_y), 2)
+
+    def far_pair(head):
+        parts = [columns(w, head, HEAD_SIZE) for w in (far[:, :wide], far[:, wide:])]
+        return jnp.concatenate(parts, axis=1)
+
+    other1 = across_x(after(tok1, other0, own_y))
+    tok3 = across_z(after(tok2, tok1, x_out, own_y), 1)
+    xy_out = across_y(after(x_out, own_y))
+    other2 = across_x(after(tok2, other1))
+    near = across_z(after(jnp.stack([pair(z ^ 1), far_pair(1 - z % 2)]), y_out), 1)
+    query2 = across_z(after(columns(w_query, z ^ 2, group), far), 2)
+    query3 = across_z(after(columns(w_query, z ^ 3, group), far, tok3, other1), 3)
+    other3 = across_x(after(tok3, other1))
+    query1 = across_z(after(columns(w_query, z ^ 1, group), far, near), 1)
+    token_pieces = [tokens, other0, tok1, other1, tok2, other2, tok3, other3]
+
+    both = jnp.stack([own, own_y])
+    both_core = across_core(after(both, other1))
+    kv_rest = jnp.stack([near[0], far_pair(z % 2), near[1]])
+    kv_rest_y = across_y(after(kv_rest, both_core, y_out, xy_out, other2))
+    query2_y = across_y(after(query2, kv_rest_y))
+    query31_y = across_y(after(jnp.stack([query3, query1]), kv_rest_y))
+    kv_core = across_core(after(jnp.concatenate([kv_rest, kv_rest_y]), other3))
+    kv_weights = [both, both_core, kv_rest, kv_rest_y, kv_core]
+    kv_plan = ((0, 2), (1, 3), (4, 8, 12), (6, 10, 14), (5, 9, 13, 7, 11, 15))
 
     slot = jnp.arange(4, dtype=jnp.int32)[:, None]
     positions = (ctx ^ (4 * slot)) * rows + jnp.arange(rows, dtype=jnp.int32)[None, :]
@@ -422,31 +448,47 @@
     sine = jnp.concatenate([-sine, sine], axis=1)
 
     own_kv = project(
-        kv_kernel, (4, rows, 2 * HEAD_SIZE), place, token_pieces, kv_weights, cosine, sine
+        kv_kernel,
+        (4, rows, wide),
+        place,
+        token_pieces,
+        kv_weights,
+        kv_plan,
+        wide,
+        cosine,
+        sine,
     )
     y_kv = across_y(own_kv)
     kv = [own_kv, across_core(own_kv), y_kv, across_core(y_kv)]
-
-    query_weights = spread_weights(w_query, z)
-    group = w_query.shape[1] // 4
+    query_rest = jnp.stack([query1, query2, query3, query31_y[1], query2_y, query31_y[0]])
+    query_core = across_core(after(query_rest, own_kv))
+    query_weights = [both, both_core, query_rest, query_core]
+    query_plan = ((0, 2), (1, 3), (4, 8, 12, 6, 10, 14), (5, 9, 13, 7, 11, 15))
     queries = project(
         query_kernel,
         (4, group // HEAD_SIZE * rows, HEAD_SIZE),
         place,
         token_pieces,
         query_weights,
+        query_plan,
+        group,
         cosine,
         sine,
     )
     mine, other = attend(place, queries, kv)
+    out_weights = []
+    for piece in (w_out, x_out, y_out, xy_out):
+        out_weights += [piece, across_core(piece)]
+    mine, other = after(mine, *out_weights), after(other, *out_weights)
+    mine2 = across_z(mine, 2)
+    mine1 = across_z(mine, 1)
     from_x = across_x(other)
-    attn = [mine] + [across_z(mine, m) for m in (1, 2, 3)]
-    attn += [from_x] + [across_z(from_x, m) for m in (1, 2, 3)]
-
-    y_out = across_y(w_out)
-    out_weights = []
-    for piece in (w_out, across_x(w_out), y_out, across_x(y_out)):
-        out_weights += [piece, across_core(piece)]
+    from_x2 = across_z(from_x, 2)
+    from_x1 = across_z(after(from_x, mine1), 1)
+    mine3 = across_z(mine2, 1)
+    from_x3 = across_z(from_x2, 1)
+    attn = [mine, mine1, mine2, mine3, from_x, from_x1, from_x2, from_x3]
+
     first, second = project_out(place, attn, out_weights)
 
     def home(m):

time: 263 us -> 195 us (0.74)
  waiting for transfers between devices: 165 us -> 121 us
  starting transfers between devices: 56.3 us -> 33.5 us
  other arithmetic: 3.67 us -> 7.49 us
  local copies, waits for them, and re-layouts: 10.5 us -> 6.89 us
    ppermute x38, waiting for transfers between devices: 165 us -> 121 us  [move(): return lax.ppermute(array, AXES, moves(target))]
    ppermute x38, starting transfers between devices: 56.3 us -> 33.5 us  [move(): return lax.ppermute(array, AXES, moves(target))]
    unnamed x35 -> x19, local copies, waits for them, and re-layouts: 9.23 us -> 0.12 us
    dynamic_slice x0 -> x5, local copies, waits for them, and re-layouts: none -> 4.78 us  [columns(): return lax.dynamic_slice_in_dim(weight, head * width, width, 1)]
  transfers between devices with their start and end apart: 38 -> 38, of which waited for: 16 -> 22; matrix products, arithmetic and copies ran while one was open for 1% -> 7% of each run, Pallas kernels for 8% -> 7%
where the time goes in v2:
time: 195 us
  waiting for transfers between devices  121 us (62%)
  starting transfers between devices  33.5 us (17%)
  Pallas kernels  25.7 us (13%)
  other arithmetic  7.49 us (4%)
  local copies, waits for them, and re-layouts  6.89 us (4%)
    ppermute x38, waiting for transfers between devices, move(): return lax.ppermute(array, AXES, moves(target))  121 us
    ppermute x38, starting transfers between devices, move(): return lax.ppermute(array, AXES, moves(target))  33.5 us
    pallas_call x2, Pallas kernels, project(): pl.pallas_call(functools.partial(kernel, plan), out_shape=jax.ShapeDtypeS...  10.1 us
    pallas_call x1, Pallas kernels, attend(): pl.pallas_call(attend_kernel, out_shape=(shape, shape), in_specs=[smem_sp...  9.04 us
    pallas_call x1, Pallas kernels, project_out(): pl.pallas_call(output_kernel, out_shape=(shape, shape), in_specs=[smem_sp...  6.6 us
    dynamic_slice x5, local copies, waits for them, and re-layouts, columns(): return lax.dynamic_slice_in_dim(weight, head * width, width, 1)  4.78 us
  transfers between devices with their start and end apart: 38, of which 22 were waited for; matrix products, arithmetic and copies ran while one was open for 7% of the time, Pallas kernels for 7%

profile of v2, /device:TPU:2, one launch (start us, length us, event | category | flops | bytes accessed | tf_op | source)
XLA Modules:
  0.0 194.6 jit_solution(8933534549528781150)
XLA Ops:
  0.0 2.1 %collective-permute-start.1 = (bf16[128,2048]{1,0:T(8,128)(2,1)}, bf16[128,2048]{1,0:T(8,128)(2,1)}, u32[]{:S(2)}, u32[]{:S(2)}) collective-permute-start(bf16[128,2048]{1,0:T(8,128)(2,1)} %refs_0_.3), channel_id=1, source_target_pairs={{0,8},{1,9},{2,10},{3,11},{4,12},{5,13},{6,14},{7,15},{8,0},{9,1},... | collective-permute-start | bytes 1572872 | tf_op jit(solution)/shard_map/ppermute | solution.py:134
  2.1 2.6 %collective-permute-start.4 = (bf16[128,2048]{1,0:T(8,128)(2,1)}, bf16[128,2048]{1,0:T(8,128)(2,1)}, u32[]{:S(2)}, u32[]{:S(2)}) collective-permute-start(bf16[128,2048]{1,0:T(8,128)(2,1)} %refs_0_.3), channel_id=1, source_target_pairs={{0,16},{1,17},{2,18},{3,19},{4,20},{5,21},{6,22},{7,23},{8,24},{9,... | collective-permute-start | bytes 1572872 | tf_op jit(solution)/shard_map/ppermute | solution.py:134
  4.7 1.6 constant_dynamic-slice_fusion.6
  6.3 2.2 %constant_dynamic-slice_fusion.2 = (bf16[256,512]{1,0:T(8,128)(2,1)}, bf16[256,512]{1,0:T(8,128)(2,1)}, bf16[256,512]{1,0:T(8,128)(2,1)S(1)}, bf16[256,512]{1,0:T(8,128)(2,1)}) fusion(bf16[256,2048]{1,0:T(8,128)(2,1)} %param.6, s32[]{:T(128)S(6)} %select_n.74, s32[]{:T(128)S(6)} %select_n.68, s32[]{:T(128)S(6)} %select_n.67, s32[]{:T(128)S(6)} %select_n.73), kind=kLoop, calls=%fused_computation.26 | loop fusion | bytes 2097168 | tf_op jit(solution)/shard_map/dynamic_slice | solution.py:401
  8.6 1.6 collective-permute-start.2
  10.2 1.5 collective-permute-start.6
  11.7 0.9 constant_dynamic-slice_fusion.8
  12.6 0.7 pad_maximum_fusion.6
  13.4 5.4 %collective-permute-done.2 = bf16[256,768]{1,0:T(8,128)(2,1)} collective-permute-done((bf16[256,768]{1,0:T(8,128)(2,1)S(1)}, bf16[256,768]{1,0:T(8,128)(2,1)}, u32[]{:S(2)}, u32[]{:S(2)}) %collective-permute-start.2) | collective-permute-done | bytes 393248 | tf_op jit(solution)/shard_map/ppermute | solution.py:134
  18.8 1.5 collective-permute-start.11
  20.3 4.9 %collective-permute-done.1.refs_2_ = bf16[128,2048]{1,0:T(8,128)(2,1)} collective-permute-done((bf16[128,2048]{1,0:T(8,128)(2,1)}, bf16[128,2048]{1,0:T(8,128)(2,1)}, u32[]{:S(2)}, u32[]{:S(2)}) %collective-permute-start.1) | collective-permute-done | bytes 524320 | tf_op jit(solution)/shard_map/ppermute | solution.py:134
  25.2 0.7 collective-permute-start.10
  25.9 0.9 maximum_bitcast_fusion
  26.8 2.0 %pad_maximum_fusion.refs_8_ = bf16[2,256,768]{2,1,0:T(8,128)(2,1)} fusion(bf16[1,256,768]{2,1,0:T(8,128)(2,1)} %bitcast.3, bf16[1,256,768]{2,1,0:T(8,128)(2,1)S(1)} %get-tuple-element.59), kind=kLoop, calls=%fused_computation | loop fusion | flops 393216 | bytes 1572864 | tf_op jit(solution)/shard_map/stack | solution.py:434
  28.8 1.5 collective-permute-start.3
  30.3 8.9 %collective-permute-done.10 = bf16[256,512]{1,0:T(8,128)(2,1)} collective-permute-done((bf16[256,512]{1,0:T(8,128)(2,1)}, bf16[256,512]{1,0:T(8,128)(2,1)}, u32[]{:S(2)}, u32[]{:S(2)}) %collective-permute-start.10) | collective-permute-done | bytes 262176 | tf_op jit(solution)/shard_map/ppermute | solution.py:134
  39.1 1.0 fusion.3
  40.2 1.5 collective-permute-start.16
  41.8 0.7 pad_maximum_fusion.7
  42.5 5.1 %collective-permute-done.3.refs_3_ = bf16[128,2048]{1,0:T(8,128)(2,1)S(1)} collective-permute-done((bf16[128,2048]{1,0:T(8,128)(2,1)}, bf16[128,2048]{1,0:T(8,128)(2,1)S(1)}, u32[]{:S(2)}, u32[]{:S(2)}) %collective-permute-start.3) | collective-permute-done | bytes 524320 | tf_op jit(solution)/shard_map/ppermute | solution.py:134
  47.6 1.6 collective-permute-start.12
  49.2 1.0 fusion
  50.2 0.6 collective-permute-start.5
  50.8 0.9 pad_maximum_fusion.8
  51.7 5.2 %collective-permute-done.7.refs_6_ = bf16[128,2048]{1,0:T(8,128)(2,1)} collective-permute-done((bf16[128,2048]{1,0:T(8,128)(2,1)}, bf16[128,2048]{1,0:T(8,128)(2,1)}, u32[]{:S(2)}, u32[]{:S(2)}) %collective-permute-start.7) | collective-permute-done | bytes 524320 | tf_op jit(solution)/shard_map/ppermute | solution.py:134
  56.9 2.4 %collective-permute-start.15 = (bf16[256,512]{1,0:T(8,128)(2,1)}, bf16[256,512]{1,0:T(8,128)(2,1)S(1)}, u32[]{:S(2)}, u32[]{:S(2)}) collective-permute-start(bf16[256,512]{1,0:T(8,128)(2,1)} %get-tuple-element.39), channel_id=1, source_target_pairs={{0,24},{1,25},{2,26},{3,27},{4,28},{5,29},{6,30},{7,31},{8,16},{9,... | collective-permute-start | bytes 786440 | tf_op jit(solution)/shard_map/ppermute | solution.py:134
  59.3 3.1 %collective-permute-done.12 = bf16[2,256,256]{2,1,0:T(8,128)(2,1)} collective-permute-done((bf16[2,256,256]{2,1,0:T(8,128)(2,1)}, bf16[2,256,256]{2,1,0:T(8,128)(2,1)}, u32[]{:S(2)}, u32[]{:S(2)}) %collective-permute-start.12) | collective-permute-done | bytes 262176 | tf_op jit(solution)/shard_map/ppermute | solution.py:134
  62.5 1.0 fusion.2
  63.5 1.1 collective-permute-done.5.refs_5_
  64.6 0.9 collective-permute-done.16.refs_14_
  65.5 1.3 collective-permute-start.17
  66.9 1.9 collective-permute-start.14
  68.8 0.5 collective-permute-start.8
  69.3 6.9 %collective-permute-done.13 = bf16[256,512]{1,0:T(8,128)(2,1)S(1)} collective-permute-done((bf16[256,512]{1,0:T(8,128)(2,1)}, bf16[256,512]{1,0:T(8,128)(2,1)S(1)}, u32[]{:S(2)}, u32[]{:S(2)}) %collective-permute-start.13) | collective-permute-done | bytes 262176 | tf_op jit(solution)/shard_map/ppermute | solution.py:134
  76.3 0.7 collective-permute-start.18
  77.0 3.6 %collective-permute-done.14 = bf16[256,512]{1,0:T(8,128)(2,1)S(1)} collective-permute-done((bf16[256,512]{1,0:T(8,128)(2,1)S(1)}, bf16[256,512]{1,0:T(8,128)(2,1)S(1)}, u32[]{:S(2)}, u32[]{:S(2)}) %collective-permute-start.14) | collective-permute-done | bytes 262176 | tf_op jit(solution)/shard_map/ppermute | solution.py:134
  80.6 0.9 collective-permute-start.19
  81.5 0.1 pad_maximum_fusion.1
  81.7 9.4 %collective-permute-done.18 = bf16[2,256,512]{2,1,0:T(8,128)(2,1)S(1)} collective-permute-done((bf16[2,256,512]{2,1,0:T(8,128)(2,1)S(1)}, bf16[2,256,512]{2,1,0:T(8,128)(2,1)S(1)}, u32[]{:S(2)}, u32[]{:S(2)}) %collective-permute-start.18) | collective-permute-done | bytes 524320 | tf_op jit(solution)/shard_map/ppermute | solution.py:134
  91.2 4.5 %collective-permute-done.19 = bf16[256,512]{1,0:T(8,128)(2,1)S(1)} collective-permute-done((bf16[256,512]{1,0:T(8,128)(2,1)S(1)}, bf16[256,512]{1,0:T(8,128)(2,1)S(1)}, u32[]{:S(2)}, u32[]{:S(2)}) %collective-permute-start.19) | collective-permute-done | bytes 262176 | tf_op jit(solution)/shard_map/ppermute | solution.py:134
  95.8 4.7 %shard_map.55.kv0 = bf16[4,128,256]{2,1,0:T(8,128)(2,1)S(1)} custom-call(s32[2]{0:T(128)S(1)} %pad_add_fusion.place, bf16[128,2048]{1,0:T(8,128)(2,1)S(1)} %copy-done.2, bf16[128,2048]{1,0:T(8,128)(2,1)} %collective-permute-done.refs_1_, bf16[128,2048]{1,0:T(8,128)(2,1)} %collective-permute-done.1.refs_2_, bf16[128,2048]{1,0:T(8,128)(2,1)S(1)} %copy-done.4, ...), custom_call_target="tpu_custom_call" | custom-call | flops 17179869184 | bytes 8388608 | tf_op jit(solution)/shard_map/pallas_call | solution.py:228
  100.6 0.5 collective-permute-start.22
  101.1 0.3 collective-permute-start.23
  101.4 0.5 collective-permute-start.26
  101.9 2.5 %collective-permute-done.22.kv1 = bf16[4,128,256]{2,1,0:T(8,128)(2,1)S(1)} collective-permute-done((bf16[4,128,256]{2,1,0:T(8,128)(2,1)S(1)}, bf16[4,128,256]{2,1,0:T(8,128)(2,1)S(1)}, u32[]{:S(2)}, u32[]{:S(2)}) %collective-permute-start.22) | collective-permute-done | bytes 262176 | tf_op jit(solution)/shard_map/ppermute | solution.py:134
  104.3 0.1 collective-permute-start.27
  104.5 4.9 %collective-permute-done.23.kv2 = bf16[4,128,256]{2,1,0:T(8,128)(2,1)S(1)} collective-permute-done((bf16[4,128,256]{2,1,0:T(8,128)(2,1)S(1)}, bf16[4,128,256]{2,1,0:T(8,128)(2,1)S(1)}, u32[]{:S(2)}, u32[]{:S(2)}) %collective-permute-start.23) | collective-permute-done | bytes 262176 | tf_op jit(solution)/shard_map/ppermute | solution.py:134
  109.4 0.5 collective-permute-start.24
  109.9 5.4 %shard_map.56.queries = bf16[4,512,128]{2,1,0:T(8,128)(2,1)S(1)} custom-call(s32[2]{0:T(128)S(1)} %pad_add_fusion.place, bf16[128,2048]{1,0:T(8,128)(2,1)S(1)} %copy-done.2, bf16[128,2048]{1,0:T(8,128)(2,1)} %collective-permute-done.refs_1_, bf16[128,2048]{1,0:T(8,128)(2,1)} %collective-permute-done.1.refs_2_, bf16[128,2048]{1,0:T(8,128)(2,1)S(1)} %copy-done.4, ...), custom_call_target="tpu_custom_call" | custom-call | flops 17179869184 | bytes 8388608 | tf_op jit(solution)/shard_map/pallas_call | solution.py:228
  115.2 9.0 %shard_map.57 = (bf16[2,128,512]{2,1,0:T(8,128)(2,1)S(1)}, bf16[2,128,512]{2,1,0:T(8,128)(2,1)S(1)}) custom-call(s32[2]{0:T(128)S(1)} %pad_add_fusion.place, bf16[4,512,128]{2,1,0:T(8,128)(2,1)S(1)} %shard_map.56.queries, bf16[4,128,256]{2,1,0:T(8,128)(2,1)S(1)} %shard_map.55.kv0, bf16[4,128,256]{2,1,0:T(8,128)(2,1)S(1)} %collective-permute-done.22.kv1, ...), custom_call_target="tpu_custom_call" | custom-call | flops 10737418240 | bytes 4194304 | tf_op jit(solution)/shard_map/pallas_call | solution.py:301
  124.3 1.5 collective-permute-start.32
  125.9 2.7 %collective-permute-start.30 = (bf16[2,128,512]{2,1,0:T(8,128)(2,1)S(1)}, bf16[2,128,512]{2,1,0:T(8,128)(2,1)S(1)}, u32[]{:S(2)}, u32[]{:S(2)}) collective-permute-start(bf16[2,128,512]{2,1,0:T(8,128)(2,1)S(1)} %get-tuple-element.47.refs_0_), channel_id=1, source_target_pairs={{0,16},{1,17},{2,18},{3,19},{4,20},{5,21},{6,22},{7,23},{8,24},{9,... | collective-permute-start | bytes 786440 | tf_op jit(solution)/shard_map/ppermute | solution.py:134
  128.6 4.0 %collective-permute-done.32.refs_4_ = bf16[2,128,512]{2,1,0:T(8,128)(2,1)S(1)} collective-permute-done((bf16[2,128,512]{2,1,0:T(8,128)(2,1)S(1)}, bf16[2,128,512]{2,1,0:T(8,128)(2,1)S(1)}, u32[]{:S(2)}, u32[]{:S(2)}) %collective-permute-start.32) | collective-permute-done | bytes 262176 | tf_op jit(solution)/shard_map/ppermute | solution.py:134
  132.7 6.3 %collective-permute-done.29.refs_1_ = bf16[2,128,512]{2,1,0:T(8,128)(2,1)S(1)} collective-permute-done((bf16[2,128,512]{2,1,0:T(8,128)(2,1)S(1)}, bf16[2,128,512]{2,1,0:T(8,128)(2,1)S(1)}, u32[]{:S(2)}, u32[]{:S(2)}) %collective-permute-start.29) | collective-permute-done | bytes 262176 | tf_op jit(solution)/shard_map/ppermute | solution.py:134
  139.0 7.4 %collective-permute-done.30.refs_2_ = bf16[2,128,512]{2,1,0:T(8,128)(2,1)S(1)} collective-permute-done((bf16[2,128,512]{2,1,0:T(8,128)(2,1)S(1)}, bf16[2,128,512]{2,1,0:T(8,128)(2,1)S(1)}, u32[]{:S(2)}, u32[]{:S(2)}) %collective-permute-start.30) | collective-permute-done | bytes 262176 | tf_op jit(solution)/shard_map/ppermute | solution.py:134
  146.4 5.4 %collective-permute-done.34.refs_6_ = bf16[2,128,512]{2,1,0:T(8,128)(2,1)S(1)} collective-permute-done((bf16[2,128,512]{2,1,0:T(8,128)(2,1)S(1)}, bf16[2,128,512]{2,1,0:T(8,128)(2,1)S(1)}, u32[]{:S(2)}, u32[]{:S(2)}) %collective-permute-start.34) | collective-permute-done | bytes 262176 | tf_op jit(solution)/shard_map/ppermute | solution.py:134
  151.7 8.2 %collective-permute-done.31.refs_3_ = bf16[2,128,512]{2,1,0:T(8,128)(2,1)S(1)} collective-permute-done((bf16[2,128,512]{2,1,0:T(8,128)(2,1)S(1)}, bf16[2,128,512]{2,1,0:T(8,128)(2,1)S(1)}, u32[]{:S(2)}, u32[]{:S(2)}) %collective-permute-start.31) | collective-permute-done | bytes 262176 | tf_op jit(solution)/shard_map/ppermute | solution.py:134
  159.9 3.7 %collective-permute-done.35.refs_7_ = bf16[2,128,512]{2,1,0:T(8,128)(2,1)S(1)} collective-permute-done((bf16[2,128,512]{2,1,0:T(8,128)(2,1)S(1)}, bf16[2,128,512]{2,1,0:T(8,128)(2,1)S(1)}, u32[]{:S(2)}, u32[]{:S(2)}) %collective-permute-start.35) | collective-permute-done | bytes 262176 | tf_op jit(solution)/shard_map/ppermute | solution.py:134
  163.6 6.6 %shard_map.58 = (bf16[128,1024]{1,0:T(8,128)(2,1)S(1)}, bf16[128,1024]{1,0:T(8,128)(2,1)}) custom-call(s32[2]{0:T(128)S(1)} %pad_add_fusion.place, bf16[2,128,512]{2,1,0:T(8,128)(2,1)S(1)} %get-tuple-element.47.refs_0_, bf16[2,128,512]{2,1,0:T(8,128)(2,1)S(1)} %collective-permute-done.29.refs_1_, bf16[2,128,512]{2,1,0:T(8,128)(2,1)S(1)} %collective-permute-done.30.refs_2_, ...), custom_call_target="tpu_custom_call" | custom-call | flops 2147483648 | bytes 12582912 | tf_op jit(solution)/shard_map/pallas_call | solution.py:372
  170.2 2.1 %collective-permute-start.36 = (bf16[128,1024]{1,0:T(8,128)(2,1)}, bf16[128,1024]{1,0:T(8,128)(2,1)S(1)}, u32[]{:S(2)}, u32[]{:S(2)}) collective-permute-start(bf16[128,1024]{1,0:T(8,128)(2,1)} %get-tuple-element.51), channel_id=1, source_target_pairs={{0,8},{1,24},{2,10},{3,26},{4,12},{5,28},{6,14},{7,30},{8,0},{9,16... | collective-permute-start | bytes 786440 | tf_op jit(solution)/shard_map/ppermute | solution.py:134
  172.2 1.9 collective-permute-start.37
  174.2 8.3 %collective-permute-done.36 = bf16[128,1024]{1,0:T(8,128)(2,1)S(1)} collective-permute-done((bf16[128,1024]{1,0:T(8,128)(2,1)}, bf16[128,1024]{1,0:T(8,128)(2,1)S(1)}, u32[]{:S(2)}, u32[]{:S(2)}) %collective-permute-start.36) | collective-permute-done | bytes 262176 | tf_op jit(solution)/shard_map/ppermute | solution.py:134
  182.4 11.3 %collective-permute-done.37 = bf16[128,1024]{1,0:T(8,128)(2,1)S(1)} collective-permute-done((bf16[128,1024]{1,0:T(8,128)(2,1)S(1)}, bf16[128,1024]{1,0:T(8,128)(2,1)S(1)}, u32[]{:S(2)}, u32[]{:S(2)}) %collective-permute-start.37) | collective-permute-done | bytes 262176 | tf_op jit(solution)/shard_map/ppermute | solution.py:134
  193.7 0.8 pad_maximum_fusion.3
  (61 shorter events, 1.0 us)
Async XLA Ops:
  0.0 20.3 %collective-permute-start = (bf16[128,2048]{1,0:T(8,128)(2,1)}, bf16[128,2048]{1,0:T(8,128)(2,1)}, u32[]{:S(2)}, u32[]{:S(2)}) collective-permute-start(bf16[128,2048]{1,0:T(8,128)(2,1)} %refs_0_.3), channel_id=1, source_target_pairs={{0,1},{1,0},{2,3},{3,2},{4,5},{5,4},{6,7},{7,6},{8,9},{9,8},{10,11... | collective-permute-start | bytes 1572872 | tf_op jit(solution)/shard_map/ppermute | solution.py:134
  0.0 25.2 %collective-permute-start.1 = (bf16[128,2048]{1,0:T(8,128)(2,1)}, bf16[128,2048]{1,0:T(8,128)(2,1)}, u32[]{:S(2)}, u32[]{:S(2)}) collective-permute-start(bf16[128,2048]{1,0:T(8,128)(2,1)} %refs_0_.3), channel_id=1, source_target_pairs={{0,8},{1,9},{2,10},{3,11},{4,12},{5,13},{6,14},{7,15},{8,0},{9,1},... | collective-permute-start | bytes 1572872 | tf_op jit(solution)/shard_map/ppermute | solution.py:134
  2.1 39.6 %collective-permute-start.4 = (bf16[128,2048]{1,0:T(8,128)(2,1)}, bf16[128,2048]{1,0:T(8,128)(2,1)}, u32[]{:S(2)}, u32[]{:S(2)}) collective-permute-start(bf16[128,2048]{1,0:T(8,128)(2,1)} %refs_0_.3), channel_id=1, source_target_pairs={{0,16},{1,17},{2,18},{3,19},{4,20},{5,21},{6,22},{7,23},{8,24},{9,... | collective-permute-start | bytes 1572872 | tf_op jit(solution)/shard_map/ppermute | solution.py:134
  6.3 3.8 %copy-start = (bf16[2048,256]{1,0:T(8,128)(2,1)S(1)}, bf16[2048,256]{1,0:T(8,128)(2,1)}, u32[]{:S(2)}) copy-start(bf16[2048,256]{1,0:T(8,128)(2,1)} %refs_8_.1) | copy-start | bytes 3145732
  6.3 5.3 %copy-start.6 = (bf16[256,512]{1,0:T(8,128)(2,1)S(1)}, bf16[256,512]{1,0:T(8,128)(2,1)}, u32[]{:S(2)}) copy-start(bf16[256,512]{1,0:T(8,128)(2,1)} %param.8) | copy-start | bytes 786436
  8.6 10.2 %collective-permute-start.2 = (bf16[256,768]{1,0:T(8,128)(2,1)S(1)}, bf16[256,768]{1,0:T(8,128)(2,1)}, u32[]{:S(2)}, u32[]{:S(2)}) collective-permute-start(bf16[256,768]{1,0:T(8,128)(2,1)S(1)} %get-tuple-element.60), channel_id=1, source_target_pairs={{0,4},{1,5},{2,6},{3,7},{4,0},{5,1},{6,2},{7,3},{8,12},{9,13},{10,... | collective-permute-start | bytes 1179656 | tf_op jit(solution)/shard_map/ppermute | solution.py:134
  10.2 30.0 %collective-permute-start.6 = (bf16[2048,256]{1,0:T(8,128)(2,1)S(1)}, bf16[2048,256]{1,0:T(8,128)(2,1)S(1)}, u32[]{:S(2)}, u32[]{:S(2)}) collective-permute-start(bf16[2048,256]{1,0:T(8,128)(2,1)S(1)} %copy-done), channel_id=1, source_target_pairs={{0,1},{1,0},{2,3},{3,2},{4,5},{5,4},{6,7},{7,6},{8,9},{9,8},{10,11... | collective-permute-start | bytes 3145736 | tf_op jit(solution)/shard_map/ppermute | solution.py:134
  18.8 28.8 %collective-permute-start.11 = (bf16[2048,256]{1,0:T(8,128)(2,1)S(1)}, bf16[2048,256]{1,0:T(8,128)(2,1)S(1)}, u32[]{:S(2)}, u32[]{:S(2)}) collective-permute-start(bf16[2048,256]{1,0:T(8,128)(2,1)S(1)} %copy-done), channel_id=1, source_target_pairs={{0,4},{1,5},{2,6},{3,7},{4,0},{5,1},{6,2},{7,3},{8,12},{9,13},{10,... | collective-permute-start | bytes 3145736 | tf_op jit(solution)/shard_map/ppermute | solution.py:134
  25.2 13.9 %collective-permute-start.10 = (bf16[256,512]{1,0:T(8,128)(2,1)}, bf16[256,512]{1,0:T(8,128)(2,1)}, u32[]{:S(2)}, u32[]{:S(2)}) collective-permute-start(bf16[256,512]{1,0:T(8,128)(2,1)} %pad_maximum_fusion.6), channel_id=1, source_target_pairs={{0,16},{1,17},{2,18},{3,19},{4,20},{5,21},{6,22},{7,23},{8,24},{9,... | collective-permute-start | bytes 786440 | tf_op jit(solution)/shard_map/ppermute | solution.py:134
  28.8 18.8 %collective-permute-start.3 = (bf16[128,2048]{1,0:T(8,128)(2,1)}, bf16[128,2048]{1,0:T(8,128)(2,1)S(1)}, u32[]{:S(2)}, u32[]{:S(2)}) collective-permute-start(bf16[128,2048]{1,0:T(8,128)(2,1)} %collective-permute-done.1.refs_2_), channel_id=1, source_target_pairs={{0,1},{1,0},{2,3},{3,2},{4,5},{5,4},{6,7},{7,6},{8,9},{9,8},{10,11... | collective-permute-start | bytes 1572872 | tf_op jit(solution)/shard_map/ppermute | solution.py:134
  40.2 25.4 %collective-permute-start.16 = (bf16[2048,256]{1,0:T(8,128)(2,1)S(1)}, bf16[2048,256]{1,0:T(8,128)(2,1)}, u32[]{:S(2)}, u32[]{:S(2)}) collective-permute-start(bf16[2048,256]{1,0:T(8,128)(2,1)S(1)} %collective-permute-done.6.refs_10_), channel_id=1, source_target_pairs={{0,4},{1,5},{2,6},{3,7},{4,0},{5,1},{6,2},{7,3},{8,12},{9,13},{10,... | collective-permute-start | bytes 3145736 | tf_op jit(solution)/shard_map/ppermute | solution.py:134
  41.7 15.2 %collective-permute-start.7 = (bf16[128,2048]{1,0:T(8,128)(2,1)}, bf16[128,2048]{1,0:T(8,128)(2,1)}, u32[]{:S(2)}, u32[]{:S(2)}) collective-permute-start(bf16[128,2048]{1,0:T(8,128)(2,1)} %collective-permute-done.4.refs_4_), channel_id=1, source_target_pairs={{0,8},{1,9},{2,10},{3,11},{4,12},{5,13},{6,14},{7,15},{8,0},{9,1},... | collective-permute-start | bytes 1572872 | tf_op jit(solution)/shard_map/ppermute | solution.py:134
  47.6 3.3 %copy-start.3 = (bf16[128,2048]{1,0:T(8,128)(2,1)}, bf16[128,2048]{1,0:T(8,128)(2,1)S(1)}, u32[]{:S(2)}) copy-start(bf16[128,2048]{1,0:T(8,128)(2,1)S(1)} %collective-permute-done.3.refs_3_) | copy-start | bytes 1572868
  47.6 17.0 %collective-permute-start.9 = (bf16[2,256,768]{2,1,0:T(8,128)(2,1)}, bf16[2,256,768]{2,1,0:T(8,128)(2,1)}, u32[]{:S(2)}, u32[]{:S(2)}) collective-permute-start(bf16[2,256,768]{2,1,0:T(8,128)(2,1)} %pad_maximum_fusion.refs_8_), channel_id=1, source_target_pairs={{0,2},{1,3},{2,0},{3,1},{4,6},{5,7},{6,4},{7,5},{8,10},{9,11},{10,... | collective-permute-start | bytes 2359304 | tf_op jit(solution)/shard_map/ppermute | solution.py:134
  47.6 14.8 %collective-permute-start.12 = (bf16[2,256,256]{2,1,0:T(8,128)(2,1)}, bf16[2,256,256]{2,1,0:T(8,128)(2,1)}, u32[]{:S(2)}, u32[]{:S(2)}) collective-permute-start(bf16[2,256,256]{2,1,0:T(8,128)(2,1)} %pad_maximum_fusion.7), channel_id=1, source_target_pairs={{0,8},{1,9},{2,10},{3,11},{4,12},{5,13},{6,14},{7,15},{8,0},{9,1},... | collective-permute-start | bytes 786440 | tf_op jit(solution)/shard_map/ppermute | solution.py:134
  50.2 14.4 %collective-permute-start.5 = (bf16[128,2048]{1,0:T(8,128)(2,1)}, bf16[128,2048]{1,0:T(8,128)(2,1)}, u32[]{:S(2)}, u32[]{:S(2)}) collective-permute-start(bf16[128,2048]{1,0:T(8,128)(2,1)} %collective-permute-done.4.refs_4_), channel_id=1, source_target_pairs={{0,1},{1,0},{2,3},{3,2},{4,5},{5,4},{6,7},{7,6},{8,9},{9,8},{10,11... | collective-permute-start | bytes 1572872 | tf_op jit(solution)/shard_map/ppermute | solution.py:134
  51.7 15.2 %copy-start.5 = (bf16[256,512]{1,0:T(8,128)(2,1)S(1)}, bf16[256,512]{1,0:T(8,128)(2,1)}, u32[]{:S(2)}) copy-start(bf16[256,512]{1,0:T(8,128)(2,1)} %get-tuple-element.38) | copy-start | bytes 786436
  56.9 19.3 %collective-permute-start.15 = (bf16[256,512]{1,0:T(8,128)(2,1)}, bf16[256,512]{1,0:T(8,128)(2,1)S(1)}, u32[]{:S(2)}, u32[]{:S(2)}) collective-permute-start(bf16[256,512]{1,0:T(8,128)(2,1)} %get-tuple-element.39), channel_id=1, source_target_pairs={{0,24},{1,25},{2,26},{3,27},{4,28},{5,29},{6,30},{7,31},{8,16},{9,... | collective-permute-start | bytes 786440 | tf_op jit(solution)/shard_map/ppermute | solution.py:134
  62.4 13.8 %collective-permute-start.13 = (bf16[256,512]{1,0:T(8,128)(2,1)}, bf16[256,512]{1,0:T(8,128)(2,1)S(1)}, u32[]{:S(2)}, u32[]{:S(2)}) collective-permute-start(bf16[256,512]{1,0:T(8,128)(2,1)} %get-tuple-element.37), channel_id=1, source_target_pairs={{0,8},{1,9},{2,10},{3,11},{4,12},{5,13},{6,14},{7,15},{8,0},{9,1},... | collective-permute-start | bytes 786440 | tf_op jit(solution)/shard_map/ppermute | solution.py:134
  65.5 10.8 %collective-permute-start.17 = (bf16[3,256,256]{2,1,0:T(8,128)(2,1)S(1)}, bf16[3,256,256]{2,1,0:T(8,128)(2,1)S(1)}, u32[]{:S(2)}, u32[]{:S(2)}) collective-permute-start(bf16[3,256,256]{2,1,0:T(8,128)(2,1)S(1)} %pad_maximum_fusion.5.refs_10_), channel_id=1, source_target_pairs={{0,4},{1,5},{2,6},{3,7},{4,0},{5,1},{6,2},{7,3},{8,12},{9,13},{10,... | collective-permute-start | bytes 1179656 | tf_op jit(solution)/shard_map/ppermute | solution.py:134
  66.9 13.7 %collective-permute-start.14 = (bf16[256,512]{1,0:T(8,128)(2,1)S(1)}, bf16[256,512]{1,0:T(8,128)(2,1)S(1)}, u32[]{:S(2)}, u32[]{:S(2)}) collective-permute-start(bf16[256,512]{1,0:T(8,128)(2,1)S(1)} %copy-done.5), channel_id=1, source_target_pairs={{0,16},{1,17},{2,18},{3,19},{4,20},{5,21},{6,22},{7,23},{8,24},{9,... | collective-permute-start | bytes 786440 | tf_op jit(solution)/shard_map/ppermute | solution.py:134
  68.8 12.8 %collective-permute-start.8 = (bf16[128,2048]{1,0:T(8,128)(2,1)}, bf16[128,2048]{1,0:T(8,128)(2,1)S(1)}, u32[]{:S(2)}, u32[]{:S(2)}) collective-permute-start(bf16[128,2048]{1,0:T(8,128)(2,1)} %collective-permute-done.7.refs_6_), channel_id=1, source_target_pairs={{0,1},{1,0},{2,3},{3,2},{4,5},{5,4},{6,7},{7,6},{8,9},{9,8},{10,11... | collective-permute-start | bytes 1572872 | tf_op jit(solution)/shard_map/ppermute | solution.py:134
  76.3 14.9 %collective-permute-start.18 = (bf16[2,256,512]{2,1,0:T(8,128)(2,1)S(1)}, bf16[2,256,512]{2,1,0:T(8,128)(2,1)S(1)}, u32[]{:S(2)}, u32[]{:S(2)}) collective-permute-start(bf16[2,256,512]{2,1,0:T(8,128)(2,1)S(1)} %pad_maximum_fusion.2), channel_id=1, source_target_pairs={{0,4},{1,5},{2,6},{3,7},{4,0},{5,1},{6,2},{7,3},{8,12},{9,13},{10,... | collective-permute-start | bytes 1572872 | tf_op jit(solution)/shard_map/ppermute | solution.py:134
  80.6 15.1 %copy-start.1 = (f32[512,128]{1,0:T(8,128)S(1)}, f32[512,128]{1,0:T(8,128)}, u32[]{:S(2)}) copy-start(f32[512,128]{1,0:T(8,128)} %get-tuple-element.81.refs_14_.refs_13_) | copy-start | bytes 786436
  80.6 15.1 %copy-start.2 = (bf16[128,2048]{1,0:T(8,128)(2,1)S(1)}, bf16[128,2048]{1,0:T(8,128)(2,1)}, u32[]{:S(2)}) copy-start(bf16[128,2048]{1,0:T(8,128)(2,1)} %refs_0_.3) | copy-start | bytes 1572868
  80.6 15.1 %copy-start.4 = (bf16[128,2048]{1,0:T(8,128)(2,1)S(1)}, bf16[128,2048]{1,0:T(8,128)(2,1)}, u32[]{:S(2)}) copy-start(bf16[128,2048]{1,0:T(8,128)(2,1)} %copy-done.3) | copy-start | bytes 1572868
  80.6 15.0 %collective-permute-start.19 = (bf16[256,512]{1,0:T(8,128)(2,1)S(1)}, bf16[256,512]{1,0:T(8,128)(2,1)S(1)}, u32[]{:S(2)}, u32[]{:S(2)}) collective-permute-start(bf16[256,512]{1,0:T(8,128)(2,1)S(1)} %collective-permute-done.14), channel_id=1, source_target_pairs={{0,4},{1,5},{2,6},{3,7},{4,0},{5,1},{6,2},{7,3},{8,12},{9,13},{10,... | collective-permute-start | bytes 786440 | tf_op jit(solution)/shard_map/ppermute | solution.py:134
  81.6 14.1 %collective-permute-start.20 = (bf16[6,256,256]{2,1,0:T(8,128)(2,1)S(1)}, bf16[6,256,256]{2,1,0:T(8,128)(2,1)S(1)}, u32[]{:S(2)}, u32[]{:S(2)}) collective-permute-start(bf16[6,256,256]{2,1,0:T(8,128)(2,1)S(1)} %pad_maximum_fusion.1), channel_id=1, source_target_pairs={{0,2},{1,3},{2,0},{3,1},{4,6},{5,7},{6,4},{7,5},{8,10},{9,11},{10,... | collective-permute-start | bytes 2359304 | tf_op jit(solution)/shard_map/ppermute | solution.py:134
  100.5 8.9 %collective-permute-start.21 = (bf16[6,256,512]{2,1,0:T(8,128)(2,1)S(1)}, bf16[6,256,512]{2,1,0:T(8,128)(2,1)S(1)}, u32[]{:S(2)}, u32[]{:S(2)}) collective-permute-start(bf16[6,256,512]{2,1,0:T(8,128)(2,1)S(1)} %slice_dynamic-update-slice_fusion.refs_10_), channel_id=1, source_target_pairs={{0,2},{1,3},{2,0},{3,1},{4,6},{5,7},{6,4},{7,5},{8,10},{9,11},{10,... | collective-permute-start | bytes 4718600 | tf_op jit(solution)/shard_map/ppermute | solution.py:134
  100.6 3.8 %collective-permute-start.22 = (bf16[4,128,256]{2,1,0:T(8,128)(2,1)S(1)}, bf16[4,128,256]{2,1,0:T(8,128)(2,1)S(1)}, u32[]{:S(2)}, u32[]{:S(2)}) collective-permute-start(bf16[4,128,256]{2,1,0:T(8,128)(2,1)S(1)} %shard_map.55.kv0), channel_id=1, source_target_pairs={{0,2},{1,3},{2,0},{3,1},{4,6},{5,7},{6,4},{7,5},{8,10},{9,11},{10,... | collective-permute-start | bytes 786440 | tf_op jit(solution)/shard_map/ppermute | solution.py:134
  101.1 8.3 %collective-permute-start.23 = (bf16[4,128,256]{2,1,0:T(8,128)(2,1)S(1)}, bf16[4,128,256]{2,1,0:T(8,128)(2,1)S(1)}, u32[]{:S(2)}, u32[]{:S(2)}) collective-permute-start(bf16[4,128,256]{2,1,0:T(8,128)(2,1)S(1)} %shard_map.55.kv0), channel_id=1, source_target_pairs={{0,4},{1,5},{2,6},{3,7},{4,0},{5,1},{6,2},{7,3},{8,12},{9,13},{10,... | collective-permute-start | bytes 786440 | tf_op jit(solution)/shard_map/ppermute | solution.py:134
  101.4 22.9 %collective-permute-start.25 = (bf16[2048,256]{1,0:T(8,128)(2,1)S(1)}, bf16[2048,256]{1,0:T(8,128)(2,1)S(1)}, u32[]{:S(2)}, u32[]{:S(2)}) collective-permute-start(bf16[2048,256]{1,0:T(8,128)(2,1)S(1)} %copy-done), channel_id=1, source_target_pairs={{0,2},{1,3},{2,0},{3,1},{4,6},{5,7},{6,4},{7,5},{8,10},{9,11},{10,... | collective-permute-start | bytes 3145736 | tf_op jit(solution)/shard_map/ppermute | solution.py:134
  101.4 22.9 %collective-permute-start.26 = (bf16[2048,256]{1,0:T(8,128)(2,1)S(1)}, bf16[2048,256]{1,0:T(8,128)(2,1)S(1)}, u32[]{:S(2)}, u32[]{:S(2)}) collective-permute-start(bf16[2048,256]{1,0:T(8,128)(2,1)S(1)} %collective-permute-done.6.refs_10_), channel_id=1, source_target_pairs={{0,2},{1,3},{2,0},{3,1},{4,6},{5,7},{6,4},{7,5},{8,10},{9,11},{10,... | collective-permute-start | bytes 3145736 | tf_op jit(solution)/shard_map/ppermute | solution.py:134
  104.3 20.0 %collective-permute-start.27 = (bf16[2048,256]{1,0:T(8,128)(2,1)S(1)}, bf16[2048,256]{1,0:T(8,128)(2,1)S(1)}, u32[]{:S(2)}, u32[]{:S(2)}) collective-permute-start(bf16[2048,256]{1,0:T(8,128)(2,1)S(1)} %collective-permute-done.11.refs_12_), channel_id=1, source_target_pairs={{0,2},{1,3},{2,0},{3,1},{4,6},{5,7},{6,4},{7,5},{8,10},{9,11},{10,... | collective-permute-start | bytes 3145736 | tf_op jit(solution)/shard_map/ppermute | solution.py:134
  109.4 15.0 %collective-permute-start.28 = (bf16[2048,256]{1,0:T(8,128)(2,1)}, bf16[2048,256]{1,0:T(8,128)(2,1)S(1)}, u32[]{:S(2)}, u32[]{:S(2)}) collective-permute-start(bf16[2048,256]{1,0:T(8,128)(2,1)} %collective-permute-done.16.refs_14_), channel_id=1, source_target_pairs={{0,2},{1,3},{2,0},{3,1},{4,6},{5,7},{6,4},{7,5},{8,10},{9,11},{10,... | collective-permute-start | bytes 3145736 | tf_op jit(solution)/shard_map/ppermute | solution.py:134
  109.4 5.9 %collective-permute-start.24 = (bf16[4,128,256]{2,1,0:T(8,128)(2,1)S(1)}, bf16[4,128,256]{2,1,0:T(8,128)(2,1)S(1)}, u32[]{:S(2)}, u32[]{:S(2)}) collective-permute-start(bf16[4,128,256]{2,1,0:T(8,128)(2,1)S(1)} %collective-permute-done.23.kv2), channel_id=1, source_target_pairs={{0,2},{1,3},{2,0},{3,1},{4,6},{5,7},{6,4},{7,5},{8,10},{9,11},{10,... | collective-permute-start | bytes 786440 | tf_op jit(solution)/shard_map/ppermute | solution.py:134
  124.3 8.3 %collective-permute-start.32 = (bf16[2,128,512]{2,1,0:T(8,128)(2,1)S(1)}, bf16[2,128,512]{2,1,0:T(8,128)(2,1)S(1)}, u32[]{:S(2)}, u32[]{:S(2)}) collective-permute-start(bf16[2,128,512]{2,1,0:T(8,128)(2,1)S(1)} %get-tuple-element.49), channel_id=1, source_target_pairs={{0,1},{1,0},{2,3},{3,2},{4,5},{5,4},{6,7},{7,6},{8,9},{9,8},{10,11... | collective-permute-start | bytes 786440 | tf_op jit(solution)/shard_map/ppermute | solution.py:134
  125.9 13.1 %collective-permute-start.29 = (bf16[2,128,512]{2,1,0:T(8,128)(2,1)S(1)}, bf16[2,128,512]{2,1,0:T(8,128)(2,1)S(1)}, u32[]{:S(2)}, u32[]{:S(2)}) collective-permute-start(bf16[2,128,512]{2,1,0:T(8,128)(2,1)S(1)} %get-tuple-element.47.refs_0_), channel_id=1, source_target_pairs={{0,8},{1,9},{2,10},{3,11},{4,12},{5,13},{6,14},{7,15},{8,0},{9,1},... | collective-permute-start | bytes 786440 | tf_op jit(solution)/shard_map/ppermute | solution.py:134
  125.9 20.5 %collective-permute-start.30 = (bf16[2,128,512]{2,1,0:T(8,128)(2,1)S(1)}, bf16[2,128,512]{2,1,0:T(8,128)(2,1)S(1)}, u32[]{:S(2)}, u32[]{:S(2)}) collective-permute-start(bf16[2,128,512]{2,1,0:T(8,128)(2,1)S(1)} %get-tuple-element.47.refs_0_), channel_id=1, source_target_pairs={{0,16},{1,17},{2,18},{3,19},{4,20},{5,21},{6,22},{7,23},{8,24},{9,... | collective-permute-start | bytes 786440 | tf_op jit(solution)/shard_map/ppermute | solution.py:134
  132.6 19.1 %collective-permute-start.34 = (bf16[2,128,512]{2,1,0:T(8,128)(2,1)S(1)}, bf16[2,128,512]{2,1,0:T(8,128)(2,1)S(1)}, u32[]{:S(2)}, u32[]{:S(2)}) collective-permute-start(bf16[2,128,512]{2,1,0:T(8,128)(2,1)S(1)} %collective-permute-done.32.refs_4_), channel_id=1, source_target_pairs={{0,16},{1,17},{2,18},{3,19},{4,20},{5,21},{6,22},{7,23},{8,24},{9,... | collective-permute-start | bytes 786440 | tf_op jit(solution)/shard_map/ppermute | solution.py:134
  139.0 20.9 %collective-permute-start.33 = (bf16[2,128,512]{2,1,0:T(8,128)(2,1)S(1)}, bf16[2,128,512]{2,1,0:T(8,128)(2,1)S(1)}, u32[]{:S(2)}, u32[]{:S(2)}) collective-permute-start(bf16[2,128,512]{2,1,0:T(8,128)(2,1)S(1)} %collective-permute-done.32.refs_4_), channel_id=1, source_target_pairs={{0,8},{1,9},{2,10},{3,11},{4,12},{5,13},{6,14},{7,15},{8,0},{9,1},... | collective-permute-start | bytes 786440 | tf_op jit(solution)/shard_map/ppermute | solution.py:134
  146.4 13.5 %collective-permute-start.31 = (bf16[2,128,512]{2,1,0:T(8,128)(2,1)S(1)}, bf16[2,128,512]{2,1,0:T(8,128)(2,1)S(1)}, u32[]{:S(2)}, u32[]{:S(2)}) collective-permute-start(bf16[2,128,512]{2,1,0:T(8,128)(2,1)S(1)} %collective-permute-done.30.refs_2_), channel_id=1, source_target_pairs={{0,8},{1,9},{2,10},{3,11},{4,12},{5,13},{6,14},{7,15},{8,0},{9,1},... | collective-permute-start | bytes 786440 | tf_op jit(solution)/shard_map/ppermute | solution.py:134
  151.7 11.8 %collective-permute-start.35 = (bf16[2,128,512]{2,1,0:T(8,128)(2,1)S(1)}, bf16[2,128,512]{2,1,0:T(8,128)(2,1)S(1)}, u32[]{:S(2)}, u32[]{:S(2)}) collective-permute-start(bf16[2,128,512]{2,1,0:T(8,128)(2,1)S(1)} %collective-permute-done.34.refs_6_), channel_id=1, source_target_pairs={{0,8},{1,9},{2,10},{3,11},{4,12},{5,13},{6,14},{7,15},{8,0},{9,1},... | collective-permute-start | bytes 786440 | tf_op jit(solution)/shard_map/ppermute | solution.py:134
  170.2 12.3 %collective-permute-start.36 = (bf16[128,1024]{1,0:T(8,128)(2,1)}, bf16[128,1024]{1,0:T(8,128)(2,1)S(1)}, u32[]{:S(2)}, u32[]{:S(2)}) collective-permute-start(bf16[128,1024]{1,0:T(8,128)(2,1)} %get-tuple-element.51), channel_id=1, source_target_pairs={{0,8},{1,24},{2,10},{3,26},{4,12},{5,28},{6,14},{7,30},{8,0},{9,16... | collective-permute-start | bytes 786440 | tf_op jit(solution)/shard_map/ppermute | solution.py:134
  172.2 21.5 %collective-permute-start.37 = (bf16[128,1024]{1,0:T(8,128)(2,1)S(1)}, bf16[128,1024]{1,0:T(8,128)(2,1)S(1)}, u32[]{:S(2)}, u32[]{:S(2)}) collective-permute-start(bf16[128,1024]{1,0:T(8,128)(2,1)S(1)} %get-tuple-element.52), channel_id=1, source_target_pairs={{0,0},{1,16},{2,2},{3,18},{4,4},{5,20},{6,6},{7,22},{8,8},{9,24},{... | collective-permute-start | bytes 786440 | tf_op jit(solution)/shard_map/ppermute | solution.py:134

commit v3 on v2

--- a/solution.py
+++ b/solution.py
@@ -254,42 +254,44 @@
     for handle in handles:
         handle.wait()
     z, e = ctx // 4, ctx % 4
-    scale = 1.0 / math.sqrt(HEAD_SIZE)
+    scale = math.log2(math.e) / math.sqrt(HEAD_SIZE)
     span = 4 * rows
     heads = queries.shape[1] // rows
     group = 2
-    for block in range(4):
+    row = lax.broadcasted_iota(jnp.int32, (group * rows, span), 0) % rows + e * rows
+    column = lax.broadcasted_iota(jnp.int32, (group * rows, span), 1)
+    allowed = column <= row
+
+    def block_of(block, out):
         count = (block + 1) * span
-        slot = z ^ block
         keys, values = store[:count, :HEAD_SIZE], store[:count, HEAD_SIZE:]
-        row = lax.broadcasted_iota(jnp.int32, (group * rows, span), 0) % rows + e * rows
-        column = lax.broadcasted_iota(jnp.int32, (group * rows, span), 1)
-        allowed = column <= row
         for first in range(0, heads, group):
-            query = queries[slot, pl.ds(first * rows, group * rows), :]
+            query = queries[z ^ block, pl.ds(first * rows, group * rows), :]
             scores = lax.dot_general(
                 query, keys, (((1,), (1,)), ((), ())), preferred_element_type=jnp.float32
-            ) * jnp.float32(scale)
+            )
             last = jnp.where(allowed, scores[:, count - span :], jnp.float32(-1e30))
             scores = jnp.concatenate([scores[:, : count - span], last], axis=1) if block else last
             top = jnp.max(scores, axis=1, keepdims=True)
-            weights = jnp.exp(scores - top)
+            weights = jnp.exp2((scores - top) * jnp.float32(scale))
             total = jnp.sum(weights, axis=1, keepdims=True)
             summed = jnp.dot(
                 weights.astype(jnp.bfloat16), values, preferred_element_type=jnp.float32
             )
             normed = (summed / total).astype(jnp.bfloat16)
             for k in range(group):
-                head = first + k
-                piece = normed[k * rows : (k + 1) * rows]
-
-                @pl.when(x == block // 2)
-                def _():
-                    mine[block % 2, :, head * HEAD_SIZE : (head + 1) * HEAD_SIZE] = piece
-
-                @pl.when(x != block // 2)
-                def _():
-                    other[block % 2, :, head * HEAD_SIZE : (head + 1) * HEAD_SIZE] = piece
+                at = slice((first + k) * HEAD_SIZE, (first + k + 1) * HEAD_SIZE)
+                out[block // 2, :, at] = normed[k * rows : (k + 1) * rows]
+
+    @pl.when(x == 0)
+    def _():
+        for block in range(4):
+            block_of(block, mine if block in (0, 3) else other)
+
+    @pl.when(x == 1)
+    def _():
+        for block in range(4):
+            block_of(block, mine if block in (1, 2) else other)
 
 
 def attend(place, queries, kv):
@@ -492,10 +494,10 @@
     first, second = project_out(place, attn, out_weights)
 
     def home(m):
-        return lambda z, y, c, x: (2 * x + (z % 2 ^ m), y, c, z // 2)
+        return lambda z, y, c, x: (x ^ 3 * (z % 2 ^ m), y, c, z // 2)
 
     first, second = move(first, home(0)), move(second, home(1))
-    odd = z % 2 == 1
+    odd = z // 2 == 1
     return jnp.concatenate(
         [jnp.where(odd, second, first), jnp.where(odd, first, second)], axis=1
     )

time: 195 us -> 191 us (0.979)
  the two profiles are of different devices: /device:TPU:2 before, /device:TPU:0 now
where the time goes in v3:
time: 191 us; the launch traced here: 190 us
  waiting for transfers between devices  117 us (61%)
  starting transfers between devices  34.8 us (18%)
  Pallas kernels  23.8 us (12%)
  other arithmetic  7.49 us (4%)
  local copies, waits for them, and re-layouts  6.89 us (4%)
    ppermute x38, waiting for transfers between devices, move(): return lax.ppermute(array, AXES, moves(target))  117 us
    ppermute x38, starting transfers between devices, move(): return lax.ppermute(array, AXES, moves(target))  34.8 us
    pallas_call x2, Pallas kernels, project(): pl.pallas_call(functools.partial(kernel, plan), out_shape=jax.ShapeDtypeS...  10.1 us
    pallas_call x1, Pallas kernels, attend(): pl.pallas_call(attend_kernel, out_shape=(shape, shape), in_specs=[smem_sp...  7.08 us
    pallas_call x1, Pallas kernels, project_out(): pl.pallas_call(output_kernel, out_shape=(shape, shape), in_specs=[smem_sp...  6.61 us
    dynamic_slice x5, local copies, waits for them, and re-layouts, columns(): return lax.dynamic_slice_in_dim(weight, head * width, width, 1)  4.78 us
  transfers between devices with their start and end apart: 38, of which 21 were waited for; matrix products, arithmetic and copies ran while one was open for 7% of the time, Pallas kernels for 7%

profile of v3, /device:TPU:0, one launch (start us, length us, event | category | flops | bytes accessed | tf_op | source)
XLA Modules:
  0.0 190.2 jit_solution(15324287794496425204)
XLA Ops:
  0.0 2.9 %collective-permute-start = (bf16[128,2048]{1,0:T(8,128)(2,1)}, bf16[128,2048]{1,0:T(8,128)(2,1)}, u32[]{:S(2)}, u32[]{:S(2)}) collective-permute-start(bf16[128,2048]{1,0:T(8,128)(2,1)} %refs_0_.3), channel_id=1, source_target_pairs={{0,1},{1,0},{2,3},{3,2},{4,5},{5,4},{6,7},{7,6},{8,9},{9,8},{10,11... | collective-permute-start | bytes 1572872 | tf_op jit(solution)/shard_map/ppermute | solution.py:134
  2.9 1.6 collective-permute-start.1
  4.5 2.6 %collective-permute-start.4 = (bf16[128,2048]{1,0:T(8,128)(2,1)}, bf16[128,2048]{1,0:T(8,128)(2,1)}, u32[]{:S(2)}, u32[]{:S(2)}) collective-permute-start(bf16[128,2048]{1,0:T(8,128)(2,1)} %refs_0_.3), channel_id=1, source_target_pairs={{0,16},{1,17},{2,18},{3,19},{4,20},{5,21},{6,22},{7,23},{8,24},{9,... | collective-permute-start | bytes 1572872 | tf_op jit(solution)/shard_map/ppermute | solution.py:134
  7.1 1.6 constant_dynamic-slice_fusion.6
  8.7 2.2 %constant_dynamic-slice_fusion.2 = (bf16[256,512]{1,0:T(8,128)(2,1)}, bf16[256,512]{1,0:T(8,128)(2,1)}, bf16[256,512]{1,0:T(8,128)(2,1)S(1)}, bf16[256,512]{1,0:T(8,128)(2,1)}) fusion(bf16[256,2048]{1,0:T(8,128)(2,1)} %param.6, s32[]{:T(128)S(6)} %select_n.73, s32[]{:T(128)S(6)} %select_n.67, s32[]{:T(128)S(6)} %select_n.66, s32[]{:T(128)S(6)} %select_n.72), kind=kLoop, calls=%fused_computation.26 | loop fusion | bytes 2097168 | tf_op jit(solution)/shard_map/dynamic_slice | solution.py:403
  11.0 1.6 collective-permute-start.2
  12.6 0.5 collective-permute-start.6
  13.1 0.9 constant_dynamic-slice_fusion.8
  14.0 0.7 pad_maximum_fusion.6
  14.8 6.3 %collective-permute-done.2 = bf16[256,768]{1,0:T(8,128)(2,1)} collective-permute-done((bf16[256,768]{1,0:T(8,128)(2,1)S(1)}, bf16[256,768]{1,0:T(8,128)(2,1)}, u32[]{:S(2)}, u32[]{:S(2)}) %collective-permute-start.2) | collective-permute-done | bytes 393248 | tf_op jit(solution)/shard_map/ppermute | solution.py:134
  21.2 1.5 collective-permute-start.11
  22.7 5.0 %collective-permute-done.1.refs_2_ = bf16[128,2048]{1,0:T(8,128)(2,1)} collective-permute-done((bf16[128,2048]{1,0:T(8,128)(2,1)}, bf16[128,2048]{1,0:T(8,128)(2,1)}, u32[]{:S(2)}, u32[]{:S(2)}) %collective-permute-start.1) | collective-permute-done | bytes 524320 | tf_op jit(solution)/shard_map/ppermute | solution.py:134
  27.7 0.6 collective-permute-start.10
  28.3 0.9 maximum_bitcast_fusion
  29.2 2.0 %pad_maximum_fusion.refs_8_ = bf16[2,256,768]{2,1,0:T(8,128)(2,1)} fusion(bf16[1,256,768]{2,1,0:T(8,128)(2,1)} %bitcast.3, bf16[1,256,768]{2,1,0:T(8,128)(2,1)S(1)} %get-tuple-element.59), kind=kLoop, calls=%fused_computation | loop fusion | flops 393216 | bytes 1572864 | tf_op jit(solution)/shard_map/stack | solution.py:436
  31.2 0.5 collective-permute-start.3
  31.7 9.7 %collective-permute-done.10 = bf16[256,512]{1,0:T(8,128)(2,1)} collective-permute-done((bf16[256,512]{1,0:T(8,128)(2,1)}, bf16[256,512]{1,0:T(8,128)(2,1)}, u32[]{:S(2)}, u32[]{:S(2)}) %collective-permute-start.10) | collective-permute-done | bytes 262176 | tf_op jit(solution)/shard_map/ppermute | solution.py:134
  41.4 1.0 fusion.3
  42.5 1.6 collective-permute-start.16
  44.2 0.7 pad_maximum_fusion.7
  44.9 3.9 %collective-permute-done.3.refs_3_ = bf16[128,2048]{1,0:T(8,128)(2,1)S(1)} collective-permute-done((bf16[128,2048]{1,0:T(8,128)(2,1)}, bf16[128,2048]{1,0:T(8,128)(2,1)S(1)}, u32[]{:S(2)}, u32[]{:S(2)}) %collective-permute-start.3) | collective-permute-done | bytes 524320 | tf_op jit(solution)/shard_map/ppermute | solution.py:134
  48.8 1.9 collective-permute-start.12
  50.7 1.0 fusion
  51.7 1.6 collective-permute-start.5
  53.2 0.9 pad_maximum_fusion.8
  54.2 5.2 %collective-permute-done.7.refs_6_ = bf16[128,2048]{1,0:T(8,128)(2,1)} collective-permute-done((bf16[128,2048]{1,0:T(8,128)(2,1)}, bf16[128,2048]{1,0:T(8,128)(2,1)}, u32[]{:S(2)}, u32[]{:S(2)}) %collective-permute-start.7) | collective-permute-done | bytes 524320 | tf_op jit(solution)/shard_map/ppermute | solution.py:134
  59.3 2.4 %collective-permute-start.15 = (bf16[256,512]{1,0:T(8,128)(2,1)}, bf16[256,512]{1,0:T(8,128)(2,1)S(1)}, u32[]{:S(2)}, u32[]{:S(2)}) collective-permute-start(bf16[256,512]{1,0:T(8,128)(2,1)} %get-tuple-element.39), channel_id=1, source_target_pairs={{0,24},{1,25},{2,26},{3,27},{4,28},{5,29},{6,30},{7,31},{8,16},{9,... | collective-permute-start | bytes 786440 | tf_op jit(solution)/shard_map/ppermute | solution.py:134
  61.7 3.1 %collective-permute-done.12 = bf16[2,256,256]{2,1,0:T(8,128)(2,1)} collective-permute-done((bf16[2,256,256]{2,1,0:T(8,128)(2,1)}, bf16[2,256,256]{2,1,0:T(8,128)(2,1)}, u32[]{:S(2)}, u32[]{:S(2)}) %collective-permute-start.12) | collective-permute-done | bytes 262176 | tf_op jit(solution)/shard_map/ppermute | solution.py:134
  64.9 1.0 fusion.2
  65.9 0.1 collective-permute-done.5.refs_5_
  66.1 1.7 collective-permute-done.16.refs_14_
  67.7 1.5 collective-permute-start.17
  69.3 0.9 collective-permute-start.14
  70.2 1.5 collective-permute-start.8
  71.7 6.9 %collective-permute-done.13 = bf16[256,512]{1,0:T(8,128)(2,1)S(1)} collective-permute-done((bf16[256,512]{1,0:T(8,128)(2,1)}, bf16[256,512]{1,0:T(8,128)(2,1)S(1)}, u32[]{:S(2)}, u32[]{:S(2)}) %collective-permute-start.13) | collective-permute-done | bytes 262176 | tf_op jit(solution)/shard_map/ppermute | solution.py:134
  78.7 0.7 collective-permute-start.18
  79.4 3.6 %collective-permute-done.14 = bf16[256,512]{1,0:T(8,128)(2,1)S(1)} collective-permute-done((bf16[256,512]{1,0:T(8,128)(2,1)S(1)}, bf16[256,512]{1,0:T(8,128)(2,1)S(1)}, u32[]{:S(2)}, u32[]{:S(2)}) %collective-permute-start.14) | collective-permute-done | bytes 262176 | tf_op jit(solution)/shard_map/ppermute | solution.py:134
  83.0 0.6 collective-permute-start.19
  83.8 9.8 %collective-permute-done.18 = bf16[2,256,512]{2,1,0:T(8,128)(2,1)S(1)} collective-permute-done((bf16[2,256,512]{2,1,0:T(8,128)(2,1)S(1)}, bf16[2,256,512]{2,1,0:T(8,128)(2,1)S(1)}, u32[]{:S(2)}, u32[]{:S(2)}) %collective-permute-start.18) | collective-permute-done | bytes 524320 | tf_op jit(solution)/shard_map/ppermute | solution.py:134
  93.6 4.5 %collective-permute-done.19 = bf16[256,512]{1,0:T(8,128)(2,1)S(1)} collective-permute-done((bf16[256,512]{1,0:T(8,128)(2,1)S(1)}, bf16[256,512]{1,0:T(8,128)(2,1)S(1)}, u32[]{:S(2)}, u32[]{:S(2)}) %collective-permute-start.19) | collective-permute-done | bytes 262176 | tf_op jit(solution)/shard_map/ppermute | solution.py:134
  98.2 4.7 %shard_map.55.kv0 = bf16[4,128,256]{2,1,0:T(8,128)(2,1)S(1)} custom-call(s32[2]{0:T(128)S(1)} %pad_add_fusion.place, bf16[128,2048]{1,0:T(8,128)(2,1)S(1)} %copy-done.2, bf16[128,2048]{1,0:T(8,128)(2,1)} %collective-permute-done.refs_1_, bf16[128,2048]{1,0:T(8,128)(2,1)} %collective-permute-done.1.refs_2_, bf16[128,2048]{1,0:T(8,128)(2,1)S(1)} %copy-done.4, ...), custom_call_target="tpu_custom_call" | custom-call | flops 17179869184 | bytes 8388608 | tf_op jit(solution)/shard_map/pallas_call | solution.py:228
  103.0 0.5 collective-permute-start.22
  103.5 0.5 collective-permute-start.23
  104.0 0.5 collective-permute-start.26
  104.5 2.3 %collective-permute-done.22.kv1 = bf16[4,128,256]{2,1,0:T(8,128)(2,1)S(1)} collective-permute-done((bf16[4,128,256]{2,1,0:T(8,128)(2,1)S(1)}, bf16[4,128,256]{2,1,0:T(8,128)(2,1)S(1)}, u32[]{:S(2)}, u32[]{:S(2)}) %collective-permute-start.22) | collective-permute-done | bytes 262176 | tf_op jit(solution)/shard_map/ppermute | solution.py:134
  106.7 0.1 collective-permute-start.27
  106.9 4.9 %collective-permute-done.23.kv2 = bf16[4,128,256]{2,1,0:T(8,128)(2,1)S(1)} collective-permute-done((bf16[4,128,256]{2,1,0:T(8,128)(2,1)S(1)}, bf16[4,128,256]{2,1,0:T(8,128)(2,1)S(1)}, u32[]{:S(2)}, u32[]{:S(2)}) %collective-permute-start.23) | collective-permute-done | bytes 262176 | tf_op jit(solution)/shard_map/ppermute | solution.py:134
  111.8 0.5 collective-permute-start.24
  112.3 5.4 %shard_map.56.queries = bf16[4,512,128]{2,1,0:T(8,128)(2,1)S(1)} custom-call(s32[2]{0:T(128)S(1)} %pad_add_fusion.place, bf16[128,2048]{1,0:T(8,128)(2,1)S(1)} %copy-done.2, bf16[128,2048]{1,0:T(8,128)(2,1)} %collective-permute-done.refs_1_, bf16[128,2048]{1,0:T(8,128)(2,1)} %collective-permute-done.1.refs_2_, bf16[128,2048]{1,0:T(8,128)(2,1)S(1)} %copy-done.4, ...), custom_call_target="tpu_custom_call" | custom-call | flops 17179869184 | bytes 8388608 | tf_op jit(solution)/shard_map/pallas_call | solution.py:228
  117.6 7.1 %shard_map.57 = (bf16[2,128,512]{2,1,0:T(8,128)(2,1)S(1)}, bf16[2,128,512]{2,1,0:T(8,128)(2,1)S(1)}) custom-call(s32[2]{0:T(128)S(1)} %pad_add_fusion.place, bf16[4,512,128]{2,1,0:T(8,128)(2,1)S(1)} %shard_map.56.queries, bf16[4,128,256]{2,1,0:T(8,128)(2,1)S(1)} %shard_map.55.kv0, bf16[4,128,256]{2,1,0:T(8,128)(2,1)S(1)} %collective-permute-done.22.kv1, ...), custom_call_target="tpu_custom_call" | custom-call | flops 10737418240 | bytes 4194304 | tf_op jit(solution)/shard_map/pallas_call | solution.py:303
  124.8 0.6 collective-permute-start.32
  125.4 2.2 %collective-permute-start.30 = (bf16[2,128,512]{2,1,0:T(8,128)(2,1)S(1)}, bf16[2,128,512]{2,1,0:T(8,128)(2,1)S(1)}, u32[]{:S(2)}, u32[]{:S(2)}) collective-permute-start(bf16[2,128,512]{2,1,0:T(8,128)(2,1)S(1)} %get-tuple-element.47.refs_0_), channel_id=1, source_target_pairs={{0,16},{1,17},{2,18},{3,19},{4,20},{5,21},{6,22},{7,23},{8,24},{9,... | collective-permute-start | bytes 786440 | tf_op jit(solution)/shard_map/ppermute | solution.py:134
  127.6 5.4 %collective-permute-done.32.refs_4_ = bf16[2,128,512]{2,1,0:T(8,128)(2,1)S(1)} collective-permute-done((bf16[2,128,512]{2,1,0:T(8,128)(2,1)S(1)}, bf16[2,128,512]{2,1,0:T(8,128)(2,1)S(1)}, u32[]{:S(2)}, u32[]{:S(2)}) %collective-permute-start.32) | collective-permute-done | bytes 262176 | tf_op jit(solution)/shard_map/ppermute | solution.py:134
  133.1 0.3 collective-permute-start.34
  133.4 4.9 %collective-permute-done.29.refs_1_ = bf16[2,128,512]{2,1,0:T(8,128)(2,1)S(1)} collective-permute-done((bf16[2,128,512]{2,1,0:T(8,128)(2,1)S(1)}, bf16[2,128,512]{2,1,0:T(8,128)(2,1)S(1)}, u32[]{:S(2)}, u32[]{:S(2)}) %collective-permute-start.29) | collective-permute-done | bytes 262176 | tf_op jit(solution)/shard_map/ppermute | solution.py:134
  138.3 7.8 %collective-permute-done.30.refs_2_ = bf16[2,128,512]{2,1,0:T(8,128)(2,1)S(1)} collective-permute-done((bf16[2,128,512]{2,1,0:T(8,128)(2,1)S(1)}, bf16[2,128,512]{2,1,0:T(8,128)(2,1)S(1)}, u32[]{:S(2)}, u32[]{:S(2)}) %collective-permute-start.30) | collective-permute-done | bytes 262176 | tf_op jit(solution)/shard_map/ppermute | solution.py:134
  146.1 5.1 %collective-permute-done.34.refs_6_ = bf16[2,128,512]{2,1,0:T(8,128)(2,1)S(1)} collective-permute-done((bf16[2,128,512]{2,1,0:T(8,128)(2,1)S(1)}, bf16[2,128,512]{2,1,0:T(8,128)(2,1)S(1)}, u32[]{:S(2)}, u32[]{:S(2)}) %collective-permute-start.34) | collective-permute-done | bytes 262176 | tf_op jit(solution)/shard_map/ppermute | solution.py:134
  151.2 8.2 %collective-permute-done.31.refs_3_ = bf16[2,128,512]{2,1,0:T(8,128)(2,1)S(1)} collective-permute-done((bf16[2,128,512]{2,1,0:T(8,128)(2,1)S(1)}, bf16[2,128,512]{2,1,0:T(8,128)(2,1)S(1)}, u32[]{:S(2)}, u32[]{:S(2)}) %collective-permute-start.31) | collective-permute-done | bytes 262176 | tf_op jit(solution)/shard_map/ppermute | solution.py:134
  159.4 3.7 %collective-permute-done.35.refs_7_ = bf16[2,128,512]{2,1,0:T(8,128)(2,1)S(1)} collective-permute-done((bf16[2,128,512]{2,1,0:T(8,128)(2,1)S(1)}, bf16[2,128,512]{2,1,0:T(8,128)(2,1)S(1)}, u32[]{:S(2)}, u32[]{:S(2)}) %collective-permute-start.35) | collective-permute-done | bytes 262176 | tf_op jit(solution)/shard_map/ppermute | solution.py:134
  163.0 6.6 %shard_map.58 = (bf16[128,1024]{1,0:T(8,128)(2,1)S(1)}, bf16[128,1024]{1,0:T(8,128)(2,1)}) custom-call(s32[2]{0:T(128)S(1)} %pad_add_fusion.place, bf16[2,128,512]{2,1,0:T(8,128)(2,1)S(1)} %get-tuple-element.47.refs_0_, bf16[2,128,512]{2,1,0:T(8,128)(2,1)S(1)} %collective-permute-done.29.refs_1_, bf16[2,128,512]{2,1,0:T(8,128)(2,1)S(1)} %collective-permute-done.30.refs_2_, ...), custom_call_target="tpu_custom_call" | custom-call | flops 2147483648 | bytes 12582912 | tf_op jit(solution)/shard_map/pallas_call | solution.py:374
  169.7 4.0 %collective-permute-start.36 = (bf16[128,1024]{1,0:T(8,128)(2,1)}, bf16[128,1024]{1,0:T(8,128)(2,1)S(1)}, u32[]{:S(2)}, u32[]{:S(2)}) collective-permute-start(bf16[128,1024]{1,0:T(8,128)(2,1)} %get-tuple-element.51), channel_id=1, source_target_pairs={{0,24},{1,16},{2,26},{3,18},{4,28},{5,20},{6,30},{7,22},{8,0},{9,8... | collective-permute-start | bytes 786440 | tf_op jit(solution)/shard_map/ppermute | solution.py:134
  173.7 0.7 collective-permute-start.37
  174.3 15.0 %collective-permute-done.36 = bf16[128,1024]{1,0:T(8,128)(2,1)S(1)} collective-permute-done((bf16[128,1024]{1,0:T(8,128)(2,1)}, bf16[128,1024]{1,0:T(8,128)(2,1)S(1)}, u32[]{:S(2)}, u32[]{:S(2)}) %collective-permute-start.36) | collective-permute-done | bytes 262176 | tf_op jit(solution)/shard_map/ppermute | solution.py:134
  189.4 0.8 pad_maximum_fusion.3
  (61 shorter events, 1.0 us)
Async XLA Ops:
  0.0 22.7 %collective-permute-start = (bf16[128,2048]{1,0:T(8,128)(2,1)}, bf16[128,2048]{1,0:T(8,128)(2,1)}, u32[]{:S(2)}, u32[]{:S(2)}) collective-permute-start(bf16[128,2048]{1,0:T(8,128)(2,1)} %refs_0_.3), channel_id=1, source_target_pairs={{0,1},{1,0},{2,3},{3,2},{4,5},{5,4},{6,7},{7,6},{8,9},{9,8},{10,11... | collective-permute-start | bytes 1572872 | tf_op jit(solution)/shard_map/ppermute | solution.py:134
  2.9 24.8 %collective-permute-start.1 = (bf16[128,2048]{1,0:T(8,128)(2,1)}, bf16[128,2048]{1,0:T(8,128)(2,1)}, u32[]{:S(2)}, u32[]{:S(2)}) collective-permute-start(bf16[128,2048]{1,0:T(8,128)(2,1)} %refs_0_.3), channel_id=1, source_target_pairs={{0,8},{1,9},{2,10},{3,11},{4,12},{5,13},{6,14},{7,15},{8,0},{9,1},... | collective-permute-start | bytes 1572872 | tf_op jit(solution)/shard_map/ppermute | solution.py:134
  4.5 39.6 %collective-permute-start.4 = (bf16[128,2048]{1,0:T(8,128)(2,1)}, bf16[128,2048]{1,0:T(8,128)(2,1)}, u32[]{:S(2)}, u32[]{:S(2)}) collective-permute-start(bf16[128,2048]{1,0:T(8,128)(2,1)} %refs_0_.3), channel_id=1, source_target_pairs={{0,16},{1,17},{2,18},{3,19},{4,20},{5,21},{6,22},{7,23},{8,24},{9,... | collective-permute-start | bytes 1572872 | tf_op jit(solution)/shard_map/ppermute | solution.py:134
  8.7 3.8 %copy-start = (bf16[2048,256]{1,0:T(8,128)(2,1)S(1)}, bf16[2048,256]{1,0:T(8,128)(2,1)}, u32[]{:S(2)}) copy-start(bf16[2048,256]{1,0:T(8,128)(2,1)} %refs_8_.1) | copy-start | bytes 3145732
  8.7 4.4 %copy-start.6 = (bf16[256,512]{1,0:T(8,128)(2,1)S(1)}, bf16[256,512]{1,0:T(8,128)(2,1)}, u32[]{:S(2)}) copy-start(bf16[256,512]{1,0:T(8,128)(2,1)} %param.8) | copy-start | bytes 786436
  11.0 10.2 %collective-permute-start.2 = (bf16[256,768]{1,0:T(8,128)(2,1)S(1)}, bf16[256,768]{1,0:T(8,128)(2,1)}, u32[]{:S(2)}, u32[]{:S(2)}) collective-permute-start(bf16[256,768]{1,0:T(8,128)(2,1)S(1)} %get-tuple-element.60), channel_id=1, source_target_pairs={{0,4},{1,5},{2,6},{3,7},{4,0},{5,1},{6,2},{7,3},{8,12},{9,13},{10,... | collective-permute-start | bytes 1179656 | tf_op jit(solution)/shard_map/ppermute | solution.py:134
  12.6 29.9 %collective-permute-start.6 = (bf16[2048,256]{1,0:T(8,128)(2,1)S(1)}, bf16[2048,256]{1,0:T(8,128)(2,1)S(1)}, u32[]{:S(2)}, u32[]{:S(2)}) collective-permute-start(bf16[2048,256]{1,0:T(8,128)(2,1)S(1)} %copy-done), channel_id=1, source_target_pairs={{0,1},{1,0},{2,3},{3,2},{4,5},{5,4},{6,7},{7,6},{8,9},{9,8},{10,11... | collective-permute-start | bytes 3145736 | tf_op jit(solution)/shard_map/ppermute | solution.py:134
  21.2 27.6 %collective-permute-start.11 = (bf16[2048,256]{1,0:T(8,128)(2,1)S(1)}, bf16[2048,256]{1,0:T(8,128)(2,1)S(1)}, u32[]{:S(2)}, u32[]{:S(2)}) collective-permute-start(bf16[2048,256]{1,0:T(8,128)(2,1)S(1)} %copy-done), channel_id=1, source_target_pairs={{0,4},{1,5},{2,6},{3,7},{4,0},{5,1},{6,2},{7,3},{8,12},{9,13},{10,... | collective-permute-start | bytes 3145736 | tf_op jit(solution)/shard_map/ppermute | solution.py:134
  27.7 13.7 %collective-permute-start.10 = (bf16[256,512]{1,0:T(8,128)(2,1)}, bf16[256,512]{1,0:T(8,128)(2,1)}, u32[]{:S(2)}, u32[]{:S(2)}) collective-permute-start(bf16[256,512]{1,0:T(8,128)(2,1)} %pad_maximum_fusion.6), channel_id=1, source_target_pairs={{0,16},{1,17},{2,18},{3,19},{4,20},{5,21},{6,22},{7,23},{8,24},{9,... | collective-permute-start | bytes 786440 | tf_op jit(solution)/shard_map/ppermute | solution.py:134
  31.2 17.6 %collective-permute-start.3 = (bf16[128,2048]{1,0:T(8,128)(2,1)}, bf16[128,2048]{1,0:T(8,128)(2,1)S(1)}, u32[]{:S(2)}, u32[]{:S(2)}) collective-permute-start(bf16[128,2048]{1,0:T(8,128)(2,1)} %collective-permute-done.1.refs_2_), channel_id=1, source_target_pairs={{0,1},{1,0},{2,3},{3,2},{4,5},{5,4},{6,7},{7,6},{8,9},{9,8},{10,11... | collective-permute-start | bytes 1572872 | tf_op jit(solution)/shard_map/ppermute | solution.py:134
  42.5 25.2 %collective-permute-start.16 = (bf16[2048,256]{1,0:T(8,128)(2,1)S(1)}, bf16[2048,256]{1,0:T(8,128)(2,1)}, u32[]{:S(2)}, u32[]{:S(2)}) collective-permute-start(bf16[2048,256]{1,0:T(8,128)(2,1)S(1)} %collective-permute-done.6.refs_10_), channel_id=1, source_target_pairs={{0,4},{1,5},{2,6},{3,7},{4,0},{5,1},{6,2},{7,3},{8,12},{9,13},{10,... | collective-permute-start | bytes 3145736 | tf_op jit(solution)/shard_map/ppermute | solution.py:134
  44.1 15.2 %collective-permute-start.7 = (bf16[128,2048]{1,0:T(8,128)(2,1)}, bf16[128,2048]{1,0:T(8,128)(2,1)}, u32[]{:S(2)}, u32[]{:S(2)}) collective-permute-start(bf16[128,2048]{1,0:T(8,128)(2,1)} %collective-permute-done.4.refs_4_), channel_id=1, source_target_pairs={{0,8},{1,9},{2,10},{3,11},{4,12},{5,13},{6,14},{7,15},{8,0},{9,1},... | collective-permute-start | bytes 1572872 | tf_op jit(solution)/shard_map/ppermute | solution.py:134
  48.8 4.5 %copy-start.3 = (bf16[128,2048]{1,0:T(8,128)(2,1)}, bf16[128,2048]{1,0:T(8,128)(2,1)S(1)}, u32[]{:S(2)}) copy-start(bf16[128,2048]{1,0:T(8,128)(2,1)S(1)} %collective-permute-done.3.refs_3_) | copy-start | bytes 1572868
  48.8 17.3 %collective-permute-start.9 = (bf16[2,256,768]{2,1,0:T(8,128)(2,1)}, bf16[2,256,768]{2,1,0:T(8,128)(2,1)}, u32[]{:S(2)}, u32[]{:S(2)}) collective-permute-start(bf16[2,256,768]{2,1,0:T(8,128)(2,1)} %pad_maximum_fusion.refs_8_), channel_id=1, source_target_pairs={{0,2},{1,3},{2,0},{3,1},{4,6},{5,7},{6,4},{7,5},{8,10},{9,11},{10,... | collective-permute-start | bytes 2359304 | tf_op jit(solution)/shard_map/ppermute | solution.py:134
  48.8 16.0 %collective-permute-start.12 = (bf16[2,256,256]{2,1,0:T(8,128)(2,1)}, bf16[2,256,256]{2,1,0:T(8,128)(2,1)}, u32[]{:S(2)}, u32[]{:S(2)}) collective-permute-start(bf16[2,256,256]{2,1,0:T(8,128)(2,1)} %pad_maximum_fusion.7), channel_id=1, source_target_pairs={{0,8},{1,9},{2,10},{3,11},{4,12},{5,13},{6,14},{7,15},{8,0},{9,1},... | collective-permute-start | bytes 786440 | tf_op jit(solution)/shard_map/ppermute | solution.py:134
  51.7 14.4 %collective-permute-start.5 = (bf16[128,2048]{1,0:T(8,128)(2,1)}, bf16[128,2048]{1,0:T(8,128)(2,1)}, u32[]{:S(2)}, u32[]{:S(2)}) collective-permute-start(bf16[128,2048]{1,0:T(8,128)(2,1)} %collective-permute-done.4.refs_4_), channel_id=1, source_target_pairs={{0,1},{1,0},{2,3},{3,2},{4,5},{5,4},{6,7},{7,6},{8,9},{9,8},{10,11... | collective-permute-start | bytes 1572872 | tf_op jit(solution)/shard_map/ppermute | solution.py:134
  54.1 15.2 %copy-start.5 = (bf16[256,512]{1,0:T(8,128)(2,1)S(1)}, bf16[256,512]{1,0:T(8,128)(2,1)}, u32[]{:S(2)}) copy-start(bf16[256,512]{1,0:T(8,128)(2,1)} %get-tuple-element.38) | copy-start | bytes 786436
  59.3 19.3 %collective-permute-start.15 = (bf16[256,512]{1,0:T(8,128)(2,1)}, bf16[256,512]{1,0:T(8,128)(2,1)S(1)}, u32[]{:S(2)}, u32[]{:S(2)}) collective-permute-start(bf16[256,512]{1,0:T(8,128)(2,1)} %get-tuple-element.39), channel_id=1, source_target_pairs={{0,24},{1,25},{2,26},{3,27},{4,28},{5,29},{6,30},{7,31},{8,16},{9,... | collective-permute-start | bytes 786440 | tf_op jit(solution)/shard_map/ppermute | solution.py:134
  64.8 13.8 %collective-permute-start.13 = (bf16[256,512]{1,0:T(8,128)(2,1)}, bf16[256,512]{1,0:T(8,128)(2,1)S(1)}, u32[]{:S(2)}, u32[]{:S(2)}) collective-permute-start(bf16[256,512]{1,0:T(8,128)(2,1)} %get-tuple-element.37), channel_id=1, source_target_pairs={{0,8},{1,9},{2,10},{3,11},{4,12},{5,13},{6,14},{7,15},{8,0},{9,1},... | collective-permute-start | bytes 786440 | tf_op jit(solution)/shard_map/ppermute | solution.py:134
  67.7 11.0 %collective-permute-start.17 = (bf16[3,256,256]{2,1,0:T(8,128)(2,1)S(1)}, bf16[3,256,256]{2,1,0:T(8,128)(2,1)S(1)}, u32[]{:S(2)}, u32[]{:S(2)}) collective-permute-start(bf16[3,256,256]{2,1,0:T(8,128)(2,1)S(1)} %pad_maximum_fusion.5.refs_10_), channel_id=1, source_target_pairs={{0,4},{1,5},{2,6},{3,7},{4,0},{5,1},{6,2},{7,3},{8,12},{9,13},{10,... | collective-permute-start | bytes 1179656 | tf_op jit(solution)/shard_map/ppermute | solution.py:134
  69.3 13.7 %collective-permute-start.14 = (bf16[256,512]{1,0:T(8,128)(2,1)S(1)}, bf16[256,512]{1,0:T(8,128)(2,1)S(1)}, u32[]{:S(2)}, u32[]{:S(2)}) collective-permute-start(bf16[256,512]{1,0:T(8,128)(2,1)S(1)} %copy-done.5), channel_id=1, source_target_pairs={{0,16},{1,17},{2,18},{3,19},{4,20},{5,21},{6,22},{7,23},{8,24},{9,... | collective-permute-start | bytes 786440 | tf_op jit(solution)/shard_map/ppermute | solution.py:134
  70.2 13.5 %collective-permute-start.8 = (bf16[128,2048]{1,0:T(8,128)(2,1)}, bf16[128,2048]{1,0:T(8,128)(2,1)S(1)}, u32[]{:S(2)}, u32[]{:S(2)}) collective-permute-start(bf16[128,2048]{1,0:T(8,128)(2,1)} %collective-permute-done.7.refs_6_), channel_id=1, source_target_pairs={{0,1},{1,0},{2,3},{3,2},{4,5},{5,4},{6,7},{7,6},{8,9},{9,8},{10,11... | collective-permute-start | bytes 1572872 | tf_op jit(solution)/shard_map/ppermute | solution.py:134
  78.7 14.9 %collective-permute-start.18 = (bf16[2,256,512]{2,1,0:T(8,128)(2,1)S(1)}, bf16[2,256,512]{2,1,0:T(8,128)(2,1)S(1)}, u32[]{:S(2)}, u32[]{:S(2)}) collective-permute-start(bf16[2,256,512]{2,1,0:T(8,128)(2,1)S(1)} %pad_maximum_fusion.2), channel_id=1, source_target_pairs={{0,4},{1,5},{2,6},{3,7},{4,0},{5,1},{6,2},{7,3},{8,12},{9,13},{10,... | collective-permute-start | bytes 1572872 | tf_op jit(solution)/shard_map/ppermute | solution.py:134
  83.0 15.1 %copy-start.1 = (f32[512,128]{1,0:T(8,128)S(1)}, f32[512,128]{1,0:T(8,128)}, u32[]{:S(2)}) copy-start(f32[512,128]{1,0:T(8,128)} %get-tuple-element.81.refs_14_.refs_13_) | copy-start | bytes 786436
  83.0 15.1 %copy-start.2 = (bf16[128,2048]{1,0:T(8,128)(2,1)S(1)}, bf16[128,2048]{1,0:T(8,128)(2,1)}, u32[]{:S(2)}) copy-start(bf16[128,2048]{1,0:T(8,128)(2,1)} %refs_0_.3) | copy-start | bytes 1572868
  83.0 15.1 %copy-start.4 = (bf16[128,2048]{1,0:T(8,128)(2,1)S(1)}, bf16[128,2048]{1,0:T(8,128)(2,1)}, u32[]{:S(2)}) copy-start(bf16[128,2048]{1,0:T(8,128)(2,1)} %copy-done.3) | copy-start | bytes 1572868
  83.0 15.0 %collective-permute-start.19 = (bf16[256,512]{1,0:T(8,128)(2,1)S(1)}, bf16[256,512]{1,0:T(8,128)(2,1)S(1)}, u32[]{:S(2)}, u32[]{:S(2)}) collective-permute-start(bf16[256,512]{1,0:T(8,128)(2,1)S(1)} %collective-permute-done.14), channel_id=1, source_target_pairs={{0,4},{1,5},{2,6},{3,7},{4,0},{5,1},{6,2},{7,3},{8,12},{9,13},{10,... | collective-permute-start | bytes 786440 | tf_op jit(solution)/shard_map/ppermute | solution.py:134
  83.7 14.4 %collective-permute-start.20 = (bf16[6,256,256]{2,1,0:T(8,128)(2,1)S(1)}, bf16[6,256,256]{2,1,0:T(8,128)(2,1)S(1)}, u32[]{:S(2)}, u32[]{:S(2)}) collective-permute-start(bf16[6,256,256]{2,1,0:T(8,128)(2,1)S(1)} %pad_maximum_fusion.1), channel_id=1, source_target_pairs={{0,2},{1,3},{2,0},{3,1},{4,6},{5,7},{6,4},{7,5},{8,10},{9,11},{10,... | collective-permute-start | bytes 2359304 | tf_op jit(solution)/shard_map/ppermute | solution.py:134
  102.9 8.9 %collective-permute-start.21 = (bf16[6,256,512]{2,1,0:T(8,128)(2,1)S(1)}, bf16[6,256,512]{2,1,0:T(8,128)(2,1)S(1)}, u32[]{:S(2)}, u32[]{:S(2)}) collective-permute-start(bf16[6,256,512]{2,1,0:T(8,128)(2,1)S(1)} %slice_dynamic-update-slice_fusion.refs_10_), channel_id=1, source_target_pairs={{0,2},{1,3},{2,0},{3,1},{4,6},{5,7},{6,4},{7,5},{8,10},{9,11},{10,... | collective-permute-start | bytes 4718600 | tf_op jit(solution)/shard_map/ppermute | solution.py:134
  103.0 3.8 %collective-permute-start.22 = (bf16[4,128,256]{2,1,0:T(8,128)(2,1)S(1)}, bf16[4,128,256]{2,1,0:T(8,128)(2,1)S(1)}, u32[]{:S(2)}, u32[]{:S(2)}) collective-permute-start(bf16[4,128,256]{2,1,0:T(8,128)(2,1)S(1)} %shard_map.55.kv0), channel_id=1, source_target_pairs={{0,2},{1,3},{2,0},{3,1},{4,6},{5,7},{6,4},{7,5},{8,10},{9,11},{10,... | collective-permute-start | bytes 786440 | tf_op jit(solution)/shard_map/ppermute | solution.py:134
  103.5 8.3 %collective-permute-start.23 = (bf16[4,128,256]{2,1,0:T(8,128)(2,1)S(1)}, bf16[4,128,256]{2,1,0:T(8,128)(2,1)S(1)}, u32[]{:S(2)}, u32[]{:S(2)}) collective-permute-start(bf16[4,128,256]{2,1,0:T(8,128)(2,1)S(1)} %shard_map.55.kv0), channel_id=1, source_target_pairs={{0,4},{1,5},{2,6},{3,7},{4,0},{5,1},{6,2},{7,3},{8,12},{9,13},{10,... | collective-permute-start | bytes 786440 | tf_op jit(solution)/shard_map/ppermute | solution.py:134
  104.0 20.8 %collective-permute-start.25 = (bf16[2048,256]{1,0:T(8,128)(2,1)S(1)}, bf16[2048,256]{1,0:T(8,128)(2,1)S(1)}, u32[]{:S(2)}, u32[]{:S(2)}) collective-permute-start(bf16[2048,256]{1,0:T(8,128)(2,1)S(1)} %copy-done), channel_id=1, source_target_pairs={{0,2},{1,3},{2,0},{3,1},{4,6},{5,7},{6,4},{7,5},{8,10},{9,11},{10,... | collective-permute-start | bytes 3145736 | tf_op jit(solution)/shard_map/ppermute | solution.py:134
  104.0 20.8 %collective-permute-start.26 = (bf16[2048,256]{1,0:T(8,128)(2,1)S(1)}, bf16[2048,256]{1,0:T(8,128)(2,1)S(1)}, u32[]{:S(2)}, u32[]{:S(2)}) collective-permute-start(bf16[2048,256]{1,0:T(8,128)(2,1)S(1)} %collective-permute-done.6.refs_10_), channel_id=1, source_target_pairs={{0,2},{1,3},{2,0},{3,1},{4,6},{5,7},{6,4},{7,5},{8,10},{9,11},{10,... | collective-permute-start | bytes 3145736 | tf_op jit(solution)/shard_map/ppermute | solution.py:134
  106.7 18.0 %collective-permute-start.27 = (bf16[2048,256]{1,0:T(8,128)(2,1)S(1)}, bf16[2048,256]{1,0:T(8,128)(2,1)S(1)}, u32[]{:S(2)}, u32[]{:S(2)}) collective-permute-start(bf16[2048,256]{1,0:T(8,128)(2,1)S(1)} %collective-permute-done.11.refs_12_), channel_id=1, source_target_pairs={{0,2},{1,3},{2,0},{3,1},{4,6},{5,7},{6,4},{7,5},{8,10},{9,11},{10,... | collective-permute-start | bytes 3145736 | tf_op jit(solution)/shard_map/ppermute | solution.py:134
  111.8 13.0 %collective-permute-start.28 = (bf16[2048,256]{1,0:T(8,128)(2,1)}, bf16[2048,256]{1,0:T(8,128)(2,1)S(1)}, u32[]{:S(2)}, u32[]{:S(2)}) collective-permute-start(bf16[2048,256]{1,0:T(8,128)(2,1)} %collective-permute-done.16.refs_14_), channel_id=1, source_target_pairs={{0,2},{1,3},{2,0},{3,1},{4,6},{5,7},{6,4},{7,5},{8,10},{9,11},{10,... | collective-permute-start | bytes 3145736 | tf_op jit(solution)/shard_map/ppermute | solution.py:134
  111.8 5.9 %collective-permute-start.24 = (bf16[4,128,256]{2,1,0:T(8,128)(2,1)S(1)}, bf16[4,128,256]{2,1,0:T(8,128)(2,1)S(1)}, u32[]{:S(2)}, u32[]{:S(2)}) collective-permute-start(bf16[4,128,256]{2,1,0:T(8,128)(2,1)S(1)} %collective-permute-done.23.kv2), channel_id=1, source_target_pairs={{0,2},{1,3},{2,0},{3,1},{4,6},{5,7},{6,4},{7,5},{8,10},{9,11},{10,... | collective-permute-start | bytes 786440 | tf_op jit(solution)/shard_map/ppermute | solution.py:134
  124.8 8.3 %collective-permute-start.32 = (bf16[2,128,512]{2,1,0:T(8,128)(2,1)S(1)}, bf16[2,128,512]{2,1,0:T(8,128)(2,1)S(1)}, u32[]{:S(2)}, u32[]{:S(2)}) collective-permute-start(bf16[2,128,512]{2,1,0:T(8,128)(2,1)S(1)} %get-tuple-element.49), channel_id=1, source_target_pairs={{0,1},{1,0},{2,3},{3,2},{4,5},{5,4},{6,7},{7,6},{8,9},{9,8},{10,11... | collective-permute-start | bytes 786440 | tf_op jit(solution)/shard_map/ppermute | solution.py:134
  125.4 12.9 %collective-permute-start.29 = (bf16[2,128,512]{2,1,0:T(8,128)(2,1)S(1)}, bf16[2,128,512]{2,1,0:T(8,128)(2,1)S(1)}, u32[]{:S(2)}, u32[]{:S(2)}) collective-permute-start(bf16[2,128,512]{2,1,0:T(8,128)(2,1)S(1)} %get-tuple-element.47.refs_0_), channel_id=1, source_target_pairs={{0,8},{1,9},{2,10},{3,11},{4,12},{5,13},{6,14},{7,15},{8,0},{9,1},... | collective-permute-start | bytes 786440 | tf_op jit(solution)/shard_map/ppermute | solution.py:134
  125.4 20.7 %collective-permute-start.30 = (bf16[2,128,512]{2,1,0:T(8,128)(2,1)S(1)}, bf16[2,128,512]{2,1,0:T(8,128)(2,1)S(1)}, u32[]{:S(2)}, u32[]{:S(2)}) collective-permute-start(bf16[2,128,512]{2,1,0:T(8,128)(2,1)S(1)} %get-tuple-element.47.refs_0_), channel_id=1, source_target_pairs={{0,16},{1,17},{2,18},{3,19},{4,20},{5,21},{6,22},{7,23},{8,24},{9,... | collective-permute-start | bytes 786440 | tf_op jit(solution)/shard_map/ppermute | solution.py:134
  133.1 18.1 %collective-permute-start.34 = (bf16[2,128,512]{2,1,0:T(8,128)(2,1)S(1)}, bf16[2,128,512]{2,1,0:T(8,128)(2,1)S(1)}, u32[]{:S(2)}, u32[]{:S(2)}) collective-permute-start(bf16[2,128,512]{2,1,0:T(8,128)(2,1)S(1)} %collective-permute-done.32.refs_4_), channel_id=1, source_target_pairs={{0,16},{1,17},{2,18},{3,19},{4,20},{5,21},{6,22},{7,23},{8,24},{9,... | collective-permute-start | bytes 786440 | tf_op jit(solution)/shard_map/ppermute | solution.py:134
  138.3 21.1 %collective-permute-start.33 = (bf16[2,128,512]{2,1,0:T(8,128)(2,1)S(1)}, bf16[2,128,512]{2,1,0:T(8,128)(2,1)S(1)}, u32[]{:S(2)}, u32[]{:S(2)}) collective-permute-start(bf16[2,128,512]{2,1,0:T(8,128)(2,1)S(1)} %collective-permute-done.32.refs_4_), channel_id=1, source_target_pairs={{0,8},{1,9},{2,10},{3,11},{4,12},{5,13},{6,14},{7,15},{8,0},{9,1},... | collective-permute-start | bytes 786440 | tf_op jit(solution)/shard_map/ppermute | solution.py:134
  146.1 13.3 %collective-permute-start.31 = (bf16[2,128,512]{2,1,0:T(8,128)(2,1)S(1)}, bf16[2,128,512]{2,1,0:T(8,128)(2,1)S(1)}, u32[]{:S(2)}, u32[]{:S(2)}) collective-permute-start(bf16[2,128,512]{2,1,0:T(8,128)(2,1)S(1)} %collective-permute-done.30.refs_2_), channel_id=1, source_target_pairs={{0,8},{1,9},{2,10},{3,11},{4,12},{5,13},{6,14},{7,15},{8,0},{9,1},... | collective-permute-start | bytes 786440 | tf_op jit(solution)/shard_map/ppermute | solution.py:134
  151.2 11.9 %collective-permute-start.35 = (bf16[2,128,512]{2,1,0:T(8,128)(2,1)S(1)}, bf16[2,128,512]{2,1,0:T(8,128)(2,1)S(1)}, u32[]{:S(2)}, u32[]{:S(2)}) collective-permute-start(bf16[2,128,512]{2,1,0:T(8,128)(2,1)S(1)} %collective-permute-done.34.refs_6_), channel_id=1, source_target_pairs={{0,8},{1,9},{2,10},{3,11},{4,12},{5,13},{6,14},{7,15},{8,0},{9,1},... | collective-permute-start | bytes 786440 | tf_op jit(solution)/shard_map/ppermute | solution.py:134
  169.7 19.7 %collective-permute-start.36 = (bf16[128,1024]{1,0:T(8,128)(2,1)}, bf16[128,1024]{1,0:T(8,128)(2,1)S(1)}, u32[]{:S(2)}, u32[]{:S(2)}) collective-permute-start(bf16[128,1024]{1,0:T(8,128)(2,1)} %get-tuple-element.51), channel_id=1, source_target_pairs={{0,24},{1,16},{2,26},{3,18},{4,28},{5,20},{6,30},{7,22},{8,0},{9,8... | collective-permute-start | bytes 786440 | tf_op jit(solution)/shard_map/ppermute | solution.py:134
  173.7 15.7 %collective-permute-start.37 = (bf16[128,1024]{1,0:T(8,128)(2,1)S(1)}, bf16[128,1024]{1,0:T(8,128)(2,1)S(1)}, u32[]{:S(2)}, u32[]{:S(2)}) collective-permute-start(bf16[128,1024]{1,0:T(8,128)(2,1)S(1)} %get-tuple-element.52), channel_id=1, source_target_pairs={{0,0},{1,8},{2,2},{3,10},{4,4},{5,12},{6,6},{7,14},{8,24},{9,16},{... | collective-permute-start | bytes 786440 | tf_op jit(solution)/shard_map/ppermute | solution.py:134

commit v4 on v3

--- a/solution.py
+++ b/solution.py
@@ -128,26 +128,6 @@
         tz, ty, tc, tx = target(z, y, c, x)
         pairs.append((i, tz * 8 + ty * 4 + tc * 2 + tx))
     return pairs
-
-
-def move(array, target):
-    return lax.ppermute(array, AXES, moves(target))
-
-
-def across_z(array, m):
-    return move(array, lambda z, y, c, x: (z ^ m, y, c, x))
-
-
-def across_y(array):
-    return move(array, lambda z, y, c, x: (z, 1 - y, c, x))
-
-
-def across_core(array):
-    return move(array, lambda z, y, c, x: (z, y, 1 - c, x))
-
-
-def across_x(array):
-    return move(array, lambda z, y, c, x: (z, y, c, 1 - x))
 
 
 def any_specs(count):
@@ -388,8 +368,58 @@
     )(place, *attn, *weights)
 
 
-def after(array, *earlier):
-    return lax.optimization_barrier((array,) + earlier)[0]
+ORDER = {
+    "y_out": ("own_y",),
+    "far": ("tok1", "other0", "own_y"),
+    "other1": ("other0", "own_y"),
+    "tok3": ("tok2", "tok1", "x_out", "own_y"),
+    "xy_out": ("own_y",),
+    "other2": ("other1",),
+    "near": ("y_out",),
+    "query2": ("far",),
+    "query3": ("far", "tok3", "other1"),
+    "other3": ("other1",),
+    "query1": ("far", "near"),
+    "both_core": ("other1",),
+    "kv_rest_y": ("both_core", "y_out", "xy_out", "other2"),
+    "query2_y": ("kv_rest_y",),
+    "query31_y": ("kv_rest_y",),
+    "kv_core": ("other3",),
+    "query_core": ("own_kv",),
+    "mine1": ("core_w", "core_x", "core_y", "core_xy"),
+    "mine2": ("core_w", "core_x", "core_y", "core_xy"),
+    "from_x": ("core_w", "core_x", "core_y", "core_xy"),
+    "from_x1": ("mine1",),
+    "core_y_kv": ("queries",),
+}
+
+
+class Transfers:
+    def __init__(self):
+        self.there = {}
+
+    def __call__(self, name, array, target):
+        earlier = [self.there[k] for k in ORDER.get(name, ())]
+        if earlier:
+            array = lax.optimization_barrier((array, *earlier))[0]
+        self.there[name] = lax.ppermute(array, AXES, moves(target))
+        return self.there[name]
+
+
+def to_z(m):
+    return lambda z, y, c, x: (z ^ m, y, c, x)
+
+
+def to_y(z, y, c, x):
+    return (z, 1 - y, c, x)
+
+
+def to_core(z, y, c, x):
+    return (z, y, 1 - c, x)
+
+
+def to_x(z, y, c, x):
+    return (z, y, c, 1 - x)
 
 
 def split_body(tokens, w_query, key_matrix, value_matrix, w_out):
@@ -397,7 +427,8 @@
     place = jnp.stack([ctx, x]).astype(jnp.int32)
     z = ctx // 4
     rows = tokens.shape[0]
-    group = w_query.shape[1] // 4
+    group, wide = w_query.shape[1] // 4, 2 * HEAD_SIZE
+    send = Transfers()
 
     def columns(weight, head, width):
         return lax.dynamic_slice_in_dim(weight, head * width, width, 1)
@@ -406,40 +437,38 @@
         parts = [columns(w, head, HEAD_SIZE) for w in (key_matrix, value_matrix)]
         return jnp.concatenate(parts, axis=1)
 
-    wide = 2 * HEAD_SIZE
-
-    tok1 = across_z(tokens, 1)
-    tok2 = across_z(tokens, 2)
-    other0 = across_x(tokens)
-    x_out = across_x(w_out)
+    tok1 = send("tok1", tokens, to_z(1))
+    tok2 = send("tok2", tokens, to_z(2))
+    other0 = send("other0", tokens, to_x)
+    x_out = send("x_out", w_out, to_x)
     own = jnp.concatenate([pair(z), columns(w_query, z, group)], axis=1)
-    own_y = across_y(own)
-    y_out = across_y(after(w_out, own_y))
+    own_y = send("own_y", own, to_y)
+    y_out = send("y_out", w_out, to_y)
     far_half = [columns(w, 1 - z // 2, wide) for w in (key_matrix, value_matrix)]
-    far = across_z(after(jnp.concatenate(far_half, axis=1), tok1, other0, own_y), 2)
+    far = send("far", jnp.concatenate(far_half, axis=1), to_z(2))
 
     def far_pair(head):
         parts = [columns(w, head, HEAD_SIZE) for w in (far[:, :wide], far[:, wide:])]
         return jnp.concatenate(parts, axis=1)
 
-    other1 = across_x(after(tok1, other0, own_y))
-    tok3 = across_z(after(tok2, tok1, x_out, own_y), 1)
-    xy_out = across_y(after(x_out, own_y))
-    other2 = across_x(after(tok2, other1))
-    near = across_z(after(jnp.stack([pair(z ^ 1), far_pair(1 - z % 2)]), y_out), 1)
-    query2 = across_z(after(columns(w_query, z ^ 2, group), far), 2)
-    query3 = across_z(after(columns(w_query, z ^ 3, group), far, tok3, other1), 3)
-    other3 = across_x(after(tok3, other1))
-    query1 = across_z(after(columns(w_query, z ^ 1, group), far, near), 1)
+    other1 = send("other1", tok1, to_x)
+    tok3 = send("tok3", tok2, to_z(1))
+    xy_out = send("xy_out", x_out, to_y)
+    other2 = send("other2", tok2, to_x)
+    near = send("near", jnp.stack([pair(z ^ 1), far_pair(1 - z % 2)]), to_z(1))
+    query2 = send("query2", columns(w_query, z ^ 2, group), to_z(2))
+    query3 = send("query3", columns(w_query, z ^ 3, group), to_z(3))
+    other3 = send("other3", tok3, to_x)
+    query1 = send("query1", columns(w_query, z ^ 1, group), to_z(1))
     token_pieces = [tokens, other0, tok1, other1, tok2, other2, tok3, other3]
 
     both = jnp.stack([own, own_y])
-    both_core = across_core(after(both, other1))
+    both_core = send("both_core", both, to_core)
     kv_rest = jnp.stack([near[0], far_pair(z % 2), near[1]])
-    kv_rest_y = across_y(after(kv_rest, both_core, y_out, xy_out, other2))
-    query2_y = across_y(after(query2, kv_rest_y))
-    query31_y = across_y(after(jnp.stack([query3, query1]), kv_rest_y))
-    kv_core = across_core(after(jnp.concatenate([kv_rest, kv_rest_y]), other3))
+    kv_rest_y = send("kv_rest_y", kv_rest, to_y)
+    query2_y = send("query2_y", query2, to_y)
+    query31_y = send("query31_y", jnp.stack([query3, query1]), to_y)
+    kv_core = send("kv_core", jnp.concatenate([kv_rest, kv_rest_y]), to_core)
     kv_weights = [both, both_core, kv_rest, kv_rest_y, kv_core]
     kv_plan = ((0, 2), (1, 3), (4, 8, 12), (6, 10, 14), (5, 9, 13, 7, 11, 15))
 
@@ -460,10 +489,11 @@
         cosine,
         sine,
     )
-    y_kv = across_y(own_kv)
-    kv = [own_kv, across_core(own_kv), y_kv, across_core(y_kv)]
+    send.there["own_kv"] = own_kv
+    y_kv = send("y_kv", own_kv, to_y)
+    core_kv = send("core_kv", own_kv, to_core)
     query_rest = jnp.stack([query1, query2, query3, query31_y[1], query2_y, query31_y[0]])
-    query_core = across_core(after(query_rest, own_kv))
+    query_core = send("query_core", query_rest, to_core)
     query_weights = [both, both_core, query_rest, query_core]
     query_plan = ((0, 2), (1, 3), (4, 8, 12, 6, 10, 14), (5, 9, 13, 7, 11, 15))
     queries = project(
@@ -477,18 +507,21 @@
         cosine,
         sine,
     )
+    send.there["queries"] = queries
+    core_y_kv = send("core_y_kv", y_kv, to_core)
+    kv = [own_kv, core_kv, y_kv, core_y_kv]
     mine, other = attend(place, queries, kv)
+    send.there["attend"] = mine
     out_weights = []
-    for piece in (w_out, x_out, y_out, xy_out):
-        out_weights += [piece, across_core(piece)]
-    mine, other = after(mine, *out_weights), after(other, *out_weights)
-    mine2 = across_z(mine, 2)
-    mine1 = across_z(mine, 1)
-    from_x = across_x(other)
-    from_x2 = across_z(from_x, 2)
-    from_x1 = across_z(after(from_x, mine1), 1)
-    mine3 = across_z(mine2, 1)
-    from_x3 = across_z(from_x2, 1)
+    for name, piece in (("w", w_out), ("x", x_out), ("y", y_out), ("xy", xy_out)):
+        out_weights += [piece, send("core_" + name, piece, to_core)]
+    mine2 = send("mine2", mine, to_z(2))
+    mine1 = send("mine1", mine, to_z(1))
+    from_x = send("from_x", other, to_x)
+    from_x2 = send("from_x2", from_x, to_z(2))
+    from_x1 = send("from_x1", from_x, to_z(1))
+    mine3 = send("mine3", mine2, to_z(1))
+    from_x3 = send("from_x3", from_x2, to_z(1))
     attn = [mine, mine1, mine2, mine3, from_x, from_x1, from_x2, from_x3]
 
     first, second = project_out(place, attn, out_weights)
@@ -496,7 +529,7 @@
     def home(m):
         return lambda z, y, c, x: (x ^ 3 * (z % 2 ^ m), y, c, z // 2)
 
-    first, second = move(first, home(0)), move(second, home(1))
+    first, second = send("home0", first, home(0)), send("home1", second, home(1))
     odd = z // 2 == 1
     return jnp.concatenate(
         [jnp.where(odd, second, first), jnp.where(odd, first, second)], axis=1

time: 191 us -> 187 us (0.979)
  waiting for transfers between devices: 117 us -> 113 us
    ppermute x38, waiting for transfers between devices: 117 us -> 113 us  [__call__(): self.there[name] = lax.ppermute(array, AXES, moves(target))]
where the time goes in v4:
time: 187 us; the launch traced here: 186 us
  waiting for transfers between devices  113 us (60%)
  starting transfers between devices  35 us (19%)
  Pallas kernels  23.8 us (13%)
  other arithmetic  7.49 us (4%)
  local copies, waits for them, and re-layouts  6.89 us (4%)
    ppermute x38, waiting for transfers between devices, __call__(): self.there[name] = lax.ppermute(array, AXES, moves(target))  113 us
    ppermute x38, starting transfers between devices, __call__(): self.there[name] = lax.ppermute(array, AXES, moves(target))  35 us
    pallas_call x2, Pallas kernels, project(): pl.pallas_call(functools.partial(kernel, plan), out_shape=jax.ShapeDtypeS...  10.1 us
    pallas_call x1, Pallas kernels, attend(): pl.pallas_call(attend_kernel, out_shape=(shape, shape), in_specs=[smem_sp...  7.07 us
    pallas_call x1, Pallas kernels, project_out(): pl.pallas_call(output_kernel, out_shape=(shape, shape), in_specs=[smem_sp...  6.61 us
    dynamic_slice x5, local copies, waits for them, and re-layouts, columns(): return lax.dynamic_slice_in_dim(weight, head * width, width, 1)  4.78 us
  transfers between devices with their start and end apart: 38, of which 21 were waited for; matrix products, arithmetic and copies ran while one was open for 7% of the time, Pallas kernels for 7%

profile of v4, /device:TPU:0, one launch (start us, length us, event | category | flops | bytes accessed | tf_op | source)
XLA Modules:
  0.0 186.1 jit_solution(11401211207050383009)
XLA Ops:
  0.0 2.9 %collective-permute-start = (bf16[128,2048]{1,0:T(8,128)(2,1)}, bf16[128,2048]{1,0:T(8,128)(2,1)}, u32[]{:S(2)}, u32[]{:S(2)}) collective-permute-start(bf16[128,2048]{1,0:T(8,128)(2,1)} %refs_0_.3), channel_id=1, source_target_pairs={{0,1},{1,0},{2,3},{3,2},{4,5},{5,4},{6,7},{7,6},{8,9},{9,8},{10,11... | collective-permute-start | bytes 1572872 | tf_op jit(solution)/shard_map/ppermute | solution.py:405
  2.9 1.6 collective-permute-start.1
  4.5 2.6 %collective-permute-start.4 = (bf16[128,2048]{1,0:T(8,128)(2,1)}, bf16[128,2048]{1,0:T(8,128)(2,1)}, u32[]{:S(2)}, u32[]{:S(2)}) collective-permute-start(bf16[128,2048]{1,0:T(8,128)(2,1)} %refs_0_.3), channel_id=1, source_target_pairs={{0,16},{1,17},{2,18},{3,19},{4,20},{5,21},{6,22},{7,23},{8,24},{9,... | collective-permute-start | bytes 1572872 | tf_op jit(solution)/shard_map/ppermute | solution.py:405
  7.1 1.6 constant_dynamic-slice_fusion.6
  8.7 2.2 %constant_dynamic-slice_fusion.2 = (bf16[256,512]{1,0:T(8,128)(2,1)}, bf16[256,512]{1,0:T(8,128)(2,1)}, bf16[256,512]{1,0:T(8,128)(2,1)S(1)}, bf16[256,512]{1,0:T(8,128)(2,1)}) fusion(bf16[256,2048]{1,0:T(8,128)(2,1)} %param.6, s32[]{:T(128)S(6)} %select_n.73, s32[]{:T(128)S(6)} %select_n.67, s32[]{:T(128)S(6)} %select_n.66, s32[]{:T(128)S(6)} %select_n.72), kind=kLoop, calls=%fused_computation.26 | loop fusion | bytes 2097168 | tf_op jit(solution)/shard_map/dynamic_slice | solution.py:434
  11.0 1.6 collective-permute-start.2
  12.6 0.5 collective-permute-start.6
  13.1 0.9 constant_dynamic-slice_fusion.8
  14.0 0.7 pad_maximum_fusion.6
  14.8 6.3 %collective-permute-done.2 = bf16[256,768]{1,0:T(8,128)(2,1)} collective-permute-done((bf16[256,768]{1,0:T(8,128)(2,1)S(1)}, bf16[256,768]{1,0:T(8,128)(2,1)}, u32[]{:S(2)}, u32[]{:S(2)}) %collective-permute-start.2) | collective-permute-done | bytes 393248 | tf_op jit(solution)/shard_map/ppermute | solution.py:405
  21.2 1.5 collective-permute-start.11
  22.7 5.0 %collective-permute-done.1.refs_2_ = bf16[128,2048]{1,0:T(8,128)(2,1)} collective-permute-done((bf16[128,2048]{1,0:T(8,128)(2,1)}, bf16[128,2048]{1,0:T(8,128)(2,1)}, u32[]{:S(2)}, u32[]{:S(2)}) %collective-permute-start.1) | collective-permute-done | bytes 524320 | tf_op jit(solution)/shard_map/ppermute | solution.py:405
  27.7 0.6 collective-permute-start.10
  28.3 0.9 maximum_bitcast_fusion
  29.2 2.0 %pad_maximum_fusion.refs_8_ = bf16[2,256,768]{2,1,0:T(8,128)(2,1)} fusion(bf16[1,256,768]{2,1,0:T(8,128)(2,1)} %bitcast.3, bf16[1,256,768]{2,1,0:T(8,128)(2,1)S(1)} %get-tuple-element.61), kind=kLoop, calls=%fused_computation | loop fusion | flops 393216 | bytes 1572864 | tf_op jit(solution)/shard_map/stack | solution.py:465
  31.2 0.5 collective-permute-start.3
  31.7 9.7 %collective-permute-done.10 = bf16[256,512]{1,0:T(8,128)(2,1)} collective-permute-done((bf16[256,512]{1,0:T(8,128)(2,1)}, bf16[256,512]{1,0:T(8,128)(2,1)}, u32[]{:S(2)}, u32[]{:S(2)}) %collective-permute-start.10) | collective-permute-done | bytes 262176 | tf_op jit(solution)/shard_map/ppermute | solution.py:405
  41.4 1.0 fusion.3
  42.5 1.6 collective-permute-start.16
  44.2 0.7 pad_maximum_fusion.7
  44.9 3.9 %collective-permute-done.3.refs_3_ = bf16[128,2048]{1,0:T(8,128)(2,1)S(1)} collective-permute-done((bf16[128,2048]{1,0:T(8,128)(2,1)}, bf16[128,2048]{1,0:T(8,128)(2,1)S(1)}, u32[]{:S(2)}, u32[]{:S(2)}) %collective-permute-start.3) | collective-permute-done | bytes 524320 | tf_op jit(solution)/shard_map/ppermute | solution.py:405
  48.8 1.9 %collective-permute-start.12 = (bf16[2,256,256]{2,1,0:T(8,128)(2,1)}, bf16[2,256,256]{2,1,0:T(8,128)(2,1)}, u32[]{:S(2)}, u32[]{:S(2)}) collective-permute-start(bf16[2,256,256]{2,1,0:T(8,128)(2,1)} %pad_maximum_fusion.7), channel_id=1, source_target_pairs={{0,8},{1,9},{2,10},{3,11},{4,12},{5,13},{6,14},{7,15},{8,0},{9,1},... | collective-permute-start | bytes 786440 | tf_op jit(solution)/shard_map/ppermute | solution.py:405
  50.7 1.0 fusion
  51.7 1.6 collective-permute-start.5
  53.2 0.9 pad_maximum_fusion.8
  54.2 5.2 %collective-permute-done.7.refs_6_ = bf16[128,2048]{1,0:T(8,128)(2,1)} collective-permute-done((bf16[128,2048]{1,0:T(8,128)(2,1)}, bf16[128,2048]{1,0:T(8,128)(2,1)}, u32[]{:S(2)}, u32[]{:S(2)}) %collective-permute-start.7) | collective-permute-done | bytes 524320 | tf_op jit(solution)/shard_map/ppermute | solution.py:405
  59.3 2.4 %collective-permute-start.15 = (bf16[256,512]{1,0:T(8,128)(2,1)}, bf16[256,512]{1,0:T(8,128)(2,1)S(1)}, u32[]{:S(2)}, u32[]{:S(2)}) collective-permute-start(bf16[256,512]{1,0:T(8,128)(2,1)} %get-tuple-element.40), channel_id=1, source_target_pairs={{0,24},{1,25},{2,26},{3,27},{4,28},{5,29},{6,30},{7,31},{8,16},{9,... | collective-permute-start | bytes 786440 | tf_op jit(solution)/shard_map/ppermute | solution.py:405
  61.7 3.1 %collective-permute-done.12 = bf16[2,256,256]{2,1,0:T(8,128)(2,1)} collective-permute-done((bf16[2,256,256]{2,1,0:T(8,128)(2,1)}, bf16[2,256,256]{2,1,0:T(8,128)(2,1)}, u32[]{:S(2)}, u32[]{:S(2)}) %collective-permute-start.12) | collective-permute-done | bytes 262176 | tf_op jit(solution)/shard_map/ppermute | solution.py:405
  64.9 1.0 fusion.2
  66.1 1.7 collective-permute-done.16.refs_14_
  67.7 1.5 collective-permute-start.17
  69.3 0.9 collective-permute-start.14
  70.2 1.5 collective-permute-start.8
  71.7 6.9 %collective-permute-done.13 = bf16[256,512]{1,0:T(8,128)(2,1)S(1)} collective-permute-done((bf16[256,512]{1,0:T(8,128)(2,1)}, bf16[256,512]{1,0:T(8,128)(2,1)S(1)}, u32[]{:S(2)}, u32[]{:S(2)}) %collective-permute-start.13) | collective-permute-done | bytes 262176 | tf_op jit(solution)/shard_map/ppermute | solution.py:405
  78.7 0.7 collective-permute-start.18
  79.4 3.6 %collective-permute-done.14 = bf16[256,512]{1,0:T(8,128)(2,1)S(1)} collective-permute-done((bf16[256,512]{1,0:T(8,128)(2,1)S(1)}, bf16[256,512]{1,0:T(8,128)(2,1)S(1)}, u32[]{:S(2)}, u32[]{:S(2)}) %collective-permute-start.14) | collective-permute-done | bytes 262176 | tf_op jit(solution)/shard_map/ppermute | solution.py:405
  83.0 0.6 collective-permute-start.19
  83.8 9.8 %collective-permute-done.18 = bf16[2,256,512]{2,1,0:T(8,128)(2,1)S(1)} collective-permute-done((bf16[2,256,512]{2,1,0:T(8,128)(2,1)S(1)}, bf16[2,256,512]{2,1,0:T(8,128)(2,1)S(1)}, u32[]{:S(2)}, u32[]{:S(2)}) %collective-permute-start.18) | collective-permute-done | bytes 524320 | tf_op jit(solution)/shard_map/ppermute | solution.py:405
  93.6 4.5 %collective-permute-done.19 = bf16[256,512]{1,0:T(8,128)(2,1)S(1)} collective-permute-done((bf16[256,512]{1,0:T(8,128)(2,1)S(1)}, bf16[256,512]{1,0:T(8,128)(2,1)S(1)}, u32[]{:S(2)}, u32[]{:S(2)}) %collective-permute-start.19) | collective-permute-done | bytes 262176 | tf_op jit(solution)/shard_map/ppermute | solution.py:405
  98.2 4.7 %shard_map.55.kv0 = bf16[4,128,256]{2,1,0:T(8,128)(2,1)S(1)} custom-call(s32[2]{0:T(128)S(1)} %pad_add_fusion.place, bf16[128,2048]{1,0:T(8,128)(2,1)S(1)} %copy-done.2, bf16[128,2048]{1,0:T(8,128)(2,1)} %collective-permute-done.refs_1_, bf16[128,2048]{1,0:T(8,128)(2,1)} %collective-permute-done.1.refs_2_, bf16[128,2048]{1,0:T(8,128)(2,1)S(1)} %copy-done.4, ...), custom_call_target="tpu_custom_call" | custom-call | flops 17179869184 | bytes 8388608 | tf_op jit(solution)/shard_map/pallas_call | solution.py:208
  103.0 0.5 collective-permute-start.22
  103.5 0.5 collective-permute-start.23
  104.0 2.4 %collective-permute-done.21.refs_11_ = bf16[6,256,512]{2,1,0:T(8,128)(2,1)S(1)} collective-permute-done((bf16[6,256,512]{2,1,0:T(8,128)(2,1)S(1)}, bf16[6,256,512]{2,1,0:T(8,128)(2,1)S(1)}, u32[]{:S(2)}, u32[]{:S(2)}) %collective-permute-start.21) | collective-permute-done | bytes 1572896 | tf_op jit(solution)/shard_map/ppermute | solution.py:405
  106.4 5.4 %shard_map.56.queries = bf16[4,512,128]{2,1,0:T(8,128)(2,1)S(1)} custom-call(s32[2]{0:T(128)S(1)} %pad_add_fusion.place, bf16[128,2048]{1,0:T(8,128)(2,1)S(1)} %copy-done.2, bf16[128,2048]{1,0:T(8,128)(2,1)} %collective-permute-done.refs_1_, bf16[128,2048]{1,0:T(8,128)(2,1)} %collective-permute-done.1.refs_2_, bf16[128,2048]{1,0:T(8,128)(2,1)S(1)} %copy-done.4, ...), custom_call_target="tpu_custom_call" | custom-call | flops 17179869184 | bytes 8388608 | tf_op jit(solution)/shard_map/pallas_call | solution.py:208
  111.8 0.2 collective-permute-start.24
  111.9 0.4 collective-permute-start.25
  112.5 0.4 collective-permute-start.27
  112.8 0.1 collective-permute-start.28
  113.0 0.4 collective-permute-done.24.kv3
  113.3 7.1 %shard_map.57 = (bf16[2,128,512]{2,1,0:T(8,128)(2,1)S(1)}, bf16[2,128,512]{2,1,0:T(8,128)(2,1)S(1)}) custom-call(s32[2]{0:T(128)S(1)} %pad_add_fusion.place, bf16[4,512,128]{2,1,0:T(8,128)(2,1)S(1)} %shard_map.56.queries, bf16[4,128,256]{2,1,0:T(8,128)(2,1)S(1)} %shard_map.55.kv0, bf16[4,128,256]{2,1,0:T(8,128)(2,1)S(1)} %collective-permute-done.22.kv1, ...), custom_call_target="tpu_custom_call" | custom-call | flops 10737418240 | bytes 4194304 | tf_op jit(solution)/shard_map/pallas_call | solution.py:283
  120.5 0.6 collective-permute-start.32
  121.1 2.3 %collective-permute-start.30 = (bf16[2,128,512]{2,1,0:T(8,128)(2,1)S(1)}, bf16[2,128,512]{2,1,0:T(8,128)(2,1)S(1)}, u32[]{:S(2)}, u32[]{:S(2)}) collective-permute-start(bf16[2,128,512]{2,1,0:T(8,128)(2,1)S(1)} %get-tuple-element.49.refs_0_), channel_id=1, source_target_pairs={{0,16},{1,17},{2,18},{3,19},{4,20},{5,21},{6,22},{7,23},{8,24},{9,... | collective-permute-start | bytes 786440 | tf_op jit(solution)/shard_map/ppermute | solution.py:405
  123.3 5.6 %collective-permute-done.32.refs_4_ = bf16[2,128,512]{2,1,0:T(8,128)(2,1)S(1)} collective-permute-done((bf16[2,128,512]{2,1,0:T(8,128)(2,1)S(1)}, bf16[2,128,512]{2,1,0:T(8,128)(2,1)S(1)}, u32[]{:S(2)}, u32[]{:S(2)}) %collective-permute-start.32) | collective-permute-done | bytes 262176 | tf_op jit(solution)/shard_map/ppermute | solution.py:405
  128.9 0.3 collective-permute-start.34
  129.2 4.9 %collective-permute-done.29.refs_1_ = bf16[2,128,512]{2,1,0:T(8,128)(2,1)S(1)} collective-permute-done((bf16[2,128,512]{2,1,0:T(8,128)(2,1)S(1)}, bf16[2,128,512]{2,1,0:T(8,128)(2,1)S(1)}, u32[]{:S(2)}, u32[]{:S(2)}) %collective-permute-start.29) | collective-permute-done | bytes 262176 | tf_op jit(solution)/shard_map/ppermute | solution.py:405
  134.1 7.8 %collective-permute-done.30.refs_2_ = bf16[2,128,512]{2,1,0:T(8,128)(2,1)S(1)} collective-permute-done((bf16[2,128,512]{2,1,0:T(8,128)(2,1)S(1)}, bf16[2,128,512]{2,1,0:T(8,128)(2,1)S(1)}, u32[]{:S(2)}, u32[]{:S(2)}) %collective-permute-start.30) | collective-permute-done | bytes 262176 | tf_op jit(solution)/shard_map/ppermute | solution.py:405
  142.0 5.1 %collective-permute-done.34.refs_6_ = bf16[2,128,512]{2,1,0:T(8,128)(2,1)S(1)} collective-permute-done((bf16[2,128,512]{2,1,0:T(8,128)(2,1)S(1)}, bf16[2,128,512]{2,1,0:T(8,128)(2,1)S(1)}, u32[]{:S(2)}, u32[]{:S(2)}) %collective-permute-start.34) | collective-permute-done | bytes 262176 | tf_op jit(solution)/shard_map/ppermute | solution.py:405
  147.0 8.2 %collective-permute-done.31.refs_3_ = bf16[2,128,512]{2,1,0:T(8,128)(2,1)S(1)} collective-permute-done((bf16[2,128,512]{2,1,0:T(8,128)(2,1)S(1)}, bf16[2,128,512]{2,1,0:T(8,128)(2,1)S(1)}, u32[]{:S(2)}, u32[]{:S(2)}) %collective-permute-start.31) | collective-permute-done | bytes 262176 | tf_op jit(solution)/shard_map/ppermute | solution.py:405
  155.2 3.7 %collective-permute-done.35.refs_7_ = bf16[2,128,512]{2,1,0:T(8,128)(2,1)S(1)} collective-permute-done((bf16[2,128,512]{2,1,0:T(8,128)(2,1)S(1)}, bf16[2,128,512]{2,1,0:T(8,128)(2,1)S(1)}, u32[]{:S(2)}, u32[]{:S(2)}) %collective-permute-start.35) | collective-permute-done | bytes 262176 | tf_op jit(solution)/shard_map/ppermute | solution.py:405
  158.9 6.6 %shard_map.58 = (bf16[128,1024]{1,0:T(8,128)(2,1)S(1)}, bf16[128,1024]{1,0:T(8,128)(2,1)}) custom-call(s32[2]{0:T(128)S(1)} %pad_add_fusion.place, bf16[2,128,512]{2,1,0:T(8,128)(2,1)S(1)} %get-tuple-element.49.refs_0_, bf16[2,128,512]{2,1,0:T(8,128)(2,1)S(1)} %collective-permute-done.29.refs_1_, bf16[2,128,512]{2,1,0:T(8,128)(2,1)S(1)} %collective-permute-done.30.refs_2_, ...), custom_call_target="tpu_custom_call" | custom-call | flops 2147483648 | bytes 12582912 | tf_op jit(solution)/shard_map/pallas_call | solution.py:354
  165.5 4.1 %collective-permute-start.36 = (bf16[128,1024]{1,0:T(8,128)(2,1)}, bf16[128,1024]{1,0:T(8,128)(2,1)S(1)}, u32[]{:S(2)}, u32[]{:S(2)}) collective-permute-start(bf16[128,1024]{1,0:T(8,128)(2,1)} %get-tuple-element.53), channel_id=1, source_target_pairs={{0,24},{1,16},{2,26},{3,18},{4,28},{5,20},{6,30},{7,22},{8,0},{9,8... | collective-permute-start | bytes 786440 | tf_op jit(solution)/shard_map/ppermute | solution.py:405
  169.6 0.7 collective-permute-start.37
  170.3 14.9 %collective-permute-done.36 = bf16[128,1024]{1,0:T(8,128)(2,1)S(1)} collective-permute-done((bf16[128,1024]{1,0:T(8,128)(2,1)}, bf16[128,1024]{1,0:T(8,128)(2,1)S(1)}, u32[]{:S(2)}, u32[]{:S(2)}) %collective-permute-start.36) | collective-permute-done | bytes 262176 | tf_op jit(solution)/shard_map/ppermute | solution.py:405
  185.3 0.8 pad_maximum_fusion.3
  (61 shorter events, 1.3 us)
Async XLA Ops:
  0.0 22.7 %collective-permute-start = (bf16[128,2048]{1,0:T(8,128)(2,1)}, bf16[128,2048]{1,0:T(8,128)(2,1)}, u32[]{:S(2)}, u32[]{:S(2)}) collective-permute-start(bf16[128,2048]{1,0:T(8,128)(2,1)} %refs_0_.3), channel_id=1, source_target_pairs={{0,1},{1,0},{2,3},{3,2},{4,5},{5,4},{6,7},{7,6},{8,9},{9,8},{10,11... | collective-permute-start | bytes 1572872 | tf_op jit(solution)/shard_map/ppermute | solution.py:405
  2.9 24.8 %collective-permute-start.1 = (bf16[128,2048]{1,0:T(8,128)(2,1)}, bf16[128,2048]{1,0:T(8,128)(2,1)}, u32[]{:S(2)}, u32[]{:S(2)}) collective-permute-start(bf16[128,2048]{1,0:T(8,128)(2,1)} %refs_0_.3), channel_id=1, source_target_pairs={{0,8},{1,9},{2,10},{3,11},{4,12},{5,13},{6,14},{7,15},{8,0},{9,1},... | collective-permute-start | bytes 1572872 | tf_op jit(solution)/shard_map/ppermute | solution.py:405
  4.5 39.6 %collective-permute-start.4 = (bf16[128,2048]{1,0:T(8,128)(2,1)}, bf16[128,2048]{1,0:T(8,128)(2,1)}, u32[]{:S(2)}, u32[]{:S(2)}) collective-permute-start(bf16[128,2048]{1,0:T(8,128)(2,1)} %refs_0_.3), channel_id=1, source_target_pairs={{0,16},{1,17},{2,18},{3,19},{4,20},{5,21},{6,22},{7,23},{8,24},{9,... | collective-permute-start | bytes 1572872 | tf_op jit(solution)/shard_map/ppermute | solution.py:405
  8.7 3.8 %copy-start = (bf16[2048,256]{1,0:T(8,128)(2,1)S(1)}, bf16[2048,256]{1,0:T(8,128)(2,1)}, u32[]{:S(2)}) copy-start(bf16[2048,256]{1,0:T(8,128)(2,1)} %refs_8_.1) | copy-start | bytes 3145732
  8.7 4.4 %copy-start.6 = (bf16[256,512]{1,0:T(8,128)(2,1)S(1)}, bf16[256,512]{1,0:T(8,128)(2,1)}, u32[]{:S(2)}) copy-start(bf16[256,512]{1,0:T(8,128)(2,1)} %param.8) | copy-start | bytes 786436
  11.0 10.2 %collective-permute-start.2 = (bf16[256,768]{1,0:T(8,128)(2,1)S(1)}, bf16[256,768]{1,0:T(8,128)(2,1)}, u32[]{:S(2)}, u32[]{:S(2)}) collective-permute-start(bf16[256,768]{1,0:T(8,128)(2,1)S(1)} %get-tuple-element.62), channel_id=1, source_target_pairs={{0,4},{1,5},{2,6},{3,7},{4,0},{5,1},{6,2},{7,3},{8,12},{9,13},{10,... | collective-permute-start | bytes 1179656 | tf_op jit(solution)/shard_map/ppermute | solution.py:405
  12.6 29.9 %collective-permute-start.6 = (bf16[2048,256]{1,0:T(8,128)(2,1)S(1)}, bf16[2048,256]{1,0:T(8,128)(2,1)S(1)}, u32[]{:S(2)}, u32[]{:S(2)}) collective-permute-start(bf16[2048,256]{1,0:T(8,128)(2,1)S(1)} %copy-done), channel_id=1, source_target_pairs={{0,1},{1,0},{2,3},{3,2},{4,5},{5,4},{6,7},{7,6},{8,9},{9,8},{10,11... | collective-permute-start | bytes 3145736 | tf_op jit(solution)/shard_map/ppermute | solution.py:405
  21.2 27.6 %collective-permute-start.11 = (bf16[2048,256]{1,0:T(8,128)(2,1)S(1)}, bf16[2048,256]{1,0:T(8,128)(2,1)S(1)}, u32[]{:S(2)}, u32[]{:S(2)}) collective-permute-start(bf16[2048,256]{1,0:T(8,128)(2,1)S(1)} %copy-done), channel_id=1, source_target_pairs={{0,4},{1,5},{2,6},{3,7},{4,0},{5,1},{6,2},{7,3},{8,12},{9,13},{10,... | collective-permute-start | bytes 3145736 | tf_op jit(solution)/shard_map/ppermute | solution.py:405
  27.7 13.7 %collective-permute-start.10 = (bf16[256,512]{1,0:T(8,128)(2,1)}, bf16[256,512]{1,0:T(8,128)(2,1)}, u32[]{:S(2)}, u32[]{:S(2)}) collective-permute-start(bf16[256,512]{1,0:T(8,128)(2,1)} %pad_maximum_fusion.6), channel_id=1, source_target_pairs={{0,16},{1,17},{2,18},{3,19},{4,20},{5,21},{6,22},{7,23},{8,24},{9,... | collective-permute-start | bytes 786440 | tf_op jit(solution)/shard_map/ppermute | solution.py:405
  31.2 17.6 %collective-permute-start.3 = (bf16[128,2048]{1,0:T(8,128)(2,1)}, bf16[128,2048]{1,0:T(8,128)(2,1)S(1)}, u32[]{:S(2)}, u32[]{:S(2)}) collective-permute-start(bf16[128,2048]{1,0:T(8,128)(2,1)} %collective-permute-done.1.refs_2_), channel_id=1, source_target_pairs={{0,1},{1,0},{2,3},{3,2},{4,5},{5,4},{6,7},{7,6},{8,9},{9,8},{10,11... | collective-permute-start | bytes 1572872 | tf_op jit(solution)/shard_map/ppermute | solution.py:405
  42.5 25.2 %collective-permute-start.16 = (bf16[2048,256]{1,0:T(8,128)(2,1)S(1)}, bf16[2048,256]{1,0:T(8,128)(2,1)}, u32[]{:S(2)}, u32[]{:S(2)}) collective-permute-start(bf16[2048,256]{1,0:T(8,128)(2,1)S(1)} %collective-permute-done.6.refs_10_), channel_id=1, source_target_pairs={{0,4},{1,5},{2,6},{3,7},{4,0},{5,1},{6,2},{7,3},{8,12},{9,13},{10,... | collective-permute-start | bytes 3145736 | tf_op jit(solution)/shard_map/ppermute | solution.py:405
  44.1 15.2 %collective-permute-start.7 = (bf16[128,2048]{1,0:T(8,128)(2,1)}, bf16[128,2048]{1,0:T(8,128)(2,1)}, u32[]{:S(2)}, u32[]{:S(2)}) collective-permute-start(bf16[128,2048]{1,0:T(8,128)(2,1)} %collective-permute-done.4.refs_4_), channel_id=1, source_target_pairs={{0,8},{1,9},{2,10},{3,11},{4,12},{5,13},{6,14},{7,15},{8,0},{9,1},... | collective-permute-start | bytes 1572872 | tf_op jit(solution)/shard_map/ppermute | solution.py:405
  48.8 4.5 %copy-start.3 = (bf16[128,2048]{1,0:T(8,128)(2,1)}, bf16[128,2048]{1,0:T(8,128)(2,1)S(1)}, u32[]{:S(2)}) copy-start(bf16[128,2048]{1,0:T(8,128)(2,1)S(1)} %collective-permute-done.3.refs_3_) | copy-start | bytes 1572868
  48.8 17.3 %collective-permute-start.9 = (bf16[2,256,768]{2,1,0:T(8,128)(2,1)}, bf16[2,256,768]{2,1,0:T(8,128)(2,1)}, u32[]{:S(2)}, u32[]{:S(2)}) collective-permute-start(bf16[2,256,768]{2,1,0:T(8,128)(2,1)} %pad_maximum_fusion.refs_8_), channel_id=1, source_target_pairs={{0,2},{1,3},{2,0},{3,1},{4,6},{5,7},{6,4},{7,5},{8,10},{9,11},{10,... | collective-permute-start | bytes 2359304 | tf_op jit(solution)/shard_map/ppermute | solution.py:405
  48.8 16.0 %collective-permute-start.12 = (bf16[2,256,256]{2,1,0:T(8,128)(2,1)}, bf16[2,256,256]{2,1,0:T(8,128)(2,1)}, u32[]{:S(2)}, u32[]{:S(2)}) collective-permute-start(bf16[2,256,256]{2,1,0:T(8,128)(2,1)} %pad_maximum_fusion.7), channel_id=1, source_target_pairs={{0,8},{1,9},{2,10},{3,11},{4,12},{5,13},{6,14},{7,15},{8,0},{9,1},... | collective-permute-start | bytes 786440 | tf_op jit(solution)/shard_map/ppermute | solution.py:405
  51.7 14.4 %collective-permute-start.5 = (bf16[128,2048]{1,0:T(8,128)(2,1)}, bf16[128,2048]{1,0:T(8,128)(2,1)}, u32[]{:S(2)}, u32[]{:S(2)}) collective-permute-start(bf16[128,2048]{1,0:T(8,128)(2,1)} %collective-permute-done.4.refs_4_), channel_id=1, source_target_pairs={{0,1},{1,0},{2,3},{3,2},{4,5},{5,4},{6,7},{7,6},{8,9},{9,8},{10,11... | collective-permute-start | bytes 1572872 | tf_op jit(solution)/shard_map/ppermute | solution.py:405
  54.1 15.2 %copy-start.5 = (bf16[256,512]{1,0:T(8,128)(2,1)S(1)}, bf16[256,512]{1,0:T(8,128)(2,1)}, u32[]{:S(2)}) copy-start(bf16[256,512]{1,0:T(8,128)(2,1)} %get-tuple-element.39) | copy-start | bytes 786436
  59.3 19.3 %collective-permute-start.15 = (bf16[256,512]{1,0:T(8,128)(2,1)}, bf16[256,512]{1,0:T(8,128)(2,1)S(1)}, u32[]{:S(2)}, u32[]{:S(2)}) collective-permute-start(bf16[256,512]{1,0:T(8,128)(2,1)} %get-tuple-element.40), channel_id=1, source_target_pairs={{0,24},{1,25},{2,26},{3,27},{4,28},{5,29},{6,30},{7,31},{8,16},{9,... | collective-permute-start | bytes 786440 | tf_op jit(solution)/shard_map/ppermute | solution.py:405
  64.8 13.8 %collective-permute-start.13 = (bf16[256,512]{1,0:T(8,128)(2,1)}, bf16[256,512]{1,0:T(8,128)(2,1)S(1)}, u32[]{:S(2)}, u32[]{:S(2)}) collective-permute-start(bf16[256,512]{1,0:T(8,128)(2,1)} %get-tuple-element.38), channel_id=1, source_target_pairs={{0,8},{1,9},{2,10},{3,11},{4,12},{5,13},{6,14},{7,15},{8,0},{9,1},... | collective-permute-start | bytes 786440 | tf_op jit(solution)/shard_map/ppermute | solution.py:405
  67.7 11.0 %collective-permute-start.17 = (bf16[3,256,256]{2,1,0:T(8,128)(2,1)S(1)}, bf16[3,256,256]{2,1,0:T(8,128)(2,1)S(1)}, u32[]{:S(2)}, u32[]{:S(2)}) collective-permute-start(bf16[3,256,256]{2,1,0:T(8,128)(2,1)S(1)} %pad_maximum_fusion.5.refs_10_), channel_id=1, source_target_pairs={{0,4},{1,5},{2,6},{3,7},{4,0},{5,1},{6,2},{7,3},{8,12},{9,13},{10,... | collective-permute-start | bytes 1179656 | tf_op jit(solution)/shard_map/ppermute | solution.py:405
  69.3 13.7 %collective-permute-start.14 = (bf16[256,512]{1,0:T(8,128)(2,1)S(1)}, bf16[256,512]{1,0:T(8,128)(2,1)S(1)}, u32[]{:S(2)}, u32[]{:S(2)}) collective-permute-start(bf16[256,512]{1,0:T(8,128)(2,1)S(1)} %copy-done.5), channel_id=1, source_target_pairs={{0,16},{1,17},{2,18},{3,19},{4,20},{5,21},{6,22},{7,23},{8,24},{9,... | collective-permute-start | bytes 786440 | tf_op jit(solution)/shard_map/ppermute | solution.py:405
  70.2 13.5 %collective-permute-start.8 = (bf16[128,2048]{1,0:T(8,128)(2,1)}, bf16[128,2048]{1,0:T(8,128)(2,1)S(1)}, u32[]{:S(2)}, u32[]{:S(2)}) collective-permute-start(bf16[128,2048]{1,0:T(8,128)(2,1)} %collective-permute-done.7.refs_6_), channel_id=1, source_target_pairs={{0,1},{1,0},{2,3},{3,2},{4,5},{5,4},{6,7},{7,6},{8,9},{9,8},{10,11... | collective-permute-start | bytes 1572872 | tf_op jit(solution)/shard_map/ppermute | solution.py:405
  78.7 14.9 %collective-permute-start.18 = (bf16[2,256,512]{2,1,0:T(8,128)(2,1)S(1)}, bf16[2,256,512]{2,1,0:T(8,128)(2,1)S(1)}, u32[]{:S(2)}, u32[]{:S(2)}) collective-permute-start(bf16[2,256,512]{2,1,0:T(8,128)(2,1)S(1)} %pad_maximum_fusion.2), channel_id=1, source_target_pairs={{0,4},{1,5},{2,6},{3,7},{4,0},{5,1},{6,2},{7,3},{8,12},{9,13},{10,... | collective-permute-start | bytes 1572872 | tf_op jit(solution)/shard_map/ppermute | solution.py:405
  83.0 15.1 %copy-start.1 = (f32[512,128]{1,0:T(8,128)S(1)}, f32[512,128]{1,0:T(8,128)}, u32[]{:S(2)}) copy-start(f32[512,128]{1,0:T(8,128)} %get-tuple-element.83.refs_14_.refs_13_) | copy-start | bytes 786436
  83.0 15.1 %copy-start.2 = (bf16[128,2048]{1,0:T(8,128)(2,1)S(1)}, bf16[128,2048]{1,0:T(8,128)(2,1)}, u32[]{:S(2)}) copy-start(bf16[128,2048]{1,0:T(8,128)(2,1)} %refs_0_.3) | copy-start | bytes 1572868
  83.0 15.1 %copy-start.4 = (bf16[128,2048]{1,0:T(8,128)(2,1)S(1)}, bf16[128,2048]{1,0:T(8,128)(2,1)}, u32[]{:S(2)}) copy-start(bf16[128,2048]{1,0:T(8,128)(2,1)} %copy-done.3) | copy-start | bytes 1572868
  83.0 15.0 %collective-permute-start.19 = (bf16[256,512]{1,0:T(8,128)(2,1)S(1)}, bf16[256,512]{1,0:T(8,128)(2,1)S(1)}, u32[]{:S(2)}, u32[]{:S(2)}) collective-permute-start(bf16[256,512]{1,0:T(8,128)(2,1)S(1)} %collective-permute-done.14), channel_id=1, source_target_pairs={{0,4},{1,5},{2,6},{3,7},{4,0},{5,1},{6,2},{7,3},{8,12},{9,13},{10,... | collective-permute-start | bytes 786440 | tf_op jit(solution)/shard_map/ppermute | solution.py:405
  83.7 14.4 %collective-permute-start.20 = (bf16[6,256,256]{2,1,0:T(8,128)(2,1)S(1)}, bf16[6,256,256]{2,1,0:T(8,128)(2,1)S(1)}, u32[]{:S(2)}, u32[]{:S(2)}) collective-permute-start(bf16[6,256,256]{2,1,0:T(8,128)(2,1)S(1)} %pad_maximum_fusion.1), channel_id=1, source_target_pairs={{0,2},{1,3},{2,0},{3,1},{4,6},{5,7},{6,4},{7,5},{8,10},{9,11},{10,... | collective-permute-start | bytes 2359304 | tf_op jit(solution)/shard_map/ppermute | solution.py:405
  102.9 3.5 %collective-permute-start.21 = (bf16[6,256,512]{2,1,0:T(8,128)(2,1)S(1)}, bf16[6,256,512]{2,1,0:T(8,128)(2,1)S(1)}, u32[]{:S(2)}, u32[]{:S(2)}) collective-permute-start(bf16[6,256,512]{2,1,0:T(8,128)(2,1)S(1)} %slice_dynamic-update-slice_fusion.refs_10_), channel_id=1, source_target_pairs={{0,2},{1,3},{2,0},{3,1},{4,6},{5,7},{6,4},{7,5},{8,10},{9,11},{10,... | collective-permute-start | bytes 4718600 | tf_op jit(solution)/shard_map/ppermute | solution.py:405
  103.0 9.9 %collective-permute-start.22 = (bf16[4,128,256]{2,1,0:T(8,128)(2,1)S(1)}, bf16[4,128,256]{2,1,0:T(8,128)(2,1)S(1)}, u32[]{:S(2)}, u32[]{:S(2)}) collective-permute-start(bf16[4,128,256]{2,1,0:T(8,128)(2,1)S(1)} %shard_map.55.kv0), channel_id=1, source_target_pairs={{0,2},{1,3},{2,0},{3,1},{4,6},{5,7},{6,4},{7,5},{8,10},{9,11},{10,... | collective-permute-start | bytes 786440 | tf_op jit(solution)/shard_map/ppermute | solution.py:405
  103.5 8.3 %collective-permute-start.23 = (bf16[4,128,256]{2,1,0:T(8,128)(2,1)S(1)}, bf16[4,128,256]{2,1,0:T(8,128)(2,1)S(1)}, u32[]{:S(2)}, u32[]{:S(2)}) collective-permute-start(bf16[4,128,256]{2,1,0:T(8,128)(2,1)S(1)} %shard_map.55.kv0), channel_id=1, source_target_pairs={{0,4},{1,5},{2,6},{3,7},{4,0},{5,1},{6,2},{7,3},{8,12},{9,13},{10,... | collective-permute-start | bytes 786440 | tf_op jit(solution)/shard_map/ppermute | solution.py:405
  111.8 1.6 collective-permute-start.24
  111.9 8.5 %collective-permute-start.25 = (bf16[2048,256]{1,0:T(8,128)(2,1)S(1)}, bf16[2048,256]{1,0:T(8,128)(2,1)S(1)}, u32[]{:S(2)}, u32[]{:S(2)}) collective-permute-start(bf16[2048,256]{1,0:T(8,128)(2,1)S(1)} %copy-done), channel_id=1, source_target_pairs={{0,2},{1,3},{2,0},{3,1},{4,6},{5,7},{6,4},{7,5},{8,10},{9,11},{10,... | collective-permute-start | bytes 3145736 | tf_op jit(solution)/shard_map/ppermute | solution.py:405
  112.3 8.1 %collective-permute-start.26 = (bf16[2048,256]{1,0:T(8,128)(2,1)S(1)}, bf16[2048,256]{1,0:T(8,128)(2,1)S(1)}, u32[]{:S(2)}, u32[]{:S(2)}) collective-permute-start(bf16[2048,256]{1,0:T(8,128)(2,1)S(1)} %collective-permute-done.6.refs_10_), channel_id=1, source_target_pairs={{0,2},{1,3},{2,0},{3,1},{4,6},{5,7},{6,4},{7,5},{8,10},{9,11},{10,... | collective-permute-start | bytes 3145736 | tf_op jit(solution)/shard_map/ppermute | solution.py:405
  112.5 8.0 %collective-permute-start.27 = (bf16[2048,256]{1,0:T(8,128)(2,1)S(1)}, bf16[2048,256]{1,0:T(8,128)(2,1)S(1)}, u32[]{:S(2)}, u32[]{:S(2)}) collective-permute-start(bf16[2048,256]{1,0:T(8,128)(2,1)S(1)} %collective-permute-done.11.refs_12_), channel_id=1, source_target_pairs={{0,2},{1,3},{2,0},{3,1},{4,6},{5,7},{6,4},{7,5},{8,10},{9,11},{10,... | collective-permute-start | bytes 3145736 | tf_op jit(solution)/shard_map/ppermute | solution.py:405
  112.8 7.6 %collective-permute-start.28 = (bf16[2048,256]{1,0:T(8,128)(2,1)}, bf16[2048,256]{1,0:T(8,128)(2,1)S(1)}, u32[]{:S(2)}, u32[]{:S(2)}) collective-permute-start(bf16[2048,256]{1,0:T(8,128)(2,1)} %collective-permute-done.16.refs_14_), channel_id=1, source_target_pairs={{0,2},{1,3},{2,0},{3,1},{4,6},{5,7},{6,4},{7,5},{8,10},{9,11},{10,... | collective-permute-start | bytes 3145736 | tf_op jit(solution)/shard_map/ppermute | solution.py:405
  120.5 8.4 %collective-permute-start.32 = (bf16[2,128,512]{2,1,0:T(8,128)(2,1)S(1)}, bf16[2,128,512]{2,1,0:T(8,128)(2,1)S(1)}, u32[]{:S(2)}, u32[]{:S(2)}) collective-permute-start(bf16[2,128,512]{2,1,0:T(8,128)(2,1)S(1)} %get-tuple-element.51), channel_id=1, source_target_pairs={{0,1},{1,0},{2,3},{3,2},{4,5},{5,4},{6,7},{7,6},{8,9},{9,8},{10,11... | collective-permute-start | bytes 786440 | tf_op jit(solution)/shard_map/ppermute | solution.py:405
  121.0 13.1 %collective-permute-start.29 = (bf16[2,128,512]{2,1,0:T(8,128)(2,1)S(1)}, bf16[2,128,512]{2,1,0:T(8,128)(2,1)S(1)}, u32[]{:S(2)}, u32[]{:S(2)}) collective-permute-start(bf16[2,128,512]{2,1,0:T(8,128)(2,1)S(1)} %get-tuple-element.49.refs_0_), channel_id=1, source_target_pairs={{0,8},{1,9},{2,10},{3,11},{4,12},{5,13},{6,14},{7,15},{8,0},{9,1},... | collective-permute-start | bytes 786440 | tf_op jit(solution)/shard_map/ppermute | solution.py:405
  121.1 20.9 %collective-permute-start.30 = (bf16[2,128,512]{2,1,0:T(8,128)(2,1)S(1)}, bf16[2,128,512]{2,1,0:T(8,128)(2,1)S(1)}, u32[]{:S(2)}, u32[]{:S(2)}) collective-permute-start(bf16[2,128,512]{2,1,0:T(8,128)(2,1)S(1)} %get-tuple-element.49.refs_0_), channel_id=1, source_target_pairs={{0,16},{1,17},{2,18},{3,19},{4,20},{5,21},{6,22},{7,23},{8,24},{9,... | collective-permute-start | bytes 786440 | tf_op jit(solution)/shard_map/ppermute | solution.py:405
  128.9 18.1 %collective-permute-start.34 = (bf16[2,128,512]{2,1,0:T(8,128)(2,1)S(1)}, bf16[2,128,512]{2,1,0:T(8,128)(2,1)S(1)}, u32[]{:S(2)}, u32[]{:S(2)}) collective-permute-start(bf16[2,128,512]{2,1,0:T(8,128)(2,1)S(1)} %collective-permute-done.32.refs_4_), channel_id=1, source_target_pairs={{0,16},{1,17},{2,18},{3,19},{4,20},{5,21},{6,22},{7,23},{8,24},{9,... | collective-permute-start | bytes 786440 | tf_op jit(solution)/shard_map/ppermute | solution.py:405
  134.1 21.1 %collective-permute-start.33 = (bf16[2,128,512]{2,1,0:T(8,128)(2,1)S(1)}, bf16[2,128,512]{2,1,0:T(8,128)(2,1)S(1)}, u32[]{:S(2)}, u32[]{:S(2)}) collective-permute-start(bf16[2,128,512]{2,1,0:T(8,128)(2,1)S(1)} %collective-permute-done.32.refs_4_), channel_id=1, source_target_pairs={{0,8},{1,9},{2,10},{3,11},{4,12},{5,13},{6,14},{7,15},{8,0},{9,1},... | collective-permute-start | bytes 786440 | tf_op jit(solution)/shard_map/ppermute | solution.py:405
  142.0 13.3 %collective-permute-start.31 = (bf16[2,128,512]{2,1,0:T(8,128)(2,1)S(1)}, bf16[2,128,512]{2,1,0:T(8,128)(2,1)S(1)}, u32[]{:S(2)}, u32[]{:S(2)}) collective-permute-start(bf16[2,128,512]{2,1,0:T(8,128)(2,1)S(1)} %collective-permute-done.30.refs_2_), channel_id=1, source_target_pairs={{0,8},{1,9},{2,10},{3,11},{4,12},{5,13},{6,14},{7,15},{8,0},{9,1},... | collective-permute-start | bytes 786440 | tf_op jit(solution)/shard_map/ppermute | solution.py:405
  147.0 11.9 %collective-permute-start.35 = (bf16[2,128,512]{2,1,0:T(8,128)(2,1)S(1)}, bf16[2,128,512]{2,1,0:T(8,128)(2,1)S(1)}, u32[]{:S(2)}, u32[]{:S(2)}) collective-permute-start(bf16[2,128,512]{2,1,0:T(8,128)(2,1)S(1)} %collective-permute-done.34.refs_6_), channel_id=1, source_target_pairs={{0,8},{1,9},{2,10},{3,11},{4,12},{5,13},{6,14},{7,15},{8,0},{9,1},... | collective-permute-start | bytes 786440 | tf_op jit(solution)/shard_map/ppermute | solution.py:405
  165.5 19.7 %collective-permute-start.36 = (bf16[128,1024]{1,0:T(8,128)(2,1)}, bf16[128,1024]{1,0:T(8,128)(2,1)S(1)}, u32[]{:S(2)}, u32[]{:S(2)}) collective-permute-start(bf16[128,1024]{1,0:T(8,128)(2,1)} %get-tuple-element.53), channel_id=1, source_target_pairs={{0,24},{1,16},{2,26},{3,18},{4,28},{5,20},{6,30},{7,22},{8,0},{9,8... | collective-permute-start | bytes 786440 | tf_op jit(solution)/shard_map/ppermute | solution.py:405
  169.6 15.6 %collective-permute-start.37 = (bf16[128,1024]{1,0:T(8,128)(2,1)S(1)}, bf16[128,1024]{1,0:T(8,128)(2,1)S(1)}, u32[]{:S(2)}, u32[]{:S(2)}) collective-permute-start(bf16[128,1024]{1,0:T(8,128)(2,1)S(1)} %get-tuple-element.54), channel_id=1, source_target_pairs={{0,0},{1,8},{2,2},{3,10},{4,4},{5,12},{6,6},{7,14},{8,24},{9,16},{... | collective-permute-start | bytes 786440 | tf_op jit(solution)/shard_map/ppermute | solution.py:405

commit v5 on v4

--- a/solution.py
+++ b/solution.py
@@ -204,7 +204,7 @@
 def project(kernel, out_shape, place, tokens, weights, plan, width, cosine, sine):
     rows, half = tokens[0].shape
     depth = weights[0].shape[1]
-    flops = 16 * 4 * rows * 16 * depth * HEAD_SIZE * 4
+    flops = 1 * 4 * rows * 16 * depth * HEAD_SIZE * 4
     return pl.pallas_call(
         functools.partial(kernel, plan),
         out_shape=jax.ShapeDtypeStruct(out_shape, jnp.bfloat16),
@@ -291,7 +291,7 @@
         ],
         compiler_params=pltpu.CompilerParams(vmem_limit_bytes=VMEM_LIMIT),
         cost_estimate=pl.CostEstimate(
-            flops=20 * work, bytes_accessed=4 << 20, transcendentals=4 * stacked * 16 * rows
+            flops=60 * work, bytes_accessed=4 << 20, transcendentals=4 * stacked * 16 * rows
         ),
     )(place, queries, *kv)
 
@@ -369,28 +369,24 @@
 
 
 ORDER = {
-    "y_out": ("own_y",),
-    "far": ("tok1", "other0", "own_y"),
-    "other1": ("other0", "own_y"),
-    "tok3": ("tok2", "tok1", "x_out", "own_y"),
-    "xy_out": ("own_y",),
-    "other2": ("other1",),
+    "far": ("other0",),
+    "tok3": ("tok2", "tok1", "own_y"),
     "near": ("y_out",),
     "query2": ("far",),
     "query3": ("far", "tok3", "other1"),
     "other3": ("other1",),
-    "query1": ("far", "near"),
-    "both_core": ("other1",),
-    "kv_rest_y": ("both_core", "y_out", "xy_out", "other2"),
-    "query2_y": ("kv_rest_y",),
+    "query1": ("far", "near", "other1", "other0"),
+    "kv_rest_y": ("y_out", "xy_out", "other2", "tok3"),
     "query31_y": ("kv_rest_y",),
     "kv_core": ("other3",),
     "query_core": ("own_kv",),
-    "mine1": ("core_w", "core_x", "core_y", "core_xy"),
+    "mine1": ("core_w", "core_x", "core_y"),
     "mine2": ("core_w", "core_x", "core_y", "core_xy"),
-    "from_x": ("core_w", "core_x", "core_y", "core_xy"),
-    "from_x1": ("mine1",),
+    "from_x": ("core_x", "core_y", "core_xy"),
+    "from_x1": ("mine1", "queries"),
     "core_y_kv": ("queries",),
+    "from_x3": ("query_core",),
+    "y_out": ("other0",),
 }
 
 

time: 187 us -> 182 us (0.973)
  waiting for transfers between devices: 113 us -> 109 us
  starting transfers between devices: 35 us -> 38.4 us
  other arithmetic: 7.49 us -> 4.96 us
    ppermute x38, waiting for transfers between devices: 113 us -> 109 us  [__call__(): self.there[name] = lax.ppermute(array, AXES, moves(target))]
    ppermute x38, starting transfers between devices: 35 us -> 38.4 us  [__call__(): self.there[name] = lax.ppermute(array, AXES, moves(target))]
    another operation x2, other arithmetic: 2.01 us -> 0.13 us  [split_body(): both = jnp.stack([own, own_y])]
  transfers between devices with their start and end apart: 38 -> 38, of which waited for: 21 -> 23; matrix products, arithmetic and copies ran while one was open for 7% -> 6% of each run, Pallas kernels for 7% -> 6%
where the time goes in v5:
time: 182 us
  waiting for transfers between devices  109 us (60%)
  starting transfers between devices  38.4 us (21%)
  Pallas kernels  22 us (12%)
  local copies, waits for them, and re-layouts  7.42 us (4%)
  other arithmetic  4.96 us (3%)
    ppermute x38, waiting for transfers between devices, __call__(): self.there[name] = lax.ppermute(array, AXES, moves(target))  109 us
    ppermute x38, starting transfers between devices, __call__(): self.there[name] = lax.ppermute(array, AXES, moves(target))  38.4 us
    pallas_call x2, Pallas kernels, project(): pl.pallas_call(functools.partial(kernel, plan), out_shape=jax.ShapeDtypeS...  8.9 us
    pallas_call x1, Pallas kernels, attend(): pl.pallas_call(attend_kernel, out_shape=(shape, shape), in_specs=[smem_sp...  7.07 us
    pallas_call x1, Pallas kernels, project_out(): pl.pallas_call(output_kernel, out_shape=(shape, shape), in_specs=[smem_sp...  6.07 us
    dynamic_slice x5, local copies, waits for them, and re-layouts, columns(): return lax.dynamic_slice_in_dim(weight, head * width, width, 1)  5.32 us
  transfers between devices with their start and end apart: 38, of which 23 were waited for; matrix products, arithmetic and copies ran while one was open for 6% of the time, Pallas kernels for 6%

profile of v5, /device:TPU:0, one launch (start us, length us, event | category | flops | bytes accessed | tf_op | source)
XLA Modules:
  0.0 181.8 jit_solution(3760955605475480879)
XLA Ops:
  0.0 2.9 %collective-permute-start = (bf16[128,2048]{1,0:T(8,128)(2,1)}, bf16[128,2048]{1,0:T(8,128)(2,1)S(1)}, u32[]{:S(2)}, u32[]{:S(2)}) collective-permute-start(bf16[128,2048]{1,0:T(8,128)(2,1)} %refs_0_.3), channel_id=1, source_target_pairs={{0,1},{1,0},{2,3},{3,2},{4,5},{5,4},{6,7},{7,6},{8,9},{9,8},{10,11... | collective-permute-start | bytes 1572872 | tf_op jit(solution)/shard_map/ppermute | solution.py:401
  2.9 1.6 collective-permute-start.1
  4.5 2.6 %collective-permute-start.3 = (bf16[128,2048]{1,0:T(8,128)(2,1)}, bf16[128,2048]{1,0:T(8,128)(2,1)S(1)}, u32[]{:S(2)}, u32[]{:S(2)}) collective-permute-start(bf16[128,2048]{1,0:T(8,128)(2,1)} %refs_0_.3), channel_id=1, source_target_pairs={{0,16},{1,17},{2,18},{3,19},{4,20},{5,21},{6,22},{7,23},{8,24},{9,... | collective-permute-start | bytes 1572872 | tf_op jit(solution)/shard_map/ppermute | solution.py:401
  7.1 1.0 constant_dynamic-slice_fusion.6
  8.1 2.2 %constant_dynamic-slice_fusion.2 = (bf16[256,512]{1,0:T(8,128)(2,1)}, bf16[256,512]{1,0:T(8,128)(2,1)}, bf16[256,512]{1,0:T(8,128)(2,1)S(1)}, bf16[256,512]{1,0:T(8,128)(2,1)}) fusion(bf16[256,2048]{1,0:T(8,128)(2,1)} %param.6, s32[]{:T(128)S(6)} %select_n.73, s32[]{:T(128)S(6)} %select_n.67, s32[]{:T(128)S(6)} %select_n.66, s32[]{:T(128)S(6)} %select_n.72), kind=kLoop, calls=%fused_computation.26 | loop fusion | bytes 2097168 | tf_op jit(solution)/shard_map/dynamic_slice | solution.py:430
  10.3 1.6 collective-permute-start.5
  11.9 0.5 collective-permute-start.15
  12.5 0.9 constant_dynamic-slice_fusion.8
  13.4 0.7 pad_maximum_fusion.6
  14.2 1.7 collective-permute-done.refs_1_
  15.9 3.2 %collective-permute-start.9 = (bf16[256,512]{1,0:T(8,128)(2,1)}, bf16[256,512]{1,0:T(8,128)(2,1)}, u32[]{:S(2)}, u32[]{:S(2)}) collective-permute-start(bf16[256,512]{1,0:T(8,128)(2,1)} %pad_maximum_fusion.6), channel_id=1, source_target_pairs={{0,16},{1,17},{2,18},{3,19},{4,20},{5,21},{6,22},{7,23},{8,24},{9,... | collective-permute-start | bytes 786440 | tf_op jit(solution)/shard_map/ppermute | solution.py:401
  19.1 1.3 collective-permute-done.5
  20.4 1.5 collective-permute-start.10
  21.9 1.0 fusion
  22.9 4.7 %collective-permute-done.1.refs_2_ = bf16[128,2048]{1,0:T(8,128)(2,1)S(1)} collective-permute-done((bf16[128,2048]{1,0:T(8,128)(2,1)}, bf16[128,2048]{1,0:T(8,128)(2,1)S(1)}, u32[]{:S(2)}, u32[]{:S(2)}) %collective-permute-start.1) | collective-permute-done | bytes 524320 | tf_op jit(solution)/shard_map/ppermute | solution.py:401
  27.6 9.0 %collective-permute-done.3.refs_4_ = bf16[128,2048]{1,0:T(8,128)(2,1)S(1)} collective-permute-done((bf16[128,2048]{1,0:T(8,128)(2,1)}, bf16[128,2048]{1,0:T(8,128)(2,1)S(1)}, u32[]{:S(2)}, u32[]{:S(2)}) %collective-permute-start.3) | collective-permute-done | bytes 524320 | tf_op jit(solution)/shard_map/ppermute | solution.py:401
  36.7 0.5 collective-permute-start.2
  37.2 4.3 %collective-permute-done.9 = bf16[256,512]{1,0:T(8,128)(2,1)} collective-permute-done((bf16[256,512]{1,0:T(8,128)(2,1)}, bf16[256,512]{1,0:T(8,128)(2,1)}, u32[]{:S(2)}, u32[]{:S(2)}) %collective-permute-start.9) | collective-permute-done | bytes 262176 | tf_op jit(solution)/shard_map/ppermute | solution.py:401
  41.5 1.0 fusion.3
  42.5 0.6 constant_dynamic-slice_fusion.1
  43.1 1.5 collective-permute-start.16
  44.6 0.6 constant_dynamic-slice_fusion
  45.3 0.8 pad_maximum_fusion.7
  46.1 0.2 pad_maximum_fusion.8
  46.3 0.6 collective-permute-start.4
  47.0 0.9 maximum_bitcast_fusion.2
  47.9 3.1 %collective-permute-start.13 = (bf16[256,512]{1,0:T(8,128)(2,1)}, bf16[256,512]{1,0:T(8,128)(2,1)S(1)}, u32[]{:S(2)}, u32[]{:S(2)}) collective-permute-start(bf16[256,512]{1,0:T(8,128)(2,1)} %get-tuple-element.33), channel_id=1, source_target_pairs={{0,16},{1,17},{2,18},{3,19},{4,20},{5,21},{6,22},{7,23},{8,24},{9,... | collective-permute-start | bytes 786440 | tf_op jit(solution)/shard_map/ppermute | solution.py:401
  50.9 3.3 %collective-permute-start.14 = (bf16[256,512]{1,0:T(8,128)(2,1)}, bf16[256,512]{1,0:T(8,128)(2,1)S(1)}, u32[]{:S(2)}, u32[]{:S(2)}) collective-permute-start(bf16[256,512]{1,0:T(8,128)(2,1)} %get-tuple-element.34), channel_id=1, source_target_pairs={{0,24},{1,25},{2,26},{3,27},{4,28},{5,29},{6,30},{7,31},{8,16},{9,... | collective-permute-start | bytes 786440 | tf_op jit(solution)/shard_map/ppermute | solution.py:401
  54.2 3.3 %collective-permute-done.11 = bf16[2,256,256]{2,1,0:T(8,128)(2,1)} collective-permute-done((bf16[2,256,256]{2,1,0:T(8,128)(2,1)}, bf16[2,256,256]{2,1,0:T(8,128)(2,1)}, u32[]{:S(2)}, u32[]{:S(2)}) %collective-permute-start.11) | collective-permute-done | bytes 262176 | tf_op jit(solution)/shard_map/ppermute | solution.py:401
  57.6 1.0 fusion.2
  58.6 1.4 collective-permute-done.4.refs_5_
  60.0 7.3 %collective-permute-done.16.refs_14_ = bf16[2048,256]{1,0:T(8,128)(2,1)} collective-permute-done((bf16[2048,256]{1,0:T(8,128)(2,1)}, bf16[2048,256]{1,0:T(8,128)(2,1)}, u32[]{:S(2)}, u32[]{:S(2)}) %collective-permute-start.16) | collective-permute-done | bytes 1048608 | tf_op jit(solution)/shard_map/ppermute | solution.py:401
  67.3 1.5 collective-permute-start.17
  69.0 0.1 collective-permute-done.13
  69.1 1.2 collective-permute-start.7
  70.4 0.5 collective-permute-start.19
  71.0 8.4 %collective-permute-done.17.refs_11_ = bf16[3,256,256]{2,1,0:T(8,128)(2,1)S(1)} collective-permute-done((bf16[3,256,256]{2,1,0:T(8,128)(2,1)S(1)}, bf16[3,256,256]{2,1,0:T(8,128)(2,1)S(1)}, u32[]{:S(2)}, u32[]{:S(2)}) %collective-permute-start.17) | collective-permute-done | bytes 393248 | tf_op jit(solution)/shard_map/ppermute | solution.py:401
  79.4 1.5 collective-permute-start.18
  81.0 2.3 %collective-permute-done.7.refs_7_ = bf16[128,2048]{1,0:T(8,128)(2,1)S(1)} collective-permute-done((bf16[128,2048]{1,0:T(8,128)(2,1)S(1)}, bf16[128,2048]{1,0:T(8,128)(2,1)S(1)}, u32[]{:S(2)}, u32[]{:S(2)}) %collective-permute-start.7) | collective-permute-done | bytes 524320 | tf_op jit(solution)/shard_map/ppermute | solution.py:401
  83.3 9.8 %collective-permute-done.18 = bf16[2,256,512]{2,1,0:T(8,128)(2,1)S(1)} collective-permute-done((bf16[2,256,512]{2,1,0:T(8,128)(2,1)S(1)}, bf16[2,256,512]{2,1,0:T(8,128)(2,1)S(1)}, u32[]{:S(2)}, u32[]{:S(2)}) %collective-permute-start.18) | collective-permute-done | bytes 524320 | tf_op jit(solution)/shard_map/ppermute | solution.py:401
  93.3 4.9 %shard_map.55.kv0 = bf16[4,128,256]{2,1,0:T(8,128)(2,1)S(1)} custom-call(s32[2]{0:T(128)S(1)} %pad_add_fusion.place, bf16[128,2048]{1,0:T(8,128)(2,1)S(1)} %copy-done, bf16[128,2048]{1,0:T(8,128)(2,1)S(1)} %collective-permute-done.refs_1_, bf16[128,2048]{1,0:T(8,128)(2,1)S(1)} %collective-permute-done.1.refs_2_, ...), custom_call_target="tpu_custom_call" | custom-call | flops 1073741824 | bytes 8388608 | tf_op jit(solution)/shard_map/pallas_call | solution.py:208
  98.3 1.5 collective-permute-start.23
  99.8 0.2 collective-permute-start.22
  100.0 1.7 collective-permute-done.21.refs_11_
  101.7 4.0 %shard_map.56.queries = bf16[4,512,128]{2,1,0:T(8,128)(2,1)S(1)} custom-call(s32[2]{0:T(128)S(1)} %pad_add_fusion.place, bf16[128,2048]{1,0:T(8,128)(2,1)S(1)} %copy-done, bf16[128,2048]{1,0:T(8,128)(2,1)S(1)} %collective-permute-done.refs_1_, bf16[128,2048]{1,0:T(8,128)(2,1)S(1)} %collective-permute-done.1.refs_2_, ...), custom_call_target="tpu_custom_call" | custom-call | flops 1073741824 | bytes 8388608 | tf_op jit(solution)/shard_map/pallas_call | solution.py:208
  105.7 1.3 collective-permute-done.23.kv2
  107.0 0.5 collective-permute-start.25
  107.5 0.5 collective-permute-start.27
  108.0 0.8 collective-permute-done.24.kv3
  108.9 7.1 %shard_map.57 = (bf16[2,128,512]{2,1,0:T(8,128)(2,1)S(1)}, bf16[2,128,512]{2,1,0:T(8,128)(2,1)S(1)}) custom-call(s32[2]{0:T(128)S(1)} %pad_add_fusion.place, bf16[4,512,128]{2,1,0:T(8,128)(2,1)S(1)} %shard_map.56.queries, bf16[4,128,256]{2,1,0:T(8,128)(2,1)S(1)} %shard_map.55.kv0, bf16[4,128,256]{2,1,0:T(8,128)(2,1)S(1)} %collective-permute-done.22.kv1, ...), custom_call_target="tpu_custom_call" | custom-call | flops 32212254720 | bytes 4194304 | tf_op jit(solution)/shard_map/pallas_call | solution.py:283
  116.0 1.5 collective-permute-start.32
  117.5 2.2 %collective-permute-start.30 = (bf16[2,128,512]{2,1,0:T(8,128)(2,1)S(1)}, bf16[2,128,512]{2,1,0:T(8,128)(2,1)S(1)}, u32[]{:S(2)}, u32[]{:S(2)}) collective-permute-start(bf16[2,128,512]{2,1,0:T(8,128)(2,1)S(1)} %get-tuple-element.42.refs_0_), channel_id=1, source_target_pairs={{0,16},{1,17},{2,18},{3,19},{4,20},{5,21},{6,22},{7,23},{8,24},{9,... | collective-permute-start | bytes 786440 | tf_op jit(solution)/shard_map/ppermute | solution.py:401
  119.6 4.8 %collective-permute-done.32.refs_4_ = bf16[2,128,512]{2,1,0:T(8,128)(2,1)S(1)} collective-permute-done((bf16[2,128,512]{2,1,0:T(8,128)(2,1)S(1)}, bf16[2,128,512]{2,1,0:T(8,128)(2,1)S(1)}, u32[]{:S(2)}, u32[]{:S(2)}) %collective-permute-start.32) | collective-permute-done | bytes 262176 | tf_op jit(solution)/shard_map/ppermute | solution.py:401
  124.4 5.8 %collective-permute-done.28.refs_1_ = bf16[2,128,512]{2,1,0:T(8,128)(2,1)S(1)} collective-permute-done((bf16[2,128,512]{2,1,0:T(8,128)(2,1)S(1)}, bf16[2,128,512]{2,1,0:T(8,128)(2,1)S(1)}, u32[]{:S(2)}, u32[]{:S(2)}) %collective-permute-start.28) | collective-permute-done | bytes 262176 | tf_op jit(solution)/shard_map/ppermute | solution.py:401
  130.2 8.6 %collective-permute-done.30.refs_2_ = bf16[2,128,512]{2,1,0:T(8,128)(2,1)S(1)} collective-permute-done((bf16[2,128,512]{2,1,0:T(8,128)(2,1)S(1)}, bf16[2,128,512]{2,1,0:T(8,128)(2,1)S(1)}, u32[]{:S(2)}, u32[]{:S(2)}) %collective-permute-start.30) | collective-permute-done | bytes 262176 | tf_op jit(solution)/shard_map/ppermute | solution.py:401
  138.7 4.7 %collective-permute-done.34.refs_6_ = bf16[2,128,512]{2,1,0:T(8,128)(2,1)S(1)} collective-permute-done((bf16[2,128,512]{2,1,0:T(8,128)(2,1)S(1)}, bf16[2,128,512]{2,1,0:T(8,128)(2,1)S(1)}, u32[]{:S(2)}, u32[]{:S(2)}) %collective-permute-start.34) | collective-permute-done | bytes 262176 | tf_op jit(solution)/shard_map/ppermute | solution.py:401
  143.5 2.6 %collective-permute-done.33.refs_5_ = bf16[2,128,512]{2,1,0:T(8,128)(2,1)S(1)} collective-permute-done((bf16[2,128,512]{2,1,0:T(8,128)(2,1)S(1)}, bf16[2,128,512]{2,1,0:T(8,128)(2,1)S(1)}, u32[]{:S(2)}, u32[]{:S(2)}) %collective-permute-start.33) | collective-permute-done | bytes 262176 | tf_op jit(solution)/shard_map/ppermute | solution.py:401
  146.0 5.6 %collective-permute-done.31.refs_3_ = bf16[2,128,512]{2,1,0:T(8,128)(2,1)S(1)} collective-permute-done((bf16[2,128,512]{2,1,0:T(8,128)(2,1)S(1)}, bf16[2,128,512]{2,1,0:T(8,128)(2,1)S(1)}, u32[]{:S(2)}, u32[]{:S(2)}) %collective-permute-start.31) | collective-permute-done | bytes 262176 | tf_op jit(solution)/shard_map/ppermute | solution.py:401
  151.6 3.7 %collective-permute-done.35.refs_7_ = bf16[2,128,512]{2,1,0:T(8,128)(2,1)S(1)} collective-permute-done((bf16[2,128,512]{2,1,0:T(8,128)(2,1)S(1)}, bf16[2,128,512]{2,1,0:T(8,128)(2,1)S(1)}, u32[]{:S(2)}, u32[]{:S(2)}) %collective-permute-start.35) | collective-permute-done | bytes 262176 | tf_op jit(solution)/shard_map/ppermute | solution.py:401
  155.3 6.1 %shard_map.58 = (bf16[128,1024]{1,0:T(8,128)(2,1)S(1)}, bf16[128,1024]{1,0:T(8,128)(2,1)S(1)}) custom-call(s32[2]{0:T(128)S(1)} %pad_add_fusion.place, bf16[2,128,512]{2,1,0:T(8,128)(2,1)S(1)} %get-tuple-element.42.refs_0_, bf16[2,128,512]{2,1,0:T(8,128)(2,1)S(1)} %collective-permute-done.28.refs_1_, ...), custom_call_target="tpu_custom_call" | custom-call | flops 2147483648 | bytes 12582912 | tf_op jit(solution)/shard_map/pallas_call | solution.py:354
  161.4 3.5 %collective-permute-start.36 = (bf16[128,1024]{1,0:T(8,128)(2,1)S(1)}, bf16[128,1024]{1,0:T(8,128)(2,1)S(1)}, u32[]{:S(2)}, u32[]{:S(2)}) collective-permute-start(bf16[128,1024]{1,0:T(8,128)(2,1)S(1)} %get-tuple-element.47), channel_id=1, source_target_pairs={{0,24},{1,16},{2,26},{3,18},{4,28},{5,20},{6,30},{7,22},{8,0},{9,8... | collective-permute-start | bytes 786440 | tf_op jit(solution)/shard_map/ppermute | solution.py:401
  164.9 0.7 collective-permute-start.37
  165.6 15.3 %collective-permute-done.36 = bf16[128,1024]{1,0:T(8,128)(2,1)S(1)} collective-permute-done((bf16[128,1024]{1,0:T(8,128)(2,1)S(1)}, bf16[128,1024]{1,0:T(8,128)(2,1)S(1)}, u32[]{:S(2)}, u32[]{:S(2)}) %collective-permute-start.36) | collective-permute-done | bytes 262176 | tf_op jit(solution)/shard_map/ppermute | solution.py:401
  181.0 0.8 pad_maximum_fusion.3
  (55 shorter events, 0.9 us)
Async XLA Ops:
  0.0 15.9 %collective-permute-start = (bf16[128,2048]{1,0:T(8,128)(2,1)}, bf16[128,2048]{1,0:T(8,128)(2,1)S(1)}, u32[]{:S(2)}, u32[]{:S(2)}) collective-permute-start(bf16[128,2048]{1,0:T(8,128)(2,1)} %refs_0_.3), channel_id=1, source_target_pairs={{0,1},{1,0},{2,3},{3,2},{4,5},{5,4},{6,7},{7,6},{8,9},{9,8},{10,11... | collective-permute-start | bytes 1572872 | tf_op jit(solution)/shard_map/ppermute | solution.py:401
  2.9 24.7 %collective-permute-start.1 = (bf16[128,2048]{1,0:T(8,128)(2,1)}, bf16[128,2048]{1,0:T(8,128)(2,1)S(1)}, u32[]{:S(2)}, u32[]{:S(2)}) collective-permute-start(bf16[128,2048]{1,0:T(8,128)(2,1)} %refs_0_.3), channel_id=1, source_target_pairs={{0,8},{1,9},{2,10},{3,11},{4,12},{5,13},{6,14},{7,15},{8,0},{9,1},... | collective-permute-start | bytes 1572872 | tf_op jit(solution)/shard_map/ppermute | solution.py:401
  4.5 32.2 %collective-permute-start.3 = (bf16[128,2048]{1,0:T(8,128)(2,1)}, bf16[128,2048]{1,0:T(8,128)(2,1)S(1)}, u32[]{:S(2)}, u32[]{:S(2)}) collective-permute-start(bf16[128,2048]{1,0:T(8,128)(2,1)} %refs_0_.3), channel_id=1, source_target_pairs={{0,16},{1,17},{2,18},{3,19},{4,20},{5,21},{6,22},{7,23},{8,24},{9,... | collective-permute-start | bytes 1572872 | tf_op jit(solution)/shard_map/ppermute | solution.py:401
  8.1 4.4 %copy-start.3 = (bf16[256,512]{1,0:T(8,128)(2,1)S(1)}, bf16[256,512]{1,0:T(8,128)(2,1)}, u32[]{:S(2)}) copy-start(bf16[256,512]{1,0:T(8,128)(2,1)} %param.8) | copy-start | bytes 786436
  10.3 10.1 %collective-permute-start.5 = (bf16[256,768]{1,0:T(8,128)(2,1)S(1)}, bf16[256,768]{1,0:T(8,128)(2,1)S(1)}, u32[]{:S(2)}, u32[]{:S(2)}) collective-permute-start(bf16[256,768]{1,0:T(8,128)(2,1)S(1)} %get-tuple-element.56), channel_id=1, source_target_pairs={{0,4},{1,5},{2,6},{3,7},{4,0},{5,1},{6,2},{7,3},{8,12},{9,13},{10,... | collective-permute-start | bytes 1179656 | tf_op jit(solution)/shard_map/ppermute | solution.py:401
  11.9 31.2 %collective-permute-start.15 = (bf16[2048,256]{1,0:T(8,128)(2,1)}, bf16[2048,256]{1,0:T(8,128)(2,1)}, u32[]{:S(2)}, u32[]{:S(2)}) collective-permute-start(bf16[2048,256]{1,0:T(8,128)(2,1)} %refs_8_.1), channel_id=1, source_target_pairs={{0,1},{1,0},{2,3},{3,2},{4,5},{5,4},{6,7},{7,6},{8,9},{9,8},{10,11... | collective-permute-start | bytes 3145736 | tf_op jit(solution)/shard_map/ppermute | solution.py:401
  15.9 25.6 %collective-permute-start.9 = (bf16[256,512]{1,0:T(8,128)(2,1)}, bf16[256,512]{1,0:T(8,128)(2,1)}, u32[]{:S(2)}, u32[]{:S(2)}) collective-permute-start(bf16[256,512]{1,0:T(8,128)(2,1)} %pad_maximum_fusion.6), channel_id=1, source_target_pairs={{0,16},{1,17},{2,18},{3,19},{4,20},{5,21},{6,22},{7,23},{8,24},{9,... | collective-permute-start | bytes 786440 | tf_op jit(solution)/shard_map/ppermute | solution.py:401
  20.4 16.8 %copy-start.1 = (bf16[256,768]{1,0:T(8,128)(2,1)}, bf16[256,768]{1,0:T(8,128)(2,1)S(1)}, u32[]{:S(2)}) copy-start(bf16[256,768]{1,0:T(8,128)(2,1)S(1)} %collective-permute-done.5) | copy-start | bytes 1179652
  20.4 25.7 %collective-permute-start.10 = (bf16[2048,256]{1,0:T(8,128)(2,1)}, bf16[2048,256]{1,0:T(8,128)(2,1)}, u32[]{:S(2)}, u32[]{:S(2)}) collective-permute-start(bf16[2048,256]{1,0:T(8,128)(2,1)} %refs_8_.1), channel_id=1, source_target_pairs={{0,4},{1,5},{2,6},{3,7},{4,0},{5,1},{6,2},{7,3},{8,12},{9,13},{10,... | collective-permute-start | bytes 3145736 | tf_op jit(solution)/shard_map/ppermute | solution.py:401
  36.7 11.2 %collective-permute-start.6 = (bf16[128,2048]{1,0:T(8,128)(2,1)S(1)}, bf16[128,2048]{1,0:T(8,128)(2,1)S(1)}, u32[]{:S(2)}, u32[]{:S(2)}) collective-permute-start(bf16[128,2048]{1,0:T(8,128)(2,1)S(1)} %collective-permute-done.3.refs_4_), channel_id=1, source_target_pairs={{0,8},{1,9},{2,10},{3,11},{4,12},{5,13},{6,14},{7,15},{8,0},{9,1},... | collective-permute-start | bytes 1572872 | tf_op jit(solution)/shard_map/ppermute | solution.py:401
  36.7 14.3 %collective-permute-start.2 = (bf16[128,2048]{1,0:T(8,128)(2,1)S(1)}, bf16[128,2048]{1,0:T(8,128)(2,1)S(1)}, u32[]{:S(2)}, u32[]{:S(2)}) collective-permute-start(bf16[128,2048]{1,0:T(8,128)(2,1)S(1)} %collective-permute-done.1.refs_2_), channel_id=1, source_target_pairs={{0,1},{1,0},{2,3},{3,2},{4,5},{5,4},{6,7},{7,6},{8,9},{9,8},{10,11... | collective-permute-start | bytes 1572872 | tf_op jit(solution)/shard_map/ppermute | solution.py:401
  43.1 24.2 %collective-permute-start.16 = (bf16[2048,256]{1,0:T(8,128)(2,1)}, bf16[2048,256]{1,0:T(8,128)(2,1)}, u32[]{:S(2)}, u32[]{:S(2)}) collective-permute-start(bf16[2048,256]{1,0:T(8,128)(2,1)} %collective-permute-done.15.refs_10_), channel_id=1, source_target_pairs={{0,4},{1,5},{2,6},{3,7},{4,0},{5,1},{6,2},{7,3},{8,12},{9,13},{10,... | collective-permute-start | bytes 3145736 | tf_op jit(solution)/shard_map/ppermute | solution.py:401
  46.1 11.5 %collective-permute-start.11 = (bf16[2,256,256]{2,1,0:T(8,128)(2,1)}, bf16[2,256,256]{2,1,0:T(8,128)(2,1)}, u32[]{:S(2)}, u32[]{:S(2)}) collective-permute-start(bf16[2,256,256]{2,1,0:T(8,128)(2,1)} %pad_maximum_fusion.7), channel_id=1, source_target_pairs={{0,8},{1,9},{2,10},{3,11},{4,12},{5,13},{6,14},{7,15},{8,0},{9,1},... | collective-permute-start | bytes 786440 | tf_op jit(solution)/shard_map/ppermute | solution.py:401
  46.3 22.6 %copy-start.2 = (bf16[256,768]{1,0:T(8,128)(2,1)S(1)}, bf16[256,768]{1,0:T(8,128)(2,1)}, u32[]{:S(2)}) copy-start(bf16[256,768]{1,0:T(8,128)(2,1)} %copy-done.1) | copy-start | bytes 1179652
  46.3 13.7 %collective-permute-start.4 = (bf16[128,2048]{1,0:T(8,128)(2,1)S(1)}, bf16[128,2048]{1,0:T(8,128)(2,1)S(1)}, u32[]{:S(2)}, u32[]{:S(2)}) collective-permute-start(bf16[128,2048]{1,0:T(8,128)(2,1)S(1)} %collective-permute-done.3.refs_4_), channel_id=1, source_target_pairs={{0,1},{1,0},{2,3},{3,2},{4,5},{5,4},{6,7},{7,6},{8,9},{9,8},{10,11... | collective-permute-start | bytes 1572872 | tf_op jit(solution)/shard_map/ppermute | solution.py:401
  47.9 21.3 %collective-permute-start.13 = (bf16[256,512]{1,0:T(8,128)(2,1)}, bf16[256,512]{1,0:T(8,128)(2,1)S(1)}, u32[]{:S(2)}, u32[]{:S(2)}) collective-permute-start(bf16[256,512]{1,0:T(8,128)(2,1)} %get-tuple-element.33), channel_id=1, source_target_pairs={{0,16},{1,17},{2,18},{3,19},{4,20},{5,21},{6,22},{7,23},{8,24},{9,... | collective-permute-start | bytes 786440 | tf_op jit(solution)/shard_map/ppermute | solution.py:401
  50.9 20.0 %collective-permute-start.14 = (bf16[256,512]{1,0:T(8,128)(2,1)}, bf16[256,512]{1,0:T(8,128)(2,1)S(1)}, u32[]{:S(2)}, u32[]{:S(2)}) collective-permute-start(bf16[256,512]{1,0:T(8,128)(2,1)} %get-tuple-element.34), channel_id=1, source_target_pairs={{0,24},{1,25},{2,26},{3,27},{4,28},{5,29},{6,30},{7,31},{8,16},{9,... | collective-permute-start | bytes 786440 | tf_op jit(solution)/shard_map/ppermute | solution.py:401
  57.6 12.8 %collective-permute-start.12 = (bf16[256,512]{1,0:T(8,128)(2,1)}, bf16[256,512]{1,0:T(8,128)(2,1)S(1)}, u32[]{:S(2)}, u32[]{:S(2)}) collective-permute-start(bf16[256,512]{1,0:T(8,128)(2,1)} %get-tuple-element.32), channel_id=1, source_target_pairs={{0,8},{1,9},{2,10},{3,11},{4,12},{5,13},{6,14},{7,15},{8,0},{9,1},... | collective-permute-start | bytes 786440 | tf_op jit(solution)/shard_map/ppermute | solution.py:401
  67.3 12.1 %collective-permute-start.17 = (bf16[3,256,256]{2,1,0:T(8,128)(2,1)S(1)}, bf16[3,256,256]{2,1,0:T(8,128)(2,1)S(1)}, u32[]{:S(2)}, u32[]{:S(2)}) collective-permute-start(bf16[3,256,256]{2,1,0:T(8,128)(2,1)S(1)} %pad_maximum_fusion.5.refs_10_), channel_id=1, source_target_pairs={{0,4},{1,5},{2,6},{3,7},{4,0},{5,1},{6,2},{7,3},{8,12},{9,13},{10,... | collective-permute-start | bytes 1179656 | tf_op jit(solution)/shard_map/ppermute | solution.py:401
  68.9 24.3 %collective-permute-start.8 = (bf16[2,256,768]{2,1,0:T(8,128)(2,1)S(1)}, bf16[2,256,768]{2,1,0:T(8,128)(2,1)S(1)}, u32[]{:S(2)}, u32[]{:S(2)}) collective-permute-start(bf16[2,256,768]{2,1,0:T(8,128)(2,1)S(1)} %pad_maximum_fusion.refs_8_), channel_id=1, source_target_pairs={{0,2},{1,3},{2,0},{3,1},{4,6},{5,7},{6,4},{7,5},{8,10},{9,11},{10,... | collective-permute-start | bytes 2359304 | tf_op jit(solution)/shard_map/ppermute | solution.py:401
  69.1 14.2 %collective-permute-start.7 = (bf16[128,2048]{1,0:T(8,128)(2,1)S(1)}, bf16[128,2048]{1,0:T(8,128)(2,1)S(1)}, u32[]{:S(2)}, u32[]{:S(2)}) collective-permute-start(bf16[128,2048]{1,0:T(8,128)(2,1)S(1)} %collective-permute-done.6.refs_6_), channel_id=1, source_target_pairs={{0,1},{1,0},{2,3},{3,2},{4,5},{5,4},{6,7},{7,6},{8,9},{9,8},{10,11... | collective-permute-start | bytes 1572872 | tf_op jit(solution)/shard_map/ppermute | solution.py:401
  70.4 22.8 %collective-permute-start.19 = (bf16[256,512]{1,0:T(8,128)(2,1)S(1)}, bf16[256,512]{1,0:T(8,128)(2,1)S(1)}, u32[]{:S(2)}, u32[]{:S(2)}) collective-permute-start(bf16[256,512]{1,0:T(8,128)(2,1)S(1)} %collective-permute-done.13), channel_id=1, source_target_pairs={{0,4},{1,5},{2,6},{3,7},{4,0},{5,1},{6,2},{7,3},{8,12},{9,13},{10,... | collective-permute-start | bytes 786440 | tf_op jit(solution)/shard_map/ppermute | solution.py:401
  79.4 13.7 %collective-permute-start.18 = (bf16[2,256,512]{2,1,0:T(8,128)(2,1)S(1)}, bf16[2,256,512]{2,1,0:T(8,128)(2,1)S(1)}, u32[]{:S(2)}, u32[]{:S(2)}) collective-permute-start(bf16[2,256,512]{2,1,0:T(8,128)(2,1)S(1)} %pad_maximum_fusion.2), channel_id=1, source_target_pairs={{0,4},{1,5},{2,6},{3,7},{4,0},{5,1},{6,2},{7,3},{8,12},{9,13},{10,... | collective-permute-start | bytes 1572872 | tf_op jit(solution)/shard_map/ppermute | solution.py:401
  80.9 12.4 %copy-start = (bf16[128,2048]{1,0:T(8,128)(2,1)S(1)}, bf16[128,2048]{1,0:T(8,128)(2,1)}, u32[]{:S(2)}) copy-start(bf16[128,2048]{1,0:T(8,128)(2,1)} %refs_0_.3) | copy-start | bytes 1572868
  83.3 9.9 %collective-permute-start.20 = (bf16[6,256,256]{2,1,0:T(8,128)(2,1)S(1)}, bf16[6,256,256]{2,1,0:T(8,128)(2,1)S(1)}, u32[]{:S(2)}, u32[]{:S(2)}) collective-permute-start(bf16[6,256,256]{2,1,0:T(8,128)(2,1)S(1)} %pad_maximum_fusion.1), channel_id=1, source_target_pairs={{0,2},{1,3},{2,0},{3,1},{4,6},{5,7},{6,4},{7,5},{8,10},{9,11},{10,... | collective-permute-start | bytes 2359304 | tf_op jit(solution)/shard_map/ppermute | solution.py:401
  98.2 3.5 %collective-permute-start.21 = (bf16[6,256,512]{2,1,0:T(8,128)(2,1)S(1)}, bf16[6,256,512]{2,1,0:T(8,128)(2,1)S(1)}, u32[]{:S(2)}, u32[]{:S(2)}) collective-permute-start(bf16[6,256,512]{2,1,0:T(8,128)(2,1)S(1)} %slice_dynamic-update-slice_fusion.refs_10_), channel_id=1, source_target_pairs={{0,2},{1,3},{2,0},{3,1},{4,6},{5,7},{6,4},{7,5},{8,10},{9,11},{10,... | collective-permute-start | bytes 4718600 | tf_op jit(solution)/shard_map/ppermute | solution.py:401
  98.3 8.7 %collective-permute-start.23 = (bf16[4,128,256]{2,1,0:T(8,128)(2,1)S(1)}, bf16[4,128,256]{2,1,0:T(8,128)(2,1)S(1)}, u32[]{:S(2)}, u32[]{:S(2)}) collective-permute-start(bf16[4,128,256]{2,1,0:T(8,128)(2,1)S(1)} %shard_map.55.kv0), channel_id=1, source_target_pairs={{0,4},{1,5},{2,6},{3,7},{4,0},{5,1},{6,2},{7,3},{8,12},{9,13},{10,... | collective-permute-start | bytes 786440 | tf_op jit(solution)/shard_map/ppermute | solution.py:401
  99.8 8.2 %collective-permute-start.22 = (bf16[4,128,256]{2,1,0:T(8,128)(2,1)S(1)}, bf16[4,128,256]{2,1,0:T(8,128)(2,1)S(1)}, u32[]{:S(2)}, u32[]{:S(2)}) collective-permute-start(bf16[4,128,256]{2,1,0:T(8,128)(2,1)S(1)} %shard_map.55.kv0), channel_id=1, source_target_pairs={{0,2},{1,3},{2,0},{3,1},{4,6},{5,7},{6,4},{7,5},{8,10},{9,11},{10,... | collective-permute-start | bytes 786440 | tf_op jit(solution)/shard_map/ppermute | solution.py:401
  107.0 1.9 %collective-permute-start.24 = (bf16[4,128,256]{2,1,0:T(8,128)(2,1)S(1)}, bf16[4,128,256]{2,1,0:T(8,128)(2,1)S(1)}, u32[]{:S(2)}, u32[]{:S(2)}) collective-permute-start(bf16[4,128,256]{2,1,0:T(8,128)(2,1)S(1)} %collective-permute-done.23.kv2), channel_id=1, source_target_pairs={{0,2},{1,3},{2,0},{3,1},{4,6},{5,7},{6,4},{7,5},{8,10},{9,11},{10,... | collective-permute-start | bytes 786440 | tf_op jit(solution)/shard_map/ppermute | solution.py:401
  107.0 10.5 %collective-permute-start.25 = (bf16[2048,256]{1,0:T(8,128)(2,1)}, bf16[2048,256]{1,0:T(8,128)(2,1)S(1)}, u32[]{:S(2)}, u32[]{:S(2)}) collective-permute-start(bf16[2048,256]{1,0:T(8,128)(2,1)} %refs_8_.1), channel_id=1, source_target_pairs={{0,2},{1,3},{2,0},{3,1},{4,6},{5,7},{6,4},{7,5},{8,10},{9,11},{10,... | collective-permute-start | bytes 3145736 | tf_op jit(solution)/shard_map/ppermute | solution.py:401
  107.5 8.4 %collective-permute-start.26 = (bf16[2048,256]{1,0:T(8,128)(2,1)}, bf16[2048,256]{1,0:T(8,128)(2,1)S(1)}, u32[]{:S(2)}, u32[]{:S(2)}) collective-permute-start(bf16[2048,256]{1,0:T(8,128)(2,1)} %collective-permute-done.15.refs_10_), channel_id=1, source_target_pairs={{0,2},{1,3},{2,0},{3,1},{4,6},{5,7},{6,4},{7,5},{8,10},{9,11},{10,... | collective-permute-start | bytes 3145736 | tf_op jit(solution)/shard_map/ppermute | solution.py:401
  107.5 8.5 %collective-permute-start.27 = (bf16[2048,256]{1,0:T(8,128)(2,1)}, bf16[2048,256]{1,0:T(8,128)(2,1)S(1)}, u32[]{:S(2)}, u32[]{:S(2)}) collective-permute-start(bf16[2048,256]{1,0:T(8,128)(2,1)} %collective-permute-done.10.refs_12_), channel_id=1, source_target_pairs={{0,2},{1,3},{2,0},{3,1},{4,6},{5,7},{6,4},{7,5},{8,10},{9,11},{10,... | collective-permute-start | bytes 3145736 | tf_op jit(solution)/shard_map/ppermute | solution.py:401
  108.0 8.0 %collective-permute-start.29 = (bf16[2048,256]{1,0:T(8,128)(2,1)}, bf16[2048,256]{1,0:T(8,128)(2,1)S(1)}, u32[]{:S(2)}, u32[]{:S(2)}) collective-permute-start(bf16[2048,256]{1,0:T(8,128)(2,1)} %collective-permute-done.16.refs_14_), channel_id=1, source_target_pairs={{0,2},{1,3},{2,0},{3,1},{4,6},{5,7},{6,4},{7,5},{8,10},{9,11},{10,... | collective-permute-start | bytes 3145736 | tf_op jit(solution)/shard_map/ppermute | solution.py:401
  116.0 8.4 %collective-permute-start.32 = (bf16[2,128,512]{2,1,0:T(8,128)(2,1)S(1)}, bf16[2,128,512]{2,1,0:T(8,128)(2,1)S(1)}, u32[]{:S(2)}, u32[]{:S(2)}) collective-permute-start(bf16[2,128,512]{2,1,0:T(8,128)(2,1)S(1)} %get-tuple-element.44), channel_id=1, source_target_pairs={{0,1},{1,0},{2,3},{3,2},{4,5},{5,4},{6,7},{7,6},{8,9},{9,8},{10,11... | collective-permute-start | bytes 786440 | tf_op jit(solution)/shard_map/ppermute | solution.py:401
  117.5 12.7 %collective-permute-start.28 = (bf16[2,128,512]{2,1,0:T(8,128)(2,1)S(1)}, bf16[2,128,512]{2,1,0:T(8,128)(2,1)S(1)}, u32[]{:S(2)}, u32[]{:S(2)}) collective-permute-start(bf16[2,128,512]{2,1,0:T(8,128)(2,1)S(1)} %get-tuple-element.42.refs_0_), channel_id=1, source_target_pairs={{0,8},{1,9},{2,10},{3,11},{4,12},{5,13},{6,14},{7,15},{8,0},{9,1},... | collective-permute-start | bytes 786440 | tf_op jit(solution)/shard_map/ppermute | solution.py:401
  117.5 21.3 %collective-permute-start.30 = (bf16[2,128,512]{2,1,0:T(8,128)(2,1)S(1)}, bf16[2,128,512]{2,1,0:T(8,128)(2,1)S(1)}, u32[]{:S(2)}, u32[]{:S(2)}) collective-permute-start(bf16[2,128,512]{2,1,0:T(8,128)(2,1)S(1)} %get-tuple-element.42.refs_0_), channel_id=1, source_target_pairs={{0,16},{1,17},{2,18},{3,19},{4,20},{5,21},{6,22},{7,23},{8,24},{9,... | collective-permute-start | bytes 786440 | tf_op jit(solution)/shard_map/ppermute | solution.py:401
  124.4 19.0 %collective-permute-start.34 = (bf16[2,128,512]{2,1,0:T(8,128)(2,1)S(1)}, bf16[2,128,512]{2,1,0:T(8,128)(2,1)S(1)}, u32[]{:S(2)}, u32[]{:S(2)}) collective-permute-start(bf16[2,128,512]{2,1,0:T(8,128)(2,1)S(1)} %collective-permute-done.32.refs_4_), channel_id=1, source_target_pairs={{0,16},{1,17},{2,18},{3,19},{4,20},{5,21},{6,22},{7,23},{8,24},{9,... | collective-permute-start | bytes 786440 | tf_op jit(solution)/shard_map/ppermute | solution.py:401
  130.2 15.8 %collective-permute-start.33 = (bf16[2,128,512]{2,1,0:T(8,128)(2,1)S(1)}, bf16[2,128,512]{2,1,0:T(8,128)(2,1)S(1)}, u32[]{:S(2)}, u32[]{:S(2)}) collective-permute-start(bf16[2,128,512]{2,1,0:T(8,128)(2,1)S(1)} %collective-permute-done.32.refs_4_), channel_id=1, source_target_pairs={{0,8},{1,9},{2,10},{3,11},{4,12},{5,13},{6,14},{7,15},{8,0},{9,1},... | collective-permute-start | bytes 786440 | tf_op jit(solution)/shard_map/ppermute | solution.py:401
  138.7 12.9 %collective-permute-start.31 = (bf16[2,128,512]{2,1,0:T(8,128)(2,1)S(1)}, bf16[2,128,512]{2,1,0:T(8,128)(2,1)S(1)}, u32[]{:S(2)}, u32[]{:S(2)}) collective-permute-start(bf16[2,128,512]{2,1,0:T(8,128)(2,1)S(1)} %collective-permute-done.30.refs_2_), channel_id=1, source_target_pairs={{0,8},{1,9},{2,10},{3,11},{4,12},{5,13},{6,14},{7,15},{8,0},{9,1},... | collective-permute-start | bytes 786440 | tf_op jit(solution)/shard_map/ppermute | solution.py:401
  143.4 11.9 %collective-permute-start.35 = (bf16[2,128,512]{2,1,0:T(8,128)(2,1)S(1)}, bf16[2,128,512]{2,1,0:T(8,128)(2,1)S(1)}, u32[]{:S(2)}, u32[]{:S(2)}) collective-permute-start(bf16[2,128,512]{2,1,0:T(8,128)(2,1)S(1)} %collective-permute-done.34.refs_6_), channel_id=1, source_target_pairs={{0,8},{1,9},{2,10},{3,11},{4,12},{5,13},{6,14},{7,15},{8,0},{9,1},... | collective-permute-start | bytes 786440 | tf_op jit(solution)/shard_map/ppermute | solution.py:401
  161.4 19.5 %collective-permute-start.36 = (bf16[128,1024]{1,0:T(8,128)(2,1)S(1)}, bf16[128,1024]{1,0:T(8,128)(2,1)S(1)}, u32[]{:S(2)}, u32[]{:S(2)}) collective-permute-start(bf16[128,1024]{1,0:T(8,128)(2,1)S(1)} %get-tuple-element.47), channel_id=1, source_target_pairs={{0,24},{1,16},{2,26},{3,18},{4,28},{5,20},{6,30},{7,22},{8,0},{9,8... | collective-permute-start | bytes 786440 | tf_op jit(solution)/shard_map/ppermute | solution.py:401
  164.9 16.0 %collective-permute-start.37 = (bf16[128,1024]{1,0:T(8,128)(2,1)S(1)}, bf16[128,1024]{1,0:T(8,128)(2,1)S(1)}, u32[]{:S(2)}, u32[]{:S(2)}) collective-permute-start(bf16[128,1024]{1,0:T(8,128)(2,1)S(1)} %get-tuple-element.48), channel_id=1, source_target_pairs={{0,0},{1,8},{2,2},{3,10},{4,4},{5,12},{6,6},{7,14},{8,24},{9,16},{... | collective-permute-start | bytes 786440 | tf_op jit(solution)/shard_map/ppermute | solution.py:401

commit v6 on v5

--- a/solution.py
+++ b/solution.py
@@ -372,15 +372,16 @@
     "far": ("other0",),
     "tok3": ("tok2", "tok1", "own_y"),
     "near": ("y_out",),
-    "query2": ("far",),
+    "query2": ("far", "tok1"),
     "query3": ("far", "tok3", "other1"),
     "other3": ("other1",),
     "query1": ("far", "near", "other1", "other0"),
-    "kv_rest_y": ("y_out", "xy_out", "other2", "tok3"),
+    "both_core": ("other1",),
+    "kv_rest_y": ("y_out", "xy_out", "other2"),
     "query31_y": ("kv_rest_y",),
     "kv_core": ("other3",),
     "query_core": ("own_kv",),
-    "mine1": ("core_w", "core_x", "core_y"),
+    "mine1": ("core_w", "core_x", "core_y", "core_xy"),
     "mine2": ("core_w", "core_x", "core_y", "core_xy"),
     "from_x": ("core_x", "core_y", "core_xy"),
     "from_x1": ("mine1", "queries"),
@@ -440,18 +441,12 @@
     own = jnp.concatenate([pair(z), columns(w_query, z, group)], axis=1)
     own_y = send("own_y", own, to_y)
     y_out = send("y_out", w_out, to_y)
-    far_half = [columns(w, 1 - z // 2, wide) for w in (key_matrix, value_matrix)]
-    far = send("far", jnp.concatenate(far_half, axis=1), to_z(2))
-
-    def far_pair(head):
-        parts = [columns(w, head, HEAD_SIZE) for w in (far[:, :wide], far[:, wide:])]
-        return jnp.concatenate(parts, axis=1)
-
+    far = send("far", jnp.stack([pair(z ^ 2), pair(z ^ 3)]), to_z(2))
     other1 = send("other1", tok1, to_x)
     tok3 = send("tok3", tok2, to_z(1))
     xy_out = send("xy_out", x_out, to_y)
     other2 = send("other2", tok2, to_x)
-    near = send("near", jnp.stack([pair(z ^ 1), far_pair(1 - z % 2)]), to_z(1))
+    near = send("near", jnp.stack([pair(z ^ 1), far[1]]), to_z(1))
     query2 = send("query2", columns(w_query, z ^ 2, group), to_z(2))
     query3 = send("query3", columns(w_query, z ^ 3, group), to_z(3))
     other3 = send("other3", tok3, to_x)
@@ -460,7 +455,7 @@
 
     both = jnp.stack([own, own_y])
     both_core = send("both_core", both, to_core)
-    kv_rest = jnp.stack([near[0], far_pair(z % 2), near[1]])
+    kv_rest = jnp.stack([near[0], far[0], near[1]])
     kv_rest_y = send("kv_rest_y", kv_rest, to_y)
     query2_y = send("query2_y", query2, to_y)
     query31_y = send("query31_y", jnp.stack([query3, query1]), to_y)

time: 182 us -> 179 us (0.984)
  waiting for transfers between devices: 109 us -> 105 us
  starting transfers between devices: 38.4 us -> 41.8 us
  local copies, waits for them, and re-layouts: 7.42 us -> 4.38 us
    ppermute x38, waiting for transfers between devices: 109 us -> 105 us  [__call__(): self.there[name] = lax.ppermute(array, AXES, moves(target))]
    ppermute x38, starting transfers between devices: 38.4 us -> 41.8 us  [__call__(): self.there[name] = lax.ppermute(array, AXES, moves(target))]
    dynamic_slice x5 -> x2, local copies, waits for them, and re-layouts: 5.32 us -> 2.24 us  [columns(): return lax.dynamic_slice_in_dim(weight, head * width, width, 1)]
  transfers between devices with their start and end apart: 38 -> 38, of which waited for: 23 -> 22; matrix products, arithmetic and copies ran while one was open for 6% -> 4% of each run, Pallas kernels for 6% -> 6%
where the time goes in v6:
time: 179 us
  waiting for transfers between devices  105 us (59%)
  starting transfers between devices  41.8 us (23%)
  Pallas kernels  21.8 us (12%)
  other arithmetic  5.33 us (3%)
  local copies, waits for them, and re-layouts  4.38 us (2%)
    ppermute x38, waiting for transfers between devices, __call__(): self.there[name] = lax.ppermute(array, AXES, moves(target))  105 us
    ppermute x38, starting transfers between devices, __call__(): self.there[name] = lax.ppermute(array, AXES, moves(target))  41.8 us
    pallas_call x2, Pallas kernels, project(): pl.pallas_call(functools.partial(kernel, plan), out_shape=jax.ShapeDtypeS...  8.91 us
    pallas_call x1, Pallas kernels, attend(): pl.pallas_call(attend_kernel, out_shape=(shape, shape), in_specs=[smem_sp...  7.07 us
    pallas_call x1, Pallas kernels, project_out(): pl.pallas_call(output_kernel, out_shape=(shape, shape), in_specs=[smem_sp...  5.86 us
  transfers between devices with their start and end apart: 38, of which 22 were waited for; matrix products, arithmetic and copies ran while one was open for 4% of the time, Pallas kernels for 6%

profile of v6, /device:TPU:0, one launch (start us, length us, event | category | flops | bytes accessed | tf_op | source)
XLA Modules:
  0.0 178.5 jit_solution(4119360576831973749)
XLA Ops:
  0.0 2.9 %collective-permute-start = (bf16[128,2048]{1,0:T(8,128)(2,1)}, bf16[128,2048]{1,0:T(8,128)(2,1)S(1)}, u32[]{:S(2)}, u32[]{:S(2)}) collective-permute-start(bf16[128,2048]{1,0:T(8,128)(2,1)} %refs_0_.3), channel_id=1, source_target_pairs={{0,1},{1,0},{2,3},{3,2},{4,5},{5,4},{6,7},{7,6},{8,9},{9,8},{10,11... | collective-permute-start | bytes 1572872 | tf_op jit(solution)/shard_map/ppermute | solution.py:402
  2.9 2.6 %collective-permute-start.3 = (bf16[128,2048]{1,0:T(8,128)(2,1)}, bf16[128,2048]{1,0:T(8,128)(2,1)S(1)}, u32[]{:S(2)}, u32[]{:S(2)}) collective-permute-start(bf16[128,2048]{1,0:T(8,128)(2,1)} %refs_0_.3), channel_id=1, source_target_pairs={{0,16},{1,17},{2,18},{3,19},{4,20},{5,21},{6,22},{7,23},{8,24},{9,... | collective-permute-start | bytes 1572872 | tf_op jit(solution)/shard_map/ppermute | solution.py:402
  5.5 1.6 collective-permute-start.1
  7.1 0.5 collective-permute-start.15
  7.6 2.1 %constant_dynamic-slice_fusion = (bf16[256,512]{1,0:T(8,128)(2,1)}, bf16[256,512]{1,0:T(8,128)(2,1)}, bf16[256,512]{1,0:T(8,128)(2,1)S(1)}, bf16[256,512]{1,0:T(8,128)(2,1)}) fusion(bf16[256,2048]{1,0:T(8,128)(2,1)} %param.6, s32[]{:T(128)S(6)} %select_n.58, s32[]{:T(128)S(6)} %select_n.53, s32[]{:T(128)S(6)} %select_n.52, s32[]{:T(128)S(6)} %select_n.57), kind=kLoop, calls=%fused_computation.24 | loop fusion | bytes 2097168 | tf_op jit(solution)/shard_map/dynamic_slice | solution.py:431
  9.8 0.1 constant_dynamic-slice_fusion.2
  10.0 1.6 collective-permute-start.5
  11.6 4.3 %collective-permute-done.refs_1_ = bf16[128,2048]{1,0:T(8,128)(2,1)S(1)} collective-permute-done((bf16[128,2048]{1,0:T(8,128)(2,1)}, bf16[128,2048]{1,0:T(8,128)(2,1)S(1)}, u32[]{:S(2)}, u32[]{:S(2)}) %collective-permute-start) | collective-permute-done | bytes 524320 | tf_op jit(solution)/shard_map/ppermute | solution.py:402
  15.9 2.1 %collective-permute-start.10 = (bf16[2048,256]{1,0:T(8,128)(2,1)S(1)}, bf16[2048,256]{1,0:T(8,128)(2,1)S(1)}, u32[]{:S(2)}, u32[]{:S(2)}) collective-permute-start(bf16[2048,256]{1,0:T(8,128)(2,1)S(1)} %copy-done.1), channel_id=1, source_target_pairs={{0,4},{1,5},{2,6},{3,7},{4,0},{5,1},{6,2},{7,3},{8,12},{9,13},{10,... | collective-permute-start | bytes 3145736 | tf_op jit(solution)/shard_map/ppermute | solution.py:402
  18.1 4.0 %collective-permute-done.5 = bf16[256,768]{1,0:T(8,128)(2,1)S(1)} collective-permute-done((bf16[256,768]{1,0:T(8,128)(2,1)S(1)}, bf16[256,768]{1,0:T(8,128)(2,1)S(1)}, u32[]{:S(2)}, u32[]{:S(2)}) %collective-permute-start.5) | collective-permute-done | bytes 393248 | tf_op jit(solution)/shard_map/ppermute | solution.py:402
  22.1 0.1 convert_bitcast_fusion
  22.2 12.5 %collective-permute-done.3.refs_4_ = bf16[128,2048]{1,0:T(8,128)(2,1)S(1)} collective-permute-done((bf16[128,2048]{1,0:T(8,128)(2,1)}, bf16[128,2048]{1,0:T(8,128)(2,1)S(1)}, u32[]{:S(2)}, u32[]{:S(2)}) %collective-permute-start.3) | collective-permute-done | bytes 524320 | tf_op jit(solution)/shard_map/ppermute | solution.py:402
  34.6 0.1 collective-permute-start.2
  34.7 3.8 %collective-permute-done.15.refs_10_ = bf16[2048,256]{1,0:T(8,128)(2,1)} collective-permute-done((bf16[2048,256]{1,0:T(8,128)(2,1)}, bf16[2048,256]{1,0:T(8,128)(2,1)}, u32[]{:S(2)}, u32[]{:S(2)}) %collective-permute-start.15) | collective-permute-done | bytes 1048608 | tf_op jit(solution)/shard_map/ppermute | solution.py:402
  38.5 2.1 %collective-permute-start.16 = (bf16[2048,256]{1,0:T(8,128)(2,1)}, bf16[2048,256]{1,0:T(8,128)(2,1)}, u32[]{:S(2)}, u32[]{:S(2)}) collective-permute-start(bf16[2048,256]{1,0:T(8,128)(2,1)} %collective-permute-done.15.refs_10_), channel_id=1, source_target_pairs={{0,4},{1,5},{2,6},{3,7},{4,0},{5,1},{6,2},{7,3},{8,12},{9,13},{10,... | collective-permute-start | bytes 3145736 | tf_op jit(solution)/shard_map/ppermute | solution.py:402
  40.6 0.7 pad_maximum_fusion.7
  41.3 3.2 %collective-permute-done.10.refs_12_ = bf16[2048,256]{1,0:T(8,128)(2,1)S(1)} collective-permute-done((bf16[2048,256]{1,0:T(8,128)(2,1)S(1)}, bf16[2048,256]{1,0:T(8,128)(2,1)S(1)}, u32[]{:S(2)}, u32[]{:S(2)}) %collective-permute-start.10) | collective-permute-done | bytes 1048608 | tf_op jit(solution)/shard_map/ppermute | solution.py:402
  44.6 1.0 copy-done.3
  45.6 1.8 %fusion = (f32[512,64]{1,0:T(8,128)S(1)}, f32[512,64]{1,0:T(8,128)}, f32[512,64]{1,0:T(8,128)}) fusion(f32[64]{0:T(128)S(1)} %multiply_power_fusion, f32[512]{0:T(512)S(1)} %convert_bitcast_fusion), kind=kLoop, calls=%fused_computation.21 | loop fusion | flops 65536 | bytes 395520 | tf_op jit(solution)/shard_map/neg | solution.py:470
  47.4 1.5 collective-permute-start.4
  48.9 0.1 pad_add_fusion.place
  49.0 1.3 pad_maximum_fusion.8
  50.3 1.4 collective-permute-start.13
  51.7 3.0 %collective-permute-start.14 = (bf16[256,512]{1,0:T(8,128)(2,1)}, bf16[256,512]{1,0:T(8,128)(2,1)S(1)}, u32[]{:S(2)}, u32[]{:S(2)}) collective-permute-start(bf16[256,512]{1,0:T(8,128)(2,1)} %get-tuple-element.35), channel_id=1, source_target_pairs={{0,24},{1,25},{2,26},{3,27},{4,28},{5,29},{6,30},{7,31},{8,16},{9,... | collective-permute-start | bytes 786440 | tf_op jit(solution)/shard_map/ppermute | solution.py:402
  54.8 1.0 fusion.2
  55.8 4.2 %collective-permute-done.4.refs_5_ = bf16[128,2048]{1,0:T(8,128)(2,1)S(1)} collective-permute-done((bf16[128,2048]{1,0:T(8,128)(2,1)S(1)}, bf16[128,2048]{1,0:T(8,128)(2,1)S(1)}, u32[]{:S(2)}, u32[]{:S(2)}) %collective-permute-start.4) | collective-permute-done | bytes 524320 | tf_op jit(solution)/shard_map/ppermute | solution.py:402
  60.0 4.8 %collective-permute-done.16.refs_14_ = bf16[2048,256]{1,0:T(8,128)(2,1)} collective-permute-done((bf16[2048,256]{1,0:T(8,128)(2,1)}, bf16[2048,256]{1,0:T(8,128)(2,1)}, u32[]{:S(2)}, u32[]{:S(2)}) %collective-permute-start.16) | collective-permute-done | bytes 1048608 | tf_op jit(solution)/shard_map/ppermute | solution.py:402
  64.8 1.5 collective-permute-start.17
  66.3 0.1 pad_maximum_fusion.refs_8_
  66.4 1.6 collective-permute-start.7
  68.0 2.3 %collective-permute-done.13 = bf16[256,512]{1,0:T(8,128)(2,1)S(1)} collective-permute-done((bf16[256,512]{1,0:T(8,128)(2,1)}, bf16[256,512]{1,0:T(8,128)(2,1)S(1)}, u32[]{:S(2)}, u32[]{:S(2)}) %collective-permute-start.13) | collective-permute-done | bytes 262176 | tf_op jit(solution)/shard_map/ppermute | solution.py:402
  70.3 1.5 collective-permute-start.19
  71.9 1.9 %collective-permute-done.17.refs_11_ = bf16[3,256,256]{2,1,0:T(8,128)(2,1)S(1)} collective-permute-done((bf16[3,256,256]{2,1,0:T(8,128)(2,1)S(1)}, bf16[3,256,256]{2,1,0:T(8,128)(2,1)S(1)}, u32[]{:S(2)}, u32[]{:S(2)}) %collective-permute-start.17) | collective-permute-done | bytes 393248 | tf_op jit(solution)/shard_map/ppermute | solution.py:402
  73.8 1.5 collective-permute-start.18
  75.4 0.1 pad_maximum_fusion.1
  75.4 2.4 %collective-permute-done.7.refs_7_ = bf16[128,2048]{1,0:T(8,128)(2,1)S(1)} collective-permute-done((bf16[128,2048]{1,0:T(8,128)(2,1)S(1)}, bf16[128,2048]{1,0:T(8,128)(2,1)S(1)}, u32[]{:S(2)}, u32[]{:S(2)}) %collective-permute-start.7) | collective-permute-done | bytes 524320 | tf_op jit(solution)/shard_map/ppermute | solution.py:402
  77.8 12.6 %collective-permute-done.18 = bf16[2,256,512]{2,1,0:T(8,128)(2,1)S(1)} collective-permute-done((bf16[2,256,512]{2,1,0:T(8,128)(2,1)S(1)}, bf16[2,256,512]{2,1,0:T(8,128)(2,1)S(1)}, u32[]{:S(2)}, u32[]{:S(2)}) %collective-permute-start.18) | collective-permute-done | bytes 524320 | tf_op jit(solution)/shard_map/ppermute | solution.py:402
  90.6 4.9 %shard_map.55.kv0 = bf16[4,128,256]{2,1,0:T(8,128)(2,1)S(1)} custom-call(s32[2]{0:T(128)S(1)} %pad_add_fusion.place, bf16[128,2048]{1,0:T(8,128)(2,1)S(1)} %copy-done, bf16[128,2048]{1,0:T(8,128)(2,1)S(1)} %collective-permute-done.refs_1_, bf16[128,2048]{1,0:T(8,128)(2,1)S(1)} %collective-permute-done.1.refs_2_, ...), custom_call_target="tpu_custom_call" | custom-call | flops 1073741824 | bytes 8388608 | tf_op jit(solution)/shard_map/pallas_call | solution.py:208
  95.6 0.1 collective-permute-start.21
  95.6 1.6 collective-permute-start.23
  97.2 0.2 collective-permute-start.22
  97.4 1.6 collective-permute-done.21.refs_11_
  99.0 4.0 %shard_map.56.queries = bf16[4,512,128]{2,1,0:T(8,128)(2,1)S(1)} custom-call(s32[2]{0:T(128)S(1)} %pad_add_fusion.place, bf16[128,2048]{1,0:T(8,128)(2,1)S(1)} %copy-done, bf16[128,2048]{1,0:T(8,128)(2,1)S(1)} %collective-permute-done.refs_1_, bf16[128,2048]{1,0:T(8,128)(2,1)S(1)} %collective-permute-done.1.refs_2_, ...), custom_call_target="tpu_custom_call" | custom-call | flops 1073741824 | bytes 8388608 | tf_op jit(solution)/shard_map/pallas_call | solution.py:208
  103.0 1.3 collective-permute-done.23.kv2
  104.4 0.5 collective-permute-start.25
  104.9 0.5 collective-permute-start.27
  105.5 0.4 collective-permute-done.24.kv3
  105.9 7.1 %shard_map.57 = (bf16[2,128,512]{2,1,0:T(8,128)(2,1)S(1)}, bf16[2,128,512]{2,1,0:T(8,128)(2,1)S(1)}) custom-call(s32[2]{0:T(128)S(1)} %pad_add_fusion.place, bf16[4,512,128]{2,1,0:T(8,128)(2,1)S(1)} %shard_map.56.queries, bf16[4,128,256]{2,1,0:T(8,128)(2,1)S(1)} %shard_map.55.kv0, bf16[4,128,256]{2,1,0:T(8,128)(2,1)S(1)} %collective-permute-done.22.kv1, ...), custom_call_target="tpu_custom_call" | custom-call | flops 32212254720 | bytes 4194304 | tf_op jit(solution)/shard_map/pallas_call | solution.py:283
  113.0 1.6 collective-permute-start.32
  114.6 1.0 collective-permute-start.29
  115.5 2.8 %collective-permute-start.30 = (bf16[2,128,512]{2,1,0:T(8,128)(2,1)S(1)}, bf16[2,128,512]{2,1,0:T(8,128)(2,1)S(1)}, u32[]{:S(2)}, u32[]{:S(2)}) collective-permute-start(bf16[2,128,512]{2,1,0:T(8,128)(2,1)S(1)} %get-tuple-element.42.refs_0_), channel_id=1, source_target_pairs={{0,16},{1,17},{2,18},{3,19},{4,20},{5,21},{6,22},{7,23},{8,24},{9,... | collective-permute-start | bytes 786440 | tf_op jit(solution)/shard_map/ppermute | solution.py:402
  118.3 3.1 %collective-permute-done.32.refs_4_ = bf16[2,128,512]{2,1,0:T(8,128)(2,1)S(1)} collective-permute-done((bf16[2,128,512]{2,1,0:T(8,128)(2,1)S(1)}, bf16[2,128,512]{2,1,0:T(8,128)(2,1)S(1)}, u32[]{:S(2)}, u32[]{:S(2)}) %collective-permute-start.32) | collective-permute-done | bytes 262176 | tf_op jit(solution)/shard_map/ppermute | solution.py:402
  121.4 2.1 %collective-permute-start.34 = (bf16[2,128,512]{2,1,0:T(8,128)(2,1)S(1)}, bf16[2,128,512]{2,1,0:T(8,128)(2,1)S(1)}, u32[]{:S(2)}, u32[]{:S(2)}) collective-permute-start(bf16[2,128,512]{2,1,0:T(8,128)(2,1)S(1)} %collective-permute-done.32.refs_4_), channel_id=1, source_target_pairs={{0,16},{1,17},{2,18},{3,19},{4,20},{5,21},{6,22},{7,23},{8,24},{9,... | collective-permute-start | bytes 786440 | tf_op jit(solution)/shard_map/ppermute | solution.py:402
  123.5 4.5 %collective-permute-done.29.refs_1_ = bf16[2,128,512]{2,1,0:T(8,128)(2,1)S(1)} collective-permute-done((bf16[2,128,512]{2,1,0:T(8,128)(2,1)S(1)}, bf16[2,128,512]{2,1,0:T(8,128)(2,1)S(1)}, u32[]{:S(2)}, u32[]{:S(2)}) %collective-permute-start.29) | collective-permute-done | bytes 262176 | tf_op jit(solution)/shard_map/ppermute | solution.py:402
  128.0 8.3 %collective-permute-done.30.refs_2_ = bf16[2,128,512]{2,1,0:T(8,128)(2,1)S(1)} collective-permute-done((bf16[2,128,512]{2,1,0:T(8,128)(2,1)S(1)}, bf16[2,128,512]{2,1,0:T(8,128)(2,1)S(1)}, u32[]{:S(2)}, u32[]{:S(2)}) %collective-permute-start.30) | collective-permute-done | bytes 262176 | tf_op jit(solution)/shard_map/ppermute | solution.py:402
  136.3 5.0 %collective-permute-done.34.refs_6_ = bf16[2,128,512]{2,1,0:T(8,128)(2,1)S(1)} collective-permute-done((bf16[2,128,512]{2,1,0:T(8,128)(2,1)S(1)}, bf16[2,128,512]{2,1,0:T(8,128)(2,1)S(1)}, u32[]{:S(2)}, u32[]{:S(2)}) %collective-permute-start.34) | collective-permute-done | bytes 262176 | tf_op jit(solution)/shard_map/ppermute | solution.py:402
  141.4 1.7 collective-permute-done.33.refs_5_
  143.1 5.6 %collective-permute-done.31.refs_3_ = bf16[2,128,512]{2,1,0:T(8,128)(2,1)S(1)} collective-permute-done((bf16[2,128,512]{2,1,0:T(8,128)(2,1)S(1)}, bf16[2,128,512]{2,1,0:T(8,128)(2,1)S(1)}, u32[]{:S(2)}, u32[]{:S(2)}) %collective-permute-start.31) | collective-permute-done | bytes 262176 | tf_op jit(solution)/shard_map/ppermute | solution.py:402
  148.7 3.6 %collective-permute-done.35.refs_7_ = bf16[2,128,512]{2,1,0:T(8,128)(2,1)S(1)} collective-permute-done((bf16[2,128,512]{2,1,0:T(8,128)(2,1)S(1)}, bf16[2,128,512]{2,1,0:T(8,128)(2,1)S(1)}, u32[]{:S(2)}, u32[]{:S(2)}) %collective-permute-start.35) | collective-permute-done | bytes 262176 | tf_op jit(solution)/shard_map/ppermute | solution.py:402
  152.3 5.9 %shard_map.58 = (bf16[128,1024]{1,0:T(8,128)(2,1)S(1)}, bf16[128,1024]{1,0:T(8,128)(2,1)S(1)}) custom-call(s32[2]{0:T(128)S(1)} %pad_add_fusion.place, bf16[2,128,512]{2,1,0:T(8,128)(2,1)S(1)} %get-tuple-element.42.refs_0_, bf16[2,128,512]{2,1,0:T(8,128)(2,1)S(1)} %collective-permute-done.29.refs_1_, ...), custom_call_target="tpu_custom_call" | custom-call | flops 2147483648 | bytes 12582912 | tf_op jit(solution)/shard_map/pallas_call | solution.py:354
  158.2 5.2 %collective-permute-start.36 = (bf16[128,1024]{1,0:T(8,128)(2,1)S(1)}, bf16[128,1024]{1,0:T(8,128)(2,1)S(1)}, u32[]{:S(2)}, u32[]{:S(2)}) collective-permute-start(bf16[128,1024]{1,0:T(8,128)(2,1)S(1)} %get-tuple-element.47), channel_id=1, source_target_pairs={{0,24},{1,16},{2,26},{3,18},{4,28},{5,20},{6,30},{7,22},{8,0},{9,8... | collective-permute-start | bytes 786440 | tf_op jit(solution)/shard_map/ppermute | solution.py:402
  163.4 0.7 collective-permute-start.37
  164.1 13.5 %collective-permute-done.36 = bf16[128,1024]{1,0:T(8,128)(2,1)S(1)} collective-permute-done((bf16[128,1024]{1,0:T(8,128)(2,1)S(1)}, bf16[128,1024]{1,0:T(8,128)(2,1)S(1)}, u32[]{:S(2)}, u32[]{:S(2)}) %collective-permute-start.36) | collective-permute-done | bytes 262176 | tf_op jit(solution)/shard_map/ppermute | solution.py:402
  177.7 0.8 pad_maximum_fusion.3
  (62 shorter events, 0.6 us)
Async XLA Ops:
  0.0 9.8 %copy-start.8 = (bf16[256,512]{1,0:T(8,128)(2,1)S(1)}, bf16[256,512]{1,0:T(8,128)(2,1)}, u32[]{:S(2)}) copy-start(bf16[256,512]{1,0:T(8,128)(2,1)} %param.7) | copy-start | bytes 786436
  0.0 9.8 %copy-start.7 = (bf16[256,512]{1,0:T(8,128)(2,1)S(1)}, bf16[256,512]{1,0:T(8,128)(2,1)}, u32[]{:S(2)}) copy-start(bf16[256,512]{1,0:T(8,128)(2,1)} %param.8) | copy-start | bytes 786436
  0.0 15.9 %collective-permute-start = (bf16[128,2048]{1,0:T(8,128)(2,1)}, bf16[128,2048]{1,0:T(8,128)(2,1)S(1)}, u32[]{:S(2)}, u32[]{:S(2)}) collective-permute-start(bf16[128,2048]{1,0:T(8,128)(2,1)} %refs_0_.3), channel_id=1, source_target_pairs={{0,1},{1,0},{2,3},{3,2},{4,5},{5,4},{6,7},{7,6},{8,9},{9,8},{10,11... | collective-permute-start | bytes 1572872 | tf_op jit(solution)/shard_map/ppermute | solution.py:402
  2.9 31.7 %collective-permute-start.3 = (bf16[128,2048]{1,0:T(8,128)(2,1)}, bf16[128,2048]{1,0:T(8,128)(2,1)S(1)}, u32[]{:S(2)}, u32[]{:S(2)}) collective-permute-start(bf16[128,2048]{1,0:T(8,128)(2,1)} %refs_0_.3), channel_id=1, source_target_pairs={{0,16},{1,17},{2,18},{3,19},{4,20},{5,21},{6,22},{7,23},{8,24},{9,... | collective-permute-start | bytes 1572872 | tf_op jit(solution)/shard_map/ppermute | solution.py:402
  5.5 29.1 %collective-permute-start.1 = (bf16[128,2048]{1,0:T(8,128)(2,1)}, bf16[128,2048]{1,0:T(8,128)(2,1)S(1)}, u32[]{:S(2)}, u32[]{:S(2)}) collective-permute-start(bf16[128,2048]{1,0:T(8,128)(2,1)} %refs_0_.3), channel_id=1, source_target_pairs={{0,8},{1,9},{2,10},{3,11},{4,12},{5,13},{6,14},{7,15},{8,0},{9,1},... | collective-permute-start | bytes 1572872 | tf_op jit(solution)/shard_map/ppermute | solution.py:402
  7.1 31.4 %collective-permute-start.15 = (bf16[2048,256]{1,0:T(8,128)(2,1)}, bf16[2048,256]{1,0:T(8,128)(2,1)}, u32[]{:S(2)}, u32[]{:S(2)}) collective-permute-start(bf16[2048,256]{1,0:T(8,128)(2,1)} %refs_8_.1), channel_id=1, source_target_pairs={{0,1},{1,0},{2,3},{3,2},{4,5},{5,4},{6,7},{7,6},{8,9},{9,8},{10,11... | collective-permute-start | bytes 3145736 | tf_op jit(solution)/shard_map/ppermute | solution.py:402
  9.8 6.1 %copy-start.1 = (bf16[2048,256]{1,0:T(8,128)(2,1)S(1)}, bf16[2048,256]{1,0:T(8,128)(2,1)}, u32[]{:S(2)}) copy-start(bf16[2048,256]{1,0:T(8,128)(2,1)} %refs_8_.1) | copy-start | bytes 3145732
  10.0 12.1 %collective-permute-start.5 = (bf16[256,768]{1,0:T(8,128)(2,1)S(1)}, bf16[256,768]{1,0:T(8,128)(2,1)S(1)}, u32[]{:S(2)}, u32[]{:S(2)}) collective-permute-start(bf16[256,768]{1,0:T(8,128)(2,1)S(1)} %get-tuple-element.56), channel_id=1, source_target_pairs={{0,4},{1,5},{2,6},{3,7},{4,0},{5,1},{6,2},{7,3},{8,12},{9,13},{10,... | collective-permute-start | bytes 1179656 | tf_op jit(solution)/shard_map/ppermute | solution.py:402
  15.9 28.7 %collective-permute-start.10 = (bf16[2048,256]{1,0:T(8,128)(2,1)S(1)}, bf16[2048,256]{1,0:T(8,128)(2,1)S(1)}, u32[]{:S(2)}, u32[]{:S(2)}) collective-permute-start(bf16[2048,256]{1,0:T(8,128)(2,1)S(1)} %copy-done.1), channel_id=1, source_target_pairs={{0,4},{1,5},{2,6},{3,7},{4,0},{5,1},{6,2},{7,3},{8,12},{9,13},{10,... | collective-permute-start | bytes 3145736 | tf_op jit(solution)/shard_map/ppermute | solution.py:402
  22.1 12.5 %copy-start.5 = (bf16[256,768]{1,0:T(8,128)(2,1)}, bf16[256,768]{1,0:T(8,128)(2,1)S(1)}, u32[]{:S(2)}) copy-start(bf16[256,768]{1,0:T(8,128)(2,1)S(1)} %collective-permute-done.5) | copy-start | bytes 1179652
  22.1 18.5 %collective-permute-start.9 = (bf16[2,256,256]{2,1,0:T(8,128)(2,1)S(1)}, bf16[2,256,256]{2,1,0:T(8,128)(2,1)S(1)}, u32[]{:S(2)}, u32[]{:S(2)}) collective-permute-start(bf16[2,256,256]{2,1,0:T(8,128)(2,1)S(1)} %pad_maximum_fusion.6), channel_id=1, source_target_pairs={{0,16},{1,17},{2,18},{3,19},{4,20},{5,21},{6,22},{7,23},{8,24},{9,... | collective-permute-start | bytes 786440 | tf_op jit(solution)/shard_map/ppermute | solution.py:402
  34.6 15.7 %collective-permute-start.6 = (bf16[128,2048]{1,0:T(8,128)(2,1)S(1)}, bf16[128,2048]{1,0:T(8,128)(2,1)S(1)}, u32[]{:S(2)}, u32[]{:S(2)}) collective-permute-start(bf16[128,2048]{1,0:T(8,128)(2,1)S(1)} %collective-permute-done.3.refs_4_), channel_id=1, source_target_pairs={{0,8},{1,9},{2,10},{3,11},{4,12},{5,13},{6,14},{7,15},{8,0},{9,1},... | collective-permute-start | bytes 1572872 | tf_op jit(solution)/shard_map/ppermute | solution.py:402
  34.6 17.1 %collective-permute-start.2 = (bf16[128,2048]{1,0:T(8,128)(2,1)S(1)}, bf16[128,2048]{1,0:T(8,128)(2,1)S(1)}, u32[]{:S(2)}, u32[]{:S(2)}) collective-permute-start(bf16[128,2048]{1,0:T(8,128)(2,1)S(1)} %collective-permute-done.1.refs_2_), channel_id=1, source_target_pairs={{0,1},{1,0},{2,3},{3,2},{4,5},{5,4},{6,7},{7,6},{8,9},{9,8},{10,11... | collective-permute-start | bytes 1572872 | tf_op jit(solution)/shard_map/ppermute | solution.py:402
  38.5 26.3 %collective-permute-start.16 = (bf16[2048,256]{1,0:T(8,128)(2,1)}, bf16[2048,256]{1,0:T(8,128)(2,1)}, u32[]{:S(2)}, u32[]{:S(2)}) collective-permute-start(bf16[2048,256]{1,0:T(8,128)(2,1)} %collective-permute-done.15.refs_10_), channel_id=1, source_target_pairs={{0,4},{1,5},{2,6},{3,7},{4,0},{5,1},{6,2},{7,3},{8,12},{9,13},{10,... | collective-permute-start | bytes 3145736 | tf_op jit(solution)/shard_map/ppermute | solution.py:402
  44.6 1.0 copy-start.3
  45.6 9.2 %collective-permute-start.11 = (bf16[2,256,256]{2,1,0:T(8,128)(2,1)}, bf16[2,256,256]{2,1,0:T(8,128)(2,1)}, u32[]{:S(2)}, u32[]{:S(2)}) collective-permute-start(bf16[2,256,256]{2,1,0:T(8,128)(2,1)} %pad_maximum_fusion.7), channel_id=1, source_target_pairs={{0,8},{1,9},{2,10},{3,11},{4,12},{5,13},{6,14},{7,15},{8,0},{9,1},... | collective-permute-start | bytes 786440 | tf_op jit(solution)/shard_map/ppermute | solution.py:402
  47.4 18.9 %copy-start.6 = (bf16[256,768]{1,0:T(8,128)(2,1)S(1)}, bf16[256,768]{1,0:T(8,128)(2,1)}, u32[]{:S(2)}) copy-start(bf16[256,768]{1,0:T(8,128)(2,1)} %copy-done.5) | copy-start | bytes 1179652
  47.4 12.6 %collective-permute-start.4 = (bf16[128,2048]{1,0:T(8,128)(2,1)S(1)}, bf16[128,2048]{1,0:T(8,128)(2,1)S(1)}, u32[]{:S(2)}, u32[]{:S(2)}) collective-permute-start(bf16[128,2048]{1,0:T(8,128)(2,1)S(1)} %collective-permute-done.3.refs_4_), channel_id=1, source_target_pairs={{0,1},{1,0},{2,3},{3,2},{4,5},{5,4},{6,7},{7,6},{8,9},{9,8},{10,11... | collective-permute-start | bytes 1572872 | tf_op jit(solution)/shard_map/ppermute | solution.py:402
  50.3 20.0 %collective-permute-start.13 = (bf16[256,512]{1,0:T(8,128)(2,1)}, bf16[256,512]{1,0:T(8,128)(2,1)S(1)}, u32[]{:S(2)}, u32[]{:S(2)}) collective-permute-start(bf16[256,512]{1,0:T(8,128)(2,1)} %get-tuple-element.34), channel_id=1, source_target_pairs={{0,16},{1,17},{2,18},{3,19},{4,20},{5,21},{6,22},{7,23},{8,24},{9,... | collective-permute-start | bytes 786440 | tf_op jit(solution)/shard_map/ppermute | solution.py:402
  51.7 20.1 %collective-permute-start.14 = (bf16[256,512]{1,0:T(8,128)(2,1)}, bf16[256,512]{1,0:T(8,128)(2,1)S(1)}, u32[]{:S(2)}, u32[]{:S(2)}) collective-permute-start(bf16[256,512]{1,0:T(8,128)(2,1)} %get-tuple-element.35), channel_id=1, source_target_pairs={{0,24},{1,25},{2,26},{3,27},{4,28},{5,29},{6,30},{7,31},{8,16},{9,... | collective-permute-start | bytes 786440 | tf_op jit(solution)/shard_map/ppermute | solution.py:402
  54.8 15.5 %collective-permute-start.12 = (bf16[256,512]{1,0:T(8,128)(2,1)}, bf16[256,512]{1,0:T(8,128)(2,1)S(1)}, u32[]{:S(2)}, u32[]{:S(2)}) collective-permute-start(bf16[256,512]{1,0:T(8,128)(2,1)} %get-tuple-element.33), channel_id=1, source_target_pairs={{0,8},{1,9},{2,10},{3,11},{4,12},{5,13},{6,14},{7,15},{8,0},{9,1},... | collective-permute-start | bytes 786440 | tf_op jit(solution)/shard_map/ppermute | solution.py:402
  64.8 9.0 %collective-permute-start.17 = (bf16[3,256,256]{2,1,0:T(8,128)(2,1)S(1)}, bf16[3,256,256]{2,1,0:T(8,128)(2,1)S(1)}, u32[]{:S(2)}, u32[]{:S(2)}) collective-permute-start(bf16[3,256,256]{2,1,0:T(8,128)(2,1)S(1)} %pad_maximum_fusion.5.refs_10_), channel_id=1, source_target_pairs={{0,4},{1,5},{2,6},{3,7},{4,0},{5,1},{6,2},{7,3},{8,12},{9,13},{10,... | collective-permute-start | bytes 1179656 | tf_op jit(solution)/shard_map/ppermute | solution.py:402
  66.4 11.4 %collective-permute-start.7 = (bf16[128,2048]{1,0:T(8,128)(2,1)S(1)}, bf16[128,2048]{1,0:T(8,128)(2,1)S(1)}, u32[]{:S(2)}, u32[]{:S(2)}) collective-permute-start(bf16[128,2048]{1,0:T(8,128)(2,1)S(1)} %collective-permute-done.6.refs_6_), channel_id=1, source_target_pairs={{0,1},{1,0},{2,3},{3,2},{4,5},{5,4},{6,7},{7,6},{8,9},{9,8},{10,11... | collective-permute-start | bytes 1572872 | tf_op jit(solution)/shard_map/ppermute | solution.py:402
  70.3 20.3 %collective-permute-start.8 = (bf16[2,256,768]{2,1,0:T(8,128)(2,1)S(1)}, bf16[2,256,768]{2,1,0:T(8,128)(2,1)S(1)}, u32[]{:S(2)}, u32[]{:S(2)}) collective-permute-start(bf16[2,256,768]{2,1,0:T(8,128)(2,1)S(1)} %pad_maximum_fusion.refs_8_), channel_id=1, source_target_pairs={{0,2},{1,3},{2,0},{3,1},{4,6},{5,7},{6,4},{7,5},{8,10},{9,11},{10,... | collective-permute-start | bytes 2359304 | tf_op jit(solution)/shard_map/ppermute | solution.py:402
  70.3 20.2 %collective-permute-start.19 = (bf16[256,512]{1,0:T(8,128)(2,1)S(1)}, bf16[256,512]{1,0:T(8,128)(2,1)S(1)}, u32[]{:S(2)}, u32[]{:S(2)}) collective-permute-start(bf16[256,512]{1,0:T(8,128)(2,1)S(1)} %collective-permute-done.13), channel_id=1, source_target_pairs={{0,4},{1,5},{2,6},{3,7},{4,0},{5,1},{6,2},{7,3},{8,12},{9,13},{10,... | collective-permute-start | bytes 786440 | tf_op jit(solution)/shard_map/ppermute | solution.py:402
  73.8 16.7 %collective-permute-start.18 = (bf16[2,256,512]{2,1,0:T(8,128)(2,1)S(1)}, bf16[2,256,512]{2,1,0:T(8,128)(2,1)S(1)}, u32[]{:S(2)}, u32[]{:S(2)}) collective-permute-start(bf16[2,256,512]{2,1,0:T(8,128)(2,1)S(1)} %pad_maximum_fusion.2), channel_id=1, source_target_pairs={{0,4},{1,5},{2,6},{3,7},{4,0},{5,1},{6,2},{7,3},{8,12},{9,13},{10,... | collective-permute-start | bytes 1572872 | tf_op jit(solution)/shard_map/ppermute | solution.py:402
  75.3 15.2 %copy-start = (bf16[128,2048]{1,0:T(8,128)(2,1)S(1)}, bf16[128,2048]{1,0:T(8,128)(2,1)}, u32[]{:S(2)}) copy-start(bf16[128,2048]{1,0:T(8,128)(2,1)} %refs_0_.3) | copy-start | bytes 1572868
  77.8 12.8 %collective-permute-start.20 = (bf16[6,256,256]{2,1,0:T(8,128)(2,1)S(1)}, bf16[6,256,256]{2,1,0:T(8,128)(2,1)S(1)}, u32[]{:S(2)}, u32[]{:S(2)}) collective-permute-start(bf16[6,256,256]{2,1,0:T(8,128)(2,1)S(1)} %pad_maximum_fusion.1), channel_id=1, source_target_pairs={{0,2},{1,3},{2,0},{3,1},{4,6},{5,7},{6,4},{7,5},{8,10},{9,11},{10,... | collective-permute-start | bytes 2359304 | tf_op jit(solution)/shard_map/ppermute | solution.py:402
  95.5 8.8 %copy-start.2 = (bf16[2048,256]{1,0:T(8,128)(2,1)S(1)}, bf16[2048,256]{1,0:T(8,128)(2,1)}, u32[]{:S(2)}) copy-start(bf16[2048,256]{1,0:T(8,128)(2,1)} %refs_8_.1) | copy-start | bytes 3145732
  95.5 9.3 %copy-start.4 = (bf16[2048,256]{1,0:T(8,128)(2,1)S(1)}, bf16[2048,256]{1,0:T(8,128)(2,1)}, u32[]{:S(2)}) copy-start(bf16[2048,256]{1,0:T(8,128)(2,1)} %copy-done.3) | copy-start | bytes 3145732
  95.6 3.5 %collective-permute-start.21 = (bf16[6,256,512]{2,1,0:T(8,128)(2,1)S(1)}, bf16[6,256,512]{2,1,0:T(8,128)(2,1)S(1)}, u32[]{:S(2)}, u32[]{:S(2)}) collective-permute-start(bf16[6,256,512]{2,1,0:T(8,128)(2,1)S(1)} %slice_dynamic-update-slice_fusion.refs_10_), channel_id=1, source_target_pairs={{0,2},{1,3},{2,0},{3,1},{4,6},{5,7},{6,4},{7,5},{8,10},{9,11},{10,... | collective-permute-start | bytes 4718600 | tf_op jit(solution)/shard_map/ppermute | solution.py:402
  95.6 8.7 %collective-permute-start.23 = (bf16[4,128,256]{2,1,0:T(8,128)(2,1)S(1)}, bf16[4,128,256]{2,1,0:T(8,128)(2,1)S(1)}, u32[]{:S(2)}, u32[]{:S(2)}) collective-permute-start(bf16[4,128,256]{2,1,0:T(8,128)(2,1)S(1)} %shard_map.55.kv0), channel_id=1, source_target_pairs={{0,4},{1,5},{2,6},{3,7},{4,0},{5,1},{6,2},{7,3},{8,12},{9,13},{10,... | collective-permute-start | bytes 786440 | tf_op jit(solution)/shard_map/ppermute | solution.py:402
  97.2 8.2 %collective-permute-start.22 = (bf16[4,128,256]{2,1,0:T(8,128)(2,1)S(1)}, bf16[4,128,256]{2,1,0:T(8,128)(2,1)S(1)}, u32[]{:S(2)}, u32[]{:S(2)}) collective-permute-start(bf16[4,128,256]{2,1,0:T(8,128)(2,1)S(1)} %shard_map.55.kv0), channel_id=1, source_target_pairs={{0,2},{1,3},{2,0},{3,1},{4,6},{5,7},{6,4},{7,5},{8,10},{9,11},{10,... | collective-permute-start | bytes 786440 | tf_op jit(solution)/shard_map/ppermute | solution.py:402
  104.4 1.5 collective-permute-start.24
  104.4 10.2 %collective-permute-start.25 = (bf16[2048,256]{1,0:T(8,128)(2,1)S(1)}, bf16[2048,256]{1,0:T(8,128)(2,1)S(1)}, u32[]{:S(2)}, u32[]{:S(2)}) collective-permute-start(bf16[2048,256]{1,0:T(8,128)(2,1)S(1)} %copy-done.2), channel_id=1, source_target_pairs={{0,2},{1,3},{2,0},{3,1},{4,6},{5,7},{6,4},{7,5},{8,10},{9,11},{10,... | collective-permute-start | bytes 3145736 | tf_op jit(solution)/shard_map/ppermute | solution.py:402
  104.9 8.1 %collective-permute-start.26 = (bf16[2048,256]{1,0:T(8,128)(2,1)}, bf16[2048,256]{1,0:T(8,128)(2,1)S(1)}, u32[]{:S(2)}, u32[]{:S(2)}) collective-permute-start(bf16[2048,256]{1,0:T(8,128)(2,1)} %collective-permute-done.15.refs_10_), channel_id=1, source_target_pairs={{0,2},{1,3},{2,0},{3,1},{4,6},{5,7},{6,4},{7,5},{8,10},{9,11},{10,... | collective-permute-start | bytes 3145736 | tf_op jit(solution)/shard_map/ppermute | solution.py:402
  104.9 8.1 %collective-permute-start.27 = (bf16[2048,256]{1,0:T(8,128)(2,1)S(1)}, bf16[2048,256]{1,0:T(8,128)(2,1)S(1)}, u32[]{:S(2)}, u32[]{:S(2)}) collective-permute-start(bf16[2048,256]{1,0:T(8,128)(2,1)S(1)} %copy-done.4), channel_id=1, source_target_pairs={{0,2},{1,3},{2,0},{3,1},{4,6},{5,7},{6,4},{7,5},{8,10},{9,11},{10,... | collective-permute-start | bytes 3145736 | tf_op jit(solution)/shard_map/ppermute | solution.py:402
  105.4 7.6 %collective-permute-start.28 = (bf16[2048,256]{1,0:T(8,128)(2,1)}, bf16[2048,256]{1,0:T(8,128)(2,1)S(1)}, u32[]{:S(2)}, u32[]{:S(2)}) collective-permute-start(bf16[2048,256]{1,0:T(8,128)(2,1)} %collective-permute-done.16.refs_14_), channel_id=1, source_target_pairs={{0,2},{1,3},{2,0},{3,1},{4,6},{5,7},{6,4},{7,5},{8,10},{9,11},{10,... | collective-permute-start | bytes 3145736 | tf_op jit(solution)/shard_map/ppermute | solution.py:402
  113.0 8.4 %collective-permute-start.32 = (bf16[2,128,512]{2,1,0:T(8,128)(2,1)S(1)}, bf16[2,128,512]{2,1,0:T(8,128)(2,1)S(1)}, u32[]{:S(2)}, u32[]{:S(2)}) collective-permute-start(bf16[2,128,512]{2,1,0:T(8,128)(2,1)S(1)} %get-tuple-element.44), channel_id=1, source_target_pairs={{0,1},{1,0},{2,3},{3,2},{4,5},{5,4},{6,7},{7,6},{8,9},{9,8},{10,11... | collective-permute-start | bytes 786440 | tf_op jit(solution)/shard_map/ppermute | solution.py:402
  114.6 13.5 %collective-permute-start.29 = (bf16[2,128,512]{2,1,0:T(8,128)(2,1)S(1)}, bf16[2,128,512]{2,1,0:T(8,128)(2,1)S(1)}, u32[]{:S(2)}, u32[]{:S(2)}) collective-permute-start(bf16[2,128,512]{2,1,0:T(8,128)(2,1)S(1)} %get-tuple-element.42.refs_0_), channel_id=1, source_target_pairs={{0,8},{1,9},{2,10},{3,11},{4,12},{5,13},{6,14},{7,15},{8,0},{9,1},... | collective-permute-start | bytes 786440 | tf_op jit(solution)/shard_map/ppermute | solution.py:402
  115.5 20.8 %collective-permute-start.30 = (bf16[2,128,512]{2,1,0:T(8,128)(2,1)S(1)}, bf16[2,128,512]{2,1,0:T(8,128)(2,1)S(1)}, u32[]{:S(2)}, u32[]{:S(2)}) collective-permute-start(bf16[2,128,512]{2,1,0:T(8,128)(2,1)S(1)} %get-tuple-element.42.refs_0_), channel_id=1, source_target_pairs={{0,16},{1,17},{2,18},{3,19},{4,20},{5,21},{6,22},{7,23},{8,24},{9,... | collective-permute-start | bytes 786440 | tf_op jit(solution)/shard_map/ppermute | solution.py:402
  121.4 20.0 %collective-permute-start.34 = (bf16[2,128,512]{2,1,0:T(8,128)(2,1)S(1)}, bf16[2,128,512]{2,1,0:T(8,128)(2,1)S(1)}, u32[]{:S(2)}, u32[]{:S(2)}) collective-permute-start(bf16[2,128,512]{2,1,0:T(8,128)(2,1)S(1)} %collective-permute-done.32.refs_4_), channel_id=1, source_target_pairs={{0,16},{1,17},{2,18},{3,19},{4,20},{5,21},{6,22},{7,23},{8,24},{9,... | collective-permute-start | bytes 786440 | tf_op jit(solution)/shard_map/ppermute | solution.py:402
  128.0 15.1 %collective-permute-start.33 = (bf16[2,128,512]{2,1,0:T(8,128)(2,1)S(1)}, bf16[2,128,512]{2,1,0:T(8,128)(2,1)S(1)}, u32[]{:S(2)}, u32[]{:S(2)}) collective-permute-start(bf16[2,128,512]{2,1,0:T(8,128)(2,1)S(1)} %collective-permute-done.32.refs_4_), channel_id=1, source_target_pairs={{0,8},{1,9},{2,10},{3,11},{4,12},{5,13},{6,14},{7,15},{8,0},{9,1},... | collective-permute-start | bytes 786440 | tf_op jit(solution)/shard_map/ppermute | solution.py:402
  136.3 12.4 %collective-permute-start.31 = (bf16[2,128,512]{2,1,0:T(8,128)(2,1)S(1)}, bf16[2,128,512]{2,1,0:T(8,128)(2,1)S(1)}, u32[]{:S(2)}, u32[]{:S(2)}) collective-permute-start(bf16[2,128,512]{2,1,0:T(8,128)(2,1)S(1)} %collective-permute-done.30.refs_2_), channel_id=1, source_target_pairs={{0,8},{1,9},{2,10},{3,11},{4,12},{5,13},{6,14},{7,15},{8,0},{9,1},... | collective-permute-start | bytes 786440 | tf_op jit(solution)/shard_map/ppermute | solution.py:402
  141.4 10.9 %collective-permute-start.35 = (bf16[2,128,512]{2,1,0:T(8,128)(2,1)S(1)}, bf16[2,128,512]{2,1,0:T(8,128)(2,1)S(1)}, u32[]{:S(2)}, u32[]{:S(2)}) collective-permute-start(bf16[2,128,512]{2,1,0:T(8,128)(2,1)S(1)} %collective-permute-done.34.refs_6_), channel_id=1, source_target_pairs={{0,8},{1,9},{2,10},{3,11},{4,12},{5,13},{6,14},{7,15},{8,0},{9,1},... | collective-permute-start | bytes 786440 | tf_op jit(solution)/shard_map/ppermute | solution.py:402
  158.2 19.5 %collective-permute-start.36 = (bf16[128,1024]{1,0:T(8,128)(2,1)S(1)}, bf16[128,1024]{1,0:T(8,128)(2,1)S(1)}, u32[]{:S(2)}, u32[]{:S(2)}) collective-permute-start(bf16[128,1024]{1,0:T(8,128)(2,1)S(1)} %get-tuple-element.47), channel_id=1, source_target_pairs={{0,24},{1,16},{2,26},{3,18},{4,28},{5,20},{6,30},{7,22},{8,0},{9,8... | collective-permute-start | bytes 786440 | tf_op jit(solution)/shard_map/ppermute | solution.py:402
  163.4 14.2 %collective-permute-start.37 = (bf16[128,1024]{1,0:T(8,128)(2,1)S(1)}, bf16[128,1024]{1,0:T(8,128)(2,1)S(1)}, u32[]{:S(2)}, u32[]{:S(2)}) collective-permute-start(bf16[128,1024]{1,0:T(8,128)(2,1)S(1)} %get-tuple-element.48), channel_id=1, source_target_pairs={{0,0},{1,8},{2,2},{3,10},{4,4},{5,12},{6,6},{7,14},{8,24},{9,16},{... | collective-permute-start | bytes 786440 | tf_op jit(solution)/shard_map/ppermute | solution.py:402

commit v7 on v6

--- a/solution.py
+++ b/solution.py
@@ -323,28 +323,26 @@
     for handle in handles:
         handle.wait()
     low = z % 2
-    for part in range(4):
-        at = slice(part * cols, (part + 1) * cols)
-        terms = []
-        for f in range(2):
-            term = jnp.dot(
-                attn[:, :, f * depth : (f + 1) * depth].reshape(2 * rows, depth),
-                wgt[f * depth : (f + 1) * depth, at],
-                preferred_element_type=jnp.float32,
-            )
-            terms.append(term.astype(jnp.bfloat16).astype(jnp.float32))
-        mixed = (terms[0] + terms[1]).astype(jnp.bfloat16)
-        first, second = mixed[:rows], mixed[rows:]
-
-        @pl.when(low == 0)
-        def _():
-            out0[:, at] = first
-            out1[:, at] = second
-
-        @pl.when(low == 1)
-        def _():
-            out0[:, at] = second
-            out1[:, at] = first
+    terms = []
+    for f in range(2):
+        term = jnp.dot(
+            attn[:, :, f * depth : (f + 1) * depth].reshape(2 * rows, depth),
+            wgt[f * depth : (f + 1) * depth, :],
+            preferred_element_type=jnp.float32,
+        )
+        terms.append(term.astype(jnp.bfloat16).astype(jnp.float32))
+    mixed = (terms[0] + terms[1]).astype(jnp.bfloat16)
+    first, second = mixed[:rows], mixed[rows:]
+
+    @pl.when(low == 0)
+    def _():
+        out0[...] = first
+        out1[...] = second
+
+    @pl.when(low == 1)
+    def _():
+        out0[...] = second
+        out1[...] = first
 
 
 def project_out(place, attn, weights):

time: 179 us -> 179 us (level)
  no operation moved by 1% of the time
where the time goes in v7:
time: 179 us; the launch traced here: 178 us
  waiting for transfers between devices  105 us (59%)
  starting transfers between devices  41.8 us (23%)
  Pallas kernels  21.3 us (12%)
  other arithmetic  5.33 us (3%)
  local copies, waits for them, and re-layouts  4.38 us (2%)
    ppermute x38, waiting for transfers between devices, __call__(): self.there[name] = lax.ppermute(array, AXES, moves(target))  105 us
    ppermute x38, starting transfers between devices, __call__(): self.there[name] = lax.ppermute(array, AXES, moves(target))  41.8 us
    pallas_call x2, Pallas kernels, project(): pl.pallas_call(functools.partial(kernel, plan), out_shape=jax.ShapeDtypeS...  8.91 us
    pallas_call x1, Pallas kernels, attend(): pl.pallas_call(attend_kernel, out_shape=(shape, shape), in_specs=[smem_sp...  7.07 us
    pallas_call x1, Pallas kernels, project_out(): pl.pallas_call(output_kernel, out_shape=(shape, shape), in_specs=[smem_sp...  5.3 us
  transfers between devices with their start and end apart: 38, of which 22 were waited for; matrix products, arithmetic and copies ran while one was open for 4% of the time, Pallas kernels for 6%

profile of v7, /device:TPU:0, one launch (start us, length us, event | category | flops | bytes accessed | tf_op | source)
XLA Modules:
  0.0 178.0 jit_solution(18402554317723650458)
XLA Ops:
  0.0 2.9 %collective-permute-start = (bf16[128,2048]{1,0:T(8,128)(2,1)}, bf16[128,2048]{1,0:T(8,128)(2,1)S(1)}, u32[]{:S(2)}, u32[]{:S(2)}) collective-permute-start(bf16[128,2048]{1,0:T(8,128)(2,1)} %refs_0_.3), channel_id=1, source_target_pairs={{0,1},{1,0},{2,3},{3,2},{4,5},{5,4},{6,7},{7,6},{8,9},{9,8},{10,11... | collective-permute-start | bytes 1572872 | tf_op jit(solution)/shard_map/ppermute | solution.py:400
  2.9 2.6 %collective-permute-start.3 = (bf16[128,2048]{1,0:T(8,128)(2,1)}, bf16[128,2048]{1,0:T(8,128)(2,1)S(1)}, u32[]{:S(2)}, u32[]{:S(2)}) collective-permute-start(bf16[128,2048]{1,0:T(8,128)(2,1)} %refs_0_.3), channel_id=1, source_target_pairs={{0,16},{1,17},{2,18},{3,19},{4,20},{5,21},{6,22},{7,23},{8,24},{9,... | collective-permute-start | bytes 1572872 | tf_op jit(solution)/shard_map/ppermute | solution.py:400
  5.5 1.6 collective-permute-start.1
  7.1 0.5 collective-permute-start.15
  7.6 2.1 %constant_dynamic-slice_fusion = (bf16[256,512]{1,0:T(8,128)(2,1)}, bf16[256,512]{1,0:T(8,128)(2,1)}, bf16[256,512]{1,0:T(8,128)(2,1)S(1)}, bf16[256,512]{1,0:T(8,128)(2,1)}) fusion(bf16[256,2048]{1,0:T(8,128)(2,1)} %param.6, s32[]{:T(128)S(6)} %select_n.58, s32[]{:T(128)S(6)} %select_n.53, s32[]{:T(128)S(6)} %select_n.52, s32[]{:T(128)S(6)} %select_n.57), kind=kLoop, calls=%fused_computation.24 | loop fusion | bytes 2097168 | tf_op jit(solution)/shard_map/dynamic_slice | solution.py:429
  9.8 0.1 constant_dynamic-slice_fusion.2
  10.0 1.6 collective-permute-start.5
  11.6 4.3 %collective-permute-done.refs_1_ = bf16[128,2048]{1,0:T(8,128)(2,1)S(1)} collective-permute-done((bf16[128,2048]{1,0:T(8,128)(2,1)}, bf16[128,2048]{1,0:T(8,128)(2,1)S(1)}, u32[]{:S(2)}, u32[]{:S(2)}) %collective-permute-start) | collective-permute-done | bytes 524320 | tf_op jit(solution)/shard_map/ppermute | solution.py:400
  15.9 2.1 %collective-permute-start.10 = (bf16[2048,256]{1,0:T(8,128)(2,1)S(1)}, bf16[2048,256]{1,0:T(8,128)(2,1)S(1)}, u32[]{:S(2)}, u32[]{:S(2)}) collective-permute-start(bf16[2048,256]{1,0:T(8,128)(2,1)S(1)} %copy-done.1), channel_id=1, source_target_pairs={{0,4},{1,5},{2,6},{3,7},{4,0},{5,1},{6,2},{7,3},{8,12},{9,13},{10,... | collective-permute-start | bytes 3145736 | tf_op jit(solution)/shard_map/ppermute | solution.py:400
  18.1 4.0 %collective-permute-done.5 = bf16[256,768]{1,0:T(8,128)(2,1)S(1)} collective-permute-done((bf16[256,768]{1,0:T(8,128)(2,1)S(1)}, bf16[256,768]{1,0:T(8,128)(2,1)S(1)}, u32[]{:S(2)}, u32[]{:S(2)}) %collective-permute-start.5) | collective-permute-done | bytes 393248 | tf_op jit(solution)/shard_map/ppermute | solution.py:400
  22.1 0.1 convert_bitcast_fusion
  22.2 12.5 %collective-permute-done.3.refs_4_ = bf16[128,2048]{1,0:T(8,128)(2,1)S(1)} collective-permute-done((bf16[128,2048]{1,0:T(8,128)(2,1)}, bf16[128,2048]{1,0:T(8,128)(2,1)S(1)}, u32[]{:S(2)}, u32[]{:S(2)}) %collective-permute-start.3) | collective-permute-done | bytes 524320 | tf_op jit(solution)/shard_map/ppermute | solution.py:400
  34.6 0.1 collective-permute-start.2
  34.7 3.8 %collective-permute-done.15.refs_10_ = bf16[2048,256]{1,0:T(8,128)(2,1)} collective-permute-done((bf16[2048,256]{1,0:T(8,128)(2,1)}, bf16[2048,256]{1,0:T(8,128)(2,1)}, u32[]{:S(2)}, u32[]{:S(2)}) %collective-permute-start.15) | collective-permute-done | bytes 1048608 | tf_op jit(solution)/shard_map/ppermute | solution.py:400
  38.5 2.1 %collective-permute-start.16 = (bf16[2048,256]{1,0:T(8,128)(2,1)}, bf16[2048,256]{1,0:T(8,128)(2,1)}, u32[]{:S(2)}, u32[]{:S(2)}) collective-permute-start(bf16[2048,256]{1,0:T(8,128)(2,1)} %collective-permute-done.15.refs_10_), channel_id=1, source_target_pairs={{0,4},{1,5},{2,6},{3,7},{4,0},{5,1},{6,2},{7,3},{8,12},{9,13},{10,... | collective-permute-start | bytes 3145736 | tf_op jit(solution)/shard_map/ppermute | solution.py:400
  40.6 0.7 pad_maximum_fusion.7
  41.3 3.2 %collective-permute-done.10.refs_12_ = bf16[2048,256]{1,0:T(8,128)(2,1)S(1)} collective-permute-done((bf16[2048,256]{1,0:T(8,128)(2,1)S(1)}, bf16[2048,256]{1,0:T(8,128)(2,1)S(1)}, u32[]{:S(2)}, u32[]{:S(2)}) %collective-permute-start.10) | collective-permute-done | bytes 1048608 | tf_op jit(solution)/shard_map/ppermute | solution.py:400
  44.6 1.0 copy-done.3
  45.6 1.8 %fusion = (f32[512,64]{1,0:T(8,128)S(1)}, f32[512,64]{1,0:T(8,128)}, f32[512,64]{1,0:T(8,128)}) fusion(f32[64]{0:T(128)S(1)} %multiply_power_fusion, f32[512]{0:T(512)S(1)} %convert_bitcast_fusion), kind=kLoop, calls=%fused_computation.21 | loop fusion | flops 65536 | bytes 395520 | tf_op jit(solution)/shard_map/neg | solution.py:468
  47.4 1.5 collective-permute-start.4
  48.9 0.1 pad_add_fusion.place
  49.0 1.3 pad_maximum_fusion.8
  50.3 1.4 collective-permute-start.13
  51.7 3.0 %collective-permute-start.14 = (bf16[256,512]{1,0:T(8,128)(2,1)}, bf16[256,512]{1,0:T(8,128)(2,1)S(1)}, u32[]{:S(2)}, u32[]{:S(2)}) collective-permute-start(bf16[256,512]{1,0:T(8,128)(2,1)} %get-tuple-element.35), channel_id=1, source_target_pairs={{0,24},{1,25},{2,26},{3,27},{4,28},{5,29},{6,30},{7,31},{8,16},{9,... | collective-permute-start | bytes 786440 | tf_op jit(solution)/shard_map/ppermute | solution.py:400
  54.8 1.0 fusion.2
  55.8 4.2 %collective-permute-done.4.refs_5_ = bf16[128,2048]{1,0:T(8,128)(2,1)S(1)} collective-permute-done((bf16[128,2048]{1,0:T(8,128)(2,1)S(1)}, bf16[128,2048]{1,0:T(8,128)(2,1)S(1)}, u32[]{:S(2)}, u32[]{:S(2)}) %collective-permute-start.4) | collective-permute-done | bytes 524320 | tf_op jit(solution)/shard_map/ppermute | solution.py:400
  60.0 4.8 %collective-permute-done.16.refs_14_ = bf16[2048,256]{1,0:T(8,128)(2,1)} collective-permute-done((bf16[2048,256]{1,0:T(8,128)(2,1)}, bf16[2048,256]{1,0:T(8,128)(2,1)}, u32[]{:S(2)}, u32[]{:S(2)}) %collective-permute-start.16) | collective-permute-done | bytes 1048608 | tf_op jit(solution)/shard_map/ppermute | solution.py:400
  64.8 1.5 collective-permute-start.17
  66.3 0.1 pad_maximum_fusion.refs_8_
  66.4 1.6 collective-permute-start.7
  68.0 2.3 %collective-permute-done.13 = bf16[256,512]{1,0:T(8,128)(2,1)S(1)} collective-permute-done((bf16[256,512]{1,0:T(8,128)(2,1)}, bf16[256,512]{1,0:T(8,128)(2,1)S(1)}, u32[]{:S(2)}, u32[]{:S(2)}) %collective-permute-start.13) | collective-permute-done | bytes 262176 | tf_op jit(solution)/shard_map/ppermute | solution.py:400
  70.3 1.5 collective-permute-start.19
  71.9 1.9 %collective-permute-done.17.refs_11_ = bf16[3,256,256]{2,1,0:T(8,128)(2,1)S(1)} collective-permute-done((bf16[3,256,256]{2,1,0:T(8,128)(2,1)S(1)}, bf16[3,256,256]{2,1,0:T(8,128)(2,1)S(1)}, u32[]{:S(2)}, u32[]{:S(2)}) %collective-permute-start.17) | collective-permute-done | bytes 393248 | tf_op jit(solution)/shard_map/ppermute | solution.py:400
  73.8 1.5 collective-permute-start.18
  75.4 0.1 pad_maximum_fusion.1
  75.4 2.4 %collective-permute-done.7.refs_7_ = bf16[128,2048]{1,0:T(8,128)(2,1)S(1)} collective-permute-done((bf16[128,2048]{1,0:T(8,128)(2,1)S(1)}, bf16[128,2048]{1,0:T(8,128)(2,1)S(1)}, u32[]{:S(2)}, u32[]{:S(2)}) %collective-permute-start.7) | collective-permute-done | bytes 524320 | tf_op jit(solution)/shard_map/ppermute | solution.py:400
  77.8 12.6 %collective-permute-done.18 = bf16[2,256,512]{2,1,0:T(8,128)(2,1)S(1)} collective-permute-done((bf16[2,256,512]{2,1,0:T(8,128)(2,1)S(1)}, bf16[2,256,512]{2,1,0:T(8,128)(2,1)S(1)}, u32[]{:S(2)}, u32[]{:S(2)}) %collective-permute-start.18) | collective-permute-done | bytes 524320 | tf_op jit(solution)/shard_map/ppermute | solution.py:400
  90.6 4.9 %shard_map.55.kv0 = bf16[4,128,256]{2,1,0:T(8,128)(2,1)S(1)} custom-call(s32[2]{0:T(128)S(1)} %pad_add_fusion.place, bf16[128,2048]{1,0:T(8,128)(2,1)S(1)} %copy-done, bf16[128,2048]{1,0:T(8,128)(2,1)S(1)} %collective-permute-done.refs_1_, bf16[128,2048]{1,0:T(8,128)(2,1)S(1)} %collective-permute-done.1.refs_2_, ...), custom_call_target="tpu_custom_call" | custom-call | flops 1073741824 | bytes 8388608 | tf_op jit(solution)/shard_map/pallas_call | solution.py:208
  95.6 0.1 collective-permute-start.21
  95.6 1.6 collective-permute-start.23
  97.2 0.2 collective-permute-start.22
  97.4 1.6 collective-permute-done.21.refs_11_
  99.0 4.0 %shard_map.56.queries = bf16[4,512,128]{2,1,0:T(8,128)(2,1)S(1)} custom-call(s32[2]{0:T(128)S(1)} %pad_add_fusion.place, bf16[128,2048]{1,0:T(8,128)(2,1)S(1)} %copy-done, bf16[128,2048]{1,0:T(8,128)(2,1)S(1)} %collective-permute-done.refs_1_, bf16[128,2048]{1,0:T(8,128)(2,1)S(1)} %collective-permute-done.1.refs_2_, ...), custom_call_target="tpu_custom_call" | custom-call | flops 1073741824 | bytes 8388608 | tf_op jit(solution)/shard_map/pallas_call | solution.py:208
  103.0 1.3 collective-permute-done.23.kv2
  104.4 0.5 collective-permute-start.25
  104.9 0.5 collective-permute-start.27
  105.5 0.4 collective-permute-done.24.kv3
  105.9 7.1 %shard_map.57 = (bf16[2,128,512]{2,1,0:T(8,128)(2,1)S(1)}, bf16[2,128,512]{2,1,0:T(8,128)(2,1)S(1)}) custom-call(s32[2]{0:T(128)S(1)} %pad_add_fusion.place, bf16[4,512,128]{2,1,0:T(8,128)(2,1)S(1)} %shard_map.56.queries, bf16[4,128,256]{2,1,0:T(8,128)(2,1)S(1)} %shard_map.55.kv0, bf16[4,128,256]{2,1,0:T(8,128)(2,1)S(1)} %collective-permute-done.22.kv1, ...), custom_call_target="tpu_custom_call" | custom-call | flops 32212254720 | bytes 4194304 | tf_op jit(solution)/shard_map/pallas_call | solution.py:283
  113.0 1.6 collective-permute-start.32
  114.6 1.0 collective-permute-start.29
  115.5 2.8 %collective-permute-start.30 = (bf16[2,128,512]{2,1,0:T(8,128)(2,1)S(1)}, bf16[2,128,512]{2,1,0:T(8,128)(2,1)S(1)}, u32[]{:S(2)}, u32[]{:S(2)}) collective-permute-start(bf16[2,128,512]{2,1,0:T(8,128)(2,1)S(1)} %get-tuple-element.42.refs_0_), channel_id=1, source_target_pairs={{0,16},{1,17},{2,18},{3,19},{4,20},{5,21},{6,22},{7,23},{8,24},{9,... | collective-permute-start | bytes 786440 | tf_op jit(solution)/shard_map/ppermute | solution.py:400
  118.3 3.1 %collective-permute-done.32.refs_4_ = bf16[2,128,512]{2,1,0:T(8,128)(2,1)S(1)} collective-permute-done((bf16[2,128,512]{2,1,0:T(8,128)(2,1)S(1)}, bf16[2,128,512]{2,1,0:T(8,128)(2,1)S(1)}, u32[]{:S(2)}, u32[]{:S(2)}) %collective-permute-start.32) | collective-permute-done | bytes 262176 | tf_op jit(solution)/shard_map/ppermute | solution.py:400
  121.4 2.1 %collective-permute-start.34 = (bf16[2,128,512]{2,1,0:T(8,128)(2,1)S(1)}, bf16[2,128,512]{2,1,0:T(8,128)(2,1)S(1)}, u32[]{:S(2)}, u32[]{:S(2)}) collective-permute-start(bf16[2,128,512]{2,1,0:T(8,128)(2,1)S(1)} %collective-permute-done.32.refs_4_), channel_id=1, source_target_pairs={{0,16},{1,17},{2,18},{3,19},{4,20},{5,21},{6,22},{7,23},{8,24},{9,... | collective-permute-start | bytes 786440 | tf_op jit(solution)/shard_map/ppermute | solution.py:400
  123.5 4.5 %collective-permute-done.29.refs_1_ = bf16[2,128,512]{2,1,0:T(8,128)(2,1)S(1)} collective-permute-done((bf16[2,128,512]{2,1,0:T(8,128)(2,1)S(1)}, bf16[2,128,512]{2,1,0:T(8,128)(2,1)S(1)}, u32[]{:S(2)}, u32[]{:S(2)}) %collective-permute-start.29) | collective-permute-done | bytes 262176 | tf_op jit(solution)/shard_map/ppermute | solution.py:400
  128.0 8.3 %collective-permute-done.30.refs_2_ = bf16[2,128,512]{2,1,0:T(8,128)(2,1)S(1)} collective-permute-done((bf16[2,128,512]{2,1,0:T(8,128)(2,1)S(1)}, bf16[2,128,512]{2,1,0:T(8,128)(2,1)S(1)}, u32[]{:S(2)}, u32[]{:S(2)}) %collective-permute-start.30) | collective-permute-done | bytes 262176 | tf_op jit(solution)/shard_map/ppermute | solution.py:400
  136.3 5.0 %collective-permute-done.34.refs_6_ = bf16[2,128,512]{2,1,0:T(8,128)(2,1)S(1)} collective-permute-done((bf16[2,128,512]{2,1,0:T(8,128)(2,1)S(1)}, bf16[2,128,512]{2,1,0:T(8,128)(2,1)S(1)}, u32[]{:S(2)}, u32[]{:S(2)}) %collective-permute-start.34) | collective-permute-done | bytes 262176 | tf_op jit(solution)/shard_map/ppermute | solution.py:400
  141.4 1.7 collective-permute-done.33.refs_5_
  143.1 5.6 %collective-permute-done.31.refs_3_ = bf16[2,128,512]{2,1,0:T(8,128)(2,1)S(1)} collective-permute-done((bf16[2,128,512]{2,1,0:T(8,128)(2,1)S(1)}, bf16[2,128,512]{2,1,0:T(8,128)(2,1)S(1)}, u32[]{:S(2)}, u32[]{:S(2)}) %collective-permute-start.31) | collective-permute-done | bytes 262176 | tf_op jit(solution)/shard_map/ppermute | solution.py:400
  148.7 3.6 %collective-permute-done.35.refs_7_ = bf16[2,128,512]{2,1,0:T(8,128)(2,1)S(1)} collective-permute-done((bf16[2,128,512]{2,1,0:T(8,128)(2,1)S(1)}, bf16[2,128,512]{2,1,0:T(8,128)(2,1)S(1)}, u32[]{:S(2)}, u32[]{:S(2)}) %collective-permute-start.35) | collective-permute-done | bytes 262176 | tf_op jit(solution)/shard_map/ppermute | solution.py:400
  152.3 5.3 %shard_map.58 = (bf16[128,1024]{1,0:T(8,128)(2,1)S(1)}, bf16[128,1024]{1,0:T(8,128)(2,1)S(1)}) custom-call(s32[2]{0:T(128)S(1)} %pad_add_fusion.place, bf16[2,128,512]{2,1,0:T(8,128)(2,1)S(1)} %get-tuple-element.42.refs_0_, bf16[2,128,512]{2,1,0:T(8,128)(2,1)S(1)} %collective-permute-done.29.refs_1_, ...), custom_call_target="tpu_custom_call" | custom-call | flops 2147483648 | bytes 12582912 | tf_op jit(solution)/shard_map/pallas_call | solution.py:352
  157.6 5.2 %collective-permute-start.36 = (bf16[128,1024]{1,0:T(8,128)(2,1)S(1)}, bf16[128,1024]{1,0:T(8,128)(2,1)S(1)}, u32[]{:S(2)}, u32[]{:S(2)}) collective-permute-start(bf16[128,1024]{1,0:T(8,128)(2,1)S(1)} %get-tuple-element.47), channel_id=1, source_target_pairs={{0,24},{1,16},{2,26},{3,18},{4,28},{5,20},{6,30},{7,22},{8,0},{9,8... | collective-permute-start | bytes 786440 | tf_op jit(solution)/shard_map/ppermute | solution.py:400
  162.8 0.7 collective-permute-start.37
  163.6 13.5 %collective-permute-done.36 = bf16[128,1024]{1,0:T(8,128)(2,1)S(1)} collective-permute-done((bf16[128,1024]{1,0:T(8,128)(2,1)S(1)}, bf16[128,1024]{1,0:T(8,128)(2,1)S(1)}, u32[]{:S(2)}, u32[]{:S(2)}) %collective-permute-start.36) | collective-permute-done | bytes 262176 | tf_op jit(solution)/shard_map/ppermute | solution.py:400
  177.1 0.8 pad_maximum_fusion.3
  (62 shorter events, 0.6 us)
Async XLA Ops:
  0.0 9.8 %copy-start.8 = (bf16[256,512]{1,0:T(8,128)(2,1)S(1)}, bf16[256,512]{1,0:T(8,128)(2,1)}, u32[]{:S(2)}) copy-start(bf16[256,512]{1,0:T(8,128)(2,1)} %param.7) | copy-start | bytes 786436
  0.0 9.8 %copy-start.7 = (bf16[256,512]{1,0:T(8,128)(2,1)S(1)}, bf16[256,512]{1,0:T(8,128)(2,1)}, u32[]{:S(2)}) copy-start(bf16[256,512]{1,0:T(8,128)(2,1)} %param.8) | copy-start | bytes 786436
  0.0 15.9 %collective-permute-start = (bf16[128,2048]{1,0:T(8,128)(2,1)}, bf16[128,2048]{1,0:T(8,128)(2,1)S(1)}, u32[]{:S(2)}, u32[]{:S(2)}) collective-permute-start(bf16[128,2048]{1,0:T(8,128)(2,1)} %refs_0_.3), channel_id=1, source_target_pairs={{0,1},{1,0},{2,3},{3,2},{4,5},{5,4},{6,7},{7,6},{8,9},{9,8},{10,11... | collective-permute-start | bytes 1572872 | tf_op jit(solution)/shard_map/ppermute | solution.py:400
  2.9 31.7 %collective-permute-start.3 = (bf16[128,2048]{1,0:T(8,128)(2,1)}, bf16[128,2048]{1,0:T(8,128)(2,1)S(1)}, u32[]{:S(2)}, u32[]{:S(2)}) collective-permute-start(bf16[128,2048]{1,0:T(8,128)(2,1)} %refs_0_.3), channel_id=1, source_target_pairs={{0,16},{1,17},{2,18},{3,19},{4,20},{5,21},{6,22},{7,23},{8,24},{9,... | collective-permute-start | bytes 1572872 | tf_op jit(solution)/shard_map/ppermute | solution.py:400
  5.5 29.1 %collective-permute-start.1 = (bf16[128,2048]{1,0:T(8,128)(2,1)}, bf16[128,2048]{1,0:T(8,128)(2,1)S(1)}, u32[]{:S(2)}, u32[]{:S(2)}) collective-permute-start(bf16[128,2048]{1,0:T(8,128)(2,1)} %refs_0_.3), channel_id=1, source_target_pairs={{0,8},{1,9},{2,10},{3,11},{4,12},{5,13},{6,14},{7,15},{8,0},{9,1},... | collective-permute-start | bytes 1572872 | tf_op jit(solution)/shard_map/ppermute | solution.py:400
  7.1 31.4 %collective-permute-start.15 = (bf16[2048,256]{1,0:T(8,128)(2,1)}, bf16[2048,256]{1,0:T(8,128)(2,1)}, u32[]{:S(2)}, u32[]{:S(2)}) collective-permute-start(bf16[2048,256]{1,0:T(8,128)(2,1)} %refs_8_.1), channel_id=1, source_target_pairs={{0,1},{1,0},{2,3},{3,2},{4,5},{5,4},{6,7},{7,6},{8,9},{9,8},{10,11... | collective-permute-start | bytes 3145736 | tf_op jit(solution)/shard_map/ppermute | solution.py:400
  9.8 6.1 %copy-start.1 = (bf16[2048,256]{1,0:T(8,128)(2,1)S(1)}, bf16[2048,256]{1,0:T(8,128)(2,1)}, u32[]{:S(2)}) copy-start(bf16[2048,256]{1,0:T(8,128)(2,1)} %refs_8_.1) | copy-start | bytes 3145732
  10.0 12.1 %collective-permute-start.5 = (bf16[256,768]{1,0:T(8,128)(2,1)S(1)}, bf16[256,768]{1,0:T(8,128)(2,1)S(1)}, u32[]{:S(2)}, u32[]{:S(2)}) collective-permute-start(bf16[256,768]{1,0:T(8,128)(2,1)S(1)} %get-tuple-element.56), channel_id=1, source_target_pairs={{0,4},{1,5},{2,6},{3,7},{4,0},{5,1},{6,2},{7,3},{8,12},{9,13},{10,... | collective-permute-start | bytes 1179656 | tf_op jit(solution)/shard_map/ppermute | solution.py:400
  15.9 28.7 %collective-permute-start.10 = (bf16[2048,256]{1,0:T(8,128)(2,1)S(1)}, bf16[2048,256]{1,0:T(8,128)(2,1)S(1)}, u32[]{:S(2)}, u32[]{:S(2)}) collective-permute-start(bf16[2048,256]{1,0:T(8,128)(2,1)S(1)} %copy-done.1), channel_id=1, source_target_pairs={{0,4},{1,5},{2,6},{3,7},{4,0},{5,1},{6,2},{7,3},{8,12},{9,13},{10,... | collective-permute-start | bytes 3145736 | tf_op jit(solution)/shard_map/ppermute | solution.py:400
  22.1 12.5 %copy-start.5 = (bf16[256,768]{1,0:T(8,128)(2,1)}, bf16[256,768]{1,0:T(8,128)(2,1)S(1)}, u32[]{:S(2)}) copy-start(bf16[256,768]{1,0:T(8,128)(2,1)S(1)} %collective-permute-done.5) | copy-start | bytes 1179652
  22.1 18.5 %collective-permute-start.9 = (bf16[2,256,256]{2,1,0:T(8,128)(2,1)S(1)}, bf16[2,256,256]{2,1,0:T(8,128)(2,1)S(1)}, u32[]{:S(2)}, u32[]{:S(2)}) collective-permute-start(bf16[2,256,256]{2,1,0:T(8,128)(2,1)S(1)} %pad_maximum_fusion.6), channel_id=1, source_target_pairs={{0,16},{1,17},{2,18},{3,19},{4,20},{5,21},{6,22},{7,23},{8,24},{9,... | collective-permute-start | bytes 786440 | tf_op jit(solution)/shard_map/ppermute | solution.py:400
  34.6 15.7 %collective-permute-start.6 = (bf16[128,2048]{1,0:T(8,128)(2,1)S(1)}, bf16[128,2048]{1,0:T(8,128)(2,1)S(1)}, u32[]{:S(2)}, u32[]{:S(2)}) collective-permute-start(bf16[128,2048]{1,0:T(8,128)(2,1)S(1)} %collective-permute-done.3.refs_4_), channel_id=1, source_target_pairs={{0,8},{1,9},{2,10},{3,11},{4,12},{5,13},{6,14},{7,15},{8,0},{9,1},... | collective-permute-start | bytes 1572872 | tf_op jit(solution)/shard_map/ppermute | solution.py:400
  34.6 17.1 %collective-permute-start.2 = (bf16[128,2048]{1,0:T(8,128)(2,1)S(1)}, bf16[128,2048]{1,0:T(8,128)(2,1)S(1)}, u32[]{:S(2)}, u32[]{:S(2)}) collective-permute-start(bf16[128,2048]{1,0:T(8,128)(2,1)S(1)} %collective-permute-done.1.refs_2_), channel_id=1, source_target_pairs={{0,1},{1,0},{2,3},{3,2},{4,5},{5,4},{6,7},{7,6},{8,9},{9,8},{10,11... | collective-permute-start | bytes 1572872 | tf_op jit(solution)/shard_map/ppermute | solution.py:400
  38.5 26.3 %collective-permute-start.16 = (bf16[2048,256]{1,0:T(8,128)(2,1)}, bf16[2048,256]{1,0:T(8,128)(2,1)}, u32[]{:S(2)}, u32[]{:S(2)}) collective-permute-start(bf16[2048,256]{1,0:T(8,128)(2,1)} %collective-permute-done.15.refs_10_), channel_id=1, source_target_pairs={{0,4},{1,5},{2,6},{3,7},{4,0},{5,1},{6,2},{7,3},{8,12},{9,13},{10,... | collective-permute-start | bytes 3145736 | tf_op jit(solution)/shard_map/ppermute | solution.py:400
  44.6 1.0 copy-start.3
  45.6 9.2 %collective-permute-start.11 = (bf16[2,256,256]{2,1,0:T(8,128)(2,1)}, bf16[2,256,256]{2,1,0:T(8,128)(2,1)}, u32[]{:S(2)}, u32[]{:S(2)}) collective-permute-start(bf16[2,256,256]{2,1,0:T(8,128)(2,1)} %pad_maximum_fusion.7), channel_id=1, source_target_pairs={{0,8},{1,9},{2,10},{3,11},{4,12},{5,13},{6,14},{7,15},{8,0},{9,1},... | collective-permute-start | bytes 786440 | tf_op jit(solution)/shard_map/ppermute | solution.py:400
  47.4 18.9 %copy-start.6 = (bf16[256,768]{1,0:T(8,128)(2,1)S(1)}, bf16[256,768]{1,0:T(8,128)(2,1)}, u32[]{:S(2)}) copy-start(bf16[256,768]{1,0:T(8,128)(2,1)} %copy-done.5) | copy-start | bytes 1179652
  47.4 12.6 %collective-permute-start.4 = (bf16[128,2048]{1,0:T(8,128)(2,1)S(1)}, bf16[128,2048]{1,0:T(8,128)(2,1)S(1)}, u32[]{:S(2)}, u32[]{:S(2)}) collective-permute-start(bf16[128,2048]{1,0:T(8,128)(2,1)S(1)} %collective-permute-done.3.refs_4_), channel_id=1, source_target_pairs={{0,1},{1,0},{2,3},{3,2},{4,5},{5,4},{6,7},{7,6},{8,9},{9,8},{10,11... | collective-permute-start | bytes 1572872 | tf_op jit(solution)/shard_map/ppermute | solution.py:400
  50.3 20.0 %collective-permute-start.13 = (bf16[256,512]{1,0:T(8,128)(2,1)}, bf16[256,512]{1,0:T(8,128)(2,1)S(1)}, u32[]{:S(2)}, u32[]{:S(2)}) collective-permute-start(bf16[256,512]{1,0:T(8,128)(2,1)} %get-tuple-element.34), channel_id=1, source_target_pairs={{0,16},{1,17},{2,18},{3,19},{4,20},{5,21},{6,22},{7,23},{8,24},{9,... | collective-permute-start | bytes 786440 | tf_op jit(solution)/shard_map/ppermute | solution.py:400
  51.7 20.1 %collective-permute-start.14 = (bf16[256,512]{1,0:T(8,128)(2,1)}, bf16[256,512]{1,0:T(8,128)(2,1)S(1)}, u32[]{:S(2)}, u32[]{:S(2)}) collective-permute-start(bf16[256,512]{1,0:T(8,128)(2,1)} %get-tuple-element.35), channel_id=1, source_target_pairs={{0,24},{1,25},{2,26},{3,27},{4,28},{5,29},{6,30},{7,31},{8,16},{9,... | collective-permute-start | bytes 786440 | tf_op jit(solution)/shard_map/ppermute | solution.py:400
  54.8 15.5 %collective-permute-start.12 = (bf16[256,512]{1,0:T(8,128)(2,1)}, bf16[256,512]{1,0:T(8,128)(2,1)S(1)}, u32[]{:S(2)}, u32[]{:S(2)}) collective-permute-start(bf16[256,512]{1,0:T(8,128)(2,1)} %get-tuple-element.33), channel_id=1, source_target_pairs={{0,8},{1,9},{2,10},{3,11},{4,12},{5,13},{6,14},{7,15},{8,0},{9,1},... | collective-permute-start | bytes 786440 | tf_op jit(solution)/shard_map/ppermute | solution.py:400
  64.8 9.0 %collective-permute-start.17 = (bf16[3,256,256]{2,1,0:T(8,128)(2,1)S(1)}, bf16[3,256,256]{2,1,0:T(8,128)(2,1)S(1)}, u32[]{:S(2)}, u32[]{:S(2)}) collective-permute-start(bf16[3,256,256]{2,1,0:T(8,128)(2,1)S(1)} %pad_maximum_fusion.5.refs_10_), channel_id=1, source_target_pairs={{0,4},{1,5},{2,6},{3,7},{4,0},{5,1},{6,2},{7,3},{8,12},{9,13},{10,... | collective-permute-start | bytes 1179656 | tf_op jit(solution)/shard_map/ppermute | solution.py:400
  66.4 11.4 %collective-permute-start.7 = (bf16[128,2048]{1,0:T(8,128)(2,1)S(1)}, bf16[128,2048]{1,0:T(8,128)(2,1)S(1)}, u32[]{:S(2)}, u32[]{:S(2)}) collective-permute-start(bf16[128,2048]{1,0:T(8,128)(2,1)S(1)} %collective-permute-done.6.refs_6_), channel_id=1, source_target_pairs={{0,1},{1,0},{2,3},{3,2},{4,5},{5,4},{6,7},{7,6},{8,9},{9,8},{10,11... | collective-permute-start | bytes 1572872 | tf_op jit(solution)/shard_map/ppermute | solution.py:400
  70.3 20.3 %collective-permute-start.8 = (bf16[2,256,768]{2,1,0:T(8,128)(2,1)S(1)}, bf16[2,256,768]{2,1,0:T(8,128)(2,1)S(1)}, u32[]{:S(2)}, u32[]{:S(2)}) collective-permute-start(bf16[2,256,768]{2,1,0:T(8,128)(2,1)S(1)} %pad_maximum_fusion.refs_8_), channel_id=1, source_target_pairs={{0,2},{1,3},{2,0},{3,1},{4,6},{5,7},{6,4},{7,5},{8,10},{9,11},{10,... | collective-permute-start | bytes 2359304 | tf_op jit(solution)/shard_map/ppermute | solution.py:400
  70.3 20.2 %collective-permute-start.19 = (bf16[256,512]{1,0:T(8,128)(2,1)S(1)}, bf16[256,512]{1,0:T(8,128)(2,1)S(1)}, u32[]{:S(2)}, u32[]{:S(2)}) collective-permute-start(bf16[256,512]{1,0:T(8,128)(2,1)S(1)} %collective-permute-done.13), channel_id=1, source_target_pairs={{0,4},{1,5},{2,6},{3,7},{4,0},{5,1},{6,2},{7,3},{8,12},{9,13},{10,... | collective-permute-start | bytes 786440 | tf_op jit(solution)/shard_map/ppermute | solution.py:400
  73.8 16.7 %collective-permute-start.18 = (bf16[2,256,512]{2,1,0:T(8,128)(2,1)S(1)}, bf16[2,256,512]{2,1,0:T(8,128)(2,1)S(1)}, u32[]{:S(2)}, u32[]{:S(2)}) collective-permute-start(bf16[2,256,512]{2,1,0:T(8,128)(2,1)S(1)} %pad_maximum_fusion.2), channel_id=1, source_target_pairs={{0,4},{1,5},{2,6},{3,7},{4,0},{5,1},{6,2},{7,3},{8,12},{9,13},{10,... | collective-permute-start | bytes 1572872 | tf_op jit(solution)/shard_map/ppermute | solution.py:400
  75.3 15.2 %copy-start = (bf16[128,2048]{1,0:T(8,128)(2,1)S(1)}, bf16[128,2048]{1,0:T(8,128)(2,1)}, u32[]{:S(2)}) copy-start(bf16[128,2048]{1,0:T(8,128)(2,1)} %refs_0_.3) | copy-start | bytes 1572868
  77.8 12.8 %collective-permute-start.20 = (bf16[6,256,256]{2,1,0:T(8,128)(2,1)S(1)}, bf16[6,256,256]{2,1,0:T(8,128)(2,1)S(1)}, u32[]{:S(2)}, u32[]{:S(2)}) collective-permute-start(bf16[6,256,256]{2,1,0:T(8,128)(2,1)S(1)} %pad_maximum_fusion.1), channel_id=1, source_target_pairs={{0,2},{1,3},{2,0},{3,1},{4,6},{5,7},{6,4},{7,5},{8,10},{9,11},{10,... | collective-permute-start | bytes 2359304 | tf_op jit(solution)/shard_map/ppermute | solution.py:400
  95.5 8.8 %copy-start.2 = (bf16[2048,256]{1,0:T(8,128)(2,1)S(1)}, bf16[2048,256]{1,0:T(8,128)(2,1)}, u32[]{:S(2)}) copy-start(bf16[2048,256]{1,0:T(8,128)(2,1)} %refs_8_.1) | copy-start | bytes 3145732
  95.5 9.3 %copy-start.4 = (bf16[2048,256]{1,0:T(8,128)(2,1)S(1)}, bf16[2048,256]{1,0:T(8,128)(2,1)}, u32[]{:S(2)}) copy-start(bf16[2048,256]{1,0:T(8,128)(2,1)} %copy-done.3) | copy-start | bytes 3145732
  95.6 3.5 %collective-permute-start.21 = (bf16[6,256,512]{2,1,0:T(8,128)(2,1)S(1)}, bf16[6,256,512]{2,1,0:T(8,128)(2,1)S(1)}, u32[]{:S(2)}, u32[]{:S(2)}) collective-permute-start(bf16[6,256,512]{2,1,0:T(8,128)(2,1)S(1)} %slice_dynamic-update-slice_fusion.refs_10_), channel_id=1, source_target_pairs={{0,2},{1,3},{2,0},{3,1},{4,6},{5,7},{6,4},{7,5},{8,10},{9,11},{10,... | collective-permute-start | bytes 4718600 | tf_op jit(solution)/shard_map/ppermute | solution.py:400
  95.6 8.7 %collective-permute-start.23 = (bf16[4,128,256]{2,1,0:T(8,128)(2,1)S(1)}, bf16[4,128,256]{2,1,0:T(8,128)(2,1)S(1)}, u32[]{:S(2)}, u32[]{:S(2)}) collective-permute-start(bf16[4,128,256]{2,1,0:T(8,128)(2,1)S(1)} %shard_map.55.kv0), channel_id=1, source_target_pairs={{0,4},{1,5},{2,6},{3,7},{4,0},{5,1},{6,2},{7,3},{8,12},{9,13},{10,... | collective-permute-start | bytes 786440 | tf_op jit(solution)/shard_map/ppermute | solution.py:400
  97.2 8.2 %collective-permute-start.22 = (bf16[4,128,256]{2,1,0:T(8,128)(2,1)S(1)}, bf16[4,128,256]{2,1,0:T(8,128)(2,1)S(1)}, u32[]{:S(2)}, u32[]{:S(2)}) collective-permute-start(bf16[4,128,256]{2,1,0:T(8,128)(2,1)S(1)} %shard_map.55.kv0), channel_id=1, source_target_pairs={{0,2},{1,3},{2,0},{3,1},{4,6},{5,7},{6,4},{7,5},{8,10},{9,11},{10,... | collective-permute-start | bytes 786440 | tf_op jit(solution)/shard_map/ppermute | solution.py:400
  104.4 1.5 collective-permute-start.24
  104.4 10.2 %collective-permute-start.25 = (bf16[2048,256]{1,0:T(8,128)(2,1)S(1)}, bf16[2048,256]{1,0:T(8,128)(2,1)S(1)}, u32[]{:S(2)}, u32[]{:S(2)}) collective-permute-start(bf16[2048,256]{1,0:T(8,128)(2,1)S(1)} %copy-done.2), channel_id=1, source_target_pairs={{0,2},{1,3},{2,0},{3,1},{4,6},{5,7},{6,4},{7,5},{8,10},{9,11},{10,... | collective-permute-start | bytes 3145736 | tf_op jit(solution)/shard_map/ppermute | solution.py:400
  104.9 8.1 %collective-permute-start.26 = (bf16[2048,256]{1,0:T(8,128)(2,1)}, bf16[2048,256]{1,0:T(8,128)(2,1)S(1)}, u32[]{:S(2)}, u32[]{:S(2)}) collective-permute-start(bf16[2048,256]{1,0:T(8,128)(2,1)} %collective-permute-done.15.refs_10_), channel_id=1, source_target_pairs={{0,2},{1,3},{2,0},{3,1},{4,6},{5,7},{6,4},{7,5},{8,10},{9,11},{10,... | collective-permute-start | bytes 3145736 | tf_op jit(solution)/shard_map/ppermute | solution.py:400
  104.9 8.1 %collective-permute-start.27 = (bf16[2048,256]{1,0:T(8,128)(2,1)S(1)}, bf16[2048,256]{1,0:T(8,128)(2,1)S(1)}, u32[]{:S(2)}, u32[]{:S(2)}) collective-permute-start(bf16[2048,256]{1,0:T(8,128)(2,1)S(1)} %copy-done.4), channel_id=1, source_target_pairs={{0,2},{1,3},{2,0},{3,1},{4,6},{5,7},{6,4},{7,5},{8,10},{9,11},{10,... | collective-permute-start | bytes 3145736 | tf_op jit(solution)/shard_map/ppermute | solution.py:400
  105.4 7.6 %collective-permute-start.28 = (bf16[2048,256]{1,0:T(8,128)(2,1)}, bf16[2048,256]{1,0:T(8,128)(2,1)S(1)}, u32[]{:S(2)}, u32[]{:S(2)}) collective-permute-start(bf16[2048,256]{1,0:T(8,128)(2,1)} %collective-permute-done.16.refs_14_), channel_id=1, source_target_pairs={{0,2},{1,3},{2,0},{3,1},{4,6},{5,7},{6,4},{7,5},{8,10},{9,11},{10,... | collective-permute-start | bytes 3145736 | tf_op jit(solution)/shard_map/ppermute | solution.py:400
  113.0 8.4 %collective-permute-start.32 = (bf16[2,128,512]{2,1,0:T(8,128)(2,1)S(1)}, bf16[2,128,512]{2,1,0:T(8,128)(2,1)S(1)}, u32[]{:S(2)}, u32[]{:S(2)}) collective-permute-start(bf16[2,128,512]{2,1,0:T(8,128)(2,1)S(1)} %get-tuple-element.44), channel_id=1, source_target_pairs={{0,1},{1,0},{2,3},{3,2},{4,5},{5,4},{6,7},{7,6},{8,9},{9,8},{10,11... | collective-permute-start | bytes 786440 | tf_op jit(solution)/shard_map/ppermute | solution.py:400
  114.6 13.5 %collective-permute-start.29 = (bf16[2,128,512]{2,1,0:T(8,128)(2,1)S(1)}, bf16[2,128,512]{2,1,0:T(8,128)(2,1)S(1)}, u32[]{:S(2)}, u32[]{:S(2)}) collective-permute-start(bf16[2,128,512]{2,1,0:T(8,128)(2,1)S(1)} %get-tuple-element.42.refs_0_), channel_id=1, source_target_pairs={{0,8},{1,9},{2,10},{3,11},{4,12},{5,13},{6,14},{7,15},{8,0},{9,1},... | collective-permute-start | bytes 786440 | tf_op jit(solution)/shard_map/ppermute | solution.py:400
  115.5 20.8 %collective-permute-start.30 = (bf16[2,128,512]{2,1,0:T(8,128)(2,1)S(1)}, bf16[2,128,512]{2,1,0:T(8,128)(2,1)S(1)}, u32[]{:S(2)}, u32[]{:S(2)}) collective-permute-start(bf16[2,128,512]{2,1,0:T(8,128)(2,1)S(1)} %get-tuple-element.42.refs_0_), channel_id=1, source_target_pairs={{0,16},{1,17},{2,18},{3,19},{4,20},{5,21},{6,22},{7,23},{8,24},{9,... | collective-permute-start | bytes 786440 | tf_op jit(solution)/shard_map/ppermute | solution.py:400
  121.4 20.0 %collective-permute-start.34 = (bf16[2,128,512]{2,1,0:T(8,128)(2,1)S(1)}, bf16[2,128,512]{2,1,0:T(8,128)(2,1)S(1)}, u32[]{:S(2)}, u32[]{:S(2)}) collective-permute-start(bf16[2,128,512]{2,1,0:T(8,128)(2,1)S(1)} %collective-permute-done.32.refs_4_), channel_id=1, source_target_pairs={{0,16},{1,17},{2,18},{3,19},{4,20},{5,21},{6,22},{7,23},{8,24},{9,... | collective-permute-start | bytes 786440 | tf_op jit(solution)/shard_map/ppermute | solution.py:400
  128.0 15.1 %collective-permute-start.33 = (bf16[2,128,512]{2,1,0:T(8,128)(2,1)S(1)}, bf16[2,128,512]{2,1,0:T(8,128)(2,1)S(1)}, u32[]{:S(2)}, u32[]{:S(2)}) collective-permute-start(bf16[2,128,512]{2,1,0:T(8,128)(2,1)S(1)} %collective-permute-done.32.refs_4_), channel_id=1, source_target_pairs={{0,8},{1,9},{2,10},{3,11},{4,12},{5,13},{6,14},{7,15},{8,0},{9,1},... | collective-permute-start | bytes 786440 | tf_op jit(solution)/shard_map/ppermute | solution.py:400
  136.3 12.4 %collective-permute-start.31 = (bf16[2,128,512]{2,1,0:T(8,128)(2,1)S(1)}, bf16[2,128,512]{2,1,0:T(8,128)(2,1)S(1)}, u32[]{:S(2)}, u32[]{:S(2)}) collective-permute-start(bf16[2,128,512]{2,1,0:T(8,128)(2,1)S(1)} %collective-permute-done.30.refs_2_), channel_id=1, source_target_pairs={{0,8},{1,9},{2,10},{3,11},{4,12},{5,13},{6,14},{7,15},{8,0},{9,1},... | collective-permute-start | bytes 786440 | tf_op jit(solution)/shard_map/ppermute | solution.py:400
  141.4 10.9 %collective-permute-start.35 = (bf16[2,128,512]{2,1,0:T(8,128)(2,1)S(1)}, bf16[2,128,512]{2,1,0:T(8,128)(2,1)S(1)}, u32[]{:S(2)}, u32[]{:S(2)}) collective-permute-start(bf16[2,128,512]{2,1,0:T(8,128)(2,1)S(1)} %collective-permute-done.34.refs_6_), channel_id=1, source_target_pairs={{0,8},{1,9},{2,10},{3,11},{4,12},{5,13},{6,14},{7,15},{8,0},{9,1},... | collective-permute-start | bytes 786440 | tf_op jit(solution)/shard_map/ppermute | solution.py:400
  157.6 19.5 %collective-permute-start.36 = (bf16[128,1024]{1,0:T(8,128)(2,1)S(1)}, bf16[128,1024]{1,0:T(8,128)(2,1)S(1)}, u32[]{:S(2)}, u32[]{:S(2)}) collective-permute-start(bf16[128,1024]{1,0:T(8,128)(2,1)S(1)} %get-tuple-element.47), channel_id=1, source_target_pairs={{0,24},{1,16},{2,26},{3,18},{4,28},{5,20},{6,30},{7,22},{8,0},{9,8... | collective-permute-start | bytes 786440 | tf_op jit(solution)/shard_map/ppermute | solution.py:400
  162.8 14.3 %collective-permute-start.37 = (bf16[128,1024]{1,0:T(8,128)(2,1)S(1)}, bf16[128,1024]{1,0:T(8,128)(2,1)S(1)}, u32[]{:S(2)}, u32[]{:S(2)}) collective-permute-start(bf16[128,1024]{1,0:T(8,128)(2,1)S(1)} %get-tuple-element.48), channel_id=1, source_target_pairs={{0,0},{1,8},{2,2},{3,10},{4,4},{5,12},{6,6},{7,14},{8,24},{9,16},{... | collective-permute-start | bytes 786440 | tf_op jit(solution)/shard_map/ppermute | solution.py:400

commit v8 on v7

--- a/solution.py
+++ b/solution.py
@@ -291,7 +291,7 @@
         ],
         compiler_params=pltpu.CompilerParams(vmem_limit_bytes=VMEM_LIMIT),
         cost_estimate=pl.CostEstimate(
-            flops=60 * work, bytes_accessed=4 << 20, transcendentals=4 * stacked * 16 * rows
+            flops=150 * work, bytes_accessed=4 << 20, transcendentals=4 * stacked * 16 * rows
         ),
     )(place, queries, *kv)
 

time: 179 us -> 179 us (level)
  no operation moved by 1% of the time
where the time goes in v8:
time: 179 us; the launch traced here: 178 us
  waiting for transfers between devices  105 us (59%)
  starting transfers between devices  41.8 us (23%)
  Pallas kernels  21.3 us (12%)
  other arithmetic  5.33 us (3%)
  local copies, waits for them, and re-layouts  4.38 us (2%)
    ppermute x38, waiting for transfers between devices, __call__(): self.there[name] = lax.ppermute(array, AXES, moves(target))  105 us
    ppermute x38, starting transfers between devices, __call__(): self.there[name] = lax.ppermute(array, AXES, moves(target))  41.8 us
    pallas_call x2, Pallas kernels, project(): pl.pallas_call(functools.partial(kernel, plan), out_shape=jax.ShapeDtypeS...  8.91 us
    pallas_call x1, Pallas kernels, attend(): pl.pallas_call(attend_kernel, out_shape=(shape, shape), in_specs=[smem_sp...  7.07 us
    pallas_call x1, Pallas kernels, project_out(): pl.pallas_call(output_kernel, out_shape=(shape, shape), in_specs=[smem_sp...  5.3 us
  transfers between devices with their start and end apart: 38, of which 22 were waited for; matrix products, arithmetic and copies ran while one was open for 4% of the time, Pallas kernels for 6%

profile of v8, /device:TPU:0, one launch (start us, length us, event | category | flops | bytes accessed | tf_op | source)
XLA Modules:
  0.0 178.0 jit_solution(18402554317723650458)
XLA Ops:
  0.0 2.9 %collective-permute-start = (bf16[128,2048]{1,0:T(8,128)(2,1)}, bf16[128,2048]{1,0:T(8,128)(2,1)S(1)}, u32[]{:S(2)}, u32[]{:S(2)}) collective-permute-start(bf16[128,2048]{1,0:T(8,128)(2,1)} %refs_0_.3), channel_id=1, source_target_pairs={{0,1},{1,0},{2,3},{3,2},{4,5},{5,4},{6,7},{7,6},{8,9},{9,8},{10,11... | collective-permute-start | bytes 1572872 | tf_op jit(solution)/shard_map/ppermute | solution.py:400
  2.9 2.6 %collective-permute-start.3 = (bf16[128,2048]{1,0:T(8,128)(2,1)}, bf16[128,2048]{1,0:T(8,128)(2,1)S(1)}, u32[]{:S(2)}, u32[]{:S(2)}) collective-permute-start(bf16[128,2048]{1,0:T(8,128)(2,1)} %refs_0_.3), channel_id=1, source_target_pairs={{0,16},{1,17},{2,18},{3,19},{4,20},{5,21},{6,22},{7,23},{8,24},{9,... | collective-permute-start | bytes 1572872 | tf_op jit(solution)/shard_map/ppermute | solution.py:400
  5.5 1.6 collective-permute-start.1
  7.1 0.5 collective-permute-start.15
  7.6 2.1 %constant_dynamic-slice_fusion = (bf16[256,512]{1,0:T(8,128)(2,1)}, bf16[256,512]{1,0:T(8,128)(2,1)}, bf16[256,512]{1,0:T(8,128)(2,1)S(1)}, bf16[256,512]{1,0:T(8,128)(2,1)}) fusion(bf16[256,2048]{1,0:T(8,128)(2,1)} %param.6, s32[]{:T(128)S(6)} %select_n.58, s32[]{:T(128)S(6)} %select_n.53, s32[]{:T(128)S(6)} %select_n.52, s32[]{:T(128)S(6)} %select_n.57), kind=kLoop, calls=%fused_computation.24 | loop fusion | bytes 2097168 | tf_op jit(solution)/shard_map/dynamic_slice | solution.py:429
  9.8 0.1 constant_dynamic-slice_fusion.2
  10.0 1.6 collective-permute-start.5
  11.6 4.3 %collective-permute-done.refs_1_ = bf16[128,2048]{1,0:T(8,128)(2,1)S(1)} collective-permute-done((bf16[128,2048]{1,0:T(8,128)(2,1)}, bf16[128,2048]{1,0:T(8,128)(2,1)S(1)}, u32[]{:S(2)}, u32[]{:S(2)}) %collective-permute-start) | collective-permute-done | bytes 524320 | tf_op jit(solution)/shard_map/ppermute | solution.py:400
  15.9 2.1 %collective-permute-start.10 = (bf16[2048,256]{1,0:T(8,128)(2,1)S(1)}, bf16[2048,256]{1,0:T(8,128)(2,1)S(1)}, u32[]{:S(2)}, u32[]{:S(2)}) collective-permute-start(bf16[2048,256]{1,0:T(8,128)(2,1)S(1)} %copy-done.1), channel_id=1, source_target_pairs={{0,4},{1,5},{2,6},{3,7},{4,0},{5,1},{6,2},{7,3},{8,12},{9,13},{10,... | collective-permute-start | bytes 3145736 | tf_op jit(solution)/shard_map/ppermute | solution.py:400
  18.1 4.0 %collective-permute-done.5 = bf16[256,768]{1,0:T(8,128)(2,1)S(1)} collective-permute-done((bf16[256,768]{1,0:T(8,128)(2,1)S(1)}, bf16[256,768]{1,0:T(8,128)(2,1)S(1)}, u32[]{:S(2)}, u32[]{:S(2)}) %collective-permute-start.5) | collective-permute-done | bytes 393248 | tf_op jit(solution)/shard_map/ppermute | solution.py:400
  22.1 0.1 convert_bitcast_fusion
  22.2 12.5 %collective-permute-done.3.refs_4_ = bf16[128,2048]{1,0:T(8,128)(2,1)S(1)} collective-permute-done((bf16[128,2048]{1,0:T(8,128)(2,1)}, bf16[128,2048]{1,0:T(8,128)(2,1)S(1)}, u32[]{:S(2)}, u32[]{:S(2)}) %collective-permute-start.3) | collective-permute-done | bytes 524320 | tf_op jit(solution)/shard_map/ppermute | solution.py:400
  34.6 0.1 collective-permute-start.2
  34.7 3.8 %collective-permute-done.15.refs_10_ = bf16[2048,256]{1,0:T(8,128)(2,1)} collective-permute-done((bf16[2048,256]{1,0:T(8,128)(2,1)}, bf16[2048,256]{1,0:T(8,128)(2,1)}, u32[]{:S(2)}, u32[]{:S(2)}) %collective-permute-start.15) | collective-permute-done | bytes 1048608 | tf_op jit(solution)/shard_map/ppermute | solution.py:400
  38.5 2.1 %collective-permute-start.16 = (bf16[2048,256]{1,0:T(8,128)(2,1)}, bf16[2048,256]{1,0:T(8,128)(2,1)}, u32[]{:S(2)}, u32[]{:S(2)}) collective-permute-start(bf16[2048,256]{1,0:T(8,128)(2,1)} %collective-permute-done.15.refs_10_), channel_id=1, source_target_pairs={{0,4},{1,5},{2,6},{3,7},{4,0},{5,1},{6,2},{7,3},{8,12},{9,13},{10,... | collective-permute-start | bytes 3145736 | tf_op jit(solution)/shard_map/ppermute | solution.py:400
  40.6 0.7 pad_maximum_fusion.7
  41.3 3.2 %collective-permute-done.10.refs_12_ = bf16[2048,256]{1,0:T(8,128)(2,1)S(1)} collective-permute-done((bf16[2048,256]{1,0:T(8,128)(2,1)S(1)}, bf16[2048,256]{1,0:T(8,128)(2,1)S(1)}, u32[]{:S(2)}, u32[]{:S(2)}) %collective-permute-start.10) | collective-permute-done | bytes 1048608 | tf_op jit(solution)/shard_map/ppermute | solution.py:400
  44.6 1.0 copy-done.3
  45.6 1.8 %fusion = (f32[512,64]{1,0:T(8,128)S(1)}, f32[512,64]{1,0:T(8,128)}, f32[512,64]{1,0:T(8,128)}) fusion(f32[64]{0:T(128)S(1)} %multiply_power_fusion, f32[512]{0:T(512)S(1)} %convert_bitcast_fusion), kind=kLoop, calls=%fused_computation.21 | loop fusion | flops 65536 | bytes 395520 | tf_op jit(solution)/shard_map/neg | solution.py:468
  47.4 1.5 collective-permute-start.4
  48.9 0.1 pad_add_fusion.place
  49.0 1.3 pad_maximum_fusion.8
  50.3 1.4 collective-permute-start.13
  51.7 3.0 %collective-permute-start.14 = (bf16[256,512]{1,0:T(8,128)(2,1)}, bf16[256,512]{1,0:T(8,128)(2,1)S(1)}, u32[]{:S(2)}, u32[]{:S(2)}) collective-permute-start(bf16[256,512]{1,0:T(8,128)(2,1)} %get-tuple-element.35), channel_id=1, source_target_pairs={{0,24},{1,25},{2,26},{3,27},{4,28},{5,29},{6,30},{7,31},{8,16},{9,... | collective-permute-start | bytes 786440 | tf_op jit(solution)/shard_map/ppermute | solution.py:400
  54.8 1.0 fusion.2
  55.8 4.2 %collective-permute-done.4.refs_5_ = bf16[128,2048]{1,0:T(8,128)(2,1)S(1)} collective-permute-done((bf16[128,2048]{1,0:T(8,128)(2,1)S(1)}, bf16[128,2048]{1,0:T(8,128)(2,1)S(1)}, u32[]{:S(2)}, u32[]{:S(2)}) %collective-permute-start.4) | collective-permute-done | bytes 524320 | tf_op jit(solution)/shard_map/ppermute | solution.py:400
  60.0 4.8 %collective-permute-done.16.refs_14_ = bf16[2048,256]{1,0:T(8,128)(2,1)} collective-permute-done((bf16[2048,256]{1,0:T(8,128)(2,1)}, bf16[2048,256]{1,0:T(8,128)(2,1)}, u32[]{:S(2)}, u32[]{:S(2)}) %collective-permute-start.16) | collective-permute-done | bytes 1048608 | tf_op jit(solution)/shard_map/ppermute | solution.py:400
  64.8 1.5 collective-permute-start.17
  66.3 0.1 pad_maximum_fusion.refs_8_
  66.4 1.6 collective-permute-start.7
  68.0 2.3 %collective-permute-done.13 = bf16[256,512]{1,0:T(8,128)(2,1)S(1)} collective-permute-done((bf16[256,512]{1,0:T(8,128)(2,1)}, bf16[256,512]{1,0:T(8,128)(2,1)S(1)}, u32[]{:S(2)}, u32[]{:S(2)}) %collective-permute-start.13) | collective-permute-done | bytes 262176 | tf_op jit(solution)/shard_map/ppermute | solution.py:400
  70.3 1.5 collective-permute-start.19
  71.9 1.9 %collective-permute-done.17.refs_11_ = bf16[3,256,256]{2,1,0:T(8,128)(2,1)S(1)} collective-permute-done((bf16[3,256,256]{2,1,0:T(8,128)(2,1)S(1)}, bf16[3,256,256]{2,1,0:T(8,128)(2,1)S(1)}, u32[]{:S(2)}, u32[]{:S(2)}) %collective-permute-start.17) | collective-permute-done | bytes 393248 | tf_op jit(solution)/shard_map/ppermute | solution.py:400
  73.8 1.5 collective-permute-start.18
  75.4 0.1 pad_maximum_fusion.1
  75.4 2.4 %collective-permute-done.7.refs_7_ = bf16[128,2048]{1,0:T(8,128)(2,1)S(1)} collective-permute-done((bf16[128,2048]{1,0:T(8,128)(2,1)S(1)}, bf16[128,2048]{1,0:T(8,128)(2,1)S(1)}, u32[]{:S(2)}, u32[]{:S(2)}) %collective-permute-start.7) | collective-permute-done | bytes 524320 | tf_op jit(solution)/shard_map/ppermute | solution.py:400
  77.8 12.6 %collective-permute-done.18 = bf16[2,256,512]{2,1,0:T(8,128)(2,1)S(1)} collective-permute-done((bf16[2,256,512]{2,1,0:T(8,128)(2,1)S(1)}, bf16[2,256,512]{2,1,0:T(8,128)(2,1)S(1)}, u32[]{:S(2)}, u32[]{:S(2)}) %collective-permute-start.18) | collective-permute-done | bytes 524320 | tf_op jit(solution)/shard_map/ppermute | solution.py:400
  90.6 4.9 %shard_map.55.kv0 = bf16[4,128,256]{2,1,0:T(8,128)(2,1)S(1)} custom-call(s32[2]{0:T(128)S(1)} %pad_add_fusion.place, bf16[128,2048]{1,0:T(8,128)(2,1)S(1)} %copy-done, bf16[128,2048]{1,0:T(8,128)(2,1)S(1)} %collective-permute-done.refs_1_, bf16[128,2048]{1,0:T(8,128)(2,1)S(1)} %collective-permute-done.1.refs_2_, ...), custom_call_target="tpu_custom_call" | custom-call | flops 1073741824 | bytes 8388608 | tf_op jit(solution)/shard_map/pallas_call | solution.py:208
  95.6 0.1 collective-permute-start.21
  95.6 1.6 collective-permute-start.23
  97.2 0.2 collective-permute-start.22
  97.4 1.6 collective-permute-done.21.refs_11_
  99.0 4.0 %shard_map.56.queries = bf16[4,512,128]{2,1,0:T(8,128)(2,1)S(1)} custom-call(s32[2]{0:T(128)S(1)} %pad_add_fusion.place, bf16[128,2048]{1,0:T(8,128)(2,1)S(1)} %copy-done, bf16[128,2048]{1,0:T(8,128)(2,1)S(1)} %collective-permute-done.refs_1_, bf16[128,2048]{1,0:T(8,128)(2,1)S(1)} %collective-permute-done.1.refs_2_, ...), custom_call_target="tpu_custom_call" | custom-call | flops 1073741824 | bytes 8388608 | tf_op jit(solution)/shard_map/pallas_call | solution.py:208
  103.0 1.3 collective-permute-done.23.kv2
  104.4 0.5 collective-permute-start.25
  104.9 0.5 collective-permute-start.27
  105.5 0.4 collective-permute-done.24.kv3
  105.9 7.1 %shard_map.57 = (bf16[2,128,512]{2,1,0:T(8,128)(2,1)S(1)}, bf16[2,128,512]{2,1,0:T(8,128)(2,1)S(1)}) custom-call(s32[2]{0:T(128)S(1)} %pad_add_fusion.place, bf16[4,512,128]{2,1,0:T(8,128)(2,1)S(1)} %shard_map.56.queries, bf16[4,128,256]{2,1,0:T(8,128)(2,1)S(1)} %shard_map.55.kv0, bf16[4,128,256]{2,1,0:T(8,128)(2,1)S(1)} %collective-permute-done.22.kv1, ...), custom_call_target="tpu_custom_call" | custom-call | flops 80530636800 | bytes 4194304 | tf_op jit(solution)/shard_map/pallas_call | solution.py:283
  113.0 1.6 collective-permute-start.32
  114.6 1.0 collective-permute-start.29
  115.5 2.8 %collective-permute-start.30 = (bf16[2,128,512]{2,1,0:T(8,128)(2,1)S(1)}, bf16[2,128,512]{2,1,0:T(8,128)(2,1)S(1)}, u32[]{:S(2)}, u32[]{:S(2)}) collective-permute-start(bf16[2,128,512]{2,1,0:T(8,128)(2,1)S(1)} %get-tuple-element.42.refs_0_), channel_id=1, source_target_pairs={{0,16},{1,17},{2,18},{3,19},{4,20},{5,21},{6,22},{7,23},{8,24},{9,... | collective-permute-start | bytes 786440 | tf_op jit(solution)/shard_map/ppermute | solution.py:400
  118.3 3.1 %collective-permute-done.32.refs_4_ = bf16[2,128,512]{2,1,0:T(8,128)(2,1)S(1)} collective-permute-done((bf16[2,128,512]{2,1,0:T(8,128)(2,1)S(1)}, bf16[2,128,512]{2,1,0:T(8,128)(2,1)S(1)}, u32[]{:S(2)}, u32[]{:S(2)}) %collective-permute-start.32) | collective-permute-done | bytes 262176 | tf_op jit(solution)/shard_map/ppermute | solution.py:400
  121.4 2.1 %collective-permute-start.34 = (bf16[2,128,512]{2,1,0:T(8,128)(2,1)S(1)}, bf16[2,128,512]{2,1,0:T(8,128)(2,1)S(1)}, u32[]{:S(2)}, u32[]{:S(2)}) collective-permute-start(bf16[2,128,512]{2,1,0:T(8,128)(2,1)S(1)} %collective-permute-done.32.refs_4_), channel_id=1, source_target_pairs={{0,16},{1,17},{2,18},{3,19},{4,20},{5,21},{6,22},{7,23},{8,24},{9,... | collective-permute-start | bytes 786440 | tf_op jit(solution)/shard_map/ppermute | solution.py:400
  123.5 4.5 %collective-permute-done.29.refs_1_ = bf16[2,128,512]{2,1,0:T(8,128)(2,1)S(1)} collective-permute-done((bf16[2,128,512]{2,1,0:T(8,128)(2,1)S(1)}, bf16[2,128,512]{2,1,0:T(8,128)(2,1)S(1)}, u32[]{:S(2)}, u32[]{:S(2)}) %collective-permute-start.29) | collective-permute-done | bytes 262176 | tf_op jit(solution)/shard_map/ppermute | solution.py:400
  128.0 8.3 %collective-permute-done.30.refs_2_ = bf16[2,128,512]{2,1,0:T(8,128)(2,1)S(1)} collective-permute-done((bf16[2,128,512]{2,1,0:T(8,128)(2,1)S(1)}, bf16[2,128,512]{2,1,0:T(8,128)(2,1)S(1)}, u32[]{:S(2)}, u32[]{:S(2)}) %collective-permute-start.30) | collective-permute-done | bytes 262176 | tf_op jit(solution)/shard_map/ppermute | solution.py:400
  136.3 5.0 %collective-permute-done.34.refs_6_ = bf16[2,128,512]{2,1,0:T(8,128)(2,1)S(1)} collective-permute-done((bf16[2,128,512]{2,1,0:T(8,128)(2,1)S(1)}, bf16[2,128,512]{2,1,0:T(8,128)(2,1)S(1)}, u32[]{:S(2)}, u32[]{:S(2)}) %collective-permute-start.34) | collective-permute-done | bytes 262176 | tf_op jit(solution)/shard_map/ppermute | solution.py:400
  141.4 1.7 collective-permute-done.33.refs_5_
  143.1 5.6 %collective-permute-done.31.refs_3_ = bf16[2,128,512]{2,1,0:T(8,128)(2,1)S(1)} collective-permute-done((bf16[2,128,512]{2,1,0:T(8,128)(2,1)S(1)}, bf16[2,128,512]{2,1,0:T(8,128)(2,1)S(1)}, u32[]{:S(2)}, u32[]{:S(2)}) %collective-permute-start.31) | collective-permute-done | bytes 262176 | tf_op jit(solution)/shard_map/ppermute | solution.py:400
  148.7 3.6 %collective-permute-done.35.refs_7_ = bf16[2,128,512]{2,1,0:T(8,128)(2,1)S(1)} collective-permute-done((bf16[2,128,512]{2,1,0:T(8,128)(2,1)S(1)}, bf16[2,128,512]{2,1,0:T(8,128)(2,1)S(1)}, u32[]{:S(2)}, u32[]{:S(2)}) %collective-permute-start.35) | collective-permute-done | bytes 262176 | tf_op jit(solution)/shard_map/ppermute | solution.py:400
  152.3 5.3 %shard_map.58 = (bf16[128,1024]{1,0:T(8,128)(2,1)S(1)}, bf16[128,1024]{1,0:T(8,128)(2,1)S(1)}) custom-call(s32[2]{0:T(128)S(1)} %pad_add_fusion.place, bf16[2,128,512]{2,1,0:T(8,128)(2,1)S(1)} %get-tuple-element.42.refs_0_, bf16[2,128,512]{2,1,0:T(8,128)(2,1)S(1)} %collective-permute-done.29.refs_1_, ...), custom_call_target="tpu_custom_call" | custom-call | flops 2147483648 | bytes 12582912 | tf_op jit(solution)/shard_map/pallas_call | solution.py:352
  157.6 5.2 %collective-permute-start.36 = (bf16[128,1024]{1,0:T(8,128)(2,1)S(1)}, bf16[128,1024]{1,0:T(8,128)(2,1)S(1)}, u32[]{:S(2)}, u32[]{:S(2)}) collective-permute-start(bf16[128,1024]{1,0:T(8,128)(2,1)S(1)} %get-tuple-element.47), channel_id=1, source_target_pairs={{0,24},{1,16},{2,26},{3,18},{4,28},{5,20},{6,30},{7,22},{8,0},{9,8... | collective-permute-start | bytes 786440 | tf_op jit(solution)/shard_map/ppermute | solution.py:400
  162.8 0.7 collective-permute-start.37
  163.6 13.5 %collective-permute-done.36 = bf16[128,1024]{1,0:T(8,128)(2,1)S(1)} collective-permute-done((bf16[128,1024]{1,0:T(8,128)(2,1)S(1)}, bf16[128,1024]{1,0:T(8,128)(2,1)S(1)}, u32[]{:S(2)}, u32[]{:S(2)}) %collective-permute-start.36) | collective-permute-done | bytes 262176 | tf_op jit(solution)/shard_map/ppermute | solution.py:400
  177.1 0.8 pad_maximum_fusion.3
  (62 shorter events, 0.6 us)
Async XLA Ops:
  0.0 9.8 %copy-start.8 = (bf16[256,512]{1,0:T(8,128)(2,1)S(1)}, bf16[256,512]{1,0:T(8,128)(2,1)}, u32[]{:S(2)}) copy-start(bf16[256,512]{1,0:T(8,128)(2,1)} %param.7) | copy-start | bytes 786436
  0.0 9.8 %copy-start.7 = (bf16[256,512]{1,0:T(8,128)(2,1)S(1)}, bf16[256,512]{1,0:T(8,128)(2,1)}, u32[]{:S(2)}) copy-start(bf16[256,512]{1,0:T(8,128)(2,1)} %param.8) | copy-start | bytes 786436
  0.0 15.9 %collective-permute-start = (bf16[128,2048]{1,0:T(8,128)(2,1)}, bf16[128,2048]{1,0:T(8,128)(2,1)S(1)}, u32[]{:S(2)}, u32[]{:S(2)}) collective-permute-start(bf16[128,2048]{1,0:T(8,128)(2,1)} %refs_0_.3), channel_id=1, source_target_pairs={{0,1},{1,0},{2,3},{3,2},{4,5},{5,4},{6,7},{7,6},{8,9},{9,8},{10,11... | collective-permute-start | bytes 1572872 | tf_op jit(solution)/shard_map/ppermute | solution.py:400
  2.9 31.7 %collective-permute-start.3 = (bf16[128,2048]{1,0:T(8,128)(2,1)}, bf16[128,2048]{1,0:T(8,128)(2,1)S(1)}, u32[]{:S(2)}, u32[]{:S(2)}) collective-permute-start(bf16[128,2048]{1,0:T(8,128)(2,1)} %refs_0_.3), channel_id=1, source_target_pairs={{0,16},{1,17},{2,18},{3,19},{4,20},{5,21},{6,22},{7,23},{8,24},{9,... | collective-permute-start | bytes 1572872 | tf_op jit(solution)/shard_map/ppermute | solution.py:400
  5.5 29.1 %collective-permute-start.1 = (bf16[128,2048]{1,0:T(8,128)(2,1)}, bf16[128,2048]{1,0:T(8,128)(2,1)S(1)}, u32[]{:S(2)}, u32[]{:S(2)}) collective-permute-start(bf16[128,2048]{1,0:T(8,128)(2,1)} %refs_0_.3), channel_id=1, source_target_pairs={{0,8},{1,9},{2,10},{3,11},{4,12},{5,13},{6,14},{7,15},{8,0},{9,1},... | collective-permute-start | bytes 1572872 | tf_op jit(solution)/shard_map/ppermute | solution.py:400
  7.1 31.4 %collective-permute-start.15 = (bf16[2048,256]{1,0:T(8,128)(2,1)}, bf16[2048,256]{1,0:T(8,128)(2,1)}, u32[]{:S(2)}, u32[]{:S(2)}) collective-permute-start(bf16[2048,256]{1,0:T(8,128)(2,1)} %refs_8_.1), channel_id=1, source_target_pairs={{0,1},{1,0},{2,3},{3,2},{4,5},{5,4},{6,7},{7,6},{8,9},{9,8},{10,11... | collective-permute-start | bytes 3145736 | tf_op jit(solution)/shard_map/ppermute | solution.py:400
  9.8 6.1 %copy-start.1 = (bf16[2048,256]{1,0:T(8,128)(2,1)S(1)}, bf16[2048,256]{1,0:T(8,128)(2,1)}, u32[]{:S(2)}) copy-start(bf16[2048,256]{1,0:T(8,128)(2,1)} %refs_8_.1) | copy-start | bytes 3145732
  10.0 12.1 %collective-permute-start.5 = (bf16[256,768]{1,0:T(8,128)(2,1)S(1)}, bf16[256,768]{1,0:T(8,128)(2,1)S(1)}, u32[]{:S(2)}, u32[]{:S(2)}) collective-permute-start(bf16[256,768]{1,0:T(8,128)(2,1)S(1)} %get-tuple-element.56), channel_id=1, source_target_pairs={{0,4},{1,5},{2,6},{3,7},{4,0},{5,1},{6,2},{7,3},{8,12},{9,13},{10,... | collective-permute-start | bytes 1179656 | tf_op jit(solution)/shard_map/ppermute | solution.py:400
  15.9 28.7 %collective-permute-start.10 = (bf16[2048,256]{1,0:T(8,128)(2,1)S(1)}, bf16[2048,256]{1,0:T(8,128)(2,1)S(1)}, u32[]{:S(2)}, u32[]{:S(2)}) collective-permute-start(bf16[2048,256]{1,0:T(8,128)(2,1)S(1)} %copy-done.1), channel_id=1, source_target_pairs={{0,4},{1,5},{2,6},{3,7},{4,0},{5,1},{6,2},{7,3},{8,12},{9,13},{10,... | collective-permute-start | bytes 3145736 | tf_op jit(solution)/shard_map/ppermute | solution.py:400
  22.1 12.5 %copy-start.5 = (bf16[256,768]{1,0:T(8,128)(2,1)}, bf16[256,768]{1,0:T(8,128)(2,1)S(1)}, u32[]{:S(2)}) copy-start(bf16[256,768]{1,0:T(8,128)(2,1)S(1)} %collective-permute-done.5) | copy-start | bytes 1179652
  22.1 18.5 %collective-permute-start.9 = (bf16[2,256,256]{2,1,0:T(8,128)(2,1)S(1)}, bf16[2,256,256]{2,1,0:T(8,128)(2,1)S(1)}, u32[]{:S(2)}, u32[]{:S(2)}) collective-permute-start(bf16[2,256,256]{2,1,0:T(8,128)(2,1)S(1)} %pad_maximum_fusion.6), channel_id=1, source_target_pairs={{0,16},{1,17},{2,18},{3,19},{4,20},{5,21},{6,22},{7,23},{8,24},{9,... | collective-permute-start | bytes 786440 | tf_op jit(solution)/shard_map/ppermute | solution.py:400
  34.6 15.7 %collective-permute-start.6 = (bf16[128,2048]{1,0:T(8,128)(2,1)S(1)}, bf16[128,2048]{1,0:T(8,128)(2,1)S(1)}, u32[]{:S(2)}, u32[]{:S(2)}) collective-permute-start(bf16[128,2048]{1,0:T(8,128)(2,1)S(1)} %collective-permute-done.3.refs_4_), channel_id=1, source_target_pairs={{0,8},{1,9},{2,10},{3,11},{4,12},{5,13},{6,14},{7,15},{8,0},{9,1},... | collective-permute-start | bytes 1572872 | tf_op jit(solution)/shard_map/ppermute | solution.py:400
  34.6 17.1 %collective-permute-start.2 = (bf16[128,2048]{1,0:T(8,128)(2,1)S(1)}, bf16[128,2048]{1,0:T(8,128)(2,1)S(1)}, u32[]{:S(2)}, u32[]{:S(2)}) collective-permute-start(bf16[128,2048]{1,0:T(8,128)(2,1)S(1)} %collective-permute-done.1.refs_2_), channel_id=1, source_target_pairs={{0,1},{1,0},{2,3},{3,2},{4,5},{5,4},{6,7},{7,6},{8,9},{9,8},{10,11... | collective-permute-start | bytes 1572872 | tf_op jit(solution)/shard_map/ppermute | solution.py:400
  38.5 26.3 %collective-permute-start.16 = (bf16[2048,256]{1,0:T(8,128)(2,1)}, bf16[2048,256]{1,0:T(8,128)(2,1)}, u32[]{:S(2)}, u32[]{:S(2)}) collective-permute-start(bf16[2048,256]{1,0:T(8,128)(2,1)} %collective-permute-done.15.refs_10_), channel_id=1, source_target_pairs={{0,4},{1,5},{2,6},{3,7},{4,0},{5,1},{6,2},{7,3},{8,12},{9,13},{10,... | collective-permute-start | bytes 3145736 | tf_op jit(solution)/shard_map/ppermute | solution.py:400
  44.6 1.0 copy-start.3
  45.6 9.2 %collective-permute-start.11 = (bf16[2,256,256]{2,1,0:T(8,128)(2,1)}, bf16[2,256,256]{2,1,0:T(8,128)(2,1)}, u32[]{:S(2)}, u32[]{:S(2)}) collective-permute-start(bf16[2,256,256]{2,1,0:T(8,128)(2,1)} %pad_maximum_fusion.7), channel_id=1, source_target_pairs={{0,8},{1,9},{2,10},{3,11},{4,12},{5,13},{6,14},{7,15},{8,0},{9,1},... | collective-permute-start | bytes 786440 | tf_op jit(solution)/shard_map/ppermute | solution.py:400
  47.4 18.9 %copy-start.6 = (bf16[256,768]{1,0:T(8,128)(2,1)S(1)}, bf16[256,768]{1,0:T(8,128)(2,1)}, u32[]{:S(2)}) copy-start(bf16[256,768]{1,0:T(8,128)(2,1)} %copy-done.5) | copy-start | bytes 1179652
  47.4 12.6 %collective-permute-start.4 = (bf16[128,2048]{1,0:T(8,128)(2,1)S(1)}, bf16[128,2048]{1,0:T(8,128)(2,1)S(1)}, u32[]{:S(2)}, u32[]{:S(2)}) collective-permute-start(bf16[128,2048]{1,0:T(8,128)(2,1)S(1)} %collective-permute-done.3.refs_4_), channel_id=1, source_target_pairs={{0,1},{1,0},{2,3},{3,2},{4,5},{5,4},{6,7},{7,6},{8,9},{9,8},{10,11... | collective-permute-start | bytes 1572872 | tf_op jit(solution)/shard_map/ppermute | solution.py:400
  50.3 20.0 %collective-permute-start.13 = (bf16[256,512]{1,0:T(8,128)(2,1)}, bf16[256,512]{1,0:T(8,128)(2,1)S(1)}, u32[]{:S(2)}, u32[]{:S(2)}) collective-permute-start(bf16[256,512]{1,0:T(8,128)(2,1)} %get-tuple-element.34), channel_id=1, source_target_pairs={{0,16},{1,17},{2,18},{3,19},{4,20},{5,21},{6,22},{7,23},{8,24},{9,... | collective-permute-start | bytes 786440 | tf_op jit(solution)/shard_map/ppermute | solution.py:400
  51.7 20.1 %collective-permute-start.14 = (bf16[256,512]{1,0:T(8,128)(2,1)}, bf16[256,512]{1,0:T(8,128)(2,1)S(1)}, u32[]{:S(2)}, u32[]{:S(2)}) collective-permute-start(bf16[256,512]{1,0:T(8,128)(2,1)} %get-tuple-element.35), channel_id=1, source_target_pairs={{0,24},{1,25},{2,26},{3,27},{4,28},{5,29},{6,30},{7,31},{8,16},{9,... | collective-permute-start | bytes 786440 | tf_op jit(solution)/shard_map/ppermute | solution.py:400
  54.8 15.5 %collective-permute-start.12 = (bf16[256,512]{1,0:T(8,128)(2,1)}, bf16[256,512]{1,0:T(8,128)(2,1)S(1)}, u32[]{:S(2)}, u32[]{:S(2)}) collective-permute-start(bf16[256,512]{1,0:T(8,128)(2,1)} %get-tuple-element.33), channel_id=1, source_target_pairs={{0,8},{1,9},{2,10},{3,11},{4,12},{5,13},{6,14},{7,15},{8,0},{9,1},... | collective-permute-start | bytes 786440 | tf_op jit(solution)/shard_map/ppermute | solution.py:400
  64.8 9.0 %collective-permute-start.17 = (bf16[3,256,256]{2,1,0:T(8,128)(2,1)S(1)}, bf16[3,256,256]{2,1,0:T(8,128)(2,1)S(1)}, u32[]{:S(2)}, u32[]{:S(2)}) collective-permute-start(bf16[3,256,256]{2,1,0:T(8,128)(2,1)S(1)} %pad_maximum_fusion.5.refs_10_), channel_id=1, source_target_pairs={{0,4},{1,5},{2,6},{3,7},{4,0},{5,1},{6,2},{7,3},{8,12},{9,13},{10,... | collective-permute-start | bytes 1179656 | tf_op jit(solution)/shard_map/ppermute | solution.py:400
  66.4 11.4 %collective-permute-start.7 = (bf16[128,2048]{1,0:T(8,128)(2,1)S(1)}, bf16[128,2048]{1,0:T(8,128)(2,1)S(1)}, u32[]{:S(2)}, u32[]{:S(2)}) collective-permute-start(bf16[128,2048]{1,0:T(8,128)(2,1)S(1)} %collective-permute-done.6.refs_6_), channel_id=1, source_target_pairs={{0,1},{1,0},{2,3},{3,2},{4,5},{5,4},{6,7},{7,6},{8,9},{9,8},{10,11... | collective-permute-start | bytes 1572872 | tf_op jit(solution)/shard_map/ppermute | solution.py:400
  70.3 20.3 %collective-permute-start.8 = (bf16[2,256,768]{2,1,0:T(8,128)(2,1)S(1)}, bf16[2,256,768]{2,1,0:T(8,128)(2,1)S(1)}, u32[]{:S(2)}, u32[]{:S(2)}) collective-permute-start(bf16[2,256,768]{2,1,0:T(8,128)(2,1)S(1)} %pad_maximum_fusion.refs_8_), channel_id=1, source_target_pairs={{0,2},{1,3},{2,0},{3,1},{4,6},{5,7},{6,4},{7,5},{8,10},{9,11},{10,... | collective-permute-start | bytes 2359304 | tf_op jit(solution)/shard_map/ppermute | solution.py:400
  70.3 20.2 %collective-permute-start.19 = (bf16[256,512]{1,0:T(8,128)(2,1)S(1)}, bf16[256,512]{1,0:T(8,128)(2,1)S(1)}, u32[]{:S(2)}, u32[]{:S(2)}) collective-permute-start(bf16[256,512]{1,0:T(8,128)(2,1)S(1)} %collective-permute-done.13), channel_id=1, source_target_pairs={{0,4},{1,5},{2,6},{3,7},{4,0},{5,1},{6,2},{7,3},{8,12},{9,13},{10,... | collective-permute-start | bytes 786440 | tf_op jit(solution)/shard_map/ppermute | solution.py:400
  73.8 16.7 %collective-permute-start.18 = (bf16[2,256,512]{2,1,0:T(8,128)(2,1)S(1)}, bf16[2,256,512]{2,1,0:T(8,128)(2,1)S(1)}, u32[]{:S(2)}, u32[]{:S(2)}) collective-permute-start(bf16[2,256,512]{2,1,0:T(8,128)(2,1)S(1)} %pad_maximum_fusion.2), channel_id=1, source_target_pairs={{0,4},{1,5},{2,6},{3,7},{4,0},{5,1},{6,2},{7,3},{8,12},{9,13},{10,... | collective-permute-start | bytes 1572872 | tf_op jit(solution)/shard_map/ppermute | solution.py:400
  75.3 15.2 %copy-start = (bf16[128,2048]{1,0:T(8,128)(2,1)S(1)}, bf16[128,2048]{1,0:T(8,128)(2,1)}, u32[]{:S(2)}) copy-start(bf16[128,2048]{1,0:T(8,128)(2,1)} %refs_0_.3) | copy-start | bytes 1572868
  77.8 12.8 %collective-permute-start.20 = (bf16[6,256,256]{2,1,0:T(8,128)(2,1)S(1)}, bf16[6,256,256]{2,1,0:T(8,128)(2,1)S(1)}, u32[]{:S(2)}, u32[]{:S(2)}) collective-permute-start(bf16[6,256,256]{2,1,0:T(8,128)(2,1)S(1)} %pad_maximum_fusion.1), channel_id=1, source_target_pairs={{0,2},{1,3},{2,0},{3,1},{4,6},{5,7},{6,4},{7,5},{8,10},{9,11},{10,... | collective-permute-start | bytes 2359304 | tf_op jit(solution)/shard_map/ppermute | solution.py:400
  95.5 8.8 %copy-start.2 = (bf16[2048,256]{1,0:T(8,128)(2,1)S(1)}, bf16[2048,256]{1,0:T(8,128)(2,1)}, u32[]{:S(2)}) copy-start(bf16[2048,256]{1,0:T(8,128)(2,1)} %refs_8_.1) | copy-start | bytes 3145732
  95.5 9.3 %copy-start.4 = (bf16[2048,256]{1,0:T(8,128)(2,1)S(1)}, bf16[2048,256]{1,0:T(8,128)(2,1)}, u32[]{:S(2)}) copy-start(bf16[2048,256]{1,0:T(8,128)(2,1)} %copy-done.3) | copy-start | bytes 3145732
  95.6 3.5 %collective-permute-start.21 = (bf16[6,256,512]{2,1,0:T(8,128)(2,1)S(1)}, bf16[6,256,512]{2,1,0:T(8,128)(2,1)S(1)}, u32[]{:S(2)}, u32[]{:S(2)}) collective-permute-start(bf16[6,256,512]{2,1,0:T(8,128)(2,1)S(1)} %slice_dynamic-update-slice_fusion.refs_10_), channel_id=1, source_target_pairs={{0,2},{1,3},{2,0},{3,1},{4,6},{5,7},{6,4},{7,5},{8,10},{9,11},{10,... | collective-permute-start | bytes 4718600 | tf_op jit(solution)/shard_map/ppermute | solution.py:400
  95.6 8.7 %collective-permute-start.23 = (bf16[4,128,256]{2,1,0:T(8,128)(2,1)S(1)}, bf16[4,128,256]{2,1,0:T(8,128)(2,1)S(1)}, u32[]{:S(2)}, u32[]{:S(2)}) collective-permute-start(bf16[4,128,256]{2,1,0:T(8,128)(2,1)S(1)} %shard_map.55.kv0), channel_id=1, source_target_pairs={{0,4},{1,5},{2,6},{3,7},{4,0},{5,1},{6,2},{7,3},{8,12},{9,13},{10,... | collective-permute-start | bytes 786440 | tf_op jit(solution)/shard_map/ppermute | solution.py:400
  97.2 8.2 %collective-permute-start.22 = (bf16[4,128,256]{2,1,0:T(8,128)(2,1)S(1)}, bf16[4,128,256]{2,1,0:T(8,128)(2,1)S(1)}, u32[]{:S(2)}, u32[]{:S(2)}) collective-permute-start(bf16[4,128,256]{2,1,0:T(8,128)(2,1)S(1)} %shard_map.55.kv0), channel_id=1, source_target_pairs={{0,2},{1,3},{2,0},{3,1},{4,6},{5,7},{6,4},{7,5},{8,10},{9,11},{10,... | collective-permute-start | bytes 786440 | tf_op jit(solution)/shard_map/ppermute | solution.py:400
  104.4 1.5 collective-permute-start.24
  104.4 10.2 %collective-permute-start.25 = (bf16[2048,256]{1,0:T(8,128)(2,1)S(1)}, bf16[2048,256]{1,0:T(8,128)(2,1)S(1)}, u32[]{:S(2)}, u32[]{:S(2)}) collective-permute-start(bf16[2048,256]{1,0:T(8,128)(2,1)S(1)} %copy-done.2), channel_id=1, source_target_pairs={{0,2},{1,3},{2,0},{3,1},{4,6},{5,7},{6,4},{7,5},{8,10},{9,11},{10,... | collective-permute-start | bytes 3145736 | tf_op jit(solution)/shard_map/ppermute | solution.py:400
  104.9 8.1 %collective-permute-start.26 = (bf16[2048,256]{1,0:T(8,128)(2,1)}, bf16[2048,256]{1,0:T(8,128)(2,1)S(1)}, u32[]{:S(2)}, u32[]{:S(2)}) collective-permute-start(bf16[2048,256]{1,0:T(8,128)(2,1)} %collective-permute-done.15.refs_10_), channel_id=1, source_target_pairs={{0,2},{1,3},{2,0},{3,1},{4,6},{5,7},{6,4},{7,5},{8,10},{9,11},{10,... | collective-permute-start | bytes 3145736 | tf_op jit(solution)/shard_map/ppermute | solution.py:400
  104.9 8.1 %collective-permute-start.27 = (bf16[2048,256]{1,0:T(8,128)(2,1)S(1)}, bf16[2048,256]{1,0:T(8,128)(2,1)S(1)}, u32[]{:S(2)}, u32[]{:S(2)}) collective-permute-start(bf16[2048,256]{1,0:T(8,128)(2,1)S(1)} %copy-done.4), channel_id=1, source_target_pairs={{0,2},{1,3},{2,0},{3,1},{4,6},{5,7},{6,4},{7,5},{8,10},{9,11},{10,... | collective-permute-start | bytes 3145736 | tf_op jit(solution)/shard_map/ppermute | solution.py:400
  105.4 7.6 %collective-permute-start.28 = (bf16[2048,256]{1,0:T(8,128)(2,1)}, bf16[2048,256]{1,0:T(8,128)(2,1)S(1)}, u32[]{:S(2)}, u32[]{:S(2)}) collective-permute-start(bf16[2048,256]{1,0:T(8,128)(2,1)} %collective-permute-done.16.refs_14_), channel_id=1, source_target_pairs={{0,2},{1,3},{2,0},{3,1},{4,6},{5,7},{6,4},{7,5},{8,10},{9,11},{10,... | collective-permute-start | bytes 3145736 | tf_op jit(solution)/shard_map/ppermute | solution.py:400
  113.0 8.4 %collective-permute-start.32 = (bf16[2,128,512]{2,1,0:T(8,128)(2,1)S(1)}, bf16[2,128,512]{2,1,0:T(8,128)(2,1)S(1)}, u32[]{:S(2)}, u32[]{:S(2)}) collective-permute-start(bf16[2,128,512]{2,1,0:T(8,128)(2,1)S(1)} %get-tuple-element.44), channel_id=1, source_target_pairs={{0,1},{1,0},{2,3},{3,2},{4,5},{5,4},{6,7},{7,6},{8,9},{9,8},{10,11... | collective-permute-start | bytes 786440 | tf_op jit(solution)/shard_map/ppermute | solution.py:400
  114.6 13.5 %collective-permute-start.29 = (bf16[2,128,512]{2,1,0:T(8,128)(2,1)S(1)}, bf16[2,128,512]{2,1,0:T(8,128)(2,1)S(1)}, u32[]{:S(2)}, u32[]{:S(2)}) collective-permute-start(bf16[2,128,512]{2,1,0:T(8,128)(2,1)S(1)} %get-tuple-element.42.refs_0_), channel_id=1, source_target_pairs={{0,8},{1,9},{2,10},{3,11},{4,12},{5,13},{6,14},{7,15},{8,0},{9,1},... | collective-permute-start | bytes 786440 | tf_op jit(solution)/shard_map/ppermute | solution.py:400
  115.5 20.8 %collective-permute-start.30 = (bf16[2,128,512]{2,1,0:T(8,128)(2,1)S(1)}, bf16[2,128,512]{2,1,0:T(8,128)(2,1)S(1)}, u32[]{:S(2)}, u32[]{:S(2)}) collective-permute-start(bf16[2,128,512]{2,1,0:T(8,128)(2,1)S(1)} %get-tuple-element.42.refs_0_), channel_id=1, source_target_pairs={{0,16},{1,17},{2,18},{3,19},{4,20},{5,21},{6,22},{7,23},{8,24},{9,... | collective-permute-start | bytes 786440 | tf_op jit(solution)/shard_map/ppermute | solution.py:400
  121.4 20.0 %collective-permute-start.34 = (bf16[2,128,512]{2,1,0:T(8,128)(2,1)S(1)}, bf16[2,128,512]{2,1,0:T(8,128)(2,1)S(1)}, u32[]{:S(2)}, u32[]{:S(2)}) collective-permute-start(bf16[2,128,512]{2,1,0:T(8,128)(2,1)S(1)} %collective-permute-done.32.refs_4_), channel_id=1, source_target_pairs={{0,16},{1,17},{2,18},{3,19},{4,20},{5,21},{6,22},{7,23},{8,24},{9,... | collective-permute-start | bytes 786440 | tf_op jit(solution)/shard_map/ppermute | solution.py:400
  128.0 15.1 %collective-permute-start.33 = (bf16[2,128,512]{2,1,0:T(8,128)(2,1)S(1)}, bf16[2,128,512]{2,1,0:T(8,128)(2,1)S(1)}, u32[]{:S(2)}, u32[]{:S(2)}) collective-permute-start(bf16[2,128,512]{2,1,0:T(8,128)(2,1)S(1)} %collective-permute-done.32.refs_4_), channel_id=1, source_target_pairs={{0,8},{1,9},{2,10},{3,11},{4,12},{5,13},{6,14},{7,15},{8,0},{9,1},... | collective-permute-start | bytes 786440 | tf_op jit(solution)/shard_map/ppermute | solution.py:400
  136.3 12.4 %collective-permute-start.31 = (bf16[2,128,512]{2,1,0:T(8,128)(2,1)S(1)}, bf16[2,128,512]{2,1,0:T(8,128)(2,1)S(1)}, u32[]{:S(2)}, u32[]{:S(2)}) collective-permute-start(bf16[2,128,512]{2,1,0:T(8,128)(2,1)S(1)} %collective-permute-done.30.refs_2_), channel_id=1, source_target_pairs={{0,8},{1,9},{2,10},{3,11},{4,12},{5,13},{6,14},{7,15},{8,0},{9,1},... | collective-permute-start | bytes 786440 | tf_op jit(solution)/shard_map/ppermute | solution.py:400
  141.4 10.9 %collective-permute-start.35 = (bf16[2,128,512]{2,1,0:T(8,128)(2,1)S(1)}, bf16[2,128,512]{2,1,0:T(8,128)(2,1)S(1)}, u32[]{:S(2)}, u32[]{:S(2)}) collective-permute-start(bf16[2,128,512]{2,1,0:T(8,128)(2,1)S(1)} %collective-permute-done.34.refs_6_), channel_id=1, source_target_pairs={{0,8},{1,9},{2,10},{3,11},{4,12},{5,13},{6,14},{7,15},{8,0},{9,1},... | collective-permute-start | bytes 786440 | tf_op jit(solution)/shard_map/ppermute | solution.py:400
  157.6 19.5 %collective-permute-start.36 = (bf16[128,1024]{1,0:T(8,128)(2,1)S(1)}, bf16[128,1024]{1,0:T(8,128)(2,1)S(1)}, u32[]{:S(2)}, u32[]{:S(2)}) collective-permute-start(bf16[128,1024]{1,0:T(8,128)(2,1)S(1)} %get-tuple-element.47), channel_id=1, source_target_pairs={{0,24},{1,16},{2,26},{3,18},{4,28},{5,20},{6,30},{7,22},{8,0},{9,8... | collective-permute-start | bytes 786440 | tf_op jit(solution)/shard_map/ppermute | solution.py:400
  162.8 14.3 %collective-permute-start.37 = (bf16[128,1024]{1,0:T(8,128)(2,1)S(1)}, bf16[128,1024]{1,0:T(8,128)(2,1)S(1)}, u32[]{:S(2)}, u32[]{:S(2)}) collective-permute-start(bf16[128,1024]{1,0:T(8,128)(2,1)S(1)} %get-tuple-element.48), channel_id=1, source_target_pairs={{0,0},{1,8},{2,2},{3,10},{4,4},{5,12},{6,6},{7,14},{8,24},{9,16},{... | collective-permute-start | bytes 786440 | tf_op jit(solution)/shard_map/ppermute | solution.py:400
